TPU v7x, 32 devices: a whole 2x2x4 slice. The times are simulated.
32 devices in a mesh: ang: 8 (over z, y), pos: 4 (over x, core).
Axes of the slice: x: 2, y: 2, z: 4, core: 2. Of those that a mesh axis runs over, the one named last changes fastest.
Arguments:
- volume: bfloat16 [2, 256, 32768], P(None, 'ang', 'pos'), may hold values from -6 to 6
- radon_tiles: bfloat16 [32, 64, 256], replicated, may hold values from -0.375 to 0.375
- tile_blocks: int32 [32, 32, 4], replicated, may hold values from 0 to 511
- probe_field: bfloat16 [2, 256, 256], replicated, may hold values from -6 to 6
- amplitudes: bfloat16 [32, 16, 256, 256], P('ang', 'pos'), may hold values from 0.099609375 to 3
- offsets: int32 [32, 16], P('ang', 'pos'), may hold values from 0 to 2047, as said below
- counts: int32 [32, 4], P('ang', 'pos'), may hold values from 1 to 4, 12 in all within a row
Outputs:
- new_volume: float32 [2, 256, 32768], P(None, 'ang', 'pos')
- proj_grad: float32 [2, 256, 32, 2048], P(None, None, 'ang', 'pos')
Inputs may be any that keep to these rules, and one draw needn't show every extreme that they name: Each position lies in the tile of the device that holds its slot: 512 * (q // 4) <= offsets[a, q] < 512 * (q // 4 + 1). Every row of counts has an entry equal to 4.
All inputs are finite; a program needn't handle non-finite values. No bound on the sum of `counts` on one device may be relied on, other than what follows from the above.
Results may differ from a plain program's by a relative error of at most 0.0062.
Values may be sent and summed in bfloat16 or wider, within the bound.
No kernel may reach another device: no remote copies, remote signals or barrier semaphores. Data moves between devices by JAX's collectives and lax.ppermute only.
A program may use at most 192 MiB of HBM per device.

v0:
```python
import math

import jax
import jax.numpy as jnp
from jax import lax
from jax.sharding import PartitionSpec as P

step_size = 0.1


def from_behind(block, axis, distance):
    devices = range(lax.axis_size(axis))
    route = [((i - distance) % len(devices), i) for i in devices]
    return lax.ppermute(block, axis, route)


def dft_tables(width):
    index = jnp.arange(width, dtype=jnp.int32)
    phase = index[:, None] * index[None, :] % width
    turn = 2.0 * math.pi / width * phase.astype(jnp.float32)
    cosine = (jnp.cos(turn) / math.sqrt(width)).astype(jnp.bfloat16)
    sine_neg = (-jnp.sin(turn) / math.sqrt(width)).astype(jnp.bfloat16)
    return (cosine, sine_neg)


def left_mul(table, field):
    return jnp.einsum("zy,qyu->qzu", table, field, preferred_element_type=jnp.float32)


def right_mul(field, table):
    return jnp.einsum("qzy,yu->qzu", field, table, preferred_element_type=jnp.float32)


def exit_gradient(patches, probe_field, amplitude_rows, live_mask, cosine, sine_neg):
    probe_re = probe_field[0].astype(jnp.float32)
    probe_im = probe_field[1].astype(jnp.float32)
    patch_re = patches[:, 0].astype(jnp.float32)
    patch_im = patches[:, 1].astype(jnp.float32)
    wave_re = (probe_re * patch_re - probe_im * patch_im).astype(jnp.bfloat16)
    wave_im = (probe_re * patch_im + probe_im * patch_re).astype(jnp.bfloat16)
    half_re = (left_mul(cosine, wave_re) - left_mul(sine_neg, wave_im)).astype(jnp.bfloat16)
    half_im = (left_mul(cosine, wave_im) + left_mul(sine_neg, wave_re)).astype(jnp.bfloat16)
    far_re = right_mul(half_re, cosine) - right_mul(half_im, sine_neg)
    far_im = right_mul(half_re, sine_neg) + right_mul(half_im, cosine)
    modulus = jnp.sqrt(far_re * far_re + far_im * far_im)
    factor = amplitude_rows.astype(jnp.float32) / jnp.maximum(modulus, 1.0) - 1.0
    delta_re = (far_re * factor).astype(jnp.bfloat16)
    delta_im = (far_im * factor).astype(jnp.bfloat16)
    back_re = (left_mul(cosine, delta_re) + left_mul(sine_neg, delta_im)).astype(jnp.bfloat16)
    back_im = (left_mul(cosine, delta_im) - left_mul(sine_neg, delta_re)).astype(jnp.bfloat16)
    near_re = right_mul(back_re, cosine) + right_mul(back_im, sine_neg)
    near_im = right_mul(back_im, cosine) - right_mul(back_re, sine_neg)
    scale_mask = live_mask[:, None, None]
    grad_re = (probe_re * near_re + probe_im * near_im) * scale_mask
    grad_im = (probe_re * near_im - probe_im * near_re) * scale_mask
    return jnp.stack([grad_re, grad_im], axis=1)


def selector(block_ids, block_total):
    flat_ids = block_ids.reshape(-1)
    return flat_ids[:, None] == jnp.arange(block_total, dtype=jnp.int32)[None, :]


def project(volume_part, block_ids, radon_tiles):
    block_size = radon_tiles.shape[1]
    slab_count = volume_part.shape[1]
    angle_count = block_ids.shape[0]
    det_count = block_ids.shape[1]
    feeds = block_ids.shape[2]
    block_total = volume_part.shape[2] // block_size
    blocks = volume_part.reshape(2, slab_count, block_total, block_size)
    choose = selector(block_ids, block_total).astype(jnp.bfloat16)
    picked = jnp.einsum("rk,cskx->csrx", choose, blocks, preferred_element_type=jnp.float32).astype(
        jnp.bfloat16
    )
    picked = picked.reshape(2, slab_count, angle_count, det_count, feeds * block_size)
    products = jnp.einsum(
        "csaux,amx->csaum", picked, radon_tiles, preferred_element_type=jnp.float32
    )
    return products.reshape(2, slab_count, angle_count, det_count * block_size)


def back_project(grad_part, block_ids, radon_tiles, coef_count):
    block_size = radon_tiles.shape[1]
    slab_count = grad_part.shape[1]
    angle_count = block_ids.shape[0]
    det_count = block_ids.shape[1]
    feeds = block_ids.shape[2]
    block_total = coef_count // block_size
    grad_blocks = grad_part.reshape(2, slab_count, angle_count, det_count, block_size)
    contrib = jnp.einsum(
        "csaum,amx->csaux", grad_blocks, radon_tiles, preferred_element_type=jnp.float32
    )
    contrib = contrib.reshape(2, slab_count, angle_count * det_count * feeds, block_size)
    choose = selector(block_ids, block_total).astype(jnp.float32)
    summed = jnp.einsum("rk,csrx->cskx", choose, contrib, precision=lax.Precision.HIGHEST)
    return summed.reshape(2, slab_count, coef_count)


def on_device(volume, radon_tiles, tile_blocks, probe_field, amplitudes, offsets, counts):
    n_pos = lax.axis_size("pos")
    pos_index = lax.axis_index("pos")
    block_size = radon_tiles.shape[1]
    own_blocks = tile_blocks.shape[1] // n_pos
    tile_width = own_blocks * block_size
    whole_volume = lax.all_gather(volume, "pos", axis=2, tiled=True)
    own_ids = lax.dynamic_slice_in_dim(tile_blocks, pos_index * own_blocks, own_blocks, 1)
    sinogram = project(whole_volume, own_ids, radon_tiles).astype(jnp.bfloat16)
    angle_major = lax.all_to_all(sinogram, "ang", split_axis=2, concat_axis=1, tiled=True)
    nextdoor = from_behind(angle_major, "pos", -1)
    extended = jnp.concatenate([angle_major, nextdoor], axis=3)
    probe_width = probe_field.shape[1]
    cosine, sine_neg = dft_tables(probe_width)
    all_slices = angle_major.shape[1]
    slot_count = offsets.shape[1]
    per_angle = []
    for angle_idx in range(angle_major.shape[2]):
        starts = offsets[angle_idx] - pos_index * tile_width
        extended_angle = extended[:, :, angle_idx, :]
        patches = jnp.stack(
            [
                lax.dynamic_slice_in_dim(extended_angle, starts[slot], probe_width, 2)
                for slot in range(slot_count)
            ],
            axis=0,
        )
        live_mask = (jnp.arange(slot_count, dtype=jnp.int32) < counts[angle_idx, 0]).astype(
            jnp.float32
        )
        patch_grads = exit_gradient(
            patches, probe_field, amplitudes[angle_idx], live_mask, cosine, sine_neg
        )
        summed = jnp.zeros((2, all_slices, 2 * tile_width), jnp.float32)
        for slot in range(slot_count):
            current = lax.dynamic_slice_in_dim(summed, starts[slot], probe_width, 2)
            summed = lax.dynamic_update_slice_in_dim(
                summed, current + patch_grads[slot], starts[slot], 2
            )
        per_angle.append(summed)
    spread = jnp.stack(per_angle, axis=2)
    spill_over = from_behind(spread[..., tile_width:], "pos", 1)
    proj_grad = spread[..., :tile_width] + spill_over
    grad_rounded = proj_grad.astype(jnp.bfloat16)
    slice_major = lax.all_to_all(grad_rounded, "ang", split_axis=1, concat_axis=2, tiled=True)
    partial_grad = back_project(slice_major, own_ids, radon_tiles, whole_volume.shape[2])
    object_grad = lax.psum_scatter(partial_grad, "pos", scatter_dimension=2, tiled=True)
    new_volume = volume.astype(jnp.float32) + step_size * object_grad
    return (new_volume, proj_grad)


def solution(mesh):
    in_specs = (
        P(None, "ang", "pos"),
        P(),
        P(),
        P(),
        P("ang", "pos", None, None),
        P("ang", "pos"),
        P("ang", "pos"),
    )
    out_specs = (P(None, "ang", "pos"), P(None, None, "ang", "pos"))
    return jax.shard_map(
        on_device, mesh=mesh, in_specs=in_specs, out_specs=out_specs, check_vma=False
    )
```

profile of v0, /device:TPU:1, one launch (start us, length us, event | category | flops | bytes accessed | tf_op | source)
XLA Modules:
  0.0 698.5 jit_solution(3048738927655446855)
XLA Ops:
  9.3 37.3 %all-gather.2.cloned.1.call-done = bf16[2,32,32768]{2,1,0:T(8,128)(2,1)} async-done(((bf16[2,32,8192]{2,1,0:T(8,128)(2,1)}), bf16[2,32,32768]{2,1,0:T(8,128)(2,1)}) %all-gather.2.cloned.1.call-update) | async-done | bytes 4194320 | tf_op jit(solution)/shard_map/all_gather | solution.py:106
  46.6 11.4 %reshape.147 = bf16[2,32,512,64]{3,2,1,0:T(8,128)(2,1)} reshape(bf16[2,32,32768]{2,1,0:T(8,128)(2,1)} %all-gather.2.cloned.1.call-done) | data formatting | bytes 8388608 | tf_op jit(solution)/shard_map/reshape | solution.py:71
  58.0 11.9 %convert_bitcast_fusion = bf16[2,32,1024,64]{2,3,1,0:T(8,128)(2,1)} fusion(bf16[2,32,512,64]{3,2,1,0:T(8,128)(2,1)} %reshape.147, s32[1024]{0:T(1024)S(1)} %eq.10), kind=kOutput, calls=%fused_computation.4 | convolution fusion | flops 4299685888 | bytes 12587008 | tf_op jit(solution)/shard_map/rk,cskx->csrx/dot_general | solution.py:73
  70.0 15.5 %copy.170 = bf16[2,32,1024,64]{3,2,1,0:T(8,128)(2,1)} copy(bf16[2,32,1024,64]{2,3,1,0:T(8,128)(2,1)} %convert_bitcast_fusion) | data formatting | bytes 16777216 | tf_op jit(solution)/shard_map/convert_element_type | solution.py:73
  85.5 22.8 %reshape.148 = bf16[2,32,32,8,256]{4,3,2,1,0:T(8,128)(2,1)} reshape(bf16[2,32,1024,64]{3,2,1,0:T(8,128)(2,1)} %copy.170) | data formatting | bytes 16777216 | tf_op jit(solution)/shard_map/reshape | solution.py:76
  108.3 7.7 %convert_bitcast_fusion.1 = bf16[2,32,32,8,64]{4,3,1,0,2:T(8,128)(2,1)} fusion(bf16[2,32,32,8,256]{4,3,2,1,0:T(8,128)(2,1)} %reshape.148, bf16[32,64,256]{2,1,0:T(8,128)(2,1)S(1)} %copy-done), kind=kOutput, calls=%fused_computation.12 | convolution fusion | flops 537919488 | bytes 11534336 | tf_op jit(solution)/shard_map/csaux,amx->csaum/dot_general | solution.py:77
  116.0 5.4 convert_element_type.541
  121.4 52.5 %all_to_all.33 = bf16[2,32,32,512]{3,1,0,2:T(8,128)(2,1)S(1)} all-to-all(bf16[2,32,32,512]{3,1,0,2:T(8,128)(2,1)S(1)} %convert_element_type.541), channel_id=1, replica_groups=mesh['ang'=8,'pos'=4] {'ang'}, dimensions={2} | all-to-all | bytes 4194304 | tf_op jit(solution)/shard_map/all_to_all | solution.py:109
  174.1 1.7 collective-permute-start
  211.4 1.7 fusion.56
  225.5 1.6 fusion.26
  238.7 1.8 fusion.183
  251.1 1.4 convolution_add_fusion.10
  259.0 5.4 multiply_convert_fusion.7
  275.7 1.7 fusion.31
  301.5 1.5 convolution_add_fusion.4
  304.2 4.1 multiply_bitcast_fusion.6
  310.2 1.6 broadcast.44.clone.3
  311.8 3.9 dynamic_update_slice.52
  315.7 2.3 fusion.97
  318.0 3.9 dynamic_update_slice.53
  321.9 2.3 fusion.92
  324.2 3.9 dynamic_update_slice.54
  328.1 2.5 fusion.109
  331.4 1.6 broadcast.44.clone.2
  333.0 3.9 dynamic_update_slice.56
  336.9 2.3 fusion.89
  339.2 3.9 dynamic_update_slice.57
  343.1 2.3 fusion.84
  345.4 3.9 dynamic_update_slice.58
  349.3 2.5 fusion.106
  352.6 1.6 broadcast.44.clone.1
  354.2 3.9 dynamic_update_slice.60
  358.0 2.3 fusion.81
  360.3 3.9 dynamic_update_slice.61
  364.2 2.3 fusion.76
  366.5 3.9 dynamic_update_slice.62
  370.3 2.3 fusion.103
  373.5 1.6 broadcast.44.clone
  375.0 3.9 dynamic_update_slice.64
  378.9 2.2 fusion.73
  381.1 3.9 dynamic_update_slice.65
  384.9 2.2 fusion.68
  387.1 3.9 dynamic_update_slice.66
  390.9 2.2 fusion.100
  393.1 4.1 dynamic_update_slice.55
  397.2 3.9 dynamic_update_slice.59
  401.0 3.9 dynamic_update_slice.63
  404.9 5.1 dynamic_update_slice.67
  410.0 3.3 pad_maximum_fusion
  415.0 45.4 %collective-permute-done.1 = f32[2,256,4,512]{3,1,0,2:T(8,128)S(1)} collective-permute-done((f32[2,256,4,512]{3,1,0,2:T(8,128)S(1)}, f32[2,256,4,512]{3,1,0,2:T(8,128)S(1)}, u32[]{:S(2)}, u32[]{:S(2)}) %collective-permute-start.1) | collective-permute-done | bytes 4194336 | tf_op jit(solution)/shard_map/ppermute | solution.py:14
  460.5 3.1 fusion.551
  463.6 2.2 copy.246
  465.8 51.0 %all_to_all.34 = bf16[2,256,4,512]{3,0,2,1:T(2,128)(2,1)S(1)} all-to-all(bf16[2,256,4,512]{3,0,2,1:T(2,128)(2,1)S(1)} %copy.246), channel_id=1, replica_groups=mesh['ang'=8,'pos'=4] {'ang'}, dimensions={1} | all-to-all | bytes 4194304 | tf_op jit(solution)/shard_map/all_to_all | solution.py:144
  517.5 3.6 reshape.149
  521.1 4.5 convolution_bitcast_fusion
  525.6 6.2 copy.248
  531.7 24.3 %reshape.150 = f32[2,32,1024,64]{3,2,1,0:T(8,128)} reshape(f32[2,32,32,8,256]{4,3,2,1,0:T(8,128)} %copy.248) | data formatting | bytes 33554432 | tf_op jit(solution)/shard_map/reshape | solution.py:94
  556.1 35.3 %convolution_bitcast_fusion.1 = f32[2,32,512,64]{2,3,1,0:T(8,128)} fusion(f32[2,32,1024,64]{3,2,1,0:T(8,128)} %reshape.150, s32[1024]{0:T(1024)S(1)} %copy-done.11), kind=kOutput, calls=%fused_computation.13 | convolution fusion | flops 25770328064 | bytes 25169920 | tf_op jit(solution)/shard_map/rk,csrx->cskx/dot_general | solution.py:96
  591.4 12.4 %copy.250 = f32[2,32,512,64]{3,2,1,0:T(8,128)} copy(f32[2,32,512,64]{2,3,1,0:T(8,128)} %convolution_bitcast_fusion.1) | data formatting | bytes 16777216 | tf_op jit(solution)/shard_map/rk,csrx->cskx/transpose | solution.py:96
  603.8 13.0 %reshape.151 = f32[2,32,32768]{2,1,0:T(8,128)} reshape(f32[2,32,512,64]{3,2,1,0:T(8,128)} %copy.250) | data formatting | bytes 16777216 | tf_op jit(solution)/shard_map/reshape | solution.py:97
  616.8 7.0 %copy.251 = f32[2,256,4,512]{3,2,1,0:T(4,128)} copy(f32[2,256,4,512]{3,1,0,2:T(8,128)} %get-tuple-element.9) | data formatting | bytes 8388608
  623.8 64.5 %reduce-scatter.2.cloned.1.call-done = f32[2,32,8192]{2,1,0:T(8,128)} async-done(((f32[2,32,32768]{2,1,0:T(8,128)}), f32[2,32,8192]{2,1,0:T(8,128)}) %reduce-scatter.2.cloned.1.call-update) | async-done | bytes 2097168 | tf_op jit(solution)/shard_map/reduce_scatter | solution.py:146
  688.3 3.1 multiply_add_fusion
  (118 shorter events, 91.4 us)
Async XLA Ops:
  7.2 101.1 %copy-start = (bf16[32,64,256]{2,1,0:T(8,128)(2,1)S(1)}, bf16[32,64,256]{2,1,0:T(8,128)(2,1)}, u32[]{:S(2)}) copy-start(bf16[32,64,256]{2,1,0:T(8,128)(2,1)} %param.8) | copy-start | bytes 3145732
  7.2 39.4 %all-gather.2.cloned.1.call-start = ((), (), s32[]{:S(2)}) async-start(), calls=%async_computation.3 | async-start | bytes 5242880 | tf_op jit(solution)/shard_map/all_gather | solution.py:106
  7.9 680.4 %reduce-scatter.2.cloned.1.call-start = ((), (), s32[]{:S(2)}) async-start(), calls=%async_computation.4 | async-start | bytes 10485760 | tf_op jit(solution)/shard_map/reduce_scatter | solution.py:146
  9.3 48.7 %copy-start.10 = (s32[1024]{0:T(1024)}, s32[1024]{0:T(1024)S(1)}, u32[]{:S(2)}) copy-start(s32[1024]{0:T(1024)S(1)} %eq.10) | copy-start | bytes 12292
  173.9 2.0 copy-start.13
  173.9 34.0 %copy-start.12 = (s32[4,1]{0,1:T(1,128)S(1)}, s32[4,1]{0,1:T(1,128)}, u32[]{:S(2)}) copy-start(s32[4,1]{0,1:T(1,128)} %param.13) | copy-start | bytes 52
  173.9 37.3 %copy-start.9 = (bf16[2,256,256]{2,1,0:T(8,128)(2,1)S(1)}, bf16[2,256,256]{2,1,0:T(8,128)(2,1)}, u32[]{:S(2)}) copy-start(bf16[2,256,256]{2,1,0:T(8,128)(2,1)} %param.10) | copy-start | bytes 786436
  174.1 37.3 %collective-permute-start = (bf16[2,256,4,512]{3,1,0,2:T(8,128)(2,1)S(1)}, bf16[2,256,4,512]{3,1,0,2:T(8,128)(2,1)}, u32[]{:S(2)}, u32[]{:S(2)}) collective-permute-start(bf16[2,256,4,512]{3,1,0,2:T(8,128)(2,1)S(1)} %bitcast.470), channel_id=1, source_target_pairs={{1,0},{2,1},{3,2},{0,3},{5,4},{6,5},{7,6},{4,7},{9,8},{10,9},{11,1... | collective-permute-start | bytes 6291464 | tf_op jit(solution)/shard_map/ppermute | solution.py:14
  308.4 1.0 copy-start.5
  308.4 1.8 copy-start.6
  328.1 2.5 copy-start.3
  328.1 2.5 copy-start.4
  349.3 2.5 copy-start.1
  349.3 2.5 copy-start.2
  393.1 11.8 %copy-start.7 = (f32[2,256,1024]{2,1,0:T(8,128)S(1)}, f32[2,256,1024]{2,1,0:T(8,128)}, u32[]{:S(2)}) copy-start(f32[2,256,1024]{2,1,0:T(8,128)} %dynamic_update_slice.66) | copy-start | bytes 6291460
  414.0 46.5 %collective-permute-start.1 = (f32[2,256,4,512]{3,1,0,2:T(8,128)S(1)}, f32[2,256,4,512]{3,1,0,2:T(8,128)S(1)}, u32[]{:S(2)}, u32[]{:S(2)}) collective-permute-start(f32[2,256,4,512]{3,1,0,2:T(8,128)S(1)} %slice.329), channel_id=1, source_target_pairs={{3,0},{0,1},{1,2},{2,3},{7,4},{4,5},{5,6},{6,7},{11,8},{8,9},{9,10... | collective-permute-start | bytes 12582920 | tf_op jit(solution)/shard_map/ppermute | solution.py:14
  531.7 24.3 %copy-start.11 = (s32[1024]{0:T(1024)S(1)}, s32[1024]{0:T(1024)}, u32[]{:S(2)}) copy-start(s32[1024]{0:T(1024)} %copy-done.10) | copy-start | bytes 12292
  616.8 71.5 %copy-start.8 = (bf16[2,32,8192]{2,1,0:T(8,128)(2,1)S(1)}, bf16[2,32,8192]{2,1,0:T(8,128)(2,1)}, u32[]{:S(2)}) copy-start(bf16[2,32,8192]{2,1,0:T(8,128)(2,1)} %param.7) | copy-start | bytes 3145732
Sparse Core Ops, SparseCore 0:
  9.6 36.9 all-gather.1
  616.9 71.3 reduce-scatter.1
where the time goes:
time: 711 us; the launch traced here: 699 us
  local copies, waits for them, and re-layouts  202 us (28%)
  matrix products  150 us (21%)
  waiting for transfers between devices  148 us (21%)
  blocking collectives  103 us (14%)
  other arithmetic  46.4 us (7%)
  between operations  45.5 us (6%)
    reduce_scatter x1, waiting for transfers between devices, on_device(): lax.psum_scatter(partial_grad, 'pos', scatter_dimension=2, tiled=True)  64.5 us
    dynamic_update_slice x16, local copies, waits for them, and re-layouts, on_device(): lax.dynamic_update_slice_in_dim(summed, current + patch_grads[slot], star...  63.5 us
    all_to_all x1, blocking collectives, on_device(): lax.all_to_all(sinogram, 'ang', split_axis=2, concat_axis=1, tiled=True)  52.5 us
    all_to_all x1, blocking collectives, on_device(): lax.all_to_all(grad_rounded, 'ang', split_axis=1, concat_axis=2, tiled=True)  51 us
    dot_general x32, matrix products, right_mul(): jnp.einsum('qzy,yu->qzu', field, table, preferred_element_type=jnp.float32)  47.8 us
    ppermute x2, waiting for transfers between devices, from_behind(): return lax.ppermute(block, axis, route)  45.5 us
    dot_general x32, matrix products, left_mul(): jnp.einsum('zy,qyu->qzu', table, field, preferred_element_type=jnp.float32)  42.9 us
    all_gather x1, waiting for transfers between devices, on_device(): whole_volume = lax.all_gather(volume, 'pos', axis=2, tiled=True)  37.3 us
  transfers between devices with their start and end apart: 4, of which 3 were waited for; matrix products, arithmetic and copies ran while one was open for 2% of the time, Pallas kernels for 0%

commit v1 on v0

v1 whole, which is shorter than its diff:
```python
import functools
import math

import jax
import jax.numpy as jnp
import numpy as np
from jax import lax
from jax.experimental import pallas as pl
from jax.experimental.pallas import tpu as pltpu
from jax.sharding import PartitionSpec as P

step_size = 0.1
LANES = 128
ROWS = 16
GROUP = 8
VMEM_LIMIT = 50 * 1024 * 1024
everywhere = pl.BlockSpec(memory_space=pltpu.VMEM)
scalars = pl.BlockSpec(memory_space=pltpu.SMEM)


def dft_tables(width):
    index = np.arange(width)
    turn = 2.0 * math.pi / width * (index[:, None] * index[None, :] % width)
    cosine = jnp.asarray(np.cos(turn) / math.sqrt(width), jnp.bfloat16)
    sine_neg = jnp.asarray(-np.sin(turn) / math.sqrt(width), jnp.bfloat16)
    forward = jnp.block([[cosine, -sine_neg], [sine_neg, cosine]])
    inverse = jnp.block([[cosine, sine_neg], [-sine_neg, cosine]])
    return (forward, inverse)


def swap_pos(pieces):
    count = len(pieces)
    out = [pieces[0]]
    for k in range(1, count):
        out.append(lax.ppermute(pieces[k], "pos", [(i, i ^ k) for i in range(count)]))
    return out


def lower_half(shape):
    return lax.broadcasted_iota(jnp.int32, shape, len(shape) - 1) < LANES // 2


def swap_halves(tile):
    return pltpu.roll(tile, LANES // 2, 1)


def pair_tile(w_ref, tile):
    m, n = tile.shape
    w_ref[0:m, 0:n] = tile
    w_ref[m : 2 * m, n : 2 * n] = tile


def project_kernel(pieces, idx_ref, radon_ref, *refs):
    vol_refs = refs[:pieces]
    out_ref, vv_ref, lhs_ref, w_ref = refs[pieces:]
    angles = radon_ref.shape[0]
    per_piece = vol_refs[0].shape[1] // LANES
    tiles = per_piece * pieces
    pairs = out_ref.shape[2] // LANES
    feeds = idx_ref.shape[1] // (2 * pairs)
    span = radon_ref.shape[2]
    w_ref[...] = jnp.zeros_like(w_ref)
    for k in range(pieces):

        @pl.loop(0, per_piece, unroll=4)
        def _(t):
            tile = vol_refs[k][:, pl.ds(pl.multiple_of(t * LANES, LANES), LANES)]
            vv_ref[k * per_piece + t] = tile
            swapped = swap_halves(tile.astype(jnp.float32)).astype(jnp.bfloat16)
            vv_ref[tiles + k * per_piece + t] = swapped

    low = lower_half((ROWS, LANES))

    @pl.loop(0, angles // 2)
    def _(step):
        for n in range(2):
            a = step * 2 + n
            pair_tile(w_ref.at[n], radon_ref[a])
            for pair in range(pairs):
                for side in range(2):
                    for jp in range(feeds // 2):
                        at = (2 * pair + side) * feeds + 2 * jp
                        first = vv_ref[idx_ref[a, at]]
                        second = vv_ref[idx_ref[a, at + 1]]
                        lane = side * span + jp * LANES
                        lhs_ref[n, pair * ROWS : (pair + 1) * ROWS, lane : lane + LANES] = jnp.where(
                            low, first, second
                        )
        for n in range(2):
            a = step * 2 + n
            product = lax.dot_general(
                lhs_ref[n], w_ref[n], (((1,), (1,)), ((), ())), preferred_element_type=jnp.float32
            )
            for pair in range(pairs):
                out_ref[a, :, pair * LANES : (pair + 1) * LANES] = product[
                    pair * ROWS : (pair + 1) * ROWS
                ].astype(jnp.bfloat16)


def project(idx, radon_tiles, vol_pieces, columns):
    angles, block, span = radon_tiles.shape
    pieces = len(vol_pieces)
    tiles = pieces * vol_pieces[0].shape[1] // LANES
    pairs = columns // LANES
    return pl.pallas_call(
        functools.partial(project_kernel, pieces),
        out_shape=jax.ShapeDtypeStruct((angles, ROWS, columns), jnp.bfloat16),
        in_specs=[scalars, everywhere] + [everywhere] * pieces,
        out_specs=everywhere,
        scratch_shapes=[
            pltpu.VMEM((2 * tiles, ROWS, LANES), jnp.bfloat16),
            pltpu.VMEM((2, pairs * ROWS, 2 * span), jnp.bfloat16),
            pltpu.VMEM((2, 2 * block, 2 * span), jnp.bfloat16),
        ],
        compiler_params=pltpu.CompilerParams(vmem_limit_bytes=VMEM_LIMIT),
        name="project",
    )(idx, radon_tiles, *vol_pieces)


CHAINS = 4


def back_project_kernel(pieces, idx_ref, radon_ref, grad_ref, *refs):
    out_refs = refs[:pieces]
    acc_refs = refs[pieces : pieces + CHAINS]
    contrib_ref, w_ref = refs[pieces + CHAINS :]
    angles = radon_ref.shape[0]
    per_piece = out_refs[0].shape[1] // LANES
    tiles = per_piece * pieces
    pairs = grad_ref.shape[2] // LANES
    feeds = idx_ref.shape[1] // (2 * pairs)
    span = radon_ref.shape[2]
    w_ref[...] = jnp.zeros_like(w_ref)

    @pl.loop(0, 2 * tiles, unroll=8)
    def _(t):
        for acc_ref in acc_refs:
            acc_ref[t] = jnp.zeros((ROWS, LANES), jnp.float32)

    low = lower_half((ROWS, LANES))

    @pl.loop(0, angles // CHAINS)
    def _(step):
        for n in range(CHAINS):
            a = step * CHAINS + n
            pair_tile(w_ref.at[n], radon_ref[a])
            lhs = jnp.concatenate(
                [grad_ref[a, :, p * LANES : (p + 1) * LANES] for p in range(pairs)], axis=0
            )
            contrib_ref[n] = jnp.dot(lhs, w_ref[n], preferred_element_type=jnp.float32)
        for pair in range(pairs):
            for side in range(2):
                for jp in range(feeds // 2):
                    at = (2 * pair + side) * feeds + 2 * jp
                    lane = side * span + jp * LANES
                    for n in range(CHAINS):
                        a = step * CHAINS + n
                        tile = contrib_ref[n, pair * ROWS : (pair + 1) * ROWS, lane : lane + LANES]
                        first, second = idx_ref[a, at], idx_ref[a, at + 1]
                        acc_refs[n][first] += jnp.where(low, tile, 0.0)
                        acc_refs[n][second] += jnp.where(low, 0.0, tile)

    for k in range(pieces):

        @pl.loop(0, per_piece, unroll=4)
        def _(t):
            straight = acc_refs[0][k * per_piece + t]
            crossed = acc_refs[0][tiles + k * per_piece + t]
            for acc_ref in acc_refs[1:]:
                straight += acc_ref[k * per_piece + t]
                crossed += acc_ref[tiles + k * per_piece + t]
            total = straight + swap_halves(crossed)
            out_refs[k][:, pl.ds(pl.multiple_of(t * LANES, LANES), LANES)] = total.astype(jnp.bfloat16)


def back_project(idx, radon_tiles, grads, pieces, piece_width):
    angles, block, span = radon_tiles.shape
    tiles = pieces * piece_width // LANES
    pairs = grads.shape[2] // LANES
    return pl.pallas_call(
        functools.partial(back_project_kernel, pieces),
        out_shape=[jax.ShapeDtypeStruct((ROWS, piece_width), jnp.bfloat16)] * pieces,
        in_specs=[scalars, everywhere, everywhere],
        out_specs=[everywhere] * pieces,
        scratch_shapes=[pltpu.VMEM((2 * tiles, ROWS, LANES), jnp.float32)] * CHAINS
        + [
            pltpu.VMEM((CHAINS, pairs * ROWS, 2 * span), jnp.float32),
            pltpu.VMEM((CHAINS, 2 * block, 2 * span), jnp.bfloat16),
        ],
        compiler_params=pltpu.CompilerParams(vmem_limit_bytes=VMEM_LIMIT),
        name="back_project",
    )(idx, radon_tiles, grads)


def exit_kernel(pieces, meta_ref, probe_ref, forward_ref, inverse_ref, sino_ref, *refs):
    amp_refs = refs[:pieces]
    grad_ref, tile_ref, acc_ref, wave_ref, half_ref = refs[pieces:]
    pos = lax.axis_index("pos")
    groups = sino_ref.shape[0]
    width = probe_ref.shape[1]
    columns = sino_ref.shape[2]
    lane_tiles = columns // LANES
    slots = amp_refs[0].shape[0]
    chunk = 4
    crows = chunk * GROUP
    lane_id = lax.broadcasted_iota(jnp.int32, (crows, LANES), 1)
    wide = width // LANES

    @pl.loop(0, groups)
    def _(g):
        zero = jnp.zeros((GROUP, columns), jnp.float32)
        for c in range(2):
            acc_ref[c, pl.ds(pl.multiple_of(g * GROUP, GROUP), GROUP), :] = zero

    def product(left, right):
        return jnp.dot(left, right, preferred_element_type=jnp.float32)

    for k in range(pieces):
        owner = jnp.bitwise_xor(pos, k)

        def slot_step(q, carry):
            offset = meta_ref[owner, q]
            first_tile = offset // LANES
            shift = offset % LANES
            starts = [
                pl.multiple_of((first_tile + m) % lane_tiles * LANES, LANES) for m in range(wide + 1)
            ]
            keep = lane_id < LANES - shift
            back_shift = (LANES - shift) % LANES
            for ch in range(groups // chunk):
                rows = slice(ch * crows, (ch + 1) * crows)
                turned = []
                for start in starts:
                    both = sino_ref[ch * chunk : (ch + 1) * chunk, :, pl.ds(start, LANES)].astype(
                        jnp.float32
                    )
                    turned.append(
                        [
                            pltpu.roll(
                                both[:, c * GROUP : (c + 1) * GROUP].reshape(crows, LANES),
                                back_shift,
                                1,
                            )
                            for c in range(2)
                        ]
                    )
                for m in range(wide):
                    lanes = slice(m * LANES, (m + 1) * LANES)
                    patch_re = jnp.where(keep, turned[m][0], turned[m + 1][0])
                    patch_im = jnp.where(keep, turned[m][1], turned[m + 1][1])
                    probe_re = probe_ref[0, rows, lanes].astype(jnp.float32)
                    probe_im = probe_ref[1, rows, lanes].astype(jnp.float32)
                    wave_ref[rows, lanes] = (probe_re * patch_re - probe_im * patch_im).astype(
                        jnp.bfloat16
                    )
                    wave_ref[width + ch * crows : width + (ch + 1) * crows, lanes] = (
                        probe_re * patch_im + probe_im * patch_re
                    ).astype(jnp.bfloat16)
            half = product(forward_ref[...], wave_ref[...]).astype(jnp.bfloat16)
            half_ref[:, :width] = half[:width]
            half_ref[:, width:] = half[width:]
            far = product(half_ref[...], inverse_ref[...])
            for ch in range(groups // chunk):
                rows = slice(ch * crows, (ch + 1) * crows)
                far_re, far_im = far[rows, :width], far[rows, width:]
                power = far_re * far_re + far_im * far_im
                amps = amp_refs[k][q, rows, :].astype(jnp.float32)
                factor = amps * lax.rsqrt(jnp.maximum(power, 1.0)) - 1.0
                wave_ref[rows, :] = (far_re * factor).astype(jnp.bfloat16)
                wave_ref[width + ch * crows : width + (ch + 1) * crows, :] = (far_im * factor).astype(
                    jnp.bfloat16
                )
            back = product(inverse_ref[...], wave_ref[...]).astype(jnp.bfloat16)
            half_ref[:, :width] = back[:width]
            half_ref[:, width:] = back[width:]
            near = product(half_ref[...], forward_ref[...])
            past = lane_id >= shift
            for ch in range(groups // chunk):
                rows = slice(ch * crows, (ch + 1) * crows)
                turned = []
                for m in range(wide):
                    lanes = slice(m * LANES, (m + 1) * LANES)
                    probe_re = probe_ref[0, rows, lanes].astype(jnp.float32)
                    probe_im = probe_ref[1, rows, lanes].astype(jnp.float32)
                    near_re = near[rows, m * LANES : (m + 1) * LANES]
                    near_im = near[rows, width + m * LANES : width + (m + 1) * LANES]
                    turned.append(
                        [
                            pltpu.roll(probe_re * near_re + probe_im * near_im, shift, 1),
                            pltpu.roll(probe_re * near_im - probe_im * near_re, shift, 1),
                        ]
                    )
                for m in range(wide + 1):
                    for c in range(2):
                        behind = turned[m - 1][c] if m > 0 else 0.0
                        ahead = turned[m][c] if m < wide else 0.0
                        acc_ref[c, rows, pl.ds(starts[m], LANES)] += jnp.where(past, ahead, behind)
            return carry

        lax.fori_loop(0, meta_ref[owner, slots], slot_step, 0)

    @pl.loop(0, groups)
    def _(g):
        rows = pl.ds(pl.multiple_of(g * GROUP, GROUP), GROUP)
        both = jnp.concatenate([acc_ref[0, rows, :], acc_ref[1, rows, :]], axis=0)
        grad_ref[g] = both.astype(jnp.bfloat16)

    tile_width = tile_ref.shape[3]
    for k in range(pieces):
        start = pl.multiple_of(jnp.bitwise_xor(pos, k) * tile_width, tile_width)

        @pl.loop(0, groups // 2)
        def _(g):
            rows = pl.ds(pl.multiple_of(g * 2 * GROUP, 2 * GROUP), 2 * GROUP)
            for c in range(2):
                tile_ref[k, c, rows, :] = acc_ref[c, rows, pl.ds(start, tile_width)].astype(
                    jnp.bfloat16
                )


def exit_gradient(meta, probe_field, forward, inverse, sino, amp_pieces):
    groups, rows, columns = sino.shape
    width = probe_field.shape[1]
    pieces = len(amp_pieces)
    slices = groups * GROUP
    return pl.pallas_call(
        functools.partial(exit_kernel, pieces),
        out_shape=[
            jax.ShapeDtypeStruct(sino.shape, jnp.bfloat16),
            jax.ShapeDtypeStruct((pieces, 2, slices, columns // pieces), jnp.bfloat16),
        ],
        in_specs=[scalars] + [everywhere] * (4 + pieces),
        out_specs=[everywhere] * 2,
        scratch_shapes=[
            pltpu.VMEM((2, slices, columns), jnp.float32),
            pltpu.VMEM((2 * width, width), jnp.bfloat16),
            pltpu.VMEM((width, 2 * width), jnp.bfloat16),
        ],
        compiler_params=pltpu.CompilerParams(vmem_limit_bytes=VMEM_LIMIT),
        name="exit_gradient",
    )(meta, probe_field, forward, inverse, sino, *amp_pieces)


def by_owner(pieces, pos):
    count = len(pieces)
    bit = 1
    while bit < count:
        flip = (pos & bit) != 0
        pieces = [jnp.where(flip, pieces[k ^ bit], pieces[k]) for k in range(count)]
        bit *= 2
    return pieces


def to_groups(received, own_slices):
    if own_slices == GROUP:
        return received
    devices, rows, columns = received.shape
    merge = GROUP // own_slices
    split = received.reshape(devices // merge, merge, 2, own_slices, columns)
    return split.transpose(0, 2, 1, 3, 4).reshape(devices // merge, ROWS, columns)


def from_groups(grouped, own_slices):
    if own_slices == GROUP:
        return grouped
    groups, rows, columns = grouped.shape
    merge = GROUP // own_slices
    split = grouped.reshape(groups, 2, merge, own_slices, columns)
    return split.transpose(0, 2, 1, 3, 4).reshape(groups * merge, 2 * own_slices, columns)


def pad_rows(block):
    return jnp.pad(block, [(0, 0)] * (block.ndim - 2) + [(0, ROWS - block.shape[-2]), (0, 0)])


def on_device(volume, radon_tiles, tile_blocks, probe_field, amplitudes, offsets, counts):
    n_pos = lax.axis_size("pos")
    pos = lax.axis_index("pos")
    angles, det_blocks, feeds = tile_blocks.shape
    block_size = radon_tiles.shape[1]
    columns = det_blocks * block_size
    slab = volume.shape[1]
    width = volume.shape[2]
    own = slab // n_pos
    rows = 2 * own
    blocks_each = width // block_size

    def slices_of(k):
        start = jnp.bitwise_xor(pos, k) * own
        return lax.dynamic_slice_in_dim(volume, start, own, 1).reshape(rows, width)

    vol_pieces = swap_pos([slices_of(k) for k in range(n_pos)])
    meta = lax.all_gather(jnp.concatenate([offsets, counts], axis=1), "pos", axis=0)
    meta = lax.dynamic_index_in_dim(meta, pos, 1, keepdims=False)
    vol_pieces, amplitudes = lax.optimization_barrier((vol_pieces, amplitudes))
    amp_pieces = swap_pos(
        [
            lax.dynamic_index_in_dim(amplitudes, jnp.bitwise_xor(pos, k), 0, keepdims=False)
            for k in range(n_pos)
        ]
    )

    owner = tile_blocks // blocks_each
    within = tile_blocks % blocks_each
    crossed = (within + jnp.arange(feeds, dtype=jnp.int32)) % 2
    tiles_each = width // LANES
    idx = crossed * (n_pos * tiles_each) + (owner ^ pos) * tiles_each + within // 2
    idx = idx.reshape(angles, det_blocks * feeds)

    sino = project(idx, radon_tiles, [pad_rows(piece) for piece in vol_pieces], columns)[:, :rows]
    received = lax.all_to_all(sino, ("ang", "pos"), 0, 0, tiled=True)
    forward, inverse = dft_tables(probe_field.shape[1])
    grads, grad_tiles = exit_gradient(
        meta, probe_field, forward, inverse, to_groups(received, own), amp_pieces
    )
    tile_pieces = swap_pos([grad_tiles[k] for k in range(n_pos)])
    returned = lax.all_to_all(from_groups(grads, own), ("ang", "pos"), 0, 0, tiled=True)
    proj_grad = jnp.stack(by_owner(tile_pieces, pos), axis=2).astype(jnp.float32)
    obj_pieces = back_project(idx, radon_tiles, pad_rows(returned), n_pos, width)
    obj_pieces = swap_pos([piece[:rows] for piece in obj_pieces])
    obj_pieces = [piece.reshape(2, own, width) for piece in by_owner(obj_pieces, pos)]
    object_grad = jnp.concatenate(obj_pieces, axis=1).astype(jnp.float32)
    new_volume = volume.astype(jnp.float32) + step_size * object_grad
    return (new_volume, proj_grad)


def solution(mesh):
    in_specs = (
        P(None, "ang", "pos"),
        P(),
        P(),
        P(),
        P("ang", "pos", None, None),
        P("ang", "pos"),
        P("ang", "pos"),
    )
    out_specs = (P(None, "ang", "pos"), P(None, None, "ang", "pos"))
    return jax.shard_map(
        on_device, mesh=mesh, in_specs=in_specs, out_specs=out_specs, check_vma=False
    )
```

time: 711 us -> 201 us (0.28); the launches traced: 699 us -> 201 us
  local copies, waits for them, and re-layouts: 202 us -> 13 us
  matrix products: 150 us -> 0 us
  waiting for transfers between devices: 148 us -> 60.2 us
  blocking collectives: 103 us -> 43.6 us
  Pallas kernels: 0 us -> 58 us
  between operations: 45.5 us -> 0.86 us
  other arithmetic: 46.4 us -> 4.07 us
  starting transfers between devices: 2.88 us -> 21 us
    dot_general x68 -> x0, matrix products: 150 us -> none  [the longest x32 47.8 us: right_mul(): jnp.einsum('qzy,yu->qzu', field, table, preferred_element_type=jnp.float32)]
    all_to_all x2 -> x0, blocking collectives: 103 us -> none  [the longest x1 52.5 us: on_device(): lax.all_to_all(sinogram, 'ang', split_axis=2, concat_axis=1, tiled=True)]
    reshape x5 -> x2, local copies, waits for them, and re-layouts: 75.1 us -> 1.4 us  [the longest x1 1.35 us: slices_of(): return lax.dynamic_slice_in_dim(volume, start, own, 1).reshape(rows, width)]
    reduce_scatter x1 -> x0, waiting for transfers between devices: 64.5 us -> none  [on_device(): lax.psum_scatter(partial_grad, 'pos', scatter_dimension=2, tiled=True)]
    dynamic_update_slice x16 -> x0, local copies, waits for them, and re-layouts: 63.5 us -> none  [on_device(): lax.dynamic_update_slice_in_dim(summed, current + patch_grads[slot], star...]
    pallas_call x0 -> x3, Pallas kernels: none -> 58 us  [the longest x1 26.8 us: exit_gradient(): pl.pallas_call(functools.partial(exit_kernel, pieces), out_shape=[jax.Sha...]
    all_to_all x0 -> x2, waiting for transfers between devices: none -> 43.8 us  [the longest x1 43.8 us: on_device(): lax.all_to_all(from_groups(grads, own), ('ang', 'pos'), 0, 0, tiled=True)]
    all_gather x0 -> x1, blocking collectives: none -> 43.6 us  [on_device(): lax.all_gather(jnp.concatenate([offsets, counts], axis=1), 'pos', axis=0)]
  transfers between devices with their start and end apart: 4 -> 14, of which waited for: 3 -> 4; matrix products, arithmetic and copies ran while one was open for 2% -> 6% of each run, Pallas kernels for 0% -> 8%
where the time goes in v1:
time: 201 us
  waiting for transfers between devices  60.2 us (30%)
  Pallas kernels  58 us (29%)
  blocking collectives  43.6 us (22%)
  starting transfers between devices  21 us (10%)
  local copies, waits for them, and re-layouts  13 us (6%)
  other arithmetic  4.07 us (2%)
    all_to_all x1, waiting for transfers between devices, on_device(): lax.all_to_all(from_groups(grads, own), ('ang', 'pos'), 0, 0, tiled=True)  43.8 us
    all_gather x1, blocking collectives, on_device(): lax.all_gather(jnp.concatenate([offsets, counts], axis=1), 'pos', axis=0)  43.6 us
    pallas_call x1, Pallas kernels, exit_gradient(): pl.pallas_call(functools.partial(exit_kernel, pieces), out_shape=[jax.Sha...  26.8 us
    ppermute x12, waiting for transfers between devices, swap_pos(): lax.ppermute(pieces[k], 'pos', [(i, i ^ k) for i in range(count)])  16.4 us
    pallas_call x1, Pallas kernels, back_project(): pl.pallas_call(functools.partial(back_project_kernel, pieces), out_shape=...  15.9 us
    pallas_call x1, Pallas kernels, project(): pl.pallas_call(functools.partial(project_kernel, pieces), out_shape=jax.S...  15.4 us
    ppermute x12, starting transfers between devices, swap_pos(): lax.ppermute(pieces[k], 'pos', [(i, i ^ k) for i in range(count)])  9.42 us
    all_to_all x1, starting transfers between devices, on_device(): received = lax.all_to_all(sino, ('ang', 'pos'), 0, 0, tiled=True)  7.05 us
  transfers between devices with their start and end apart: 14, of which 4 were waited for; matrix products, arithmetic and copies ran while one was open for 6% of the time, Pallas kernels for 8%

profile of v1, /device:TPU:1, one launch (start us, length us, event | category | flops | bytes accessed | tf_op | source)
XLA Modules:
  0.0 200.8 jit_solution(6300619190372611043)
XLA Ops:
  0.6 0.0 copy-start.6
  0.6 0.0 copy-start
  0.7 1.4 dynamic-slice_bitcast_fusion.4
  2.0 2.7 %collective-permute-start.2 = (bf16[16,8192]{1,0:T(8,128)(2,1)S(1)}, bf16[16,8192]{1,0:T(8,128)(2,1)S(1)}, u32[]{:S(2)}, u32[]{:S(2)}) collective-permute-start(bf16[16,8192]{1,0:T(8,128)(2,1)S(1)} %get-tuple-element.45), channel_id=1, source_target_pairs={{0,3},{1,2},{2,1},{3,0},{4,7},{5,6},{6,5},{7,4},{8,11},{9,10},{10,... | collective-permute-start | bytes 786440 | tf_op jit(solution)/shard_map/ppermute | solution.py:35
  4.7 0.0 collective-permute-start
  4.7 0.2 collective-permute-start.1
  4.9 0.0 copy-done.6
  4.9 0.3 fusion.3
  5.2 0.1 copy.19
  5.3 0.1 copy.22.idx_ref
  5.3 6.2 %collective-permute-done.2.refs_3_ = bf16[16,8192]{1,0:T(8,128)(2,1)S(1)} collective-permute-done((bf16[16,8192]{1,0:T(8,128)(2,1)S(1)}, bf16[16,8192]{1,0:T(8,128)(2,1)S(1)}, u32[]{:S(2)}, u32[]{:S(2)}) %collective-permute-start.2) | collective-permute-done | bytes 262176 | tf_op jit(solution)/shard_map/ppermute | solution.py:35
  11.5 0.0 collective-permute-done.refs_1_
  11.5 4.9 %collective-permute-done.1.refs_2_ = bf16[16,8192]{1,0:T(8,128)(2,1)S(1)} collective-permute-done((bf16[16,8192]{1,0:T(8,128)(2,1)S(1)}, bf16[16,8192]{1,0:T(8,128)(2,1)S(1)}, u32[]{:S(2)}, u32[]{:S(2)}) %collective-permute-start.1) | collective-permute-done | bytes 262176 | tf_op jit(solution)/shard_map/ppermute | solution.py:35
  16.4 0.0 copy-done
  16.4 15.4 %project.1 = bf16[32,16,2048]{2,1,0:T(8,128)(2,1)} custom-call(s32[32,128]{1,0:T(8,128)S(1)} %copy.22.idx_ref, bf16[32,64,256]{2,1,0:T(8,128)(2,1)S(1)} %copy-done, bf16[16,8192]{1,0:T(8,128)(2,1)S(1)} %get-tuple-element.13.refs_0_, bf16[16,8192]{1,0:T(8,128)(2,1)S(1)} %collective-permute-done.refs_1_, bf16[16,8192]{1,0:T(8,128)(2,1)S(1)} %collective-permute-done.1.refs_2_, ...), custom_call_target="tpu_custom_call" | custom-call | tf_op jit(solution)/shard_map/project/pallas_call | solution.py:105
  31.8 7.0 %all-to-all-start = ((bf16[32,16,2048]{2,1,0:T(8,128)(2,1)}), bf16[32,16,2048]{2,1,0:T(8,128)(2,1)}, u32[]{:S(2)}, u32[]{:S(2)}) async-start(bf16[32,16,2048]{2,1,0:T(8,128)(2,1)} %project.1), calls=%async_computation | async-start | bytes 4194304 | tf_op jit(solution)/shard_map/all_to_all | solution.py:411
  38.9 0.0 copy-start.8
  38.9 0.0 copy-start.7
  38.9 0.0 copy-start.1
  38.9 0.0 copy-start.2
  38.9 0.0 copy-start.3
  38.9 2.8 %dynamic-slice_bitcast_fusion = (bf16[4,256,256]{2,1,0:T(8,128)(2,1)}, bf16[4,256,256]{2,1,0:T(8,128)(2,1)}, bf16[4,256,256]{2,1,0:T(8,128)(2,1)}, bf16[4,256,256]{2,1,0:T(8,128)(2,1)S(1)}) fusion(bf16[4,4,256,256]{3,2,1,0:T(8,128)(2,1)} %param.13, s32[]{:T(128)S(6)} %select_n.135, s32[]{:T(128)S(6)} %select_n.134, s32[]{:T(128)S(6)} %select_n.133, ...), kind=kLoop, calls=%fused_computation.11 | loop fusion | bytes 4194320 | tf_op jit(solution)/shard_map/jit(dynamic_index_in_dim)/squeeze | solution.py:398
  41.7 1.6 collective-permute-start.5
  43.3 0.1 collective-permute-start.4
  43.4 0.5 collective-permute-start.3
  43.9 0.0 copy-done.8
  43.9 0.1 copy.20
  43.9 0.0 copy-done.7
  44.0 0.1 add_bitcast_fusion
  44.0 43.6 %all-gather.1 = s32[4,4,5]{2,1,0:T(4,128)S(1)} all-gather(s32[1,4,5]{2,1,0:T(4,128)S(1)} %add_bitcast_fusion), channel_id=2, replica_groups=mesh['ang'=8,'pos'=4] {'pos'}, dimensions={0}, use_global_device_ids=true | all-gather | bytes 400 | tf_op jit(solution)/shard_map/all_gather | solution.py:393
  87.6 0.0 collective-permute-done.5.refs_3_
  87.6 0.0 collective-permute-done.4.refs_2_
  87.6 0.0 collective-permute-done.3.refs_1_
  87.6 0.0 all-to-all-done.sino_ref
  87.7 0.0 copy-done.1
  87.7 0.0 copy-done.2
  87.7 0.0 copy-done.3
  87.7 26.8 %exit_gradient.1 = (bf16[32,16,2048]{2,1,0:T(8,128)(2,1)}, bf16[4,2,256,512]{3,2,1,0:T(8,128)(2,1)}) custom-call(s32[4,5]{1,0:T(4,128)S(1)} %bitcast.53, bf16[2,256,256]{2,1,0:T(8,128)(2,1)S(1)} %copy-done.3, bf16[512,512]{1,0:T(8,128)(2,1)S(1)} %copy-done.2, bf16[512,512]{1,0:T(8,128)(2,1)S(1)} %copy-done.1, bf16[32,16,2048]{2,1,0:T(8,128)(2,1)} %all-to-all-done.sino_ref, ...), custom_call_target="tpu_custom_call" | custom-call | tf_op jit(solution)/shard_map/exit_gradient/pallas_call | solution.py:326
  114.5 4.5 %all-to-all-start.1 = ((bf16[32,16,2048]{2,1,0:T(8,128)(2,1)}), bf16[32,16,2048]{2,1,0:T(8,128)(2,1)S(1)}, u32[]{:S(2)}, u32[]{:S(2)}) async-start(bf16[32,16,2048]{2,1,0:T(8,128)(2,1)} %get-tuple-element.18), calls=%async_computation.1 | async-start | bytes 4194304 | tf_op jit(solution)/shard_map/all_to_all | solution.py:417
  119.0 2.6 %slice_bitcast_fusion = (bf16[2,256,512]{2,1,0:T(8,128)(2,1)}, bf16[2,256,512]{2,1,0:T(8,128)(2,1)}, bf16[2,256,512]{2,1,0:T(8,128)(2,1)}) fusion(bf16[4,2,256,512]{3,2,1,0:T(8,128)(2,1)} %get-tuple-element.23), kind=kLoop, calls=%fused_computation.8 | loop fusion | bytes 3145728 | tf_op jit(solution)/shard_map/squeeze | solution.py:416
  121.6 0.4 collective-permute-start.11
  122.0 1.3 collective-permute-start.10
  123.3 0.4 collective-permute-start.9
  123.7 43.8 %all-to-all-done.1.grad_ref = bf16[32,16,2048]{2,1,0:T(8,128)(2,1)S(1)} async-done(((bf16[32,16,2048]{2,1,0:T(8,128)(2,1)}), bf16[32,16,2048]{2,1,0:T(8,128)(2,1)S(1)}, u32[]{:S(2)}, u32[]{:S(2)}) %all-to-all-start.1) | async-done | bytes 2097184 | tf_op jit(solution)/shard_map/all_to_all | solution.py:417
  167.5 0.0 copy-start.4
  167.5 1.3 copy-done.4
  168.8 15.9 %back_project.1 = (bf16[16,8192]{1,0:T(8,128)(2,1)S(1)}, bf16[16,8192]{1,0:T(8,128)(2,1)S(1)}, bf16[16,8192]{1,0:T(8,128)(2,1)S(1)}, bf16[16,8192]{1,0:T(8,128)(2,1)S(1)}) custom-call(s32[32,128]{1,0:T(8,128)S(1)} %copy.22.idx_ref, bf16[32,64,256]{2,1,0:T(8,128)(2,1)S(1)} %copy-done, bf16[32,16,2048]{2,1,0:T(8,128)(2,1)} %copy-done.4), custom_call_target="tpu_custom_call" | custom-call | tf_op jit(solution)/shard_map/back_project/pallas_call | solution.py:180
  184.7 1.7 collective-permute-start.6
  186.4 0.5 collective-permute-start.7
  187.0 0.0 collective-permute-done.11
  187.0 0.0 collective-permute-start.8
  187.0 0.0 collective-permute-done.10
  187.0 0.0 collective-permute-done.9
  187.0 1.7 select_bitcast_fusion.3
  188.7 0.3 maximum_convert_fusion
  189.0 4.7 %copy.23 = f32[2,256,4,512]{3,2,1,0:T(4,128)} copy(f32[2,256,4,512]{3,1,0,2:T(8,128)S(1)} %maximum_convert_fusion) | data formatting | bytes 8388608
  193.7 0.0 copy-start.5
  193.8 0.0 collective-permute-done.6
  193.8 5.3 %collective-permute-done.7 = bf16[16,8192]{1,0:T(8,128)(2,1)S(1)} collective-permute-done((bf16[16,8192]{1,0:T(8,128)(2,1)S(1)}, bf16[16,8192]{1,0:T(8,128)(2,1)S(1)}, u32[]{:S(2)}, u32[]{:S(2)}) %collective-permute-start.7) | collective-permute-done | bytes 262176 | tf_op jit(solution)/shard_map/ppermute | solution.py:35
  199.1 0.0 collective-permute-done.8
  199.1 0.1 select_bitcast_fusion.7
  199.2 0.0 copy-done.5
  199.2 1.6 multiply_add_fusion
  (1 shorter events, 0.0 us)
Async XLA Ops:
  0.6 4.3 %copy-start.6 = (s32[32,32,4]{1,2,0:T(4,128)S(1)}, s32[32,32,4]{1,2,0:T(4,128)}, u32[]{:S(2)}) copy-start(s32[32,32,4]{1,2,0:T(4,128)} %param.11) | copy-start | bytes 49156
  0.6 15.8 %copy-start = (bf16[32,64,256]{2,1,0:T(8,128)(2,1)S(1)}, bf16[32,64,256]{2,1,0:T(8,128)(2,1)}, u32[]{:S(2)}) copy-start(bf16[32,64,256]{2,1,0:T(8,128)(2,1)} %radon_ref.3) | copy-start | bytes 3145732
  2.0 9.5 %collective-permute-start.2 = (bf16[16,8192]{1,0:T(8,128)(2,1)S(1)}, bf16[16,8192]{1,0:T(8,128)(2,1)S(1)}, u32[]{:S(2)}, u32[]{:S(2)}) collective-permute-start(bf16[16,8192]{1,0:T(8,128)(2,1)S(1)} %get-tuple-element.45), channel_id=1, source_target_pairs={{0,3},{1,2},{2,1},{3,0},{4,7},{5,6},{6,5},{7,4},{8,11},{9,10},{10,... | collective-permute-start | bytes 786440 | tf_op jit(solution)/shard_map/ppermute | solution.py:35
  4.7 6.8 %collective-permute-start = (bf16[16,8192]{1,0:T(8,128)(2,1)S(1)}, bf16[16,8192]{1,0:T(8,128)(2,1)S(1)}, u32[]{:S(2)}, u32[]{:S(2)}) collective-permute-start(bf16[16,8192]{1,0:T(8,128)(2,1)S(1)} %get-tuple-element.46), channel_id=1, source_target_pairs={{0,1},{1,0},{2,3},{3,2},{4,5},{5,4},{6,7},{7,6},{8,9},{9,8},{10,11... | collective-permute-start | bytes 786440 | tf_op jit(solution)/shard_map/ppermute | solution.py:35
  4.7 11.7 %collective-permute-start.1 = (bf16[16,8192]{1,0:T(8,128)(2,1)S(1)}, bf16[16,8192]{1,0:T(8,128)(2,1)S(1)}, u32[]{:S(2)}, u32[]{:S(2)}) collective-permute-start(bf16[16,8192]{1,0:T(8,128)(2,1)S(1)} %get-tuple-element.48), channel_id=1, source_target_pairs={{0,2},{1,3},{2,0},{3,1},{4,6},{5,7},{6,4},{7,5},{8,10},{9,11},{10,... | collective-permute-start | bytes 786440 | tf_op jit(solution)/shard_map/ppermute | solution.py:35
  31.8 55.9 %all-to-all-start = ((bf16[32,16,2048]{2,1,0:T(8,128)(2,1)}), bf16[32,16,2048]{2,1,0:T(8,128)(2,1)}, u32[]{:S(2)}, u32[]{:S(2)}) async-start(bf16[32,16,2048]{2,1,0:T(8,128)(2,1)} %project.1), calls=%async_computation | async-start | bytes 4194304 | tf_op jit(solution)/shard_map/all_to_all | solution.py:411
  38.9 5.0 %copy-start.8 = (s32[4,1]{0,1:T(1,128)S(1)}, s32[4,1]{0,1:T(1,128)}, u32[]{:S(2)}) copy-start(s32[4,1]{0,1:T(1,128)} %param.15) | copy-start | bytes 52
  38.9 5.1 %copy-start.7 = (s32[4,4]{1,0:T(4,128)S(1)}, s32[4,4]{1,0:T(4,128)}, u32[]{:S(2)}) copy-start(s32[4,4]{1,0:T(4,128)} %param.14) | copy-start | bytes 196
  38.9 48.8 %copy-start.1 = (bf16[512,512]{1,0:T(8,128)(2,1)S(1)}, bf16[512,512]{1,0:T(8,128)(2,1)}, u32[]{:S(2)}) copy-start(bf16[512,512]{1,0:T(8,128)(2,1)} %constant.94.inverse_ref) | copy-start | bytes 1572868
  38.9 48.8 %copy-start.2 = (bf16[512,512]{1,0:T(8,128)(2,1)S(1)}, bf16[512,512]{1,0:T(8,128)(2,1)}, u32[]{:S(2)}) copy-start(bf16[512,512]{1,0:T(8,128)(2,1)} %constant.91.forward_ref) | copy-start | bytes 1572868
  38.9 48.8 %copy-start.3 = (bf16[2,256,256]{2,1,0:T(8,128)(2,1)S(1)}, bf16[2,256,256]{2,1,0:T(8,128)(2,1)}, u32[]{:S(2)}) copy-start(bf16[2,256,256]{2,1,0:T(8,128)(2,1)} %probe_ref.1) | copy-start | bytes 786436
  41.7 45.9 %collective-permute-start.5 = (bf16[4,256,256]{2,1,0:T(8,128)(2,1)}, bf16[4,256,256]{2,1,0:T(8,128)(2,1)S(1)}, u32[]{:S(2)}, u32[]{:S(2)}) collective-permute-start(bf16[4,256,256]{2,1,0:T(8,128)(2,1)} %get-tuple-element.37), channel_id=1, source_target_pairs={{0,3},{1,2},{2,1},{3,0},{4,7},{5,6},{6,5},{7,4},{8,11},{9,10},{10,... | collective-permute-start | bytes 1572872 | tf_op jit(solution)/shard_map/ppermute | solution.py:35
  43.3 44.3 %collective-permute-start.4 = (bf16[4,256,256]{2,1,0:T(8,128)(2,1)}, bf16[4,256,256]{2,1,0:T(8,128)(2,1)}, u32[]{:S(2)}, u32[]{:S(2)}) collective-permute-start(bf16[4,256,256]{2,1,0:T(8,128)(2,1)} %get-tuple-element.38), channel_id=1, source_target_pairs={{0,2},{1,3},{2,0},{3,1},{4,6},{5,7},{6,4},{7,5},{8,10},{9,11},{10,... | collective-permute-start | bytes 1572872 | tf_op jit(solution)/shard_map/ppermute | solution.py:35
  43.4 44.2 %collective-permute-start.3 = (bf16[4,256,256]{2,1,0:T(8,128)(2,1)}, bf16[4,256,256]{2,1,0:T(8,128)(2,1)}, u32[]{:S(2)}, u32[]{:S(2)}) collective-permute-start(bf16[4,256,256]{2,1,0:T(8,128)(2,1)} %get-tuple-element.39), channel_id=1, source_target_pairs={{0,1},{1,0},{2,3},{3,2},{4,5},{5,4},{6,7},{7,6},{8,9},{9,8},{10,11... | collective-permute-start | bytes 1572872 | tf_op jit(solution)/shard_map/ppermute | solution.py:35
  114.5 53.0 %all-to-all-start.1 = ((bf16[32,16,2048]{2,1,0:T(8,128)(2,1)}), bf16[32,16,2048]{2,1,0:T(8,128)(2,1)S(1)}, u32[]{:S(2)}, u32[]{:S(2)}) async-start(bf16[32,16,2048]{2,1,0:T(8,128)(2,1)} %get-tuple-element.18), calls=%async_computation.1 | async-start | bytes 4194304 | tf_op jit(solution)/shard_map/all_to_all | solution.py:417
  121.6 65.4 %collective-permute-start.11 = (bf16[2,256,512]{2,1,0:T(8,128)(2,1)}, bf16[2,256,512]{2,1,0:T(8,128)(2,1)}, u32[]{:S(2)}, u32[]{:S(2)}) collective-permute-start(bf16[2,256,512]{2,1,0:T(8,128)(2,1)} %get-tuple-element.34), channel_id=1, source_target_pairs={{0,1},{1,0},{2,3},{3,2},{4,5},{5,4},{6,7},{7,6},{8,9},{9,8},{10,11... | collective-permute-start | bytes 1572872 | tf_op jit(solution)/shard_map/ppermute | solution.py:35
  122.0 65.0 %collective-permute-start.10 = (bf16[2,256,512]{2,1,0:T(8,128)(2,1)}, bf16[2,256,512]{2,1,0:T(8,128)(2,1)}, u32[]{:S(2)}, u32[]{:S(2)}) collective-permute-start(bf16[2,256,512]{2,1,0:T(8,128)(2,1)} %get-tuple-element.35), channel_id=1, source_target_pairs={{0,2},{1,3},{2,0},{3,1},{4,6},{5,7},{6,4},{7,5},{8,10},{9,11},{10,... | collective-permute-start | bytes 1572872 | tf_op jit(solution)/shard_map/ppermute | solution.py:35
  123.3 63.7 %collective-permute-start.9 = (bf16[2,256,512]{2,1,0:T(8,128)(2,1)}, bf16[2,256,512]{2,1,0:T(8,128)(2,1)}, u32[]{:S(2)}, u32[]{:S(2)}) collective-permute-start(bf16[2,256,512]{2,1,0:T(8,128)(2,1)} %get-tuple-element.36), channel_id=1, source_target_pairs={{0,3},{1,2},{2,1},{3,0},{4,7},{5,6},{6,5},{7,4},{8,11},{9,10},{10,... | collective-permute-start | bytes 1572872 | tf_op jit(solution)/shard_map/ppermute | solution.py:35
  167.5 1.3 copy-start.4
  184.7 9.1 %collective-permute-start.6 = (bf16[16,8192]{1,0:T(8,128)(2,1)S(1)}, bf16[16,8192]{1,0:T(8,128)(2,1)S(1)}, u32[]{:S(2)}, u32[]{:S(2)}) collective-permute-start(bf16[16,8192]{1,0:T(8,128)(2,1)S(1)} %get-tuple-element.19), channel_id=1, source_target_pairs={{0,3},{1,2},{2,1},{3,0},{4,7},{5,6},{6,5},{7,4},{8,11},{9,10},{10,... | collective-permute-start | bytes 786440 | tf_op jit(solution)/shard_map/ppermute | solution.py:35
  186.4 12.6 %collective-permute-start.7 = (bf16[16,8192]{1,0:T(8,128)(2,1)S(1)}, bf16[16,8192]{1,0:T(8,128)(2,1)S(1)}, u32[]{:S(2)}, u32[]{:S(2)}) collective-permute-start(bf16[16,8192]{1,0:T(8,128)(2,1)S(1)} %get-tuple-element.20), channel_id=1, source_target_pairs={{0,2},{1,3},{2,0},{3,1},{4,6},{5,7},{6,4},{7,5},{8,10},{9,11},{10,... | collective-permute-start | bytes 786440 | tf_op jit(solution)/shard_map/ppermute | solution.py:35
  187.0 12.1 %collective-permute-start.8 = (bf16[16,8192]{1,0:T(8,128)(2,1)S(1)}, bf16[16,8192]{1,0:T(8,128)(2,1)S(1)}, u32[]{:S(2)}, u32[]{:S(2)}) collective-permute-start(bf16[16,8192]{1,0:T(8,128)(2,1)S(1)} %get-tuple-element.21), channel_id=1, source_target_pairs={{0,1},{1,0},{2,3},{3,2},{4,5},{5,4},{6,7},{7,6},{8,9},{9,8},{10,11... | collective-permute-start | bytes 786440 | tf_op jit(solution)/shard_map/ppermute | solution.py:35
  193.7 5.4 %copy-start.5 = (bf16[2,32,8192]{2,1,0:T(8,128)(2,1)S(1)}, bf16[2,32,8192]{2,1,0:T(8,128)(2,1)}, u32[]{:S(2)}) copy-start(bf16[2,32,8192]{2,1,0:T(8,128)(2,1)} %param.9) | copy-start | bytes 3145732

commit v2 on v1

v2 whole, which is shorter than its diff:
```python
import functools
import math

import jax
import jax.numpy as jnp
import numpy as np
from jax import lax
from jax.experimental import pallas as pl
from jax.experimental.pallas import tpu as pltpu
from jax.sharding import PartitionSpec as P

step_size = 0.1
LANES = 128
ROWS = 16
GROUP = 8
VMEM_LIMIT = 50 * 1024 * 1024
everywhere = pl.BlockSpec(memory_space=pltpu.VMEM)
scalars = pl.BlockSpec(memory_space=pltpu.SMEM)
CHAINS = 4


def dft_tables(width):
    index = np.arange(width)
    turn = 2.0 * math.pi / width * (index[:, None] * index[None, :] % width)
    cosine = jnp.asarray(np.cos(turn) / math.sqrt(width), jnp.bfloat16)
    sine_neg = jnp.asarray(-np.sin(turn) / math.sqrt(width), jnp.bfloat16)
    forward = jnp.block([[cosine, -sine_neg], [sine_neg, cosine]])
    inverse = jnp.block([[cosine, sine_neg], [-sine_neg, cosine]])
    return (forward, inverse)


def rotate_pos(pieces, sign):
    count = len(pieces)
    return [pieces[0]] + [
        lax.ppermute(pieces[j], "pos", [(i, (i + sign * j) % count) for i in range(count)])
        for j in range(1, count)
    ]


def in_order(pieces, first):
    count = len(pieces)
    bit = 1
    while bit < count:
        flip = (first & bit) != 0
        pieces = [jnp.where(flip, pieces[(k + bit) % count], pieces[k]) for k in range(count)]
        bit *= 2
    return pieces


def lower_half(shape):
    return lax.broadcasted_iota(jnp.int32, shape, len(shape) - 1) < LANES // 2


def swap_halves(tile):
    return pltpu.roll(tile, LANES // 2, 1)


def arrange_kernel(pieces, *refs):
    vol_refs, vv_ref = refs[:pieces], refs[pieces]
    per_piece = vol_refs[0].shape[1] // LANES
    tiles = per_piece * pieces
    for k in range(pieces):

        @pl.loop(0, per_piece, unroll=4)
        def _(t):
            tile = vol_refs[k][:, pl.ds(pl.multiple_of(t * LANES, LANES), LANES)]
            vv_ref[k * per_piece + t] = tile
            swapped = swap_halves(tile.astype(jnp.float32)).astype(jnp.bfloat16)
            vv_ref[tiles + k * per_piece + t] = swapped


def project_chunk(chunks, idx_ref, radon_ref, vv_ref, out_refs, lhs_ref):
    angles, block, span = radon_ref.shape
    blocks = out_refs[0].shape[2] // block
    feeds = span // block
    low = lower_half((ROWS, LANES))

    @pl.loop(0, angles // 2)
    def _(step):
        for n in range(2):
            a = step * 2 + n
            for i, chunk in enumerate(chunks):
                for b in range(blocks):
                    row = (i * blocks + b) * ROWS
                    for jp in range(feeds // 2):
                        at = (chunk * blocks + b) * feeds + 2 * jp
                        first = vv_ref[idx_ref[a, at]]
                        second = vv_ref[idx_ref[a, at + 1]]
                        lhs_ref[n, row : row + ROWS, jp * LANES : (jp + 1) * LANES] = jnp.where(
                            low, first, second
                        )
        for n in range(2):
            a = step * 2 + n
            product = lax.dot_general(
                lhs_ref[n], radon_ref[a], (((1,), (1,)), ((), ())), preferred_element_type=jnp.float32
            )
            for i in range(len(chunks)):
                for pair in range(blocks // 2):
                    row = (i * blocks + 2 * pair) * ROWS
                    tile = jnp.concatenate(
                        [product[row : row + ROWS], product[row + ROWS : row + 2 * ROWS]], axis=1
                    )
                    out_refs[i][a, :, pair * LANES : (pair + 1) * LANES] = tile.astype(jnp.bfloat16)


def project_first_kernel(pieces, idx_ref, radon_ref, *refs):
    vol_refs = refs[:pieces]
    out_ref, vv_ref, lhs_ref = refs[pieces:]
    arrange_kernel(pieces, *vol_refs, vv_ref)
    project_chunk([0], idx_ref, radon_ref, vv_ref, [out_ref], lhs_ref)


def project_rest_kernel(pieces, idx_ref, radon_ref, vv_ref, *refs):
    out_refs, lhs_ref = refs[: pieces - 1], refs[pieces - 1]
    project_chunk(list(range(1, pieces)), idx_ref, radon_ref, vv_ref, out_refs, lhs_ref)


def project(idx, radon_tiles, vol_pieces, tile_width):
    angles, block, span = radon_tiles.shape
    pieces = len(vol_pieces)
    tiles = pieces * vol_pieces[0].shape[1] // LANES
    rows = tile_width // block * ROWS
    chunk_shape = jax.ShapeDtypeStruct((angles, ROWS, tile_width), jnp.bfloat16)
    params = pltpu.CompilerParams(vmem_limit_bytes=VMEM_LIMIT)
    first, vv = pl.pallas_call(
        functools.partial(project_first_kernel, pieces),
        out_shape=[chunk_shape, jax.ShapeDtypeStruct((2 * tiles, ROWS, LANES), jnp.bfloat16)],
        in_specs=[scalars, everywhere] + [everywhere] * pieces,
        out_specs=[everywhere] * 2,
        scratch_shapes=[pltpu.VMEM((2, rows, span), jnp.bfloat16)],
        compiler_params=params,
        name="project_first",
    )(idx, radon_tiles, *vol_pieces)
    rest = pl.pallas_call(
        functools.partial(project_rest_kernel, pieces),
        out_shape=[chunk_shape] * (pieces - 1),
        in_specs=[scalars, everywhere, everywhere],
        out_specs=[everywhere] * (pieces - 1),
        scratch_shapes=[pltpu.VMEM((2, (pieces - 1) * rows, span), jnp.bfloat16)],
        compiler_params=params,
        name="project_rest",
    )(idx, radon_tiles, vv)
    return [first] + list(rest)


def back_project_kernel(chunks, pieces, has_start, idx_ref, radon_ref, *refs):
    grad_refs, refs = refs[: len(chunks)], refs[len(chunks) :]
    start_refs, refs = (refs[:pieces], refs[pieces:]) if has_start else (None, refs)
    out_refs, refs = refs[:pieces], refs[pieces:]
    acc_refs, contrib_ref = refs[:CHAINS], refs[CHAINS]
    angles, block, span = radon_ref.shape
    per_piece = out_refs[0].shape[1] // LANES
    tiles = per_piece * pieces
    blocks = grad_refs[0].shape[2] // block
    pairs = blocks // 2
    feeds = span // block

    @pl.loop(0, 2 * tiles, unroll=8)
    def _(t):
        for acc_ref in acc_refs:
            acc_ref[t] = jnp.zeros((ROWS, LANES), jnp.float32)

    low = lower_half((ROWS, LANES))

    @pl.loop(0, angles // CHAINS)
    def _(step):
        for n in range(CHAINS):
            a = step * CHAINS + n
            lhs = []
            for grad_ref in grad_refs:
                for pair in range(pairs):
                    tile = grad_ref[a, :, pair * LANES : (pair + 1) * LANES]
                    lhs += [tile[:, :block], tile[:, block:]]
            contrib_ref[n] = jnp.dot(
                jnp.concatenate(lhs, axis=0), radon_ref[a], preferred_element_type=jnp.float32
            )
        for i, chunk in enumerate(chunks):
            for b in range(blocks):
                row = (i * blocks + b) * ROWS
                for jp in range(feeds // 2):
                    at = (chunk * blocks + b) * feeds + 2 * jp
                    for n in range(CHAINS):
                        a = step * CHAINS + n
                        tile = contrib_ref[n, row : row + ROWS, jp * LANES : (jp + 1) * LANES]
                        first, second = idx_ref[a, at], idx_ref[a, at + 1]
                        acc_refs[n][first] += jnp.where(low, tile, 0.0)
                        acc_refs[n][second] += jnp.where(low, 0.0, tile)

    for k in range(pieces):

        @pl.loop(0, per_piece, unroll=4)
        def _(t):
            lanes = pl.ds(pl.multiple_of(t * LANES, LANES), LANES)
            straight = acc_refs[0][k * per_piece + t]
            crossed = acc_refs[0][tiles + k * per_piece + t]
            for acc_ref in acc_refs[1:]:
                straight += acc_ref[k * per_piece + t]
                crossed += acc_ref[tiles + k * per_piece + t]
            total = straight + swap_halves(crossed)
            if has_start:
                total += start_refs[k][:, lanes]
            out_refs[k][:, lanes] = total.astype(out_refs[k].dtype)


def back_project(idx, radon_tiles, grads, chunks, start, pieces, piece_width, out_type, name):
    angles, block, span = radon_tiles.shape
    tiles = pieces * piece_width // LANES
    rows = len(chunks) * grads[0].shape[2] // block * ROWS
    has_start = start is not None
    operands = [idx, radon_tiles] + list(grads) + (list(start) if has_start else [])
    return pl.pallas_call(
        functools.partial(back_project_kernel, chunks, pieces, has_start),
        out_shape=[jax.ShapeDtypeStruct((ROWS, piece_width), out_type)] * pieces,
        in_specs=[scalars] + [everywhere] * (len(operands) - 1),
        out_specs=[everywhere] * pieces,
        scratch_shapes=[pltpu.VMEM((2 * tiles, ROWS, LANES), jnp.float32)] * CHAINS
        + [pltpu.VMEM((CHAINS, rows, span), jnp.float32)],
        compiler_params=pltpu.CompilerParams(vmem_limit_bytes=VMEM_LIMIT),
        name=name,
    )(*operands)


def exit_kernel(
    step, last, meta_ref, probe_ref, forward_ref, inverse_ref, own_ref, next_ref, amp_ref, *refs
):
    spill_in_ref, refs = (refs[0], refs[1:]) if step > 0 else (None, refs)
    partial_ref, refs = (refs[0], refs[1:]) if step == last else (None, refs)
    out_ref, beyond_ref, ext_ref, acc_ref, wave_ref, half_ref = refs
    owner = lax.rem(lax.axis_index("pos") + step, last + 1)
    groups = own_ref.shape[0]
    width = probe_ref.shape[1]
    tile_width = own_ref.shape[2]
    reach = tile_width + width
    slots = amp_ref.shape[0]
    chunk = 4
    crows = chunk * GROUP
    lane_id = lax.broadcasted_iota(jnp.int32, (crows, LANES), 1)
    wide = width // LANES

    @pl.loop(0, groups)
    def _(g):
        ext_ref[g, :, :tile_width] = own_ref[g]
        ext_ref[g, :, tile_width:] = next_ref[g, :, :width]
        rows = pl.ds(pl.multiple_of(g * GROUP, GROUP), GROUP)
        for c in range(2):
            if step > 0:
                acc_ref[c, rows, :width] = spill_in_ref[c, rows, :]
                acc_ref[c, rows, width:] = jnp.zeros((GROUP, tile_width), jnp.float32)
            else:
                acc_ref[c, rows, :] = jnp.zeros((GROUP, reach), jnp.float32)

    def product(left, right):
        return jnp.dot(left, right, preferred_element_type=jnp.float32)

    def slot_step(q, carry):
        offset = meta_ref[owner, q] - owner * tile_width
        first_tile = offset // LANES
        shift = offset % LANES
        starts = [pl.multiple_of((first_tile + m) * LANES, LANES) for m in range(wide + 1)]
        keep = lane_id < LANES - shift
        back_shift = (LANES - shift) % LANES
        for ch in range(groups // chunk):
            rows = slice(ch * crows, (ch + 1) * crows)
            turned = []
            for start in starts:
                both = ext_ref[ch * chunk : (ch + 1) * chunk, :, pl.ds(start, LANES)].astype(
                    jnp.float32
                )
                turned.append(
                    [
                        pltpu.roll(
                            both[:, c * GROUP : (c + 1) * GROUP].reshape(crows, LANES), back_shift, 1
                        )
                        for c in range(2)
                    ]
                )
            for m in range(wide):
                lanes = slice(m * LANES, (m + 1) * LANES)
                patch_re = jnp.where(keep, turned[m][0], turned[m + 1][0])
                patch_im = jnp.where(keep, turned[m][1], turned[m + 1][1])
                probe_re = probe_ref[0, rows, lanes].astype(jnp.float32)
                probe_im = probe_ref[1, rows, lanes].astype(jnp.float32)
                wave_ref[rows, lanes] = (probe_re * patch_re - probe_im * patch_im).astype(
                    jnp.bfloat16
                )
                wave_ref[width + ch * crows : width + (ch + 1) * crows, lanes] = (
                    probe_re * patch_im + probe_im * patch_re
                ).astype(jnp.bfloat16)
        half = product(forward_ref[...], wave_ref[...]).astype(jnp.bfloat16)
        half_ref[:, :width] = half[:width]
        half_ref[:, width:] = half[width:]
        far = product(half_ref[...], inverse_ref[...])
        for ch in range(groups // chunk):
            rows = slice(ch * crows, (ch + 1) * crows)
            far_re, far_im = far[rows, :width], far[rows, width:]
            power = far_re * far_re + far_im * far_im
            amps = amp_ref[q, rows, :].astype(jnp.float32)
            factor = amps * lax.rsqrt(jnp.maximum(power, 1.0)) - 1.0
            wave_ref[rows, :] = (far_re * factor).astype(jnp.bfloat16)
            wave_ref[width + ch * crows : width + (ch + 1) * crows, :] = (far_im * factor).astype(
                jnp.bfloat16
            )
        back = product(inverse_ref[...], wave_ref[...]).astype(jnp.bfloat16)
        half_ref[:, :width] = back[:width]
        half_ref[:, width:] = back[width:]
        near = product(half_ref[...], forward_ref[...])
        past = lane_id >= shift
        for ch in range(groups // chunk):
            rows = slice(ch * crows, (ch + 1) * crows)
            turned = []
            for m in range(wide):
                lanes = slice(m * LANES, (m + 1) * LANES)
                probe_re = probe_ref[0, rows, lanes].astype(jnp.float32)
                probe_im = probe_ref[1, rows, lanes].astype(jnp.float32)
                near_re = near[rows, m * LANES : (m + 1) * LANES]
                near_im = near[rows, width + m * LANES : width + (m + 1) * LANES]
                turned.append(
                    [
                        pltpu.roll(probe_re * near_re + probe_im * near_im, shift, 1),
                        pltpu.roll(probe_re * near_im - probe_im * near_re, shift, 1),
                    ]
                )
            for m in range(wide + 1):
                for c in range(2):
                    behind = turned[m - 1][c] if m > 0 else 0.0
                    ahead = turned[m][c] if m < wide else 0.0
                    acc_ref[c, rows, pl.ds(starts[m], LANES)] += jnp.where(past, ahead, behind)
        return carry

    lax.fori_loop(0, meta_ref[owner, slots], slot_step, 0)

    @pl.loop(0, groups)
    def _(g):
        rows = pl.ds(pl.multiple_of(g * GROUP, GROUP), GROUP)
        if step == 0:
            for c in range(2):
                out_ref[c, rows, :] = acc_ref[c, rows, :tile_width]
        else:
            both = [acc_ref[c, rows, :tile_width] for c in range(2)]
            out_ref[g] = jnp.concatenate(both, axis=0).astype(jnp.bfloat16)
        if step == last:
            both = []
            for c in range(2):
                whole = partial_ref[c, rows, :]
                spilled = whole[:, :width] + acc_ref[c, rows, tile_width:]
                both.append(jnp.concatenate([spilled, whole[:, width:]], axis=1))
            beyond_ref[g] = jnp.concatenate(both, axis=0).astype(jnp.bfloat16)
        else:
            for c in range(2):
                beyond_ref[c, rows, :] = acc_ref[c, rows, tile_width:]


def exit_gradient(step, last, meta, probe_field, tables, own, ahead, amps, spill, partial):
    groups, rows, tile_width = own.shape
    width = probe_field.shape[1]
    slices = groups * GROUP
    grad_shape = jax.ShapeDtypeStruct(own.shape, jnp.bfloat16)
    partial_shape = jax.ShapeDtypeStruct((2, slices, tile_width), jnp.float32)
    spill_shape = jax.ShapeDtypeStruct((2, slices, width), jnp.float32)
    operands = [meta, probe_field, *tables, own, ahead, amps]
    if step > 0:
        operands.append(spill)
    if step == last:
        operands.append(partial)
    return pl.pallas_call(
        functools.partial(exit_kernel, step, last),
        out_shape=[
            partial_shape if step == 0 else grad_shape,
            grad_shape if step == last else spill_shape,
        ],
        in_specs=[scalars] + [everywhere] * (len(operands) - 1),
        out_specs=[everywhere] * 2,
        scratch_shapes=[
            pltpu.VMEM((groups, rows, tile_width + width), jnp.bfloat16),
            pltpu.VMEM((2, slices, tile_width + width), jnp.float32),
            pltpu.VMEM((2 * width, width), jnp.bfloat16),
            pltpu.VMEM((width, 2 * width), jnp.bfloat16),
        ],
        compiler_params=pltpu.CompilerParams(vmem_limit_bytes=VMEM_LIMIT),
        name="exit_gradient_" + str(step),
    )(*operands)


def to_groups(received, own_slices):
    if own_slices == GROUP:
        return received
    devices, rows, columns = received.shape
    merge = GROUP // own_slices
    split = received.reshape(devices // merge, merge, 2, own_slices, columns)
    return split.transpose(0, 2, 1, 3, 4).reshape(devices // merge, ROWS, columns)


def from_groups(grouped, own_slices):
    if own_slices == GROUP:
        return grouped
    groups, rows, columns = grouped.shape
    merge = GROUP // own_slices
    split = grouped.reshape(groups, 2, merge, own_slices, columns)
    return split.transpose(0, 2, 1, 3, 4).reshape(groups * merge, 2 * own_slices, columns)


def pad_rows(block):
    return jnp.pad(block, [(0, 0)] * (block.ndim - 2) + [(0, ROWS - block.shape[-2]), (0, 0)])


def everyone(chunk):
    return lax.all_to_all(chunk, ("ang", "pos"), 0, 0, tiled=True)


def on_device(volume, radon_tiles, tile_blocks, probe_field, amplitudes, offsets, counts):
    n_pos = lax.axis_size("pos")
    pos = lax.axis_index("pos")
    angles, det_blocks, feeds = tile_blocks.shape
    block_size = radon_tiles.shape[1]
    columns = det_blocks * block_size
    tile_width = columns // n_pos
    slab = volume.shape[1]
    width = volume.shape[2]
    own = slab // n_pos
    rows = 2 * own
    blocks_each = width // block_size
    last = n_pos - 1

    def slices_for(j):
        start = (pos + j) % n_pos * own
        return lax.dynamic_slice_in_dim(volume, start, own, 1).reshape(rows, width)

    vol_pieces = rotate_pos([slices_for(j) for j in range(n_pos)], 1)
    meta = lax.all_gather(jnp.concatenate([offsets, counts], axis=1), "pos", axis=0)
    meta = lax.dynamic_index_in_dim(meta, pos, 1, keepdims=False)
    vol_pieces, amplitudes = lax.optimization_barrier((vol_pieces, amplitudes))
    amp_pieces = rotate_pos(
        [
            lax.dynamic_index_in_dim(amplitudes, (pos - j) % n_pos, 0, keepdims=False)
            for j in range(n_pos)
        ],
        -1,
    )

    owner = tile_blocks // blocks_each
    within = tile_blocks % blocks_each
    crossed = (within + jnp.arange(feeds, dtype=jnp.int32)) % 2
    tiles_each = width // LANES
    idx = crossed * (n_pos * tiles_each) + (pos - owner) % n_pos * tiles_each + within // 2
    idx = idx.reshape(angles // n_pos, n_pos, n_pos, det_blocks // n_pos * feeds)
    idx = jnp.stack([jnp.roll(idx[:, p], -p, axis=1) for p in range(n_pos)], axis=1)
    idx = idx.reshape(angles, det_blocks * feeds)

    sino = project(idx, radon_tiles, [pad_rows(piece) for piece in vol_pieces], tile_width)
    received = [to_groups(everyone(chunk[:, :rows]), own) for chunk in sino]
    tables = dft_tables(probe_field.shape[1])
    grads = [None] * n_pos
    partial = spill = None
    for j in range(n_pos):
        ahead = received[(j + 1) % n_pos]
        one, other = exit_gradient(
            j, last, meta, probe_field, tables, received[j], ahead, amp_pieces[j], spill, partial
        )
        if j == 0:
            partial, spill = one, other
        elif j < last:
            grads[j], spill = one, other
        else:
            grads[j], grads[0] = one, other
    order = list(range(1, n_pos)) + [0]
    returned = {j: pad_rows(everyone(from_groups(grads[j], own))) for j in order}
    early = order[:-1]
    partial_grad = back_project(
        idx, radon_tiles, [returned[j] for j in early], early, None, n_pos, width, jnp.float32, "back_early"
    )
    tile_pieces = rotate_pos(grads, 1)
    obj_pieces = back_project(
        idx, radon_tiles, [returned[0]], [0], partial_grad, n_pos, width, jnp.bfloat16, "back_last"
    )
    groups = grads[0].shape[0]
    tile_pieces = [tile_pieces[-j % n_pos] for j in range(n_pos)]
    tile_pieces = [
        piece.reshape(groups, 2, GROUP, tile_width).transpose(1, 0, 2, 3).reshape(2, groups * GROUP, tile_width)
        for piece in tile_pieces
    ]
    proj_grad = jnp.stack(in_order(tile_pieces, -pos % n_pos), axis=2).astype(jnp.float32)
    obj_pieces = rotate_pos([piece[:rows] for piece in obj_pieces], -1)
    obj_pieces = [piece.reshape(2, own, width) for piece in in_order(obj_pieces, -pos % n_pos)]
    object_grad = jnp.concatenate(obj_pieces, axis=1).astype(jnp.float32)
    new_volume = volume.astype(jnp.float32) + step_size * object_grad
    return (new_volume, proj_grad)


def solution(mesh):
    in_specs = (
        P(None, "ang", "pos"),
        P(),
        P(),
        P(),
        P("ang", "pos", None, None),
        P("ang", "pos"),
        P("ang", "pos"),
    )
    out_specs = (P(None, "ang", "pos"), P(None, None, "ang", "pos"))
    return jax.shard_map(
        on_device, mesh=mesh, in_specs=in_specs, out_specs=out_specs, check_vma=False
    )
```

time: 201 us -> 276 us (1.37)
  blocking collectives: 43.6 us -> 141 us
  waiting for transfers between devices: 60.2 us -> 14.9 us
  Pallas kernels: 58 us -> 78 us
  local copies, waits for them, and re-layouts: 13 us -> 17.1 us
    all_to_all x0 -> x6, blocking collectives: none -> 115 us  [everyone(): return lax.all_to_all(chunk, ('ang', 'pos'), 0, 0, tiled=True)]
    all_to_all x2, waiting for transfers between devices: 43.8 us -> 0.01 us  [everyone(): return lax.all_to_all(chunk, ('ang', 'pos'), 0, 0, tiled=True)]
    pallas_call x3 -> x8, Pallas kernels: 58 us -> 78 us  [the longest x4 31.1 us: exit_gradient(): pl.pallas_call(functools.partial(exit_kernel, step, last), out_shape=[par...]
    all_gather x1, blocking collectives: 43.6 us -> 26.2 us  [on_device(): lax.all_gather(jnp.concatenate([offsets, counts], axis=1), 'pos', axis=0)]
    unnamed x20 -> x35, local copies, waits for them, and re-layouts: 6.17 us -> 12 us
    all_to_all x2, starting transfers between devices: 11.6 us -> 6.85 us  [everyone(): return lax.all_to_all(chunk, ('ang', 'pos'), 0, 0, tiled=True)]
  transfers between devices with their start and end apart: 14 -> 14, of which waited for: 4 -> 4; matrix products, arithmetic and copies ran while one was open for 6% -> 4% of each run, Pallas kernels for 8% -> 18%
where the time goes in v2:
time: 276 us; the launch traced here: 275 us
  blocking collectives  141 us (51%)
  Pallas kernels  78 us (28%)
  starting transfers between devices  18.4 us (7%)
  local copies, waits for them, and re-layouts  17.1 us (6%)
  waiting for transfers between devices  14.9 us (5%)
  other arithmetic  4.16 us (2%)
    all_to_all x6, blocking collectives, everyone(): return lax.all_to_all(chunk, ('ang', 'pos'), 0, 0, tiled=True)  115 us
    pallas_call x4, Pallas kernels, exit_gradient(): pl.pallas_call(functools.partial(exit_kernel, step, last), out_shape=[par...  31.1 us
    all_gather x1, blocking collectives, on_device(): lax.all_gather(jnp.concatenate([offsets, counts], axis=1), 'pos', axis=0)  26.2 us
    pallas_call x2, Pallas kernels, back_project(): pl.pallas_call(functools.partial(back_project_kernel, chunks, pieces, has...  25.2 us
    ppermute x12, waiting for transfers between devices, rotate_pos(): lax.ppermute(pieces[j], 'pos', [(i, (i + sign * j) % count) for i in rang...  14.8 us
    unnamed x35, local copies, waits for them, and re-layouts  12 us
    ppermute x12, starting transfers between devices, rotate_pos(): lax.ppermute(pieces[j], 'pos', [(i, (i + sign * j) % count) for i in rang...  11.6 us
    pallas_call x1, Pallas kernels, project(): pl.pallas_call(functools.partial(project_first_kernel, pieces), out_shape...  11.5 us
  transfers between devices with their start and end apart: 14, of which 4 were waited for; matrix products, arithmetic and copies ran while one was open for 4% of the time, Pallas kernels for 18%

profile of v2, /device:TPU:1, one launch (start us, length us, event | category | flops | bytes accessed | tf_op | source)
XLA Modules:
  0.0 274.6 jit_solution(974257892172505180)
XLA Ops:
  0.6 0.0 copy-start
  0.7 1.3 dynamic-slice_bitcast_fusion.4
  2.1 0.1 collective-permute-start.2
  2.2 2.6 collective-permute-start
  4.8 1.1 collective-permute-start.1
  5.9 0.3 fusion.3
  6.2 0.3 copy.30
  6.5 0.2 reshape.186
  6.9 0.1 reshape.187.idx_ref
  7.0 4.0 %collective-permute-done.2.refs_3_ = bf16[16,8192]{1,0:T(8,128)(2,1)S(1)} collective-permute-done((bf16[16,8192]{1,0:T(8,128)(2,1)S(1)}, bf16[16,8192]{1,0:T(8,128)(2,1)S(1)}, u32[]{:S(2)}, u32[]{:S(2)}) %collective-permute-start.2) | collective-permute-done | bytes 262176 | tf_op jit(solution)/shard_map/ppermute | solution.py:35
  11.0 6.2 %collective-permute-done.1.refs_2_ = bf16[16,8192]{1,0:T(8,128)(2,1)S(1)} collective-permute-done((bf16[16,8192]{1,0:T(8,128)(2,1)S(1)}, bf16[16,8192]{1,0:T(8,128)(2,1)S(1)}, u32[]{:S(2)}, u32[]{:S(2)}) %collective-permute-start.1) | collective-permute-done | bytes 262176 | tf_op jit(solution)/shard_map/ppermute | solution.py:35
  17.2 11.5 %project_first.1 = (bf16[32,16,512]{2,1,0:T(8,128)(2,1)S(1)}, bf16[512,16,128]{2,1,0:T(8,128)(2,1)}) custom-call(s32[32,128]{1,0:T(8,128)S(1)} %reshape.187.idx_ref, bf16[32,64,256]{2,1,0:T(8,128)(2,1)S(1)} %copy-done, bf16[16,8192]{1,0:T(8,128)(2,1)S(1)} %get-tuple-element.28.refs_0_, bf16[16,8192]{1,0:T(8,128)(2,1)S(1)} %collective-permute-done.refs_1_, ...), custom_call_target="tpu_custom_call" | custom-call | tf_op jit(solution)/shard_map/project_first/pallas_call | solution.py:125
  28.7 10.2 %project_rest.1 = (bf16[32,16,512]{2,1,0:T(8,128)(2,1)S(1)}, bf16[32,16,512]{2,1,0:T(8,128)(2,1)S(1)}, bf16[32,16,512]{2,1,0:T(8,128)(2,1)}) custom-call(s32[32,128]{1,0:T(8,128)S(1)} %reshape.187.idx_ref, bf16[32,64,256]{2,1,0:T(8,128)(2,1)S(1)} %copy-done, bf16[512,16,128]{2,1,0:T(8,128)(2,1)} %get-tuple-element.32.vv_ref), custom_call_target="tpu_custom_call" | custom-call | tf_op jit(solution)/shard_map/project_rest/pallas_call | solution.py:134
  38.9 21.2 %all_to_all.40.next_ref.own_ref = bf16[32,16,512]{2,1,0:T(8,128)(2,1)S(1)} all-to-all(bf16[32,16,512]{2,1,0:T(8,128)(2,1)S(1)} %get-tuple-element.36), channel_id=1, replica_groups=mesh['ang'=8,'pos'=4] {'ang','pos'}, dimensions={0} | all-to-all | bytes 1048576 | tf_op jit(solution)/shard_map/all_to_all | solution.py:407
  60.1 18.4 %all_to_all.41.next_ref.own_ref = bf16[32,16,512]{2,1,0:T(8,128)(2,1)S(1)} all-to-all(bf16[32,16,512]{2,1,0:T(8,128)(2,1)S(1)} %get-tuple-element.37), channel_id=1, replica_groups=mesh['ang'=8,'pos'=4] {'ang','pos'}, dimensions={0} | all-to-all | bytes 1048576 | tf_op jit(solution)/shard_map/all_to_all | solution.py:407
  78.5 18.4 %all_to_all.42.own_ref.next_ref = bf16[32,16,512]{2,1,0:T(8,128)(2,1)S(1)} all-to-all(bf16[32,16,512]{2,1,0:T(8,128)(2,1)S(1)} %get-tuple-element.34), channel_id=1, replica_groups=mesh['ang'=8,'pos'=4] {'ang','pos'}, dimensions={0} | all-to-all | bytes 1048576 | tf_op jit(solution)/shard_map/all_to_all | solution.py:407
  96.9 3.4 %all-to-all-start = ((bf16[32,16,512]{2,1,0:T(8,128)(2,1)}), bf16[32,16,512]{2,1,0:T(8,128)(2,1)S(1)}, u32[]{:S(2)}, u32[]{:S(2)}) async-start(bf16[32,16,512]{2,1,0:T(8,128)(2,1)} %get-tuple-element.33), calls=%async_computation | async-start | bytes 1048576 | tf_op jit(solution)/shard_map/all_to_all | solution.py:407
  100.4 0.0 copy-start.15
  100.4 0.0 copy-start.14
  100.5 0.0 copy-start.1
  100.5 0.0 copy-start.2
  100.5 0.0 copy-start.3
  100.5 3.0 %dynamic-slice_bitcast_fusion = (bf16[4,256,256]{2,1,0:T(8,128)(2,1)}, bf16[4,256,256]{2,1,0:T(8,128)(2,1)}, bf16[4,256,256]{2,1,0:T(8,128)(2,1)}, bf16[4,256,256]{2,1,0:T(8,128)(2,1)}) fusion(bf16[4,4,256,256]{3,2,1,0:T(8,128)(2,1)} %param.13, s32[]{:T(128)S(6)} %select_n.309, s32[]{:T(128)S(6)} %select_n.308, s32[]{:T(128)S(6)} %select_n.306, s32[]{:T(128)S(6)} %select_n.304), kind=kLoop, calls=%fused_computation.10 | loop fusion | bytes 4194320 | tf_op jit(solution)/shard_map/jit(dynamic_index_in_dim)/squeeze | solution.py:434
  103.5 0.3 collective-permute-start.5
  103.8 1.5 collective-permute-start.4
  105.3 1.6 collective-permute-start.3
  106.9 0.1 copy.35
  107.0 0.1 add_bitcast_fusion.3
  107.1 26.2 %all-gather.1 = s32[4,4,5]{2,1,0:T(4,128)S(1)} all-gather(s32[1,4,5]{2,1,0:T(4,128)S(1)} %add_bitcast_fusion.3), channel_id=2, replica_groups=mesh['ang'=8,'pos'=4] {'pos'}, dimensions={0}, use_global_device_ids=true | all-gather | bytes 400 | tf_op jit(solution)/shard_map/all_gather | solution.py:429
  133.3 0.0 copy-start.4
  133.3 1.0 copy-done.4
  134.3 5.5 %exit_gradient_0.1 = (f32[2,256,512]{2,1,0:T(8,128)}, f32[2,256,256]{2,1,0:T(8,128)S(1)}) custom-call(s32[4,5]{1,0:T(4,128)S(1)} %bitcast.74, bf16[2,256,256]{2,1,0:T(8,128)(2,1)S(1)} %copy-done.3, bf16[512,512]{1,0:T(8,128)(2,1)S(1)} %copy-done.2, bf16[512,512]{1,0:T(8,128)(2,1)S(1)} %copy-done.1, bf16[32,16,512]{2,1,0:T(8,128)(2,1)S(1)} %all_to_all.42.own_ref.next_ref, ...), custom_call_target="tpu_custom_call" | custom-call | tf_op jit(solution)/shard_map/exit_gradient_0/pallas_call | solution.py:365
  139.8 0.8 copy-done.10
  140.6 0.0 collective-permute-done.5.amp_ref
  140.6 9.5 %exit_gradient_1.1 = (bf16[32,16,512]{2,1,0:T(8,128)(2,1)}, f32[2,256,256]{2,1,0:T(8,128)S(1)}) custom-call(s32[4,5]{1,0:T(4,128)S(1)} %bitcast.75, bf16[2,256,256]{2,1,0:T(8,128)(2,1)S(1)} %copy-done.3, bf16[512,512]{1,0:T(8,128)(2,1)S(1)} %copy-done.2, bf16[512,512]{1,0:T(8,128)(2,1)S(1)} %copy-done.1, ...), custom_call_target="tpu_custom_call" | custom-call | tf_op jit(solution)/shard_map/exit_gradient_1/pallas_call | solution.py:365
  150.1 0.8 copy-done.9
  150.9 0.0 collective-permute-done.4.amp_ref
  150.9 0.0 all-to-all-done.next_ref.own_ref
  150.9 9.5 %exit_gradient_2.1 = (bf16[32,16,512]{2,1,0:T(8,128)(2,1)}, f32[2,256,256]{2,1,0:T(8,128)S(1)}) custom-call(s32[4,5]{1,0:T(4,128)S(1)} %bitcast.76, bf16[2,256,256]{2,1,0:T(8,128)(2,1)S(1)} %copy-done.3, bf16[512,512]{1,0:T(8,128)(2,1)S(1)} %copy-done.2, bf16[512,512]{1,0:T(8,128)(2,1)S(1)} %copy-done.1, ...), custom_call_target="tpu_custom_call" | custom-call | tf_op jit(solution)/shard_map/exit_gradient_2/pallas_call | solution.py:365
  160.4 0.8 copy-done.11
  161.2 6.6 %exit_gradient_3.1 = (bf16[32,16,512]{2,1,0:T(8,128)(2,1)}, bf16[32,16,512]{2,1,0:T(8,128)(2,1)}) custom-call(s32[4,5]{1,0:T(4,128)S(1)} %bitcast.77, bf16[2,256,256]{2,1,0:T(8,128)(2,1)S(1)} %copy-done.3, bf16[512,512]{1,0:T(8,128)(2,1)S(1)} %copy-done.2, bf16[512,512]{1,0:T(8,128)(2,1)S(1)} %copy-done.1, ...), custom_call_target="tpu_custom_call" | custom-call | tf_op jit(solution)/shard_map/exit_gradient_3/pallas_call | solution.py:365
  167.8 19.6 %all_to_all.43.refs_2_ = bf16[32,16,512]{2,1,0:T(8,128)(2,1)S(1)} all-to-all(bf16[32,16,512]{2,1,0:T(8,128)(2,1)} %get-tuple-element.45), channel_id=1, replica_groups=mesh['ang'=8,'pos'=4] {'ang','pos'}, dimensions={0} | all-to-all | bytes 1048576 | tf_op jit(solution)/shard_map/all_to_all | solution.py:407
  187.4 18.6 %all_to_all.44.refs_1_ = bf16[32,16,512]{2,1,0:T(8,128)(2,1)S(1)} all-to-all(bf16[32,16,512]{2,1,0:T(8,128)(2,1)} %get-tuple-element.44), channel_id=1, replica_groups=mesh['ang'=8,'pos'=4] {'ang','pos'}, dimensions={0} | all-to-all | bytes 1048576 | tf_op jit(solution)/shard_map/all_to_all | solution.py:407
  206.0 18.6 %all_to_all.45.refs_0_ = bf16[32,16,512]{2,1,0:T(8,128)(2,1)S(1)} all-to-all(bf16[32,16,512]{2,1,0:T(8,128)(2,1)} %get-tuple-element.43), channel_id=1, replica_groups=mesh['ang'=8,'pos'=4] {'ang','pos'}, dimensions={0} | all-to-all | bytes 1048576 | tf_op jit(solution)/shard_map/all_to_all | solution.py:407
  224.6 3.4 %all-to-all-start.4 = ((bf16[32,16,512]{2,1,0:T(8,128)(2,1)}), bf16[32,16,512]{2,1,0:T(8,128)(2,1)S(1)}, u32[]{:S(2)}, u32[]{:S(2)}) async-start(bf16[32,16,512]{2,1,0:T(8,128)(2,1)} %get-tuple-element.42), calls=%async_computation.4 | async-start | bytes 1048576 | tf_op jit(solution)/shard_map/all_to_all | solution.py:407
  228.1 0.3 collective-permute-start.11
  228.4 1.5 collective-permute-start.10
  229.9 1.6 collective-permute-start.9
  231.5 14.5 %back_early.1 = (f32[16,8192]{1,0:T(8,128)S(1)}, f32[16,8192]{1,0:T(8,128)S(1)}, f32[16,8192]{1,0:T(8,128)S(1)}, f32[16,8192]{1,0:T(8,128)S(1)}) custom-call(s32[32,128]{1,0:T(8,128)S(1)} %reshape.187.idx_ref, bf16[32,64,256]{2,1,0:T(8,128)(2,1)} %radon_ref.7, bf16[32,16,512]{2,1,0:T(8,128)(2,1)S(1)} %all_to_all.45.refs_0_, ...), custom_call_target="tpu_custom_call" | custom-call | tf_op jit(solution)/shard_map/back_early/pallas_call | solution.py:211
  246.0 0.8 copy-done.5
  246.8 0.8 copy-done.7
  247.6 1.0 copy-done.6
  248.7 1.0 copy-done.8
  249.7 10.7 %back_last.1 = (bf16[16,8192]{1,0:T(8,128)(2,1)S(1)}, bf16[16,8192]{1,0:T(8,128)(2,1)S(1)}, bf16[16,8192]{1,0:T(8,128)(2,1)S(1)}, bf16[16,8192]{1,0:T(8,128)(2,1)S(1)}) custom-call(s32[32,128]{1,0:T(8,128)S(1)} %reshape.187.idx_ref, bf16[32,64,256]{2,1,0:T(8,128)(2,1)} %radon_ref.7, bf16[32,16,512]{2,1,0:T(8,128)(2,1)S(1)} %all-to-all-done.4.refs_0_, ...), custom_call_target="tpu_custom_call" | custom-call | tf_op jit(solution)/shard_map/back_last/pallas_call | solution.py:211
  260.4 0.0 collective-permute-start.6
  260.5 0.2 collective-permute-start.7
  260.7 0.6 collective-permute-start.8
  261.3 1.7 select_bitcast_fusion.3
  263.2 0.3 maximum_convert_fusion
  263.6 4.7 %copy.40 = f32[2,256,4,512]{3,2,1,0:T(4,128)} copy(f32[2,256,4,512]{3,1,0,2:T(8,128)S(1)} %maximum_convert_fusion) | data formatting | bytes 8388608
  268.3 2.9 %collective-permute-done.7 = bf16[16,8192]{1,0:T(8,128)(2,1)S(1)} collective-permute-done((bf16[16,8192]{1,0:T(8,128)(2,1)S(1)}, bf16[16,8192]{1,0:T(8,128)(2,1)S(1)}, u32[]{:S(2)}, u32[]{:S(2)}) %collective-permute-start.7) | collective-permute-done | bytes 262176 | tf_op jit(solution)/shard_map/ppermute | solution.py:35
  271.1 1.7 collective-permute-done.8
  272.9 0.1 select_bitcast_fusion.7
  273.0 1.6 multiply_add_fusion
  (38 shorter events, 0.3 us)
Async XLA Ops:
  0.6 5.3 %copy-start.13 = (s32[32,32,4]{1,2,0:T(4,128)S(1)}, s32[32,32,4]{1,2,0:T(4,128)}, u32[]{:S(2)}) copy-start(s32[32,32,4]{1,2,0:T(4,128)} %param.11) | copy-start | bytes 49156
  0.6 16.5 %copy-start = (bf16[32,64,256]{2,1,0:T(8,128)(2,1)S(1)}, bf16[32,64,256]{2,1,0:T(8,128)(2,1)}, u32[]{:S(2)}) copy-start(bf16[32,64,256]{2,1,0:T(8,128)(2,1)} %radon_ref.7) | copy-start | bytes 3145732
  2.1 8.9 %collective-permute-start.2 = (bf16[16,8192]{1,0:T(8,128)(2,1)S(1)}, bf16[16,8192]{1,0:T(8,128)(2,1)S(1)}, u32[]{:S(2)}, u32[]{:S(2)}) collective-permute-start(bf16[16,8192]{1,0:T(8,128)(2,1)S(1)} %get-tuple-element.70), channel_id=1, source_target_pairs={{0,3},{1,0},{2,1},{3,2},{4,7},{5,4},{6,5},{7,6},{8,11},{9,8},{10,9... | collective-permute-start | bytes 786440 | tf_op jit(solution)/shard_map/ppermute | solution.py:35
  2.2 8.8 %collective-permute-start = (bf16[16,8192]{1,0:T(8,128)(2,1)S(1)}, bf16[16,8192]{1,0:T(8,128)(2,1)S(1)}, u32[]{:S(2)}, u32[]{:S(2)}) collective-permute-start(bf16[16,8192]{1,0:T(8,128)(2,1)S(1)} %get-tuple-element.71), channel_id=1, source_target_pairs={{0,1},{1,2},{2,3},{3,0},{4,5},{5,6},{6,7},{7,4},{8,9},{9,10},{10,1... | collective-permute-start | bytes 786440 | tf_op jit(solution)/shard_map/ppermute | solution.py:35
  4.8 12.4 %collective-permute-start.1 = (bf16[16,8192]{1,0:T(8,128)(2,1)S(1)}, bf16[16,8192]{1,0:T(8,128)(2,1)S(1)}, u32[]{:S(2)}, u32[]{:S(2)}) collective-permute-start(bf16[16,8192]{1,0:T(8,128)(2,1)S(1)} %get-tuple-element.73), channel_id=1, source_target_pairs={{0,2},{1,3},{2,0},{3,1},{4,6},{5,7},{6,4},{7,5},{8,10},{9,11},{10,... | collective-permute-start | bytes 786440 | tf_op jit(solution)/shard_map/ppermute | solution.py:35
  96.9 54.0 %all-to-all-start = ((bf16[32,16,512]{2,1,0:T(8,128)(2,1)}), bf16[32,16,512]{2,1,0:T(8,128)(2,1)S(1)}, u32[]{:S(2)}, u32[]{:S(2)}) async-start(bf16[32,16,512]{2,1,0:T(8,128)(2,1)} %get-tuple-element.33), calls=%async_computation | async-start | bytes 1048576 | tf_op jit(solution)/shard_map/all_to_all | solution.py:407
  100.4 6.5 %copy-start.15 = (s32[4,1]{0,1:T(1,128)S(1)}, s32[4,1]{0,1:T(1,128)}, u32[]{:S(2)}) copy-start(s32[4,1]{0,1:T(1,128)} %param.15) | copy-start | bytes 52
  100.4 6.6 %copy-start.14 = (s32[4,4]{1,0:T(4,128)S(1)}, s32[4,4]{1,0:T(4,128)}, u32[]{:S(2)}) copy-start(s32[4,4]{1,0:T(4,128)} %param.14) | copy-start | bytes 196
  100.5 32.8 %copy-start.1 = (bf16[512,512]{1,0:T(8,128)(2,1)S(1)}, bf16[512,512]{1,0:T(8,128)(2,1)}, u32[]{:S(2)}) copy-start(bf16[512,512]{1,0:T(8,128)(2,1)} %constant.146.inverse_ref) | copy-start | bytes 1572868
  100.5 32.8 %copy-start.2 = (bf16[512,512]{1,0:T(8,128)(2,1)S(1)}, bf16[512,512]{1,0:T(8,128)(2,1)}, u32[]{:S(2)}) copy-start(bf16[512,512]{1,0:T(8,128)(2,1)} %constant.143.forward_ref) | copy-start | bytes 1572868
  100.5 32.8 %copy-start.3 = (bf16[2,256,256]{2,1,0:T(8,128)(2,1)S(1)}, bf16[2,256,256]{2,1,0:T(8,128)(2,1)}, u32[]{:S(2)}) copy-start(bf16[2,256,256]{2,1,0:T(8,128)(2,1)} %probe_ref.7) | copy-start | bytes 786436
  103.5 37.1 %collective-permute-start.5 = (bf16[4,256,256]{2,1,0:T(8,128)(2,1)}, bf16[4,256,256]{2,1,0:T(8,128)(2,1)}, u32[]{:S(2)}, u32[]{:S(2)}) collective-permute-start(bf16[4,256,256]{2,1,0:T(8,128)(2,1)} %get-tuple-element.63), channel_id=1, source_target_pairs={{0,3},{1,0},{2,1},{3,2},{4,7},{5,4},{6,5},{7,6},{8,11},{9,8},{10,9... | collective-permute-start | bytes 1572872 | tf_op jit(solution)/shard_map/ppermute | solution.py:35
  103.8 47.2 %collective-permute-start.4 = (bf16[4,256,256]{2,1,0:T(8,128)(2,1)}, bf16[4,256,256]{2,1,0:T(8,128)(2,1)}, u32[]{:S(2)}, u32[]{:S(2)}) collective-permute-start(bf16[4,256,256]{2,1,0:T(8,128)(2,1)} %get-tuple-element.64), channel_id=1, source_target_pairs={{0,2},{1,3},{2,0},{3,1},{4,6},{5,7},{6,4},{7,5},{8,10},{9,11},{10,... | collective-permute-start | bytes 1572872 | tf_op jit(solution)/shard_map/ppermute | solution.py:35
  105.3 55.9 %collective-permute-start.3 = (bf16[4,256,256]{2,1,0:T(8,128)(2,1)}, bf16[4,256,256]{2,1,0:T(8,128)(2,1)}, u32[]{:S(2)}, u32[]{:S(2)}) collective-permute-start(bf16[4,256,256]{2,1,0:T(8,128)(2,1)} %get-tuple-element.65), channel_id=1, source_target_pairs={{0,1},{1,2},{2,3},{3,0},{4,5},{5,6},{6,7},{7,4},{8,9},{9,10},{10,1... | collective-permute-start | bytes 1572872 | tf_op jit(solution)/shard_map/ppermute | solution.py:35
  133.3 1.0 copy-start.4
  139.8 0.8 copy-start.10
  150.1 0.8 copy-start.9
  160.4 0.8 copy-start.11
  224.6 23.0 %all-to-all-start.4 = ((bf16[32,16,512]{2,1,0:T(8,128)(2,1)}), bf16[32,16,512]{2,1,0:T(8,128)(2,1)S(1)}, u32[]{:S(2)}, u32[]{:S(2)}) async-start(bf16[32,16,512]{2,1,0:T(8,128)(2,1)} %get-tuple-element.42), calls=%async_computation.4 | async-start | bytes 1048576 | tf_op jit(solution)/shard_map/all_to_all | solution.py:407
  228.1 32.6 %collective-permute-start.11 = (bf16[32,16,512]{2,1,0:T(8,128)(2,1)}, bf16[32,16,512]{2,1,0:T(8,128)(2,1)}, u32[]{:S(2)}, u32[]{:S(2)}) collective-permute-start(bf16[32,16,512]{2,1,0:T(8,128)(2,1)} %get-tuple-element.45), channel_id=1, source_target_pairs={{0,3},{1,0},{2,1},{3,2},{4,7},{5,4},{6,5},{7,6},{8,11},{9,8},{10,9... | collective-permute-start | bytes 1572872 | tf_op jit(solution)/shard_map/ppermute | solution.py:35
  228.4 33.0 %collective-permute-start.10 = (bf16[32,16,512]{2,1,0:T(8,128)(2,1)}, bf16[32,16,512]{2,1,0:T(8,128)(2,1)}, u32[]{:S(2)}, u32[]{:S(2)}) collective-permute-start(bf16[32,16,512]{2,1,0:T(8,128)(2,1)} %get-tuple-element.44), channel_id=1, source_target_pairs={{0,2},{1,3},{2,0},{3,1},{4,6},{5,7},{6,4},{7,5},{8,10},{9,11},{10,... | collective-permute-start | bytes 1572872 | tf_op jit(solution)/shard_map/ppermute | solution.py:35
  229.9 31.4 %collective-permute-start.9 = (bf16[32,16,512]{2,1,0:T(8,128)(2,1)}, bf16[32,16,512]{2,1,0:T(8,128)(2,1)}, u32[]{:S(2)}, u32[]{:S(2)}) collective-permute-start(bf16[32,16,512]{2,1,0:T(8,128)(2,1)} %get-tuple-element.43), channel_id=1, source_target_pairs={{0,1},{1,2},{2,3},{3,0},{4,5},{5,6},{6,7},{7,4},{8,9},{9,10},{10,1... | collective-permute-start | bytes 1572872 | tf_op jit(solution)/shard_map/ppermute | solution.py:35
  246.0 0.8 copy-start.5
  246.8 0.8 copy-start.7
  247.6 1.0 copy-start.6
  248.7 1.0 copy-start.8
  260.4 7.8 %collective-permute-start.6 = (bf16[16,8192]{1,0:T(8,128)(2,1)S(1)}, bf16[16,8192]{1,0:T(8,128)(2,1)S(1)}, u32[]{:S(2)}, u32[]{:S(2)}) collective-permute-start(bf16[16,8192]{1,0:T(8,128)(2,1)S(1)} %get-tuple-element.50), channel_id=1, source_target_pairs={{0,1},{1,2},{2,3},{3,0},{4,5},{5,6},{6,7},{7,4},{8,9},{9,10},{10,1... | collective-permute-start | bytes 786440 | tf_op jit(solution)/shard_map/ppermute | solution.py:35
  260.5 10.7 %collective-permute-start.7 = (bf16[16,8192]{1,0:T(8,128)(2,1)S(1)}, bf16[16,8192]{1,0:T(8,128)(2,1)S(1)}, u32[]{:S(2)}, u32[]{:S(2)}) collective-permute-start(bf16[16,8192]{1,0:T(8,128)(2,1)S(1)} %get-tuple-element.51), channel_id=1, source_target_pairs={{0,2},{1,3},{2,0},{3,1},{4,6},{5,7},{6,4},{7,5},{8,10},{9,11},{10,... | collective-permute-start | bytes 786440 | tf_op jit(solution)/shard_map/ppermute | solution.py:35
  260.7 12.2 %collective-permute-start.8 = (bf16[16,8192]{1,0:T(8,128)(2,1)S(1)}, bf16[16,8192]{1,0:T(8,128)(2,1)S(1)}, u32[]{:S(2)}, u32[]{:S(2)}) collective-permute-start(bf16[16,8192]{1,0:T(8,128)(2,1)S(1)} %get-tuple-element.52), channel_id=1, source_target_pairs={{0,3},{1,0},{2,1},{3,2},{4,7},{5,4},{6,5},{7,6},{8,11},{9,8},{10,9... | collective-permute-start | bytes 786440 | tf_op jit(solution)/shard_map/ppermute | solution.py:35
  268.3 4.7 %copy-start.12 = (bf16[2,32,8192]{2,1,0:T(8,128)(2,1)S(1)}, bf16[2,32,8192]{2,1,0:T(8,128)(2,1)}, u32[]{:S(2)}) copy-start(bf16[2,32,8192]{2,1,0:T(8,128)(2,1)} %param.9) | copy-start | bytes 3145732

commit v3 on v2

--- a/solution.py
+++ b/solution.py
@@ -61,7 +61,7 @@
     tiles = per_piece * pieces
     for k in range(pieces):
 
-        @pl.loop(0, per_piece, unroll=4)
+        @pl.loop(0, per_piece, unroll=16)
         def _(t):
             tile = vol_refs[k][:, pl.ds(pl.multiple_of(t * LANES, LANES), LANES)]
             vv_ref[k * per_piece + t] = tile
@@ -69,16 +69,16 @@
             vv_ref[tiles + k * per_piece + t] = swapped
 
 
-def project_chunk(chunks, idx_ref, radon_ref, vv_ref, out_refs, lhs_ref):
+def project_chunk(chunks, idx_ref, radon_ref, vv_ref, out_ref, lhs_refs):
     angles, block, span = radon_ref.shape
-    blocks = out_refs[0].shape[2] // block
+    blocks = out_ref.shape[2] // block // len(chunks)
     feeds = span // block
     low = lower_half((ROWS, LANES))
-
-    @pl.loop(0, angles // 2)
-    def _(step):
-        for n in range(2):
-            a = step * 2 + n
+    batch = lhs_refs[0].shape[0]
+
+    def gather(start, lhs_ref):
+        for n in range(batch):
+            a = start + n
             for i, chunk in enumerate(chunks):
                 for b in range(blocks):
                     row = (i * blocks + b) * ROWS
@@ -89,106 +89,138 @@
                         lhs_ref[n, row : row + ROWS, jp * LANES : (jp + 1) * LANES] = jnp.where(
                             low, first, second
                         )
-        for n in range(2):
-            a = step * 2 + n
+
+    def multiply(start, lhs_ref):
+        for n in range(batch):
+            a = start + n
             product = lax.dot_general(
                 lhs_ref[n], radon_ref[a], (((1,), (1,)), ((), ())), preferred_element_type=jnp.float32
             )
-            for i in range(len(chunks)):
-                for pair in range(blocks // 2):
-                    row = (i * blocks + 2 * pair) * ROWS
-                    tile = jnp.concatenate(
-                        [product[row : row + ROWS], product[row + ROWS : row + 2 * ROWS]], axis=1
-                    )
-                    out_refs[i][a, :, pair * LANES : (pair + 1) * LANES] = tile.astype(jnp.bfloat16)
-
-
-def project_first_kernel(pieces, idx_ref, radon_ref, *refs):
+            for pair in range(len(chunks) * blocks // 2):
+                row = 2 * pair * ROWS
+                tile = jnp.concatenate(
+                    [product[row : row + ROWS], product[row + ROWS : row + 2 * ROWS]], axis=1
+                )
+                out_ref[a, :, pair * LANES : (pair + 1) * LANES] = tile.astype(jnp.bfloat16)
+
+    gather(0, lhs_refs[0])
+
+    @pl.loop(0, angles // (2 * batch))
+    def _(step):
+        start = step * 2 * batch
+        multiply(start, lhs_refs[0])
+        gather(start + batch, lhs_refs[1])
+        multiply(start + batch, lhs_refs[1])
+        gather(jnp.minimum(start + 2 * batch, angles - batch), lhs_refs[0])
+
+
+def project_first_kernel(chunks, pieces, idx_ref, radon_ref, *refs):
     vol_refs = refs[:pieces]
-    out_ref, vv_ref, lhs_ref = refs[pieces:]
+    out_ref, vv_ref, *lhs_refs = refs[pieces:]
     arrange_kernel(pieces, *vol_refs, vv_ref)
-    project_chunk([0], idx_ref, radon_ref, vv_ref, [out_ref], lhs_ref)
-
-
-def project_rest_kernel(pieces, idx_ref, radon_ref, vv_ref, *refs):
-    out_refs, lhs_ref = refs[: pieces - 1], refs[pieces - 1]
-    project_chunk(list(range(1, pieces)), idx_ref, radon_ref, vv_ref, out_refs, lhs_ref)
-
-
-def project(idx, radon_tiles, vol_pieces, tile_width):
+    project_chunk(chunks, idx_ref, radon_ref, vv_ref, out_ref, lhs_refs)
+
+
+def project_rest_kernel(chunks, idx_ref, radon_ref, vv_ref, out_ref, *lhs_refs):
+    project_chunk(chunks, idx_ref, radon_ref, vv_ref, out_ref, lhs_refs)
+
+
+def guess(microseconds):
+    return pl.CostEstimate(
+        flops=int(microseconds * 1.15e9), bytes_accessed=int(microseconds * 1e5), transcendentals=0
+    )
+
+
+def project_first(idx, radon_tiles, vol_pieces, tile_width, chunks):
     angles, block, span = radon_tiles.shape
     pieces = len(vol_pieces)
     tiles = pieces * vol_pieces[0].shape[1] // LANES
-    rows = tile_width // block * ROWS
-    chunk_shape = jax.ShapeDtypeStruct((angles, ROWS, tile_width), jnp.bfloat16)
-    params = pltpu.CompilerParams(vmem_limit_bytes=VMEM_LIMIT)
-    first, vv = pl.pallas_call(
-        functools.partial(project_first_kernel, pieces),
-        out_shape=[chunk_shape, jax.ShapeDtypeStruct((2 * tiles, ROWS, LANES), jnp.bfloat16)],
+    rows = len(chunks) * tile_width // block * ROWS
+    return pl.pallas_call(
+        functools.partial(project_first_kernel, chunks, pieces),
+        out_shape=[
+            jax.ShapeDtypeStruct((angles, ROWS, len(chunks) * tile_width), jnp.bfloat16),
+            jax.ShapeDtypeStruct((2 * tiles, ROWS, LANES), jnp.bfloat16),
+        ],
         in_specs=[scalars, everywhere] + [everywhere] * pieces,
         out_specs=[everywhere] * 2,
-        scratch_shapes=[pltpu.VMEM((2, rows, span), jnp.bfloat16)],
-        compiler_params=params,
+        scratch_shapes=[pltpu.VMEM((2, rows, span), jnp.bfloat16)] * 2,
+        compiler_params=pltpu.CompilerParams(vmem_limit_bytes=VMEM_LIMIT),
+        cost_estimate=guess(8),
         name="project_first",
     )(idx, radon_tiles, *vol_pieces)
-    rest = pl.pallas_call(
-        functools.partial(project_rest_kernel, pieces),
-        out_shape=[chunk_shape] * (pieces - 1),
+
+
+def project_rest(idx, radon_tiles, vv, tile_width, chunks):
+    angles, block, span = radon_tiles.shape
+    rows = len(chunks) * tile_width // block * ROWS
+    return pl.pallas_call(
+        functools.partial(project_rest_kernel, chunks),
+        out_shape=jax.ShapeDtypeStruct((angles, ROWS, len(chunks) * tile_width), jnp.bfloat16),
         in_specs=[scalars, everywhere, everywhere],
-        out_specs=[everywhere] * (pieces - 1),
-        scratch_shapes=[pltpu.VMEM((2, (pieces - 1) * rows, span), jnp.bfloat16)],
-        compiler_params=params,
+        out_specs=everywhere,
+        scratch_shapes=[pltpu.VMEM((2, rows, span), jnp.bfloat16)] * 2,
+        compiler_params=pltpu.CompilerParams(vmem_limit_bytes=VMEM_LIMIT),
+        cost_estimate=guess(5),
         name="project_rest",
     )(idx, radon_tiles, vv)
-    return [first] + list(rest)
-
-
-def back_project_kernel(chunks, pieces, has_start, idx_ref, radon_ref, *refs):
-    grad_refs, refs = refs[: len(chunks)], refs[len(chunks) :]
+
+
+def back_project_kernel(chunks, pieces, has_start, idx_ref, radon_ref, grad_ref, *refs):
     start_refs, refs = (refs[:pieces], refs[pieces:]) if has_start else (None, refs)
     out_refs, refs = refs[:pieces], refs[pieces:]
-    acc_refs, contrib_ref = refs[:CHAINS], refs[CHAINS]
+    acc_refs, contrib_refs = refs[:CHAINS], refs[CHAINS:]
     angles, block, span = radon_ref.shape
     per_piece = out_refs[0].shape[1] // LANES
     tiles = per_piece * pieces
-    blocks = grad_refs[0].shape[2] // block
-    pairs = blocks // 2
+    blocks = grad_ref.shape[2] // block // len(chunks)
+    pairs = len(chunks) * blocks // 2
     feeds = span // block
 
-    @pl.loop(0, 2 * tiles, unroll=8)
+    @pl.loop(0, 2 * tiles, unroll=16)
     def _(t):
         for acc_ref in acc_refs:
             acc_ref[t] = jnp.zeros((ROWS, LANES), jnp.float32)
 
     low = lower_half((ROWS, LANES))
 
-    @pl.loop(0, angles // CHAINS)
-    def _(step):
+    def multiply(start, contrib_ref):
         for n in range(CHAINS):
-            a = step * CHAINS + n
+            a = start + n
             lhs = []
-            for grad_ref in grad_refs:
-                for pair in range(pairs):
-                    tile = grad_ref[a, :, pair * LANES : (pair + 1) * LANES]
-                    lhs += [tile[:, :block], tile[:, block:]]
+            for pair in range(pairs):
+                tile = grad_ref[a, :, pair * LANES : (pair + 1) * LANES]
+                lhs += [tile[:, :block], tile[:, block:]]
             contrib_ref[n] = jnp.dot(
                 jnp.concatenate(lhs, axis=0), radon_ref[a], preferred_element_type=jnp.float32
             )
+
+    def scatter(start, contrib_ref):
         for i, chunk in enumerate(chunks):
             for b in range(blocks):
                 row = (i * blocks + b) * ROWS
                 for jp in range(feeds // 2):
                     at = (chunk * blocks + b) * feeds + 2 * jp
                     for n in range(CHAINS):
-                        a = step * CHAINS + n
+                        a = start + n
                         tile = contrib_ref[n, row : row + ROWS, jp * LANES : (jp + 1) * LANES]
                         first, second = idx_ref[a, at], idx_ref[a, at + 1]
                         acc_refs[n][first] += jnp.where(low, tile, 0.0)
                         acc_refs[n][second] += jnp.where(low, 0.0, tile)
 
+    multiply(0, contrib_refs[0])
+
+    @pl.loop(0, angles // (2 * CHAINS))
+    def _(step):
+        start = step * 2 * CHAINS
+        multiply(start + CHAINS, contrib_refs[1])
+        scatter(start, contrib_refs[0])
+        multiply(jnp.minimum(start + 2 * CHAINS, angles - CHAINS), contrib_refs[0])
+        scatter(start + CHAINS, contrib_refs[1])
+
     for k in range(pieces):
 
-        @pl.loop(0, per_piece, unroll=4)
+        @pl.loop(0, per_piece, unroll=16)
         def _(t):
             lanes = pl.ds(pl.multiple_of(t * LANES, LANES), LANES)
             straight = acc_refs[0][k * per_piece + t]
@@ -205,17 +237,18 @@
 def back_project(idx, radon_tiles, grads, chunks, start, pieces, piece_width, out_type, name):
     angles, block, span = radon_tiles.shape
     tiles = pieces * piece_width // LANES
-    rows = len(chunks) * grads[0].shape[2] // block * ROWS
+    rows = grads.shape[2] // block * ROWS
     has_start = start is not None
-    operands = [idx, radon_tiles] + list(grads) + (list(start) if has_start else [])
+    operands = [idx, radon_tiles, grads] + (list(start) if has_start else [])
     return pl.pallas_call(
         functools.partial(back_project_kernel, chunks, pieces, has_start),
         out_shape=[jax.ShapeDtypeStruct((ROWS, piece_width), out_type)] * pieces,
         in_specs=[scalars] + [everywhere] * (len(operands) - 1),
         out_specs=[everywhere] * pieces,
         scratch_shapes=[pltpu.VMEM((2 * tiles, ROWS, LANES), jnp.float32)] * CHAINS
-        + [pltpu.VMEM((CHAINS, rows, span), jnp.float32)],
+        + [pltpu.VMEM((CHAINS, rows, span), jnp.float32)] * 2,
         compiler_params=pltpu.CompilerParams(vmem_limit_bytes=VMEM_LIMIT),
+        cost_estimate=guess(3 + 2 * len(chunks)),
         name=name,
     )(*operands)
 
@@ -224,8 +257,10 @@
     step, last, meta_ref, probe_ref, forward_ref, inverse_ref, own_ref, next_ref, amp_ref, *refs
 ):
     spill_in_ref, refs = (refs[0], refs[1:]) if step > 0 else (None, refs)
-    partial_ref, refs = (refs[0], refs[1:]) if step == last else (None, refs)
-    out_ref, beyond_ref, ext_ref, acc_ref, wave_ref, half_ref = refs
+    (partial_ref, before_ref), refs = (refs[:2], refs[2:]) if step == last else ((None, None), refs)
+    out_ref, refs = refs[0], refs[1:]
+    beyond_ref, refs = (None, refs) if step == last else (refs[0], refs[1:])
+    ext_ref, acc_ref, wave_ref, half_ref = refs
     owner = lax.rem(lax.axis_index("pos") + step, last + 1)
     groups = own_ref.shape[0]
     width = probe_ref.shape[1]
@@ -240,7 +275,7 @@
     @pl.loop(0, groups)
     def _(g):
         ext_ref[g, :, :tile_width] = own_ref[g]
-        ext_ref[g, :, tile_width:] = next_ref[g, :, :width]
+        ext_ref[g, :, tile_width:] = next_ref[g]
         rows = pl.ds(pl.multiple_of(g * GROUP, GROUP), GROUP)
         for c in range(2):
             if step > 0:
@@ -253,7 +288,7 @@
         return jnp.dot(left, right, preferred_element_type=jnp.float32)
 
     def slot_step(q, carry):
-        offset = meta_ref[owner, q] - owner * tile_width
+        offset = meta_ref[step, q] - owner * tile_width
         first_tile = offset // LANES
         shift = offset % LANES
         starts = [pl.multiple_of((first_tile + m) * LANES, LANES) for m in range(wide + 1)]
@@ -327,7 +362,7 @@
                     acc_ref[c, rows, pl.ds(starts[m], LANES)] += jnp.where(past, ahead, behind)
         return carry
 
-    lax.fori_loop(0, meta_ref[owner, slots], slot_step, 0)
+    lax.fori_loop(0, meta_ref[step, slots], slot_step, 0)
 
     @pl.loop(0, groups)
     def _(g):
@@ -337,39 +372,55 @@
                 out_ref[c, rows, :] = acc_ref[c, rows, :tile_width]
         else:
             both = [acc_ref[c, rows, :tile_width] for c in range(2)]
-            out_ref[g] = jnp.concatenate(both, axis=0).astype(jnp.bfloat16)
+            here = jnp.concatenate(both, axis=0).astype(jnp.bfloat16)
         if step == last:
             both = []
             for c in range(2):
                 whole = partial_ref[c, rows, :]
                 spilled = whole[:, :width] + acc_ref[c, rows, tile_width:]
                 both.append(jnp.concatenate([spilled, whole[:, width:]], axis=1))
-            beyond_ref[g] = jnp.concatenate(both, axis=0).astype(jnp.bfloat16)
+            waiting = before_ref.shape[2]
+            out_ref[g, :, :waiting] = before_ref[g]
+            out_ref[g, :, waiting : waiting + tile_width] = here
+            out_ref[g, :, waiting + tile_width :] = jnp.concatenate(both, axis=0).astype(jnp.bfloat16)
         else:
+            if step > 0:
+                out_ref[g] = here
             for c in range(2):
                 beyond_ref[c, rows, :] = acc_ref[c, rows, tile_width:]
 
 
-def exit_gradient(step, last, meta, probe_field, tables, own, ahead, amps, spill, partial):
-    groups, rows, tile_width = own.shape
+def lanes_of(source, width):
+    array, at = source
+    return pl.BlockSpec(array.shape[:2] + (width,), lambda i: (0, 0, at))
+
+
+def exit_gradient(step, last, meta, probe_field, tables, own, ahead, amps, spill, partial, before):
+    groups, rows = own[0].shape[:2]
     width = probe_field.shape[1]
+    tile_width = own[2]
     slices = groups * GROUP
-    grad_shape = jax.ShapeDtypeStruct(own.shape, jnp.bfloat16)
+    grad_shape = jax.ShapeDtypeStruct((groups, rows, tile_width), jnp.bfloat16)
     partial_shape = jax.ShapeDtypeStruct((2, slices, tile_width), jnp.float32)
     spill_shape = jax.ShapeDtypeStruct((2, slices, width), jnp.float32)
-    operands = [meta, probe_field, *tables, own, ahead, amps]
+    operands = [meta, probe_field, *tables, own[0], ahead[0], amps]
+    specs = [scalars] + [everywhere] * 3
+    specs += [lanes_of(own[:2], tile_width), lanes_of(ahead[:2], width), everywhere]
     if step > 0:
         operands.append(spill)
     if step == last:
-        operands.append(partial)
+        operands += [partial, before]
+        joined = (groups, rows, before.shape[2] + 2 * tile_width)
+        out_shape = [jax.ShapeDtypeStruct(joined, jnp.bfloat16)]
+    else:
+        out_shape = [partial_shape if step == 0 else grad_shape, spill_shape]
+    specs += [everywhere] * (len(operands) - len(specs))
     return pl.pallas_call(
         functools.partial(exit_kernel, step, last),
-        out_shape=[
-            partial_shape if step == 0 else grad_shape,
-            grad_shape if step == last else spill_shape,
-        ],
-        in_specs=[scalars] + [everywhere] * (len(operands) - 1),
-        out_specs=[everywhere] * 2,
+        grid=(1,),
+        out_shape=out_shape,
+        in_specs=specs,
+        out_specs=[everywhere] * len(out_shape),
         scratch_shapes=[
             pltpu.VMEM((groups, rows, tile_width + width), jnp.bfloat16),
             pltpu.VMEM((2, slices, tile_width + width), jnp.float32),
@@ -377,6 +428,7 @@
             pltpu.VMEM((width, 2 * width), jnp.bfloat16),
         ],
         compiler_params=pltpu.CompilerParams(vmem_limit_bytes=VMEM_LIMIT),
+        cost_estimate=guess(7),
         name="exit_gradient_" + str(step),
     )(*operands)
 
@@ -426,8 +478,11 @@
         return lax.dynamic_slice_in_dim(volume, start, own, 1).reshape(rows, width)
 
     vol_pieces = rotate_pos([slices_for(j) for j in range(n_pos)], 1)
-    meta = lax.all_gather(jnp.concatenate([offsets, counts], axis=1), "pos", axis=0)
-    meta = lax.dynamic_index_in_dim(meta, pos, 1, keepdims=False)
+    meta = jnp.concatenate([offsets, counts], axis=1)
+    meta = rotate_pos(
+        [lax.dynamic_slice_in_dim(meta, (pos - j) % n_pos, 1, 0) for j in range(n_pos)], -1
+    )
+    meta = jnp.concatenate(meta, axis=0)
     vol_pieces, amplitudes = lax.optimization_barrier((vol_pieces, amplitudes))
     amp_pieces = rotate_pos(
         [
@@ -446,33 +501,55 @@
     idx = jnp.stack([jnp.roll(idx[:, p], -p, axis=1) for p in range(n_pos)], axis=1)
     idx = idx.reshape(angles, det_blocks * feeds)
 
-    sino = project(idx, radon_tiles, [pad_rows(piece) for piece in vol_pieces], tile_width)
-    received = [to_groups(everyone(chunk[:, :rows]), own) for chunk in sino]
-    tables = dft_tables(probe_field.shape[1])
-    grads = [None] * n_pos
-    partial = spill = None
+    padded = [pad_rows(piece) for piece in vol_pieces]
+    most = list(range(last))
+    sino_most, vv = project_first(idx, radon_tiles, padded, tile_width, most)
+    sino_last = project_rest(idx, radon_tiles, vv, tile_width, [last])
+    got_most = everyone(sino_most[:, :rows])
+    got_most, sino_last = lax.optimization_barrier((got_most, sino_last))
+    got_last = everyone(sino_last[:, :rows])
+    got_most, got_last = to_groups(got_most, own), to_groups(got_last, own)
+    probe_width = probe_field.shape[1]
+    tables = dft_tables(probe_width)
+
+    def tile_from(j):
+        return (got_most, j, tile_width) if j < last else (got_last, 0, tile_width)
+
+    def edge_from(j):
+        per_tile = tile_width // probe_width
+        return (got_most, j % n_pos * per_tile) if j % n_pos < last else (got_last, 0)
+
+    grads = [None] * last
+    partial = spill = before = None
     for j in range(n_pos):
-        ahead = received[(j + 1) % n_pos]
-        one, other = exit_gradient(
-            j, last, meta, probe_field, tables, received[j], ahead, amp_pieces[j], spill, partial
+        out = exit_gradient(
+            j, last, meta, probe_field, tables, tile_from(j), edge_from(j + 1), amp_pieces[j],
+            spill, partial, before,
         )
         if j == 0:
-            partial, spill = one, other
+            partial, spill = out
         elif j < last:
-            grads[j], spill = one, other
+            grads[j], spill = out
+            if j == 1:
+                first_grad, got_last = lax.optimization_barrier((grads[1], got_last))
+            else:
+                before = grads[j] if before is None else jnp.concatenate([before, grads[j]], axis=2)
         else:
-            grads[j], grads[0] = one, other
-    order = list(range(1, n_pos)) + [0]
-    returned = {j: pad_rows(everyone(from_groups(grads[j], own))) for j in order}
-    early = order[:-1]
+            joined = out[0]
+    back_first = everyone(from_groups(first_grad, own))
+    back_first, joined_sent = lax.optimization_barrier((back_first, joined))
+    back_rest = everyone(from_groups(joined_sent, own))
     partial_grad = back_project(
-        idx, radon_tiles, [returned[j] for j in early], early, None, n_pos, width, jnp.float32, "back_early"
-    )
-    tile_pieces = rotate_pos(grads, 1)
+        idx, radon_tiles, pad_rows(back_first), [1], None, n_pos, width, jnp.float32, "back_first"
+    )
+    order = list(range(2, n_pos)) + [0]
+    joined_tiles = {j: joined[:, :, i * tile_width : (i + 1) * tile_width] for i, j in enumerate(order)}
+    joined_tiles[1] = grads[1]
+    tile_pieces = rotate_pos([joined_tiles[j] for j in range(n_pos)], 1)
     obj_pieces = back_project(
-        idx, radon_tiles, [returned[0]], [0], partial_grad, n_pos, width, jnp.bfloat16, "back_last"
-    )
-    groups = grads[0].shape[0]
+        idx, radon_tiles, pad_rows(back_rest), order, partial_grad, n_pos, width, jnp.bfloat16, "back_rest"
+    )
+    groups = joined.shape[0]
     tile_pieces = [tile_pieces[-j % n_pos] for j in range(n_pos)]
     tile_pieces = [
         piece.reshape(groups, 2, GROUP, tile_width).transpose(1, 0, 2, 3).reshape(2, groups * GROUP, tile_width)

time: 276 us -> 194 us (0.70)
  blocking collectives: 141 us -> 0 us
  waiting for transfers between devices: 14.9 us -> 67 us
  starting transfers between devices: 18.4 us -> 42.2 us
  Pallas kernels: 78 us -> 60.2 us
    all_to_all x6 -> x0, blocking collectives: 115 us -> none  [everyone(): return lax.all_to_all(chunk, ('ang', 'pos'), 0, 0, tiled=True)]
    all_to_all x2 -> x4, waiting for transfers between devices: 0.01 us -> 46.9 us  [everyone(): return lax.all_to_all(chunk, ('ang', 'pos'), 0, 0, tiled=True)]
    all_gather x1 -> x0, blocking collectives: 26.2 us -> none  [on_device(): lax.all_gather(jnp.concatenate([offsets, counts], axis=1), 'pos', axis=0)]
    all_to_all x2 -> x4, starting transfers between devices: 6.85 us -> 29.3 us  [everyone(): return lax.all_to_all(chunk, ('ang', 'pos'), 0, 0, tiled=True)]
    pallas_call x2, Pallas kernels: 25.2 us -> 15.6 us  [back_project(): pl.pallas_call(functools.partial(back_project_kernel, chunks, pieces, has...]
    pallas_call x6, Pallas kernels: 52.8 us -> 44.6 us  [the longest x4 29.7 us: exit_gradient(): pl.pallas_call(functools.partial(exit_kernel, step, last), grid=(1,), out...]
    ppermute x12 -> x15, waiting for transfers between devices: 14.8 us -> 20.1 us  [rotate_pos(): lax.ppermute(pieces[j], 'pos', [(i, (i + sign * j) % count) for i in rang...]
    unnamed x35 -> x39, local copies, waits for them, and re-layouts: 12 us -> 13.6 us
  transfers between devices with their start and end apart: 14 -> 19, of which waited for: 4 -> 10; matrix products, arithmetic and copies ran while one was open for 4% -> 6% of each run, Pallas kernels for 18% -> 26%
where the time goes in v3:
time: 194 us
  waiting for transfers between devices  67 us (35%)
  Pallas kernels  60.2 us (31%)
  starting transfers between devices  42.2 us (22%)
  local copies, waits for them, and re-layouts  19.7 us (10%)
  other arithmetic  4.18 us (2%)
    all_to_all x4, waiting for transfers between devices, everyone(): return lax.all_to_all(chunk, ('ang', 'pos'), 0, 0, tiled=True)  46.9 us
    pallas_call x4, Pallas kernels, exit_gradient(): pl.pallas_call(functools.partial(exit_kernel, step, last), grid=(1,), out...  29.7 us
    all_to_all x4, starting transfers between devices, everyone(): return lax.all_to_all(chunk, ('ang', 'pos'), 0, 0, tiled=True)  29.3 us
    ppermute x15, waiting for transfers between devices, rotate_pos(): lax.ppermute(pieces[j], 'pos', [(i, (i + sign * j) % count) for i in rang...  20.1 us
    pallas_call x2, Pallas kernels, back_project(): pl.pallas_call(functools.partial(back_project_kernel, chunks, pieces, has...  15.6 us
    unnamed x39, local copies, waits for them, and re-layouts  13.6 us
    ppermute x15, starting transfers between devices, rotate_pos(): lax.ppermute(pieces[j], 'pos', [(i, (i + sign * j) % count) for i in rang...  12.9 us
    pallas_call x1, Pallas kernels, project_first(): pl.pallas_call(functools.partial(project_first_kernel, chunks, pieces), o...  10.2 us
  transfers between devices with their start and end apart: 19, of which 10 were waited for; matrix products, arithmetic and copies ran while one was open for 6% of the time, Pallas kernels for 26%

profile of v3, /device:TPU:1, one launch (start us, length us, event | category | flops | bytes accessed | tf_op | source)
XLA Modules:
  0.0 194.4 jit_solution(9251387457541716658)
XLA Ops:
  0.6 0.0 copy-start
  0.7 1.3 dynamic-slice_bitcast_fusion.4
  2.1 2.7 %collective-permute-start.3 = (bf16[16,8192]{1,0:T(8,128)(2,1)S(1)}, bf16[16,8192]{1,0:T(8,128)(2,1)S(1)}, u32[]{:S(2)}, u32[]{:S(2)}) collective-permute-start(bf16[16,8192]{1,0:T(8,128)(2,1)S(1)} %get-tuple-element.73), channel_id=1, source_target_pairs={{0,1},{1,2},{2,3},{3,0},{4,5},{5,6},{6,7},{7,4},{8,9},{9,10},{10,1... | collective-permute-start | bytes 786440 | tf_op jit(solution)/shard_map/ppermute | solution.py:35
  4.7 0.5 collective-permute-start.5
  5.2 0.3 fusion.3
  5.5 0.3 copy.19
  5.8 0.2 reshape.186
  6.1 0.1 reshape.187.idx_ref
  6.2 4.0 %collective-permute-done.3.refs_1_ = bf16[16,8192]{1,0:T(8,128)(2,1)S(1)} collective-permute-done((bf16[16,8192]{1,0:T(8,128)(2,1)S(1)}, bf16[16,8192]{1,0:T(8,128)(2,1)S(1)}, u32[]{:S(2)}, u32[]{:S(2)}) %collective-permute-start.3) | collective-permute-done | bytes 262176 | tf_op jit(solution)/shard_map/ppermute | solution.py:35
  10.2 5.6 %collective-permute-done.4.refs_2_ = bf16[16,8192]{1,0:T(8,128)(2,1)S(1)} collective-permute-done((bf16[16,8192]{1,0:T(8,128)(2,1)S(1)}, bf16[16,8192]{1,0:T(8,128)(2,1)S(1)}, u32[]{:S(2)}, u32[]{:S(2)}) %collective-permute-start.4) | collective-permute-done | bytes 262176 | tf_op jit(solution)/shard_map/ppermute | solution.py:35
  15.8 0.5 collective-permute-done.5.refs_3_
  16.3 10.2 %project_first.1 = (bf16[32,16,1536]{2,1,0:T(8,128)(2,1)}, bf16[512,16,128]{2,1,0:T(8,128)(2,1)}) custom-call(s32[32,128]{1,0:T(8,128)S(1)} %reshape.187.idx_ref, bf16[32,64,256]{2,1,0:T(8,128)(2,1)S(1)} %copy-done, bf16[16,8192]{1,0:T(8,128)(2,1)S(1)} %get-tuple-element.29.refs_0_, bf16[16,8192]{1,0:T(8,128)(2,1)S(1)} %collective-permute-done.3.refs_1_, ...), custom_call_target="tpu_custom_call" | custom-call | flops 9200000000 | bytes 800000 | tf_op jit(solution)/shard_map/project_first/pallas_call | solution.py:139
  26.6 6.6 %all-to-all-start = ((bf16[32,16,1536]{2,1,0:T(8,128)(2,1)}), bf16[32,16,1536]{2,1,0:T(8,128)(2,1)}, u32[]{:S(2)}, u32[]{:S(2)}) async-start(bf16[32,16,1536]{2,1,0:T(8,128)(2,1)} %get-tuple-element.33), calls=%async_computation | async-start | bytes 3145728 | tf_op jit(solution)/shard_map/all_to_all | solution.py:459
  33.2 0.1 copy.24
  33.3 0.1 pad_add_fusion.1
  33.4 1.7 collective-permute-start.2
  35.1 0.0 collective-permute-start.1
  35.1 0.5 collective-permute-start
  35.6 2.4 %collective-permute-done.2 = s32[1,5]{1,0:T(1,128)S(1)} collective-permute-done((s32[1,5]{1,0:T(1,128)S(1)}, s32[1,5]{1,0:T(1,128)S(1)}, u32[]{:S(2)}, u32[]{:S(2)}) %collective-permute-start.2) | collective-permute-done | bytes 52 | tf_op jit(solution)/shard_map/ppermute | solution.py:35
  38.0 1.6 collective-permute-done.1
  39.6 0.7 collective-permute-done
  40.4 0.0 copy-start.7
  40.4 2.8 %dynamic-slice_bitcast_fusion = (bf16[4,256,256]{2,1,0:T(8,128)(2,1)}, bf16[4,256,256]{2,1,0:T(8,128)(2,1)}, bf16[4,256,256]{2,1,0:T(8,128)(2,1)S(1)}, bf16[4,256,256]{2,1,0:T(8,128)(2,1)}) fusion(bf16[4,4,256,256]{3,2,1,0:T(8,128)(2,1)} %param.13, s32[]{:T(128)S(6)} %select_n.307, s32[]{:T(128)S(6)} %select_n.309, s32[]{:T(128)S(6)} %select_n.303, ...), kind=kLoop, calls=%fused_computation.10 | loop fusion | bytes 4194320 | tf_op jit(solution)/shard_map/jit(dynamic_index_in_dim)/squeeze | solution.py:489
  43.2 0.0 collective-permute-start.6
  43.3 1.7 collective-permute-start.7
  45.0 1.3 collective-permute-start.8
  46.3 4.7 %project_rest.1 = bf16[32,16,512]{2,1,0:T(8,128)(2,1)} custom-call(s32[32,128]{1,0:T(8,128)S(1)} %reshape.187.idx_ref, bf16[32,64,256]{2,1,0:T(8,128)(2,1)S(1)} %copy-done, bf16[512,16,128]{2,1,0:T(8,128)(2,1)S(1)} %copy-done.7), custom_call_target="tpu_custom_call" | custom-call | flops 5750000128 | bytes 500000 | tf_op jit(solution)/shard_map/project_rest/pallas_call | solution.py:157
  51.0 19.5 %all-to-all-done.own_ref.next_ref = bf16[32,16,1536]{2,1,0:T(8,128)(2,1)} async-done(((bf16[32,16,1536]{2,1,0:T(8,128)(2,1)}), bf16[32,16,1536]{2,1,0:T(8,128)(2,1)}, u32[]{:S(2)}, u32[]{:S(2)}) %all-to-all-start) | async-done | bytes 1572896 | tf_op jit(solution)/shard_map/all_to_all | solution.py:459
  70.5 4.3 %all-to-all-start.1 = ((bf16[32,16,512]{2,1,0:T(8,128)(2,1)}), bf16[32,16,512]{2,1,0:T(8,128)(2,1)S(1)}, u32[]{:S(2)}, u32[]{:S(2)}) async-start(bf16[32,16,512]{2,1,0:T(8,128)(2,1)} %project_rest.1), calls=%async_computation.1 | async-start | bytes 1048576 | tf_op jit(solution)/shard_map/all_to_all | solution.py:459
  74.8 0.0 copy-start.2
  74.8 1.0 copy-done.2
  75.8 1.0 copy-done.5
  76.8 5.1 %exit_gradient_0.1 = (f32[2,256,512]{2,1,0:T(8,128)S(1)}, f32[2,256,256]{2,1,0:T(8,128)S(1)}) custom-call(s32[4,5]{1,0:T(4,128)S(1)} %pad_add_fusion.2.meta_ref, bf16[2,256,256]{2,1,0:T(8,128)(2,1)S(1)} %copy-done.1, bf16[512,512]{1,0:T(8,128)(2,1)S(1)} %copy-done.2, bf16[512,512]{1,0:T(8,128)(2,1)S(1)} %copy-done.5, ...), custom_call_target="tpu_custom_call" | custom-call | flops 8049999872 | bytes 700000 | tf_op jit(solution)/shard_map/exit_gradient_0/pallas_call | solution.py:418
  82.0 0.0 copy-start.8
  82.0 1.0 copy-done.8
  83.0 9.6 %exit_gradient_1.1 = (bf16[32,16,512]{2,1,0:T(8,128)(2,1)}, f32[2,256,256]{2,1,0:T(8,128)S(1)}) custom-call(s32[4,5]{1,0:T(4,128)S(1)} %pad_add_fusion.2.meta_ref, bf16[2,256,256]{2,1,0:T(8,128)(2,1)S(1)} %copy-done.1, bf16[512,512]{1,0:T(8,128)(2,1)S(1)} %copy-done.3, bf16[512,512]{1,0:T(8,128)(2,1)S(1)} %copy-done.5, ...), custom_call_target="tpu_custom_call" | custom-call | flops 8049999872 | bytes 700000 | tf_op jit(solution)/shard_map/exit_gradient_1/pallas_call | solution.py:418
  92.5 0.8 copy-done.11
  93.3 9.1 %all-to-all-start.2 = ((bf16[32,16,512]{2,1,0:T(8,128)(2,1)}), bf16[32,16,512]{2,1,0:T(8,128)(2,1)S(1)}, u32[]{:S(2)}, u32[]{:S(2)}) async-start(bf16[32,16,512]{2,1,0:T(8,128)(2,1)} %get-tuple-element.40), calls=%async_computation.2 | async-start | bytes 1048576 | tf_op jit(solution)/shard_map/all_to_all | solution.py:459
  102.4 0.0 copy-start.4
  102.4 1.0 copy-done.4
  103.5 1.0 copy-done.6
  104.5 1.0 copy-done.12
  105.5 5.0 %exit_gradient_2.1 = (bf16[32,16,512]{2,1,0:T(8,128)(2,1)S(1)}, f32[2,256,256]{2,1,0:T(8,128)S(1)}) custom-call(s32[4,5]{1,0:T(4,128)S(1)} %pad_add_fusion.2.meta_ref, bf16[2,256,256]{2,1,0:T(8,128)(2,1)S(1)} %copy-done.1, bf16[512,512]{1,0:T(8,128)(2,1)S(1)} %copy-done.4, bf16[512,512]{1,0:T(8,128)(2,1)S(1)} %copy-done.6, ...), custom_call_target="tpu_custom_call" | custom-call | flops 8049999872 | bytes 700000 | tf_op jit(solution)/shard_map/exit_gradient_2/pallas_call | solution.py:418
  110.6 10.0 %exit_gradient_3.1 = bf16[32,16,1536]{2,1,0:T(8,128)(2,1)} custom-call(s32[4,5]{1,0:T(4,128)S(1)} %pad_add_fusion.2.meta_ref, bf16[2,256,256]{2,1,0:T(8,128)(2,1)S(1)} %copy-done.1, bf16[512,512]{1,0:T(8,128)(2,1)S(1)} %copy-done.4, bf16[512,512]{1,0:T(8,128)(2,1)S(1)} %copy-done.6, bf16[32,16,512]{2,1,0:T(8,128)(2,1)S(1)} %all-to-all-done.1.next_ref.own_ref, ...), custom_call_target="tpu_custom_call" | custom-call | flops 8049999872 | bytes 700000 | tf_op jit(solution)/shard_map/exit_gradient_3/pallas_call | solution.py:418
  120.6 9.4 %all-to-all-start.3 = ((bf16[32,16,1536]{2,1,0:T(8,128)(2,1)}), bf16[32,16,1536]{2,1,0:T(8,128)(2,1)}, u32[]{:S(2)}, u32[]{:S(2)}) async-start(bf16[32,16,1536]{2,1,0:T(8,128)(2,1)} %exit_gradient_3.1), calls=%async_computation.3 | async-start | bytes 3145728 | tf_op jit(solution)/shard_map/all_to_all | solution.py:459
  130.0 1.7 collective-permute-start.12
  131.7 1.1 fusion.10
  132.8 0.0 collective-permute-start.13
  132.9 0.5 collective-permute-start.14
  133.4 5.7 %back_first.1 = (f32[16,8192]{1,0:T(8,128)S(1)}, f32[16,8192]{1,0:T(8,128)S(1)}, f32[16,8192]{1,0:T(8,128)S(1)}, f32[16,8192]{1,0:T(8,128)S(1)}) custom-call(s32[32,128]{1,0:T(8,128)S(1)} %reshape.187.idx_ref, bf16[32,64,256]{2,1,0:T(8,128)(2,1)S(1)} %copy-done, bf16[32,16,512]{2,1,0:T(8,128)(2,1)S(1)} %all-to-all-done.2.grad_ref), custom_call_target="tpu_custom_call" | custom-call | flops 5750000128 | bytes 500000 | tf_op jit(solution)/shard_map/back_first/pallas_call | solution.py:243
  139.1 0.0 copy-start.9
  139.1 0.8 copy-done.9
  139.9 27.4 %all-to-all-done.3.grad_ref = bf16[32,16,1536]{2,1,0:T(8,128)(2,1)} async-done(((bf16[32,16,1536]{2,1,0:T(8,128)(2,1)}), bf16[32,16,1536]{2,1,0:T(8,128)(2,1)}, u32[]{:S(2)}, u32[]{:S(2)}) %all-to-all-start.3) | async-done | bytes 1572896 | tf_op jit(solution)/shard_map/all_to_all | solution.py:459
  167.3 1.0 copy-done.10
  168.3 9.9 %back_rest.1 = (bf16[16,8192]{1,0:T(8,128)(2,1)S(1)}, bf16[16,8192]{1,0:T(8,128)(2,1)S(1)}, bf16[16,8192]{1,0:T(8,128)(2,1)S(1)}, bf16[16,8192]{1,0:T(8,128)(2,1)S(1)}) custom-call(s32[32,128]{1,0:T(8,128)S(1)} %reshape.187.idx_ref, bf16[32,64,256]{2,1,0:T(8,128)(2,1)} %radon_ref.7, bf16[32,16,1536]{2,1,0:T(8,128)(2,1)} %all-to-all-done.3.grad_ref, ...), custom_call_target="tpu_custom_call" | custom-call | flops 10350000128 | bytes 900000 | tf_op jit(solution)/shard_map/back_rest/pallas_call | solution.py:243
  178.2 1.6 collective-permute-start.9
  179.8 0.7 collective-permute-start.10
  180.5 1.7 select_bitcast_fusion.3
  182.4 0.3 maximum_convert_fusion
  182.7 4.7 %copy.29 = f32[2,256,4,512]{3,2,1,0:T(4,128)} copy(f32[2,256,4,512]{3,1,0,2:T(8,128)S(1)} %maximum_convert_fusion) | data formatting | bytes 8388608
  187.4 4.6 %collective-permute-done.10 = bf16[16,8192]{1,0:T(8,128)(2,1)S(1)} collective-permute-done((bf16[16,8192]{1,0:T(8,128)(2,1)S(1)}, bf16[16,8192]{1,0:T(8,128)(2,1)S(1)}, u32[]{:S(2)}, u32[]{:S(2)}) %collective-permute-start.10) | collective-permute-done | bytes 262176 | tf_op jit(solution)/shard_map/ppermute | solution.py:35
  192.0 0.6 collective-permute-done.11
  192.7 0.1 select_bitcast_fusion.7
  192.8 1.6 multiply_add_fusion
  (47 shorter events, 0.3 us)
Async XLA Ops:
  0.6 4.6 %copy-start.15 = (s32[32,32,4]{1,2,0:T(4,128)S(1)}, s32[32,32,4]{1,2,0:T(4,128)}, u32[]{:S(2)}) copy-start(s32[32,32,4]{1,2,0:T(4,128)} %param.11) | copy-start | bytes 49156
  0.6 15.7 %copy-start = (bf16[32,64,256]{2,1,0:T(8,128)(2,1)S(1)}, bf16[32,64,256]{2,1,0:T(8,128)(2,1)}, u32[]{:S(2)}) copy-start(bf16[32,64,256]{2,1,0:T(8,128)(2,1)} %radon_ref.7) | copy-start | bytes 3145732
  2.1 8.2 %collective-permute-start.3 = (bf16[16,8192]{1,0:T(8,128)(2,1)S(1)}, bf16[16,8192]{1,0:T(8,128)(2,1)S(1)}, u32[]{:S(2)}, u32[]{:S(2)}) collective-permute-start(bf16[16,8192]{1,0:T(8,128)(2,1)S(1)} %get-tuple-element.73), channel_id=1, source_target_pairs={{0,1},{1,2},{2,3},{3,0},{4,5},{5,6},{6,7},{7,4},{8,9},{9,10},{10,1... | collective-permute-start | bytes 786440 | tf_op jit(solution)/shard_map/ppermute | solution.py:35
  4.7 11.1 %collective-permute-start.4 = (bf16[16,8192]{1,0:T(8,128)(2,1)S(1)}, bf16[16,8192]{1,0:T(8,128)(2,1)S(1)}, u32[]{:S(2)}, u32[]{:S(2)}) collective-permute-start(bf16[16,8192]{1,0:T(8,128)(2,1)S(1)} %get-tuple-element.75), channel_id=1, source_target_pairs={{0,2},{1,3},{2,0},{3,1},{4,6},{5,7},{6,4},{7,5},{8,10},{9,11},{10,... | collective-permute-start | bytes 786440 | tf_op jit(solution)/shard_map/ppermute | solution.py:35
  4.7 11.6 %collective-permute-start.5 = (bf16[16,8192]{1,0:T(8,128)(2,1)S(1)}, bf16[16,8192]{1,0:T(8,128)(2,1)S(1)}, u32[]{:S(2)}, u32[]{:S(2)}) collective-permute-start(bf16[16,8192]{1,0:T(8,128)(2,1)S(1)} %get-tuple-element.72), channel_id=1, source_target_pairs={{0,3},{1,0},{2,1},{3,2},{4,7},{5,4},{6,5},{7,6},{8,11},{9,8},{10,9... | collective-permute-start | bytes 786440 | tf_op jit(solution)/shard_map/ppermute | solution.py:35
  26.6 6.6 %copy-start.17 = (s32[4,1]{0,1:T(1,128)S(1)}, s32[4,1]{0,1:T(1,128)}, u32[]{:S(2)}) copy-start(s32[4,1]{0,1:T(1,128)} %param.15) | copy-start | bytes 52
  26.6 6.7 %copy-start.16 = (s32[4,4]{1,0:T(4,128)S(1)}, s32[4,4]{1,0:T(4,128)}, u32[]{:S(2)}) copy-start(s32[4,4]{1,0:T(4,128)} %param.14) | copy-start | bytes 196
  26.6 43.9 %all-to-all-start = ((bf16[32,16,1536]{2,1,0:T(8,128)(2,1)}), bf16[32,16,1536]{2,1,0:T(8,128)(2,1)}, u32[]{:S(2)}, u32[]{:S(2)}) async-start(bf16[32,16,1536]{2,1,0:T(8,128)(2,1)} %get-tuple-element.33), calls=%async_computation | async-start | bytes 3145728 | tf_op jit(solution)/shard_map/all_to_all | solution.py:459
  33.4 4.7 %collective-permute-start.2 = (s32[1,5]{1,0:T(1,128)S(1)}, s32[1,5]{1,0:T(1,128)S(1)}, u32[]{:S(2)}, u32[]{:S(2)}) collective-permute-start(s32[1,5]{1,0:T(1,128)S(1)} %get-tuple-element.83), channel_id=1, source_target_pairs={{0,1},{1,2},{2,3},{3,0},{4,5},{5,6},{6,7},{7,4},{8,9},{9,10},{10,1... | collective-permute-start | bytes 68 | tf_op jit(solution)/shard_map/ppermute | solution.py:35
  35.1 4.6 %collective-permute-start.1 = (s32[1,5]{1,0:T(1,128)S(1)}, s32[1,5]{1,0:T(1,128)S(1)}, u32[]{:S(2)}, u32[]{:S(2)}) collective-permute-start(s32[1,5]{1,0:T(1,128)S(1)} %get-tuple-element.84), channel_id=1, source_target_pairs={{0,2},{1,3},{2,0},{3,1},{4,6},{5,7},{6,4},{7,5},{8,10},{9,11},{10,... | collective-permute-start | bytes 68 | tf_op jit(solution)/shard_map/ppermute | solution.py:35
  35.1 5.3 %collective-permute-start = (s32[1,5]{1,0:T(1,128)S(1)}, s32[1,5]{1,0:T(1,128)S(1)}, u32[]{:S(2)}, u32[]{:S(2)}) collective-permute-start(s32[1,5]{1,0:T(1,128)S(1)} %get-tuple-element.85), channel_id=1, source_target_pairs={{0,3},{1,0},{2,1},{3,2},{4,7},{5,4},{6,5},{7,6},{8,11},{9,8},{10,9... | collective-permute-start | bytes 68 | tf_op jit(solution)/shard_map/ppermute | solution.py:35
  40.4 5.9 %copy-start.7 = (bf16[512,16,128]{2,1,0:T(8,128)(2,1)S(1)}, bf16[512,16,128]{2,1,0:T(8,128)(2,1)}, u32[]{:S(2)}) copy-start(bf16[512,16,128]{2,1,0:T(8,128)(2,1)} %get-tuple-element.34.vv_ref) | copy-start | bytes 6291460
  43.2 39.7 %collective-permute-start.6 = (bf16[4,256,256]{2,1,0:T(8,128)(2,1)}, bf16[4,256,256]{2,1,0:T(8,128)(2,1)}, u32[]{:S(2)}, u32[]{:S(2)}) collective-permute-start(bf16[4,256,256]{2,1,0:T(8,128)(2,1)} %get-tuple-element.65), channel_id=1, source_target_pairs={{0,3},{1,0},{2,1},{3,2},{4,7},{5,4},{6,5},{7,6},{8,11},{9,8},{10,9... | collective-permute-start | bytes 1572872 | tf_op jit(solution)/shard_map/ppermute | solution.py:35
  43.3 67.3 %collective-permute-start.7 = (bf16[4,256,256]{2,1,0:T(8,128)(2,1)}, bf16[4,256,256]{2,1,0:T(8,128)(2,1)S(1)}, u32[]{:S(2)}, u32[]{:S(2)}) collective-permute-start(bf16[4,256,256]{2,1,0:T(8,128)(2,1)} %get-tuple-element.63), channel_id=1, source_target_pairs={{0,1},{1,2},{2,3},{3,0},{4,5},{5,6},{6,7},{7,4},{8,9},{9,10},{10,1... | collective-permute-start | bytes 1572872 | tf_op jit(solution)/shard_map/ppermute | solution.py:35
  45.0 57.4 %collective-permute-start.8 = (bf16[4,256,256]{2,1,0:T(8,128)(2,1)}, bf16[4,256,256]{2,1,0:T(8,128)(2,1)S(1)}, u32[]{:S(2)}, u32[]{:S(2)}) collective-permute-start(bf16[4,256,256]{2,1,0:T(8,128)(2,1)} %get-tuple-element.62), channel_id=1, source_target_pairs={{0,2},{1,3},{2,0},{3,1},{4,6},{5,7},{6,4},{7,5},{8,10},{9,11},{10,... | collective-permute-start | bytes 1572872 | tf_op jit(solution)/shard_map/ppermute | solution.py:35
  46.3 28.5 %copy-start.1 = (bf16[2,256,256]{2,1,0:T(8,128)(2,1)S(1)}, bf16[2,256,256]{2,1,0:T(8,128)(2,1)}, u32[]{:S(2)}) copy-start(bf16[2,256,256]{2,1,0:T(8,128)(2,1)} %probe_ref.7) | copy-start | bytes 786436
  70.5 22.9 %all-to-all-start.1 = ((bf16[32,16,512]{2,1,0:T(8,128)(2,1)}), bf16[32,16,512]{2,1,0:T(8,128)(2,1)S(1)}, u32[]{:S(2)}, u32[]{:S(2)}) async-start(bf16[32,16,512]{2,1,0:T(8,128)(2,1)} %project_rest.1), calls=%async_computation.1 | async-start | bytes 1048576 | tf_op jit(solution)/shard_map/all_to_all | solution.py:459
  74.8 1.0 copy-start.2
  75.8 1.0 copy-start.5
  76.8 6.1 %copy-start.3 = (bf16[512,512]{1,0:T(8,128)(2,1)S(1)}, bf16[512,512]{1,0:T(8,128)(2,1)}, u32[]{:S(2)}) copy-start(bf16[512,512]{1,0:T(8,128)(2,1)} %constant.147.forward_ref) | copy-start | bytes 1572868
  82.0 1.0 copy-start.8
  92.5 0.8 copy-start.11
  93.3 27.3 %all-to-all-start.2 = ((bf16[32,16,512]{2,1,0:T(8,128)(2,1)}), bf16[32,16,512]{2,1,0:T(8,128)(2,1)S(1)}, u32[]{:S(2)}, u32[]{:S(2)}) async-start(bf16[32,16,512]{2,1,0:T(8,128)(2,1)} %get-tuple-element.40), calls=%async_computation.2 | async-start | bytes 1048576 | tf_op jit(solution)/shard_map/all_to_all | solution.py:459
  102.4 1.0 copy-start.4
  103.5 1.0 copy-start.6
  104.5 1.0 copy-start.12
  120.6 11.1 %copy-start.13 = (bf16[32,16,1536]{2,1,0:T(8,128)(2,1)S(1)}, bf16[32,16,1536]{2,1,0:T(8,128)(2,1)}, u32[]{:S(2)}) copy-start(bf16[32,16,1536]{2,1,0:T(8,128)(2,1)} %exit_gradient_3.1) | copy-start | bytes 4718596
  120.6 46.7 %all-to-all-start.3 = ((bf16[32,16,1536]{2,1,0:T(8,128)(2,1)}), bf16[32,16,1536]{2,1,0:T(8,128)(2,1)}, u32[]{:S(2)}, u32[]{:S(2)}) async-start(bf16[32,16,1536]{2,1,0:T(8,128)(2,1)} %exit_gradient_3.1), calls=%async_computation.3 | async-start | bytes 3145728 | tf_op jit(solution)/shard_map/all_to_all | solution.py:459
  130.0 50.5 %collective-permute-start.12 = (bf16[32,16,512]{2,1,0:T(8,128)(2,1)}, bf16[32,16,512]{2,1,0:T(8,128)(2,1)}, u32[]{:S(2)}, u32[]{:S(2)}) collective-permute-start(bf16[32,16,512]{2,1,0:T(8,128)(2,1)} %get-tuple-element.40), channel_id=1, source_target_pairs={{0,1},{1,2},{2,3},{3,0},{4,5},{5,6},{6,7},{7,4},{8,9},{9,10},{10,1... | collective-permute-start | bytes 1572872 | tf_op jit(solution)/shard_map/ppermute | solution.py:35
  132.8 47.7 %collective-permute-start.13 = (bf16[32,16,512]{2,1,0:T(8,128)(2,1)}, bf16[32,16,512]{2,1,0:T(8,128)(2,1)}, u32[]{:S(2)}, u32[]{:S(2)}) collective-permute-start(bf16[32,16,512]{2,1,0:T(8,128)(2,1)} %get-tuple-element.67), channel_id=1, source_target_pairs={{0,2},{1,3},{2,0},{3,1},{4,6},{5,7},{6,4},{7,5},{8,10},{9,11},{10,... | collective-permute-start | bytes 1572872 | tf_op jit(solution)/shard_map/ppermute | solution.py:35
  132.9 47.6 %collective-permute-start.14 = (bf16[32,16,512]{2,1,0:T(8,128)(2,1)}, bf16[32,16,512]{2,1,0:T(8,128)(2,1)}, u32[]{:S(2)}, u32[]{:S(2)}) collective-permute-start(bf16[32,16,512]{2,1,0:T(8,128)(2,1)} %get-tuple-element.66), channel_id=1, source_target_pairs={{0,3},{1,0},{2,1},{3,2},{4,7},{5,4},{6,5},{7,6},{8,11},{9,8},{10,9... | collective-permute-start | bytes 1572872 | tf_op jit(solution)/shard_map/ppermute | solution.py:35
  139.1 0.8 copy-start.9
  167.3 1.0 copy-start.10
  178.2 9.2 %collective-permute-start.9 = (bf16[16,8192]{1,0:T(8,128)(2,1)S(1)}, bf16[16,8192]{1,0:T(8,128)(2,1)S(1)}, u32[]{:S(2)}, u32[]{:S(2)}) collective-permute-start(bf16[16,8192]{1,0:T(8,128)(2,1)S(1)} %get-tuple-element.52), channel_id=1, source_target_pairs={{0,1},{1,2},{2,3},{3,0},{4,5},{5,6},{6,7},{7,4},{8,9},{9,10},{10,1... | collective-permute-start | bytes 786440 | tf_op jit(solution)/shard_map/ppermute | solution.py:35
  179.8 12.2 %collective-permute-start.10 = (bf16[16,8192]{1,0:T(8,128)(2,1)S(1)}, bf16[16,8192]{1,0:T(8,128)(2,1)S(1)}, u32[]{:S(2)}, u32[]{:S(2)}) collective-permute-start(bf16[16,8192]{1,0:T(8,128)(2,1)S(1)} %get-tuple-element.53), channel_id=1, source_target_pairs={{0,2},{1,3},{2,0},{3,1},{4,6},{5,7},{6,4},{7,5},{8,10},{9,11},{10,... | collective-permute-start | bytes 786440 | tf_op jit(solution)/shard_map/ppermute | solution.py:35
  180.5 12.2 %collective-permute-start.11 = (bf16[16,8192]{1,0:T(8,128)(2,1)S(1)}, bf16[16,8192]{1,0:T(8,128)(2,1)S(1)}, u32[]{:S(2)}, u32[]{:S(2)}) collective-permute-start(bf16[16,8192]{1,0:T(8,128)(2,1)S(1)} %get-tuple-element.54), channel_id=1, source_target_pairs={{0,3},{1,0},{2,1},{3,2},{4,7},{5,4},{6,5},{7,6},{8,11},{9,8},{10,9... | collective-permute-start | bytes 786440 | tf_op jit(solution)/shard_map/ppermute | solution.py:35
  187.4 5.3 %copy-start.14 = (bf16[2,32,8192]{2,1,0:T(8,128)(2,1)S(1)}, bf16[2,32,8192]{2,1,0:T(8,128)(2,1)}, u32[]{:S(2)}) copy-start(bf16[2,32,8192]{2,1,0:T(8,128)(2,1)} %param.9) | copy-start | bytes 3145732

commit v4 on v3

--- a/solution.py
+++ b/solution.py
@@ -253,184 +253,226 @@
     )(*operands)
 
 
-def exit_kernel(
-    step, last, meta_ref, probe_ref, forward_ref, inverse_ref, own_ref, next_ref, amp_ref, *refs
-):
-    spill_in_ref, refs = (refs[0], refs[1:]) if step > 0 else (None, refs)
-    (partial_ref, before_ref), refs = (refs[:2], refs[2:]) if step == last else ((None, None), refs)
-    out_ref, refs = refs[0], refs[1:]
-    beyond_ref, refs = (None, refs) if step == last else (refs[0], refs[1:])
-    ext_ref, acc_ref, wave_ref, half_ref = refs
-    owner = lax.rem(lax.axis_index("pos") + step, last + 1)
-    groups = own_ref.shape[0]
+def add_slots(meta_ref, probe_ref, forward_ref, inverse_ref, ext_ref, acc_ref, amp_refs, scratch, first):
+    wave_ref, half_ref, delta_ref, back_ref = scratch
+    n_pos = lax.axis_size("pos")
+    groups = ext_ref.shape[0]
     width = probe_ref.shape[1]
-    tile_width = own_ref.shape[2]
-    reach = tile_width + width
-    slots = amp_ref.shape[0]
+    slots = amp_refs[0].shape[0]
+    tile_width = (acc_ref.shape[2] - width) // len(amp_refs)
     chunk = 4
     crows = chunk * GROUP
+    chunks = groups // chunk
+    wide = width // LANES
     lane_id = lax.broadcasted_iota(jnp.int32, (crows, LANES), 1)
-    wide = width // LANES
-
-    @pl.loop(0, groups)
-    def _(g):
-        ext_ref[g, :, :tile_width] = own_ref[g]
-        ext_ref[g, :, tile_width:] = next_ref[g]
-        rows = pl.ds(pl.multiple_of(g * GROUP, GROUP), GROUP)
-        for c in range(2):
-            if step > 0:
-                acc_ref[c, rows, :width] = spill_in_ref[c, rows, :]
-                acc_ref[c, rows, width:] = jnp.zeros((GROUP, tile_width), jnp.float32)
-            else:
-                acc_ref[c, rows, :] = jnp.zeros((GROUP, reach), jnp.float32)
 
     def product(left, right):
         return jnp.dot(left, right, preferred_element_type=jnp.float32)
 
-    def slot_step(q, carry):
-        offset = meta_ref[step, q] - owner * tile_width
-        first_tile = offset // LANES
-        shift = offset % LANES
-        starts = [pl.multiple_of((first_tile + m) * LANES, LANES) for m in range(wide + 1)]
-        keep = lane_id < LANES - shift
-        back_shift = (LANES - shift) % LANES
-        for ch in range(groups // chunk):
-            rows = slice(ch * crows, (ch + 1) * crows)
-            turned = []
-            for start in starts:
-                both = ext_ref[ch * chunk : (ch + 1) * chunk, :, pl.ds(start, LANES)].astype(
-                    jnp.float32
+    for tile, amp_ref in enumerate(amp_refs):
+        order = first + tile
+        tile_start = lax.rem(lax.axis_index("pos") + order, n_pos) * tile_width - tile * tile_width
+        count = meta_ref[order, slots]
+
+        @pl.loop(0, (count + 1) // 2)
+        def _(step):
+            shifts, starts, lives = [], [], []
+            for n in range(2):
+                offset = meta_ref[order, step * 2 + n] - tile_start
+                shifts.append(offset % LANES)
+                lane_tile = offset // LANES
+                starts.append(
+                    [pl.multiple_of((lane_tile + m) * LANES, LANES) for m in range(wide + 1)]
                 )
-                turned.append(
-                    [
-                        pltpu.roll(
-                            both[:, c * GROUP : (c + 1) * GROUP].reshape(crows, LANES), back_shift, 1
+                lives.append((step * 2 + n < count).astype(jnp.float32))
+            for n in range(2):
+                keep = lane_id < LANES - shifts[n]
+                back_shift = (LANES - shifts[n]) % LANES
+                for ch in range(chunks):
+                    rows = slice(ch * crows, (ch + 1) * crows)
+                    low_rows = slice(width + ch * crows, width + (ch + 1) * crows)
+                    turned = []
+                    for start in starts[n]:
+                        both = ext_ref[ch * chunk : (ch + 1) * chunk, :, pl.ds(start, LANES)]
+                        both = both.astype(jnp.float32)
+                        turned.append(
+                            [
+                                pltpu.roll(
+                                    both[:, c * GROUP : (c + 1) * GROUP].reshape(crows, LANES),
+                                    back_shift,
+                                    1,
+                                )
+                                for c in range(2)
+                            ]
                         )
-                        for c in range(2)
-                    ]
-                )
-            for m in range(wide):
-                lanes = slice(m * LANES, (m + 1) * LANES)
-                patch_re = jnp.where(keep, turned[m][0], turned[m + 1][0])
-                patch_im = jnp.where(keep, turned[m][1], turned[m + 1][1])
-                probe_re = probe_ref[0, rows, lanes].astype(jnp.float32)
-                probe_im = probe_ref[1, rows, lanes].astype(jnp.float32)
-                wave_ref[rows, lanes] = (probe_re * patch_re - probe_im * patch_im).astype(
-                    jnp.bfloat16
-                )
-                wave_ref[width + ch * crows : width + (ch + 1) * crows, lanes] = (
-                    probe_re * patch_im + probe_im * patch_re
-                ).astype(jnp.bfloat16)
-        half = product(forward_ref[...], wave_ref[...]).astype(jnp.bfloat16)
-        half_ref[:, :width] = half[:width]
-        half_ref[:, width:] = half[width:]
-        far = product(half_ref[...], inverse_ref[...])
-        for ch in range(groups // chunk):
-            rows = slice(ch * crows, (ch + 1) * crows)
-            far_re, far_im = far[rows, :width], far[rows, width:]
-            power = far_re * far_re + far_im * far_im
-            amps = amp_ref[q, rows, :].astype(jnp.float32)
-            factor = amps * lax.rsqrt(jnp.maximum(power, 1.0)) - 1.0
-            wave_ref[rows, :] = (far_re * factor).astype(jnp.bfloat16)
-            wave_ref[width + ch * crows : width + (ch + 1) * crows, :] = (far_im * factor).astype(
-                jnp.bfloat16
-            )
-        back = product(inverse_ref[...], wave_ref[...]).astype(jnp.bfloat16)
-        half_ref[:, :width] = back[:width]
-        half_ref[:, width:] = back[width:]
-        near = product(half_ref[...], forward_ref[...])
-        past = lane_id >= shift
-        for ch in range(groups // chunk):
-            rows = slice(ch * crows, (ch + 1) * crows)
-            turned = []
-            for m in range(wide):
-                lanes = slice(m * LANES, (m + 1) * LANES)
-                probe_re = probe_ref[0, rows, lanes].astype(jnp.float32)
-                probe_im = probe_ref[1, rows, lanes].astype(jnp.float32)
-                near_re = near[rows, m * LANES : (m + 1) * LANES]
-                near_im = near[rows, width + m * LANES : width + (m + 1) * LANES]
-                turned.append(
-                    [
-                        pltpu.roll(probe_re * near_re + probe_im * near_im, shift, 1),
-                        pltpu.roll(probe_re * near_im - probe_im * near_re, shift, 1),
-                    ]
-                )
-            for m in range(wide + 1):
-                for c in range(2):
-                    behind = turned[m - 1][c] if m > 0 else 0.0
-                    ahead = turned[m][c] if m < wide else 0.0
-                    acc_ref[c, rows, pl.ds(starts[m], LANES)] += jnp.where(past, ahead, behind)
-        return carry
-
-    lax.fori_loop(0, meta_ref[step, slots], slot_step, 0)
+                    for m in range(wide):
+                        lanes = slice(m * LANES, (m + 1) * LANES)
+                        put = slice(n * width + m * LANES, n * width + (m + 1) * LANES)
+                        patch_re = jnp.where(keep, turned[m][0], turned[m + 1][0])
+                        patch_im = jnp.where(keep, turned[m][1], turned[m + 1][1])
+                        probe_re = probe_ref[0, rows, lanes].astype(jnp.float32)
+                        probe_im = probe_ref[1, rows, lanes].astype(jnp.float32)
+                        wave_re = probe_re * patch_re - probe_im * patch_im
+                        wave_im = probe_re * patch_im + probe_im * patch_re
+                        wave_ref[rows, put] = wave_re.astype(jnp.bfloat16)
+                        wave_ref[low_rows, put] = wave_im.astype(jnp.bfloat16)
+                mine = slice(n * width, (n + 1) * width)
+                half = product(forward_ref[...], wave_ref[:, mine]).astype(jnp.bfloat16)
+                half_ref[mine, :width] = half[:width]
+                half_ref[mine, width:] = half[width:]
+            for n in range(2):
+                mine = slice(n * width, (n + 1) * width)
+                far = product(half_ref[mine, :], inverse_ref[...])
+                for ch in range(chunks):
+                    rows = slice(ch * crows, (ch + 1) * crows)
+                    low_rows = slice(width + ch * crows, width + (ch + 1) * crows)
+                    far_re, far_im = far[rows, :width], far[rows, width:]
+                    power = far_re * far_re + far_im * far_im
+                    amps = amp_ref[step * 2 + n, rows, :].astype(jnp.float32)
+                    factor = amps * lax.rsqrt(jnp.maximum(power, 1.0)) - 1.0
+                    delta_ref[rows, mine] = (far_re * factor).astype(jnp.bfloat16)
+                    delta_ref[low_rows, mine] = (far_im * factor).astype(jnp.bfloat16)
+                back = product(inverse_ref[...], delta_ref[:, mine]).astype(jnp.bfloat16)
+                back_ref[mine, :width] = back[:width]
+                back_ref[mine, width:] = back[width:]
+            for n in range(2):
+                mine = slice(n * width, (n + 1) * width)
+                near = product(back_ref[mine, :], forward_ref[...])
+                past = lane_id >= shifts[n]
+                for ch in range(chunks):
+                    rows = slice(ch * crows, (ch + 1) * crows)
+                    turned = []
+                    for m in range(wide):
+                        lanes = slice(m * LANES, (m + 1) * LANES)
+                        probe_re = probe_ref[0, rows, lanes].astype(jnp.float32) * lives[n]
+                        probe_im = probe_ref[1, rows, lanes].astype(jnp.float32) * lives[n]
+                        near_re = near[rows, m * LANES : (m + 1) * LANES]
+                        near_im = near[rows, width + m * LANES : width + (m + 1) * LANES]
+                        turned.append(
+                            [
+                                pltpu.roll(probe_re * near_re + probe_im * near_im, shifts[n], 1),
+                                pltpu.roll(probe_re * near_im - probe_im * near_re, shifts[n], 1),
+                            ]
+                        )
+                    for m in range(wide + 1):
+                        for c in range(2):
+                            behind = turned[m - 1][c] if m > 0 else 0.0
+                            ahead = turned[m][c] if m < wide else 0.0
+                            here = (c, rows, pl.ds(starts[n][m], LANES))
+                            acc_ref[here] += jnp.where(past, ahead, behind)
+
+
+def exit_first_kernel(
+    tiles, meta_ref, probe_ref, forward_ref, inverse_ref, most_ref, *refs
+):
+    amp_refs, refs = refs[:tiles], refs[tiles:]
+    partial_ref, grad_ref, spill_ref, acc_ref, *scratch = refs
+    groups = most_ref.shape[0]
+    tile_width = partial_ref.shape[2]
+    done = tiles * tile_width
 
     @pl.loop(0, groups)
     def _(g):
         rows = pl.ds(pl.multiple_of(g * GROUP, GROUP), GROUP)
-        if step == 0:
-            for c in range(2):
-                out_ref[c, rows, :] = acc_ref[c, rows, :tile_width]
-        else:
-            both = [acc_ref[c, rows, :tile_width] for c in range(2)]
-            here = jnp.concatenate(both, axis=0).astype(jnp.bfloat16)
-        if step == last:
-            both = []
-            for c in range(2):
-                whole = partial_ref[c, rows, :]
-                spilled = whole[:, :width] + acc_ref[c, rows, tile_width:]
-                both.append(jnp.concatenate([spilled, whole[:, width:]], axis=1))
-            waiting = before_ref.shape[2]
-            out_ref[g, :, :waiting] = before_ref[g]
-            out_ref[g, :, waiting : waiting + tile_width] = here
-            out_ref[g, :, waiting + tile_width :] = jnp.concatenate(both, axis=0).astype(jnp.bfloat16)
-        else:
-            if step > 0:
-                out_ref[g] = here
-            for c in range(2):
-                beyond_ref[c, rows, :] = acc_ref[c, rows, tile_width:]
-
-
-def lanes_of(source, width):
-    array, at = source
-    return pl.BlockSpec(array.shape[:2] + (width,), lambda i: (0, 0, at))
-
-
-def exit_gradient(step, last, meta, probe_field, tables, own, ahead, amps, spill, partial, before):
-    groups, rows = own[0].shape[:2]
+        for c in range(2):
+            acc_ref[c, rows, :] = jnp.zeros((GROUP, acc_ref.shape[2]), jnp.float32)
+
+    add_slots(
+        meta_ref, probe_ref, forward_ref, inverse_ref, most_ref, acc_ref, amp_refs, scratch, 0
+    )
+
+    @pl.loop(0, groups)
+    def _(g):
+        rows = pl.ds(pl.multiple_of(g * GROUP, GROUP), GROUP)
+        whole = [acc_ref[c, rows, tile_width:done] for c in range(2)]
+        grad_ref[g] = jnp.concatenate(whole, axis=0).astype(jnp.bfloat16)
+        for c in range(2):
+            partial_ref[c, rows, :] = acc_ref[c, rows, :tile_width]
+            spill_ref[c, rows, :] = acc_ref[c, rows, done:]
+
+
+def exit_rest_kernel(
+    tiles, meta_ref, probe_ref, forward_ref, inverse_ref, most_ref, last_ref, partial_ref, spill_ref, *refs
+):
+    amp_refs, refs = refs[:tiles], refs[tiles:]
+    out_ref, ext_ref, acc_ref, *scratch = refs
+    groups = most_ref.shape[0]
+    width = probe_ref.shape[1]
+    tile_width = partial_ref.shape[2]
+    done = tiles * tile_width
+    kept = done - tile_width
+
+    @pl.loop(0, groups)
+    def _(g):
+        ext_ref[g, :, :kept] = most_ref[g, :, most_ref.shape[2] - kept :]
+        ext_ref[g, :, kept:done] = last_ref[g]
+        ext_ref[g, :, done:] = most_ref[g, :, :width]
+        rows = pl.ds(pl.multiple_of(g * GROUP, GROUP), GROUP)
+        for c in range(2):
+            acc_ref[c, rows, :width] = spill_ref[c, rows, :]
+            acc_ref[c, rows, width:] = jnp.zeros((GROUP, done), jnp.float32)
+
+    add_slots(
+        meta_ref, probe_ref, forward_ref, inverse_ref, ext_ref, acc_ref, amp_refs, scratch,
+        lax.axis_size("pos") - tiles,
+    )
+
+    @pl.loop(0, groups)
+    def _(g):
+        rows = pl.ds(pl.multiple_of(g * GROUP, GROUP), GROUP)
+        here, wrapped = [], []
+        for c in range(2):
+            here.append(acc_ref[c, rows, :done])
+            whole = partial_ref[c, rows, :]
+            spilled = whole[:, :width] + acc_ref[c, rows, done:]
+            wrapped.append(jnp.concatenate([spilled, whole[:, width:]], axis=1))
+        out_ref[g, :, :done] = jnp.concatenate(here, axis=0).astype(jnp.bfloat16)
+        out_ref[g, :, done:] = jnp.concatenate(wrapped, axis=0).astype(jnp.bfloat16)
+
+
+def exit_scratch(groups, width, reach):
+    return [pltpu.VMEM((2, groups * GROUP, reach), jnp.float32)] + [
+        pltpu.VMEM((2 * width, 2 * width), jnp.bfloat16)
+    ] * 4
+
+
+def exit_first(meta, probe_field, tables, most, amps, tile_width):
+    groups, rows = most.shape[:2]
     width = probe_field.shape[1]
-    tile_width = own[2]
+    tiles = len(amps)
     slices = groups * GROUP
-    grad_shape = jax.ShapeDtypeStruct((groups, rows, tile_width), jnp.bfloat16)
-    partial_shape = jax.ShapeDtypeStruct((2, slices, tile_width), jnp.float32)
-    spill_shape = jax.ShapeDtypeStruct((2, slices, width), jnp.float32)
-    operands = [meta, probe_field, *tables, own[0], ahead[0], amps]
-    specs = [scalars] + [everywhere] * 3
-    specs += [lanes_of(own[:2], tile_width), lanes_of(ahead[:2], width), everywhere]
-    if step > 0:
-        operands.append(spill)
-    if step == last:
-        operands += [partial, before]
-        joined = (groups, rows, before.shape[2] + 2 * tile_width)
-        out_shape = [jax.ShapeDtypeStruct(joined, jnp.bfloat16)]
-    else:
-        out_shape = [partial_shape if step == 0 else grad_shape, spill_shape]
-    specs += [everywhere] * (len(operands) - len(specs))
     return pl.pallas_call(
-        functools.partial(exit_kernel, step, last),
-        grid=(1,),
-        out_shape=out_shape,
-        in_specs=specs,
-        out_specs=[everywhere] * len(out_shape),
-        scratch_shapes=[
-            pltpu.VMEM((groups, rows, tile_width + width), jnp.bfloat16),
-            pltpu.VMEM((2, slices, tile_width + width), jnp.float32),
-            pltpu.VMEM((2 * width, width), jnp.bfloat16),
-            pltpu.VMEM((width, 2 * width), jnp.bfloat16),
+        functools.partial(exit_first_kernel, tiles),
+        out_shape=[
+            jax.ShapeDtypeStruct((2, slices, tile_width), jnp.float32),
+            jax.ShapeDtypeStruct((groups, rows, (tiles - 1) * tile_width), jnp.bfloat16),
+            jax.ShapeDtypeStruct((2, slices, width), jnp.float32),
         ],
+        in_specs=[scalars] + [everywhere] * (4 + tiles),
+        out_specs=[everywhere] * 3,
+        scratch_shapes=exit_scratch(groups, width, tiles * tile_width + width),
         compiler_params=pltpu.CompilerParams(vmem_limit_bytes=VMEM_LIMIT),
-        cost_estimate=guess(7),
-        name="exit_gradient_" + str(step),
-    )(*operands)
+        cost_estimate=guess(10),
+        name="exit_first",
+    )(meta, probe_field, *tables, most, *amps)
+
+
+def exit_rest(meta, probe_field, tables, most, final, partial, spill, amps):
+    groups, rows, tile_width = final.shape
+    width = probe_field.shape[1]
+    tiles = len(amps)
+    reach = tiles * tile_width + width
+    return pl.pallas_call(
+        functools.partial(exit_rest_kernel, tiles),
+        out_shape=jax.ShapeDtypeStruct((groups, rows, (tiles + 1) * tile_width), jnp.bfloat16),
+        in_specs=[scalars] + [everywhere] * (7 + tiles),
+        out_specs=everywhere,
+        scratch_shapes=[pltpu.VMEM((groups, rows, reach), jnp.bfloat16)]
+        + exit_scratch(groups, width, reach),
+        compiler_params=pltpu.CompilerParams(vmem_limit_bytes=VMEM_LIMIT),
+        cost_estimate=guess(10),
+        name="exit_rest",
+    )(meta, probe_field, *tables, most, final, partial, spill, *amps)
 
 
 def to_groups(received, own_slices):
@@ -509,33 +551,15 @@
     got_most, sino_last = lax.optimization_barrier((got_most, sino_last))
     got_last = everyone(sino_last[:, :rows])
     got_most, got_last = to_groups(got_most, own), to_groups(got_last, own)
-    probe_width = probe_field.shape[1]
-    tables = dft_tables(probe_width)
-
-    def tile_from(j):
-        return (got_most, j, tile_width) if j < last else (got_last, 0, tile_width)
-
-    def edge_from(j):
-        per_tile = tile_width // probe_width
-        return (got_most, j % n_pos * per_tile) if j % n_pos < last else (got_last, 0)
-
-    grads = [None] * last
-    partial = spill = before = None
-    for j in range(n_pos):
-        out = exit_gradient(
-            j, last, meta, probe_field, tables, tile_from(j), edge_from(j + 1), amp_pieces[j],
-            spill, partial, before,
-        )
-        if j == 0:
-            partial, spill = out
-        elif j < last:
-            grads[j], spill = out
-            if j == 1:
-                first_grad, got_last = lax.optimization_barrier((grads[1], got_last))
-            else:
-                before = grads[j] if before is None else jnp.concatenate([before, grads[j]], axis=2)
-        else:
-            joined = out[0]
+    tables = dft_tables(probe_field.shape[1])
+    partial, first_grad, spill = exit_first(
+        meta, probe_field, tables, got_most, amp_pieces[:2], tile_width
+    )
+    own_grad = first_grad
+    first_grad, got_last = lax.optimization_barrier((first_grad, got_last))
+    joined = exit_rest(
+        meta, probe_field, tables, got_most, got_last, partial, spill, amp_pieces[2:]
+    )
     back_first = everyone(from_groups(first_grad, own))
     back_first, joined_sent = lax.optimization_barrier((back_first, joined))
     back_rest = everyone(from_groups(joined_sent, own))
@@ -544,7 +568,7 @@
     )
     order = list(range(2, n_pos)) + [0]
     joined_tiles = {j: joined[:, :, i * tile_width : (i + 1) * tile_width] for i, j in enumerate(order)}
-    joined_tiles[1] = grads[1]
+    joined_tiles[1] = own_grad
     tile_pieces = rotate_pos([joined_tiles[j] for j in range(n_pos)], 1)
     obj_pieces = back_project(
         idx, radon_tiles, pad_rows(back_rest), order, partial_grad, n_pos, width, jnp.bfloat16, "back_rest"

time: 194 us -> 179 us (0.923)
  Pallas kernels: 60.2 us -> 49.5 us
  starting transfers between devices: 42.2 us -> 33.2 us
  waiting for transfers between devices: 67 us -> 71.8 us
    pallas_call x4 -> x2, Pallas kernels: 29.7 us -> 19 us  [the longest x1 9.7 us: exit_rest(): pl.pallas_call(functools.partial(exit_rest_kernel, tiles), out_shape=jax....]
    all_to_all x4, starting transfers between devices: 29.3 us -> 19.9 us  [everyone(): return lax.all_to_all(chunk, ('ang', 'pos'), 0, 0, tiled=True)]
    all_to_all x4, waiting for transfers between devices: 46.9 us -> 51.8 us  [everyone(): return lax.all_to_all(chunk, ('ang', 'pos'), 0, 0, tiled=True)]
    unnamed x39 -> x35, local copies, waits for them, and re-layouts: 13.6 us -> 12.7 us
  transfers between devices with their start and end apart: 19 -> 19, of which waited for: 10 -> 12; matrix products, arithmetic and copies ran while one was open for 6% -> 7% of each run, Pallas kernels for 26% -> 22%
where the time goes in v4:
time: 179 us
  waiting for transfers between devices  71.8 us (40%)
  Pallas kernels  49.5 us (28%)
  starting transfers between devices  33.2 us (19%)
  local copies, waits for them, and re-layouts  18.7 us (10%)
  other arithmetic  4.18 us (2%)
    all_to_all x4, waiting for transfers between devices, everyone(): return lax.all_to_all(chunk, ('ang', 'pos'), 0, 0, tiled=True)  51.8 us
    ppermute x15, waiting for transfers between devices, rotate_pos(): lax.ppermute(pieces[j], 'pos', [(i, (i + sign * j) % count) for i in rang...  20.1 us
    all_to_all x4, starting transfers between devices, everyone(): return lax.all_to_all(chunk, ('ang', 'pos'), 0, 0, tiled=True)  19.9 us
    pallas_call x2, Pallas kernels, back_project(): pl.pallas_call(functools.partial(back_project_kernel, chunks, pieces, has...  15.6 us
    ppermute x15, starting transfers between devices, rotate_pos(): lax.ppermute(pieces[j], 'pos', [(i, (i + sign * j) % count) for i in rang...  13.4 us
    unnamed x35, local copies, waits for them, and re-layouts  12.7 us
    pallas_call x1, Pallas kernels, project_first(): pl.pallas_call(functools.partial(project_first_kernel, chunks, pieces), o...  10.2 us
    pallas_call x1, Pallas kernels, exit_rest(): pl.pallas_call(functools.partial(exit_rest_kernel, tiles), out_shape=jax....  9.7 us
  transfers between devices with their start and end apart: 19, of which 12 were waited for; matrix products, arithmetic and copies ran while one was open for 7% of the time, Pallas kernels for 22%

profile of v4, /device:TPU:1, one launch (start us, length us, event | category | flops | bytes accessed | tf_op | source)
XLA Modules:
  0.0 178.6 jit_solution(535389732358327961)
XLA Ops:
  0.6 0.0 copy-start
  0.7 1.3 dynamic-slice_bitcast_fusion.4
  2.1 2.7 %collective-permute-start.3 = (bf16[16,8192]{1,0:T(8,128)(2,1)S(1)}, bf16[16,8192]{1,0:T(8,128)(2,1)S(1)}, u32[]{:S(2)}, u32[]{:S(2)}) collective-permute-start(bf16[16,8192]{1,0:T(8,128)(2,1)S(1)} %get-tuple-element.67), channel_id=1, source_target_pairs={{0,1},{1,2},{2,3},{3,0},{4,5},{5,6},{6,7},{7,4},{8,9},{9,10},{10,1... | collective-permute-start | bytes 786440 | tf_op jit(solution)/shard_map/ppermute | solution.py:35
  4.7 0.0 collective-permute-start.4
  4.7 0.5 collective-permute-start.5
  5.2 0.3 fusion.3
  5.5 0.3 copy.19
  5.8 0.2 reshape.186
  6.1 0.1 reshape.187.idx_ref
  6.2 4.0 %collective-permute-done.3.refs_1_ = bf16[16,8192]{1,0:T(8,128)(2,1)S(1)} collective-permute-done((bf16[16,8192]{1,0:T(8,128)(2,1)S(1)}, bf16[16,8192]{1,0:T(8,128)(2,1)S(1)}, u32[]{:S(2)}, u32[]{:S(2)}) %collective-permute-start.3) | collective-permute-done | bytes 262176 | tf_op jit(solution)/shard_map/ppermute | solution.py:35
  10.2 5.6 %collective-permute-done.4.refs_2_ = bf16[16,8192]{1,0:T(8,128)(2,1)S(1)} collective-permute-done((bf16[16,8192]{1,0:T(8,128)(2,1)S(1)}, bf16[16,8192]{1,0:T(8,128)(2,1)S(1)}, u32[]{:S(2)}, u32[]{:S(2)}) %collective-permute-start.4) | collective-permute-done | bytes 262176 | tf_op jit(solution)/shard_map/ppermute | solution.py:35
  15.8 0.5 collective-permute-done.5.refs_3_
  16.3 10.2 %project_first.1 = (bf16[32,16,1536]{2,1,0:T(8,128)(2,1)}, bf16[512,16,128]{2,1,0:T(8,128)(2,1)}) custom-call(s32[32,128]{1,0:T(8,128)S(1)} %reshape.187.idx_ref, bf16[32,64,256]{2,1,0:T(8,128)(2,1)S(1)} %copy-done, bf16[16,8192]{1,0:T(8,128)(2,1)S(1)} %get-tuple-element.26.refs_0_, bf16[16,8192]{1,0:T(8,128)(2,1)S(1)} %collective-permute-done.3.refs_1_, ...), custom_call_target="tpu_custom_call" | custom-call | flops 9200000000 | bytes 800000 | tf_op jit(solution)/shard_map/project_first/pallas_call | solution.py:139
  26.6 6.6 %all-to-all-start = ((bf16[32,16,1536]{2,1,0:T(8,128)(2,1)}), bf16[32,16,1536]{2,1,0:T(8,128)(2,1)}, u32[]{:S(2)}, u32[]{:S(2)}) async-start(bf16[32,16,1536]{2,1,0:T(8,128)(2,1)} %get-tuple-element.30), calls=%async_computation | async-start | bytes 3145728 | tf_op jit(solution)/shard_map/all_to_all | solution.py:501
  33.2 0.1 copy.24
  33.3 0.1 pad_add_fusion.1
  33.4 1.7 collective-permute-start.2
  35.1 0.0 collective-permute-start.1
  35.1 0.5 collective-permute-start
  35.6 2.4 %collective-permute-done.2 = s32[1,5]{1,0:T(1,128)S(1)} collective-permute-done((s32[1,5]{1,0:T(1,128)S(1)}, s32[1,5]{1,0:T(1,128)S(1)}, u32[]{:S(2)}, u32[]{:S(2)}) %collective-permute-start.2) | collective-permute-done | bytes 52 | tf_op jit(solution)/shard_map/ppermute | solution.py:35
  38.1 1.6 collective-permute-done.1
  39.6 0.7 collective-permute-done
  40.4 0.0 copy-start.6
  40.4 2.8 %dynamic-slice_bitcast_fusion = (bf16[4,256,256]{2,1,0:T(8,128)(2,1)}, bf16[4,256,256]{2,1,0:T(8,128)(2,1)}, bf16[4,256,256]{2,1,0:T(8,128)(2,1)}, bf16[4,256,256]{2,1,0:T(8,128)(2,1)S(1)}) fusion(bf16[4,4,256,256]{3,2,1,0:T(8,128)(2,1)} %param.13, s32[]{:T(128)S(6)} %select_n.309, s32[]{:T(128)S(6)} %select_n.307, s32[]{:T(128)S(6)} %select_n.305, ...), kind=kLoop, calls=%fused_computation.10 | loop fusion | bytes 4194320 | tf_op jit(solution)/shard_map/jit(dynamic_index_in_dim)/squeeze | solution.py:531
  43.2 0.0 collective-permute-start.6
  43.3 1.5 collective-permute-start.7
  44.8 1.8 collective-permute-start.8
  46.6 4.7 %project_rest.1 = bf16[32,16,512]{2,1,0:T(8,128)(2,1)} custom-call(s32[32,128]{1,0:T(8,128)S(1)} %reshape.187.idx_ref, bf16[32,64,256]{2,1,0:T(8,128)(2,1)S(1)} %copy-done, bf16[512,16,128]{2,1,0:T(8,128)(2,1)S(1)} %copy-done.6), custom_call_target="tpu_custom_call" | custom-call | flops 5750000128 | bytes 500000 | tf_op jit(solution)/shard_map/project_rest/pallas_call | solution.py:157
  51.2 19.2 %all-to-all-done.most_ref = bf16[32,16,1536]{2,1,0:T(8,128)(2,1)} async-done(((bf16[32,16,1536]{2,1,0:T(8,128)(2,1)}), bf16[32,16,1536]{2,1,0:T(8,128)(2,1)}, u32[]{:S(2)}, u32[]{:S(2)}) %all-to-all-start) | async-done | bytes 1572896 | tf_op jit(solution)/shard_map/all_to_all | solution.py:501
  70.5 4.3 %all-to-all-start.1 = ((bf16[32,16,512]{2,1,0:T(8,128)(2,1)}), bf16[32,16,512]{2,1,0:T(8,128)(2,1)S(1)}, u32[]{:S(2)}, u32[]{:S(2)}) async-start(bf16[32,16,512]{2,1,0:T(8,128)(2,1)} %project_rest.1), calls=%async_computation.1 | async-start | bytes 1048576 | tf_op jit(solution)/shard_map/all_to_all | solution.py:501
  74.8 0.0 collective-permute-done.6.refs_1_
  74.8 0.0 copy-start.2
  74.8 1.0 copy-done.2
  75.8 1.0 copy-done.4
  76.9 9.3 %exit_first.1 = (f32[2,256,512]{2,1,0:T(8,128)}, bf16[32,16,512]{2,1,0:T(8,128)(2,1)}, f32[2,256,256]{2,1,0:T(8,128)S(1)}) custom-call(s32[4,5]{1,0:T(4,128)S(1)} %pad_add_fusion.2.meta_ref, bf16[2,256,256]{2,1,0:T(8,128)(2,1)S(1)} %copy-done.1, bf16[512,512]{1,0:T(8,128)(2,1)S(1)} %copy-done.2, bf16[512,512]{1,0:T(8,128)(2,1)S(1)} %copy-done.4, ...), custom_call_target="tpu_custom_call" | custom-call | flops 11500000256 | bytes 1000000 | tf_op jit(solution)/shard_map/exit_first/pallas_call | solution.py:444
  86.2 0.8 copy-done.9
  87.0 3.0 %all-to-all-done.1.last_ref = bf16[32,16,512]{2,1,0:T(8,128)(2,1)S(1)} async-done(((bf16[32,16,512]{2,1,0:T(8,128)(2,1)}), bf16[32,16,512]{2,1,0:T(8,128)(2,1)S(1)}, u32[]{:S(2)}, u32[]{:S(2)}) %all-to-all-start.1) | async-done | bytes 524320 | tf_op jit(solution)/shard_map/all_to_all | solution.py:501
  90.0 3.4 %all-to-all-start.2 = ((bf16[32,16,512]{2,1,0:T(8,128)(2,1)}), bf16[32,16,512]{2,1,0:T(8,128)(2,1)S(1)}, u32[]{:S(2)}, u32[]{:S(2)}) async-start(bf16[32,16,512]{2,1,0:T(8,128)(2,1)} %get-tuple-element.36), calls=%async_computation.2 | async-start | bytes 1048576 | tf_op jit(solution)/shard_map/all_to_all | solution.py:501
  93.4 0.0 copy-start.3
  93.4 1.0 copy-done.3
  94.5 1.0 copy-done.5
  95.5 1.0 copy-done.10
  96.5 9.7 %exit_rest.1 = bf16[32,16,1536]{2,1,0:T(8,128)(2,1)} custom-call(s32[4,5]{1,0:T(4,128)S(1)} %pad_add_fusion.2.meta_ref, bf16[2,256,256]{2,1,0:T(8,128)(2,1)S(1)} %copy-done.1, bf16[512,512]{1,0:T(8,128)(2,1)S(1)} %copy-done.3, bf16[512,512]{1,0:T(8,128)(2,1)S(1)} %copy-done.5, bf16[32,16,1536]{2,1,0:T(8,128)(2,1)} %all-to-all-done.most_ref, ...), custom_call_target="tpu_custom_call" | custom-call | flops 11500000256 | bytes 1000000 | tf_op jit(solution)/shard_map/exit_rest/pallas_call | solution.py:465
  106.2 2.3 %all-to-all-done.2.grad_ref = bf16[32,16,512]{2,1,0:T(8,128)(2,1)S(1)} async-done(((bf16[32,16,512]{2,1,0:T(8,128)(2,1)}), bf16[32,16,512]{2,1,0:T(8,128)(2,1)S(1)}, u32[]{:S(2)}, u32[]{:S(2)}) %all-to-all-start.2) | async-done | bytes 524320 | tf_op jit(solution)/shard_map/all_to_all | solution.py:501
  108.6 5.6 %all-to-all-start.3 = ((bf16[32,16,1536]{2,1,0:T(8,128)(2,1)}), bf16[32,16,1536]{2,1,0:T(8,128)(2,1)}, u32[]{:S(2)}, u32[]{:S(2)}) async-start(bf16[32,16,1536]{2,1,0:T(8,128)(2,1)} %exit_rest.1), calls=%async_computation.3 | async-start | bytes 3145728 | tf_op jit(solution)/shard_map/all_to_all | solution.py:501
  114.2 1.9 %collective-permute-start.12 = (bf16[32,16,512]{2,1,0:T(8,128)(2,1)}, bf16[32,16,512]{2,1,0:T(8,128)(2,1)}, u32[]{:S(2)}, u32[]{:S(2)}) collective-permute-start(bf16[32,16,512]{2,1,0:T(8,128)(2,1)} %get-tuple-element.36), channel_id=1, source_target_pairs={{0,1},{1,2},{2,3},{3,0},{4,5},{5,6},{6,7},{7,4},{8,9},{9,10},{10,1... | collective-permute-start | bytes 1572872 | tf_op jit(solution)/shard_map/ppermute | solution.py:35
  116.1 1.1 fusion.10
  117.2 0.0 collective-permute-start.13
  117.3 0.5 collective-permute-start.14
  117.8 5.7 %back_first.1 = (f32[16,8192]{1,0:T(8,128)S(1)}, f32[16,8192]{1,0:T(8,128)S(1)}, f32[16,8192]{1,0:T(8,128)S(1)}, f32[16,8192]{1,0:T(8,128)S(1)}) custom-call(s32[32,128]{1,0:T(8,128)S(1)} %reshape.187.idx_ref, bf16[32,64,256]{2,1,0:T(8,128)(2,1)S(1)} %copy-done, bf16[32,16,512]{2,1,0:T(8,128)(2,1)S(1)} %all-to-all-done.2.grad_ref), custom_call_target="tpu_custom_call" | custom-call | flops 5750000128 | bytes 500000 | tf_op jit(solution)/shard_map/back_first/pallas_call | solution.py:243
  123.5 0.0 copy-start.7
  123.5 0.8 copy-done.7
  124.3 27.2 %all-to-all-done.3.grad_ref = bf16[32,16,1536]{2,1,0:T(8,128)(2,1)} async-done(((bf16[32,16,1536]{2,1,0:T(8,128)(2,1)}), bf16[32,16,1536]{2,1,0:T(8,128)(2,1)}, u32[]{:S(2)}, u32[]{:S(2)}) %all-to-all-start.3) | async-done | bytes 1572896 | tf_op jit(solution)/shard_map/all_to_all | solution.py:501
  151.5 1.0 copy-done.8
  152.6 9.8 %back_rest.1 = (bf16[16,8192]{1,0:T(8,128)(2,1)S(1)}, bf16[16,8192]{1,0:T(8,128)(2,1)S(1)}, bf16[16,8192]{1,0:T(8,128)(2,1)S(1)}, bf16[16,8192]{1,0:T(8,128)(2,1)S(1)}) custom-call(s32[32,128]{1,0:T(8,128)S(1)} %reshape.187.idx_ref, bf16[32,64,256]{2,1,0:T(8,128)(2,1)} %radon_ref.7, bf16[32,16,1536]{2,1,0:T(8,128)(2,1)} %all-to-all-done.3.grad_ref, ...), custom_call_target="tpu_custom_call" | custom-call | flops 10350000128 | bytes 900000 | tf_op jit(solution)/shard_map/back_rest/pallas_call | solution.py:243
  162.4 1.6 collective-permute-start.9
  164.0 0.6 collective-permute-start.10
  164.7 1.7 select_bitcast_fusion.3
  166.6 0.3 maximum_convert_fusion
  166.9 4.7 %copy.29 = f32[2,256,4,512]{3,2,1,0:T(4,128)} copy(f32[2,256,4,512]{3,1,0,2:T(8,128)S(1)} %maximum_convert_fusion) | data formatting | bytes 8388608
  171.6 4.6 %collective-permute-done.10 = bf16[16,8192]{1,0:T(8,128)(2,1)S(1)} collective-permute-done((bf16[16,8192]{1,0:T(8,128)(2,1)S(1)}, bf16[16,8192]{1,0:T(8,128)(2,1)S(1)}, u32[]{:S(2)}, u32[]{:S(2)}) %collective-permute-start.10) | collective-permute-done | bytes 262176 | tf_op jit(solution)/shard_map/ppermute | solution.py:35
  176.2 0.6 collective-permute-done.11
  176.9 0.1 select_bitcast_fusion.7
  177.0 1.6 multiply_add_fusion
  (41 shorter events, 0.3 us)
Async XLA Ops:
  0.6 4.6 %copy-start.13 = (s32[32,32,4]{1,2,0:T(4,128)S(1)}, s32[32,32,4]{1,2,0:T(4,128)}, u32[]{:S(2)}) copy-start(s32[32,32,4]{1,2,0:T(4,128)} %param.11) | copy-start | bytes 49156
  0.6 15.7 %copy-start = (bf16[32,64,256]{2,1,0:T(8,128)(2,1)S(1)}, bf16[32,64,256]{2,1,0:T(8,128)(2,1)}, u32[]{:S(2)}) copy-start(bf16[32,64,256]{2,1,0:T(8,128)(2,1)} %radon_ref.7) | copy-start | bytes 3145732
  2.1 8.2 %collective-permute-start.3 = (bf16[16,8192]{1,0:T(8,128)(2,1)S(1)}, bf16[16,8192]{1,0:T(8,128)(2,1)S(1)}, u32[]{:S(2)}, u32[]{:S(2)}) collective-permute-start(bf16[16,8192]{1,0:T(8,128)(2,1)S(1)} %get-tuple-element.67), channel_id=1, source_target_pairs={{0,1},{1,2},{2,3},{3,0},{4,5},{5,6},{6,7},{7,4},{8,9},{9,10},{10,1... | collective-permute-start | bytes 786440 | tf_op jit(solution)/shard_map/ppermute | solution.py:35
  4.7 11.1 %collective-permute-start.4 = (bf16[16,8192]{1,0:T(8,128)(2,1)S(1)}, bf16[16,8192]{1,0:T(8,128)(2,1)S(1)}, u32[]{:S(2)}, u32[]{:S(2)}) collective-permute-start(bf16[16,8192]{1,0:T(8,128)(2,1)S(1)} %get-tuple-element.69), channel_id=1, source_target_pairs={{0,2},{1,3},{2,0},{3,1},{4,6},{5,7},{6,4},{7,5},{8,10},{9,11},{10,... | collective-permute-start | bytes 786440 | tf_op jit(solution)/shard_map/ppermute | solution.py:35
  4.7 11.6 %collective-permute-start.5 = (bf16[16,8192]{1,0:T(8,128)(2,1)S(1)}, bf16[16,8192]{1,0:T(8,128)(2,1)S(1)}, u32[]{:S(2)}, u32[]{:S(2)}) collective-permute-start(bf16[16,8192]{1,0:T(8,128)(2,1)S(1)} %get-tuple-element.66), channel_id=1, source_target_pairs={{0,3},{1,0},{2,1},{3,2},{4,7},{5,4},{6,5},{7,6},{8,11},{9,8},{10,9... | collective-permute-start | bytes 786440 | tf_op jit(solution)/shard_map/ppermute | solution.py:35
  26.6 6.6 %copy-start.15 = (s32[4,1]{0,1:T(1,128)S(1)}, s32[4,1]{0,1:T(1,128)}, u32[]{:S(2)}) copy-start(s32[4,1]{0,1:T(1,128)} %param.15) | copy-start | bytes 52
  26.6 6.7 %copy-start.14 = (s32[4,4]{1,0:T(4,128)S(1)}, s32[4,4]{1,0:T(4,128)}, u32[]{:S(2)}) copy-start(s32[4,4]{1,0:T(4,128)} %param.14) | copy-start | bytes 196
  26.6 43.9 %all-to-all-start = ((bf16[32,16,1536]{2,1,0:T(8,128)(2,1)}), bf16[32,16,1536]{2,1,0:T(8,128)(2,1)}, u32[]{:S(2)}, u32[]{:S(2)}) async-start(bf16[32,16,1536]{2,1,0:T(8,128)(2,1)} %get-tuple-element.30), calls=%async_computation | async-start | bytes 3145728 | tf_op jit(solution)/shard_map/all_to_all | solution.py:501
  33.4 4.7 %collective-permute-start.2 = (s32[1,5]{1,0:T(1,128)S(1)}, s32[1,5]{1,0:T(1,128)S(1)}, u32[]{:S(2)}, u32[]{:S(2)}) collective-permute-start(s32[1,5]{1,0:T(1,128)S(1)} %get-tuple-element.77), channel_id=1, source_target_pairs={{0,1},{1,2},{2,3},{3,0},{4,5},{5,6},{6,7},{7,4},{8,9},{9,10},{10,1... | collective-permute-start | bytes 68 | tf_op jit(solution)/shard_map/ppermute | solution.py:35
  35.1 4.6 %collective-permute-start.1 = (s32[1,5]{1,0:T(1,128)S(1)}, s32[1,5]{1,0:T(1,128)S(1)}, u32[]{:S(2)}, u32[]{:S(2)}) collective-permute-start(s32[1,5]{1,0:T(1,128)S(1)} %get-tuple-element.78), channel_id=1, source_target_pairs={{0,2},{1,3},{2,0},{3,1},{4,6},{5,7},{6,4},{7,5},{8,10},{9,11},{10,... | collective-permute-start | bytes 68 | tf_op jit(solution)/shard_map/ppermute | solution.py:35
  35.1 5.3 %collective-permute-start = (s32[1,5]{1,0:T(1,128)S(1)}, s32[1,5]{1,0:T(1,128)S(1)}, u32[]{:S(2)}, u32[]{:S(2)}) collective-permute-start(s32[1,5]{1,0:T(1,128)S(1)} %get-tuple-element.79), channel_id=1, source_target_pairs={{0,3},{1,0},{2,1},{3,2},{4,7},{5,4},{6,5},{7,6},{8,11},{9,8},{10,9... | collective-permute-start | bytes 68 | tf_op jit(solution)/shard_map/ppermute | solution.py:35
  40.4 6.2 %copy-start.6 = (bf16[512,16,128]{2,1,0:T(8,128)(2,1)S(1)}, bf16[512,16,128]{2,1,0:T(8,128)(2,1)}, u32[]{:S(2)}) copy-start(bf16[512,16,128]{2,1,0:T(8,128)(2,1)} %get-tuple-element.31.vv_ref) | copy-start | bytes 6291460
  43.2 31.5 %collective-permute-start.6 = (bf16[4,256,256]{2,1,0:T(8,128)(2,1)}, bf16[4,256,256]{2,1,0:T(8,128)(2,1)}, u32[]{:S(2)}, u32[]{:S(2)}) collective-permute-start(bf16[4,256,256]{2,1,0:T(8,128)(2,1)} %get-tuple-element.58), channel_id=1, source_target_pairs={{0,3},{1,0},{2,1},{3,2},{4,7},{5,4},{6,5},{7,6},{8,11},{9,8},{10,9... | collective-permute-start | bytes 1572872 | tf_op jit(solution)/shard_map/ppermute | solution.py:35
  43.3 50.1 %collective-permute-start.7 = (bf16[4,256,256]{2,1,0:T(8,128)(2,1)}, bf16[4,256,256]{2,1,0:T(8,128)(2,1)S(1)}, u32[]{:S(2)}, u32[]{:S(2)}) collective-permute-start(bf16[4,256,256]{2,1,0:T(8,128)(2,1)} %get-tuple-element.57), channel_id=1, source_target_pairs={{0,2},{1,3},{2,0},{3,1},{4,6},{5,7},{6,4},{7,5},{8,10},{9,11},{10,... | collective-permute-start | bytes 1572872 | tf_op jit(solution)/shard_map/ppermute | solution.py:35
  44.8 48.6 %collective-permute-start.8 = (bf16[4,256,256]{2,1,0:T(8,128)(2,1)}, bf16[4,256,256]{2,1,0:T(8,128)(2,1)S(1)}, u32[]{:S(2)}, u32[]{:S(2)}) collective-permute-start(bf16[4,256,256]{2,1,0:T(8,128)(2,1)} %get-tuple-element.56), channel_id=1, source_target_pairs={{0,1},{1,2},{2,3},{3,0},{4,5},{5,6},{6,7},{7,4},{8,9},{9,10},{10,1... | collective-permute-start | bytes 1572872 | tf_op jit(solution)/shard_map/ppermute | solution.py:35
  46.6 28.2 %copy-start.1 = (bf16[2,256,256]{2,1,0:T(8,128)(2,1)S(1)}, bf16[2,256,256]{2,1,0:T(8,128)(2,1)}, u32[]{:S(2)}) copy-start(bf16[2,256,256]{2,1,0:T(8,128)(2,1)} %probe_ref.3) | copy-start | bytes 786436
  70.5 19.5 %all-to-all-start.1 = ((bf16[32,16,512]{2,1,0:T(8,128)(2,1)}), bf16[32,16,512]{2,1,0:T(8,128)(2,1)S(1)}, u32[]{:S(2)}, u32[]{:S(2)}) async-start(bf16[32,16,512]{2,1,0:T(8,128)(2,1)} %project_rest.1), calls=%async_computation.1 | async-start | bytes 1048576 | tf_op jit(solution)/shard_map/all_to_all | solution.py:501
  74.8 1.0 copy-start.2
  75.8 1.0 copy-start.4
  86.2 0.8 copy-start.9
  90.0 18.6 %all-to-all-start.2 = ((bf16[32,16,512]{2,1,0:T(8,128)(2,1)}), bf16[32,16,512]{2,1,0:T(8,128)(2,1)S(1)}, u32[]{:S(2)}, u32[]{:S(2)}) async-start(bf16[32,16,512]{2,1,0:T(8,128)(2,1)} %get-tuple-element.36), calls=%async_computation.2 | async-start | bytes 1048576 | tf_op jit(solution)/shard_map/all_to_all | solution.py:501
  93.4 1.0 copy-start.3
  94.5 1.0 copy-start.5
  95.5 1.0 copy-start.10
  106.2 9.8 %copy-start.11 = (bf16[32,16,1536]{2,1,0:T(8,128)(2,1)S(1)}, bf16[32,16,1536]{2,1,0:T(8,128)(2,1)}, u32[]{:S(2)}) copy-start(bf16[32,16,1536]{2,1,0:T(8,128)(2,1)} %exit_rest.1) | copy-start | bytes 4718596
  108.6 42.9 %all-to-all-start.3 = ((bf16[32,16,1536]{2,1,0:T(8,128)(2,1)}), bf16[32,16,1536]{2,1,0:T(8,128)(2,1)}, u32[]{:S(2)}, u32[]{:S(2)}) async-start(bf16[32,16,1536]{2,1,0:T(8,128)(2,1)} %exit_rest.1), calls=%async_computation.3 | async-start | bytes 3145728 | tf_op jit(solution)/shard_map/all_to_all | solution.py:501
  114.2 50.5 %collective-permute-start.12 = (bf16[32,16,512]{2,1,0:T(8,128)(2,1)}, bf16[32,16,512]{2,1,0:T(8,128)(2,1)}, u32[]{:S(2)}, u32[]{:S(2)}) collective-permute-start(bf16[32,16,512]{2,1,0:T(8,128)(2,1)} %get-tuple-element.36), channel_id=1, source_target_pairs={{0,1},{1,2},{2,3},{3,0},{4,5},{5,6},{6,7},{7,4},{8,9},{9,10},{10,1... | collective-permute-start | bytes 1572872 | tf_op jit(solution)/shard_map/ppermute | solution.py:35
  117.2 47.5 %collective-permute-start.13 = (bf16[32,16,512]{2,1,0:T(8,128)(2,1)}, bf16[32,16,512]{2,1,0:T(8,128)(2,1)}, u32[]{:S(2)}, u32[]{:S(2)}) collective-permute-start(bf16[32,16,512]{2,1,0:T(8,128)(2,1)} %get-tuple-element.61), channel_id=1, source_target_pairs={{0,2},{1,3},{2,0},{3,1},{4,6},{5,7},{6,4},{7,5},{8,10},{9,11},{10,... | collective-permute-start | bytes 1572872 | tf_op jit(solution)/shard_map/ppermute | solution.py:35
  117.3 47.4 %collective-permute-start.14 = (bf16[32,16,512]{2,1,0:T(8,128)(2,1)}, bf16[32,16,512]{2,1,0:T(8,128)(2,1)}, u32[]{:S(2)}, u32[]{:S(2)}) collective-permute-start(bf16[32,16,512]{2,1,0:T(8,128)(2,1)} %get-tuple-element.60), channel_id=1, source_target_pairs={{0,3},{1,0},{2,1},{3,2},{4,7},{5,4},{6,5},{7,6},{8,11},{9,8},{10,9... | collective-permute-start | bytes 1572872 | tf_op jit(solution)/shard_map/ppermute | solution.py:35
  123.5 0.8 copy-start.7
  151.5 1.0 copy-start.8
  162.4 9.2 %collective-permute-start.9 = (bf16[16,8192]{1,0:T(8,128)(2,1)S(1)}, bf16[16,8192]{1,0:T(8,128)(2,1)S(1)}, u32[]{:S(2)}, u32[]{:S(2)}) collective-permute-start(bf16[16,8192]{1,0:T(8,128)(2,1)S(1)} %get-tuple-element.46), channel_id=1, source_target_pairs={{0,1},{1,2},{2,3},{3,0},{4,5},{5,6},{6,7},{7,4},{8,9},{9,10},{10,1... | collective-permute-start | bytes 786440 | tf_op jit(solution)/shard_map/ppermute | solution.py:35
  164.0 12.2 %collective-permute-start.10 = (bf16[16,8192]{1,0:T(8,128)(2,1)S(1)}, bf16[16,8192]{1,0:T(8,128)(2,1)S(1)}, u32[]{:S(2)}, u32[]{:S(2)}) collective-permute-start(bf16[16,8192]{1,0:T(8,128)(2,1)S(1)} %get-tuple-element.47), channel_id=1, source_target_pairs={{0,2},{1,3},{2,0},{3,1},{4,6},{5,7},{6,4},{7,5},{8,10},{9,11},{10,... | collective-permute-start | bytes 786440 | tf_op jit(solution)/shard_map/ppermute | solution.py:35
  164.7 12.2 %collective-permute-start.11 = (bf16[16,8192]{1,0:T(8,128)(2,1)S(1)}, bf16[16,8192]{1,0:T(8,128)(2,1)S(1)}, u32[]{:S(2)}, u32[]{:S(2)}) collective-permute-start(bf16[16,8192]{1,0:T(8,128)(2,1)S(1)} %get-tuple-element.48), channel_id=1, source_target_pairs={{0,3},{1,0},{2,1},{3,2},{4,7},{5,4},{6,5},{7,6},{8,11},{9,8},{10,9... | collective-permute-start | bytes 786440 | tf_op jit(solution)/shard_map/ppermute | solution.py:35
  171.6 5.3 %copy-start.12 = (bf16[2,32,8192]{2,1,0:T(8,128)(2,1)S(1)}, bf16[2,32,8192]{2,1,0:T(8,128)(2,1)}, u32[]{:S(2)}) copy-start(bf16[2,32,8192]{2,1,0:T(8,128)(2,1)} %param.9) | copy-start | bytes 3145732

commit v5 on v4

--- a/solution.py
+++ b/solution.py
@@ -17,6 +17,7 @@
 everywhere = pl.BlockSpec(memory_space=pltpu.VMEM)
 scalars = pl.BlockSpec(memory_space=pltpu.SMEM)
 CHAINS = 4
+BATCH = 4
 
 
 def dft_tables(width):
@@ -55,18 +56,29 @@
     return pltpu.roll(tile, LANES // 2, 1)
 
 
-def arrange_kernel(pieces, *refs):
-    vol_refs, vv_ref = refs[:pieces], refs[pieces]
+def arrange(vol_refs, vv_ref):
     per_piece = vol_refs[0].shape[1] // LANES
-    tiles = per_piece * pieces
-    for k in range(pieces):
-
-        @pl.loop(0, per_piece, unroll=16)
-        def _(t):
-            tile = vol_refs[k][:, pl.ds(pl.multiple_of(t * LANES, LANES), LANES)]
-            vv_ref[k * per_piece + t] = tile
-            swapped = swap_halves(tile.astype(jnp.float32)).astype(jnp.bfloat16)
-            vv_ref[tiles + k * per_piece + t] = swapped
+    tiles = per_piece * len(vol_refs)
+    batch = 16
+    source = lax.broadcasted_iota(jnp.int32, (LANES, LANES), 0)
+    target = lax.broadcasted_iota(jnp.int32, (LANES, LANES), 1)
+    swap = ((source + LANES // 2) % LANES == target).astype(jnp.bfloat16)
+    for k, vol_ref in enumerate(vol_refs):
+
+        @pl.loop(0, per_piece // batch, unroll=2)
+        def _(step):
+            stack = []
+            for i in range(batch):
+                t = step * batch + i
+                tile = vol_ref[:, pl.ds(pl.multiple_of(t * LANES, LANES), LANES)]
+                vv_ref[k * per_piece + t] = tile
+                stack.append(tile)
+            swapped = jnp.dot(
+                jnp.concatenate(stack, axis=0), swap, preferred_element_type=jnp.float32
+            ).astype(jnp.bfloat16)
+            for i in range(batch):
+                t = step * batch + i
+                vv_ref[tiles + k * per_piece + t] = swapped[i * ROWS : (i + 1) * ROWS]
 
 
 def project_chunk(chunks, idx_ref, radon_ref, vv_ref, out_ref, lhs_refs):
@@ -114,14 +126,10 @@
         gather(jnp.minimum(start + 2 * batch, angles - batch), lhs_refs[0])
 
 
-def project_first_kernel(chunks, pieces, idx_ref, radon_ref, *refs):
+def project_kernel(chunks, pieces, idx_ref, radon_ref, *refs):
     vol_refs = refs[:pieces]
     out_ref, vv_ref, *lhs_refs = refs[pieces:]
-    arrange_kernel(pieces, *vol_refs, vv_ref)
-    project_chunk(chunks, idx_ref, radon_ref, vv_ref, out_ref, lhs_refs)
-
-
-def project_rest_kernel(chunks, idx_ref, radon_ref, vv_ref, out_ref, *lhs_refs):
+    arrange(vol_refs, vv_ref)
     project_chunk(chunks, idx_ref, radon_ref, vv_ref, out_ref, lhs_refs)
 
 
@@ -131,91 +139,87 @@
     )
 
 
-def project_first(idx, radon_tiles, vol_pieces, tile_width, chunks):
+def project(idx, radon_tiles, vol_pieces, tile_width, chunks, name):
     angles, block, span = radon_tiles.shape
     pieces = len(vol_pieces)
     tiles = pieces * vol_pieces[0].shape[1] // LANES
     rows = len(chunks) * tile_width // block * ROWS
     return pl.pallas_call(
-        functools.partial(project_first_kernel, chunks, pieces),
-        out_shape=[
-            jax.ShapeDtypeStruct((angles, ROWS, len(chunks) * tile_width), jnp.bfloat16),
-            jax.ShapeDtypeStruct((2 * tiles, ROWS, LANES), jnp.bfloat16),
-        ],
+        functools.partial(project_kernel, chunks, pieces),
+        out_shape=jax.ShapeDtypeStruct((angles, ROWS, len(chunks) * tile_width), jnp.bfloat16),
         in_specs=[scalars, everywhere] + [everywhere] * pieces,
-        out_specs=[everywhere] * 2,
-        scratch_shapes=[pltpu.VMEM((2, rows, span), jnp.bfloat16)] * 2,
+        out_specs=everywhere,
+        scratch_shapes=[pltpu.VMEM((2 * tiles, ROWS, LANES), jnp.bfloat16)]
+        + [pltpu.VMEM((BATCH, rows, span), jnp.bfloat16)] * 2,
         compiler_params=pltpu.CompilerParams(vmem_limit_bytes=VMEM_LIMIT),
-        cost_estimate=guess(8),
-        name="project_first",
+        cost_estimate=guess(4 + 2 * len(chunks)),
+        name=name,
     )(idx, radon_tiles, *vol_pieces)
-
-
-def project_rest(idx, radon_tiles, vv, tile_width, chunks):
-    angles, block, span = radon_tiles.shape
-    rows = len(chunks) * tile_width // block * ROWS
-    return pl.pallas_call(
-        functools.partial(project_rest_kernel, chunks),
-        out_shape=jax.ShapeDtypeStruct((angles, ROWS, len(chunks) * tile_width), jnp.bfloat16),
-        in_specs=[scalars, everywhere, everywhere],
-        out_specs=everywhere,
-        scratch_shapes=[pltpu.VMEM((2, rows, span), jnp.bfloat16)] * 2,
-        compiler_params=pltpu.CompilerParams(vmem_limit_bytes=VMEM_LIMIT),
-        cost_estimate=guess(5),
-        name="project_rest",
-    )(idx, radon_tiles, vv)
 
 
 def back_project_kernel(chunks, pieces, has_start, idx_ref, radon_ref, grad_ref, *refs):
     start_refs, refs = (refs[:pieces], refs[pieces:]) if has_start else (None, refs)
     out_refs, refs = refs[:pieces], refs[pieces:]
-    acc_refs, contrib_refs = refs[:CHAINS], refs[CHAINS:]
+    acc_refs, (w_ref, *contrib_refs) = refs[:CHAINS], refs[CHAINS:]
     angles, block, span = radon_ref.shape
     per_piece = out_refs[0].shape[1] // LANES
-    tiles = per_piece * pieces
     blocks = grad_ref.shape[2] // block // len(chunks)
     pairs = len(chunks) * blocks // 2
     feeds = span // block
 
-    @pl.loop(0, 2 * tiles, unroll=16)
+    @pl.loop(0, acc_refs[0].shape[0], unroll=16)
     def _(t):
         for acc_ref in acc_refs:
-            acc_ref[t] = jnp.zeros((ROWS, LANES), jnp.float32)
-
-    low = lower_half((ROWS, LANES))
-
-    def multiply(start, contrib_ref):
+            acc_ref[t] = jnp.zeros((GROUP, LANES), jnp.float32)
+
+    low = lower_half((GROUP, LANES))
+    low_rows = lower_half((block, LANES))
+    w_ref[...] = jnp.zeros_like(w_ref)
+
+    def widen(slot, a):
+        for jp in range(feeds // 2):
+            tile = radon_ref[a, :, jp * LANES : (jp + 1) * LANES].astype(jnp.float32)
+            turned = swap_halves(tile)
+            for side, (first, second) in enumerate(((tile, turned), (turned, tile))):
+                lanes = slice((2 * jp + side) * LANES, (2 * jp + side + 1) * LANES)
+                w_ref[slot, :block, lanes] = jnp.where(low_rows, first, 0.0).astype(jnp.bfloat16)
+                w_ref[slot, block:, lanes] = jnp.where(low_rows, 0.0, second).astype(jnp.bfloat16)
+
+    def multiply(start, half, contrib_ref):
         for n in range(CHAINS):
             a = start + n
+            widen(half * CHAINS + n, a)
             lhs = []
             for pair in range(pairs):
-                tile = grad_ref[a, :, pair * LANES : (pair + 1) * LANES]
-                lhs += [tile[:, :block], tile[:, block:]]
+                tile = grad_ref[a, :, pair * LANES : (pair + 1) * LANES].astype(jnp.float32)
+                real, imag = tile[:GROUP], tile[GROUP:]
+                even = jnp.where(low, real, swap_halves(imag))
+                odd = jnp.where(low, swap_halves(real), imag)
+                lhs.append(jnp.concatenate([even, odd], axis=0).astype(jnp.bfloat16))
             contrib_ref[n] = jnp.dot(
-                jnp.concatenate(lhs, axis=0), radon_ref[a], preferred_element_type=jnp.float32
+                jnp.concatenate(lhs, axis=0),
+                w_ref[half * CHAINS + n],
+                preferred_element_type=jnp.float32,
             )
 
     def scatter(start, contrib_ref):
         for i, chunk in enumerate(chunks):
             for b in range(blocks):
-                row = (i * blocks + b) * ROWS
-                for jp in range(feeds // 2):
-                    at = (chunk * blocks + b) * feeds + 2 * jp
+                row = (i * blocks + b) * GROUP
+                for j in range(feeds):
+                    at = (chunk * blocks + b) * feeds + j
                     for n in range(CHAINS):
-                        a = start + n
-                        tile = contrib_ref[n, row : row + ROWS, jp * LANES : (jp + 1) * LANES]
-                        first, second = idx_ref[a, at], idx_ref[a, at + 1]
-                        acc_refs[n][first] += jnp.where(low, tile, 0.0)
-                        acc_refs[n][second] += jnp.where(low, 0.0, tile)
-
-    multiply(0, contrib_refs[0])
+                        tile = contrib_ref[n, row : row + GROUP, j * LANES : (j + 1) * LANES]
+                        acc_refs[n][idx_ref[start + n, at]] += tile
+
+    multiply(0, 0, contrib_refs[0])
 
     @pl.loop(0, angles // (2 * CHAINS))
     def _(step):
         start = step * 2 * CHAINS
-        multiply(start + CHAINS, contrib_refs[1])
+        multiply(start + CHAINS, 1, contrib_refs[1])
         scatter(start, contrib_refs[0])
-        multiply(jnp.minimum(start + 2 * CHAINS, angles - CHAINS), contrib_refs[0])
+        multiply(jnp.minimum(start + 2 * CHAINS, angles - CHAINS), 0, contrib_refs[0])
         scatter(start + CHAINS, contrib_refs[1])
 
     for k in range(pieces):
@@ -223,12 +227,14 @@
         @pl.loop(0, per_piece, unroll=16)
         def _(t):
             lanes = pl.ds(pl.multiple_of(t * LANES, LANES), LANES)
-            straight = acc_refs[0][k * per_piece + t]
-            crossed = acc_refs[0][tiles + k * per_piece + t]
+            at = 2 * (k * per_piece + t)
+            even, odd = acc_refs[0][at], acc_refs[0][at + 1]
             for acc_ref in acc_refs[1:]:
-                straight += acc_ref[k * per_piece + t]
-                crossed += acc_ref[tiles + k * per_piece + t]
-            total = straight + swap_halves(crossed)
+                even += acc_ref[at]
+                odd += acc_ref[at + 1]
+            real = jnp.where(low, even, swap_halves(odd))
+            imag = jnp.where(low, swap_halves(even), odd)
+            total = jnp.concatenate([real, imag], axis=0)
             if has_start:
                 total += start_refs[k][:, lanes]
             out_refs[k][:, lanes] = total.astype(out_refs[k].dtype)
@@ -236,8 +242,8 @@
 
 def back_project(idx, radon_tiles, grads, chunks, start, pieces, piece_width, out_type, name):
     angles, block, span = radon_tiles.shape
-    tiles = pieces * piece_width // LANES
-    rows = grads.shape[2] // block * ROWS
+    coef_blocks = pieces * piece_width // block
+    rows = grads.shape[2] // block * GROUP
     has_start = start is not None
     operands = [idx, radon_tiles, grads] + (list(start) if has_start else [])
     return pl.pallas_call(
@@ -245,8 +251,9 @@
         out_shape=[jax.ShapeDtypeStruct((ROWS, piece_width), out_type)] * pieces,
         in_specs=[scalars] + [everywhere] * (len(operands) - 1),
         out_specs=[everywhere] * pieces,
-        scratch_shapes=[pltpu.VMEM((2 * tiles, ROWS, LANES), jnp.float32)] * CHAINS
-        + [pltpu.VMEM((CHAINS, rows, span), jnp.float32)] * 2,
+        scratch_shapes=[pltpu.VMEM((coef_blocks, GROUP, LANES), jnp.float32)] * CHAINS
+        + [pltpu.VMEM((2 * CHAINS, 2 * block, 2 * span), jnp.bfloat16)]
+        + [pltpu.VMEM((CHAINS, rows, 2 * span), jnp.float32)] * 2,
         compiler_params=pltpu.CompilerParams(vmem_limit_bytes=VMEM_LIMIT),
         cost_estimate=guess(3 + 2 * len(chunks)),
         name=name,
@@ -493,8 +500,21 @@
     return split.transpose(0, 2, 1, 3, 4).reshape(groups * merge, 2 * own_slices, columns)
 
 
-def pad_rows(block):
-    return jnp.pad(block, [(0, 0)] * (block.ndim - 2) + [(0, ROWS - block.shape[-2]), (0, 0)])
+def pad_rows(block, own_slices):
+    if own_slices == GROUP:
+        return block
+    lead, columns = block.shape[:-2], block.shape[-1]
+    split = block.reshape(lead + (2, own_slices, columns))
+    more = [(0, 0)] * (split.ndim - 2) + [(0, GROUP - own_slices), (0, 0)]
+    return jnp.pad(split, more).reshape(lead + (ROWS, columns))
+
+
+def cut_rows(block, own_slices):
+    if own_slices == GROUP:
+        return block
+    lead, columns = block.shape[:-2], block.shape[-1]
+    split = block.reshape(lead + (2, GROUP, columns))[..., :own_slices, :]
+    return split.reshape(lead + (2 * own_slices, columns))
 
 
 def everyone(chunk):
@@ -536,20 +556,25 @@
 
     owner = tile_blocks // blocks_each
     within = tile_blocks % blocks_each
+    piece = (pos - owner) % n_pos
     crossed = (within + jnp.arange(feeds, dtype=jnp.int32)) % 2
     tiles_each = width // LANES
-    idx = crossed * (n_pos * tiles_each) + (pos - owner) % n_pos * tiles_each + within // 2
-    idx = idx.reshape(angles // n_pos, n_pos, n_pos, det_blocks // n_pos * feeds)
-    idx = jnp.stack([jnp.roll(idx[:, p], -p, axis=1) for p in range(n_pos)], axis=1)
-    idx = idx.reshape(angles, det_blocks * feeds)
-
-    padded = [pad_rows(piece) for piece in vol_pieces]
+
+    def by_chunk(idx):
+        idx = idx.reshape(angles // n_pos, n_pos, n_pos, det_blocks // n_pos * feeds)
+        idx = jnp.stack([jnp.roll(idx[:, p], -p, axis=1) for p in range(n_pos)], axis=1)
+        return idx.reshape(angles, det_blocks * feeds)
+
+    tile_idx = by_chunk(crossed * (n_pos * tiles_each) + piece * tiles_each + within // 2)
+    block_idx = by_chunk(piece * blocks_each + within)
+    padded = [pad_rows(piece, own) for piece in vol_pieces]
     most = list(range(last))
-    sino_most, vv = project_first(idx, radon_tiles, padded, tile_width, most)
-    sino_last = project_rest(idx, radon_tiles, vv, tile_width, [last])
-    got_most = everyone(sino_most[:, :rows])
+    sino_most = project(tile_idx, radon_tiles, padded, tile_width, most, "project_most")
+    sino_most, padded = lax.optimization_barrier((sino_most, padded))
+    sino_last = project(tile_idx, radon_tiles, padded, tile_width, [last], "project_last")
+    got_most = everyone(cut_rows(sino_most, own))
     got_most, sino_last = lax.optimization_barrier((got_most, sino_last))
-    got_last = everyone(sino_last[:, :rows])
+    got_last = everyone(cut_rows(sino_last, own))
     got_most, got_last = to_groups(got_most, own), to_groups(got_last, own)
     tables = dft_tables(probe_field.shape[1])
     partial, first_grad, spill = exit_first(
@@ -564,14 +589,14 @@
     back_first, joined_sent = lax.optimization_barrier((back_first, joined))
     back_rest = everyone(from_groups(joined_sent, own))
     partial_grad = back_project(
-        idx, radon_tiles, pad_rows(back_first), [1], None, n_pos, width, jnp.float32, "back_first"
+        block_idx, radon_tiles, pad_rows(back_first, own), [1], None, n_pos, width, jnp.float32, "back_first"
     )
     order = list(range(2, n_pos)) + [0]
     joined_tiles = {j: joined[:, :, i * tile_width : (i + 1) * tile_width] for i, j in enumerate(order)}
     joined_tiles[1] = own_grad
     tile_pieces = rotate_pos([joined_tiles[j] for j in range(n_pos)], 1)
     obj_pieces = back_project(
-        idx, radon_tiles, pad_rows(back_rest), order, partial_grad, n_pos, width, jnp.bfloat16, "back_rest"
+        block_idx, radon_tiles, pad_rows(back_rest, own), order, partial_grad, n_pos, width, jnp.bfloat16, "back_rest"
     )
     groups = joined.shape[0]
     tile_pieces = [tile_pieces[-j % n_pos] for j in range(n_pos)]
@@ -580,7 +605,7 @@
         for piece in tile_pieces
     ]
     proj_grad = jnp.stack(in_order(tile_pieces, -pos % n_pos), axis=2).astype(jnp.float32)
-    obj_pieces = rotate_pos([piece[:rows] for piece in obj_pieces], -1)
+    obj_pieces = rotate_pos([cut_rows(piece, own) for piece in obj_pieces], -1)
     obj_pieces = [piece.reshape(2, own, width) for piece in in_order(obj_pieces, -pos % n_pos)]
     object_grad = jnp.concatenate(obj_pieces, axis=1).astype(jnp.float32)
     new_volume = volume.astype(jnp.float32) + step_size * object_grad

time: 179 us -> 181 us (1.011)
  local copies, waits for them, and re-layouts: 18.7 us -> 23 us
  waiting for transfers between devices: 71.8 us -> 68.5 us
    all_to_all x4, waiting for transfers between devices: 51.8 us -> 48.2 us  [everyone(): return lax.all_to_all(chunk, ('ang', 'pos'), 0, 0, tiled=True)]
    pallas_call x1, Pallas kernels: 9.33 us -> 11.4 us  [exit_first(): pl.pallas_call(functools.partial(exit_first_kernel, tiles), out_shape=[ja...]
    unnamed x35 -> x48, local copies, waits for them, and re-layouts: 12.7 us -> 14.6 us
    pallas_call x1, Pallas kernels: 9.7 us -> 7.83 us  [exit_rest(): pl.pallas_call(functools.partial(exit_rest_kernel, tiles), out_shape=jax....]
  transfers between devices with their start and end apart: 19 -> 19, of which waited for: 12 -> 12; matrix products, arithmetic and copies ran while one was open for 7% -> 8% of each run, Pallas kernels for 22% -> 22%
where the time goes in v5:
time: 181 us; the launch traced here: 180 us
  waiting for transfers between devices  68.5 us (38%)
  Pallas kernels  48.8 us (27%)
  starting transfers between devices  33.7 us (19%)
  local copies, waits for them, and re-layouts  23 us (13%)
  other arithmetic  4.24 us (2%)
    all_to_all x4, waiting for transfers between devices, everyone(): return lax.all_to_all(chunk, ('ang', 'pos'), 0, 0, tiled=True)  48.2 us
    all_to_all x4, starting transfers between devices, everyone(): return lax.all_to_all(chunk, ('ang', 'pos'), 0, 0, tiled=True)  20.6 us
    ppermute x15, waiting for transfers between devices, rotate_pos(): lax.ppermute(pieces[j], 'pos', [(i, (i + sign * j) % count) for i in rang...  20.3 us
    pallas_call x2, Pallas kernels, back_project(): pl.pallas_call(functools.partial(back_project_kernel, chunks, pieces, has...  15.4 us
    unnamed x48, local copies, waits for them, and re-layouts  14.6 us
    pallas_call x2, Pallas kernels, project(): pl.pallas_call(functools.partial(project_kernel, chunks, pieces), out_sha...  14.2 us
    ppermute x15, starting transfers between devices, rotate_pos(): lax.ppermute(pieces[j], 'pos', [(i, (i + sign * j) % count) for i in rang...  13.1 us
    pallas_call x1, Pallas kernels, exit_first(): pl.pallas_call(functools.partial(exit_first_kernel, tiles), out_shape=[ja...  11.4 us
  transfers between devices with their start and end apart: 19, of which 12 were waited for; matrix products, arithmetic and copies ran while one was open for 8% of the time, Pallas kernels for 22%

profile of v5, /device:TPU:1, one launch (start us, length us, event | category | flops | bytes accessed | tf_op | source)
XLA Modules:
  0.0 179.5 jit_solution(12378570195926865918)
XLA Ops:
  0.7 2.0 %dynamic-slice_bitcast_fusion.4 = (bf16[16,8192]{1,0:T(8,128)(2,1)S(1)}, bf16[16,8192]{1,0:T(8,128)(2,1)}, bf16[16,8192]{1,0:T(8,128)(2,1)S(1)}, bf16[16,8192]{1,0:T(8,128)(2,1)S(1)}) fusion(bf16[2,32,8192]{2,1,0:T(8,128)(2,1)} %param.9, s32[]{:T(128)S(6)} %select_n.316, s32[]{:T(128)S(6)} %select_n.312, s32[]{:T(128)S(6)} %select_n.310, s32[]{:T(128)S(6)} %select_n.314), kind=kLoop, calls=%fused_computation.22 | loop fusion | bytes 2097168 | tf_op jit(solution)/shard_map/reshape | solution.py:540
  2.8 2.6 %collective-permute-start.3 = (bf16[16,8192]{1,0:T(8,128)(2,1)}, bf16[16,8192]{1,0:T(8,128)(2,1)S(1)}, u32[]{:S(2)}, u32[]{:S(2)}) collective-permute-start(bf16[16,8192]{1,0:T(8,128)(2,1)} %get-tuple-element.73), channel_id=1, source_target_pairs={{0,1},{1,2},{2,3},{3,0},{4,5},{5,6},{6,7},{7,4},{8,9},{9,10},{10,1... | collective-permute-start | bytes 786440 | tf_op jit(solution)/shard_map/ppermute | solution.py:36
  5.4 0.4 collective-permute-start.5
  5.8 0.3 fusion.5
  6.1 0.3 copy.28
  6.4 0.2 reshape.194
  6.8 0.1 reshape.195.idx_ref
  6.9 4.6 %collective-permute-done.3.refs_1_ = bf16[16,8192]{1,0:T(8,128)(2,1)S(1)} collective-permute-done((bf16[16,8192]{1,0:T(8,128)(2,1)}, bf16[16,8192]{1,0:T(8,128)(2,1)S(1)}, u32[]{:S(2)}, u32[]{:S(2)}) %collective-permute-start.3) | collective-permute-done | bytes 262176 | tf_op jit(solution)/shard_map/ppermute | solution.py:36
  11.5 5.5 %collective-permute-done.4.refs_2_ = bf16[16,8192]{1,0:T(8,128)(2,1)S(1)} collective-permute-done((bf16[16,8192]{1,0:T(8,128)(2,1)S(1)}, bf16[16,8192]{1,0:T(8,128)(2,1)S(1)}, u32[]{:S(2)}, u32[]{:S(2)}) %collective-permute-start.4) | collective-permute-done | bytes 262176 | tf_op jit(solution)/shard_map/ppermute | solution.py:36
  17.0 0.2 collective-permute-done.5.refs_3_
  17.2 8.8 %project_most.1 = bf16[32,16,1536]{2,1,0:T(8,128)(2,1)} custom-call(s32[32,128]{1,0:T(8,128)S(1)} %reshape.195.idx_ref, bf16[32,64,256]{2,1,0:T(8,128)(2,1)S(1)} %copy-done, bf16[16,8192]{1,0:T(8,128)(2,1)S(1)} %get-tuple-element.34.refs_0_, bf16[16,8192]{1,0:T(8,128)(2,1)S(1)} %collective-permute-done.3.refs_1_, ...), custom_call_target="tpu_custom_call" | custom-call | flops 11500000256 | bytes 1000000 | tf_op jit(solution)/shard_map/project_most/pallas_call | solution.py:147
  26.0 6.6 %all-to-all-start = ((bf16[32,16,1536]{2,1,0:T(8,128)(2,1)}), bf16[32,16,1536]{2,1,0:T(8,128)(2,1)}, u32[]{:S(2)}, u32[]{:S(2)}) async-start(bf16[32,16,1536]{2,1,0:T(8,128)(2,1)} %project_most.1), calls=%async_computation | async-start | bytes 3145728 | tf_op jit(solution)/shard_map/all_to_all | solution.py:521
  32.6 0.1 copy.27
  32.7 0.1 pad_add_fusion.2
  32.8 1.7 collective-permute-start.2
  34.5 0.0 collective-permute-start.1
  34.6 0.5 collective-permute-start
  35.1 2.4 %collective-permute-done.2 = s32[1,5]{1,0:T(1,128)S(1)} collective-permute-done((s32[1,5]{1,0:T(1,128)S(1)}, s32[1,5]{1,0:T(1,128)S(1)}, u32[]{:S(2)}, u32[]{:S(2)}) %collective-permute-start.2) | collective-permute-done | bytes 52 | tf_op jit(solution)/shard_map/ppermute | solution.py:36
  37.5 1.6 collective-permute-done.1
  39.1 0.7 collective-permute-done
  39.9 2.8 %dynamic-slice_bitcast_fusion = (bf16[4,256,256]{2,1,0:T(8,128)(2,1)}, bf16[4,256,256]{2,1,0:T(8,128)(2,1)}, bf16[4,256,256]{2,1,0:T(8,128)(2,1)}, bf16[4,256,256]{2,1,0:T(8,128)(2,1)S(1)}) fusion(bf16[4,4,256,256]{3,2,1,0:T(8,128)(2,1)} %param.13, s32[]{:T(128)S(6)} %select_n.307, s32[]{:T(128)S(6)} %select_n.305, s32[]{:T(128)S(6)} %select_n.303, ...), kind=kLoop, calls=%fused_computation.10 | loop fusion | bytes 4194320 | tf_op jit(solution)/shard_map/jit(dynamic_index_in_dim)/squeeze | solution.py:551
  42.6 0.0 collective-permute-start.6
  42.7 1.5 collective-permute-start.7
  44.2 1.8 collective-permute-start.8
  46.0 5.5 %project_last.1 = bf16[32,16,512]{2,1,0:T(8,128)(2,1)} custom-call(s32[32,128]{1,0:T(8,128)S(1)} %reshape.195.idx_ref, bf16[32,64,256]{2,1,0:T(8,128)(2,1)S(1)} %copy-done, bf16[16,8192]{1,0:T(8,128)(2,1)S(1)} %get-tuple-element.34.refs_0_, bf16[16,8192]{1,0:T(8,128)(2,1)S(1)} %copy-done.3, bf16[16,8192]{1,0:T(8,128)(2,1)S(1)} %copy-done.5, ...), custom_call_target="tpu_custom_call" | custom-call | flops 6899999744 | bytes 600000 | tf_op jit(solution)/shard_map/project_last/pallas_call | solution.py:147
  51.4 18.5 %all-to-all-done.most_ref = bf16[32,16,1536]{2,1,0:T(8,128)(2,1)} async-done(((bf16[32,16,1536]{2,1,0:T(8,128)(2,1)}), bf16[32,16,1536]{2,1,0:T(8,128)(2,1)}, u32[]{:S(2)}, u32[]{:S(2)}) %all-to-all-start) | async-done | bytes 1572896 | tf_op jit(solution)/shard_map/all_to_all | solution.py:521
  69.9 4.3 %all-to-all-start.1 = ((bf16[32,16,512]{2,1,0:T(8,128)(2,1)}), bf16[32,16,512]{2,1,0:T(8,128)(2,1)S(1)}, u32[]{:S(2)}, u32[]{:S(2)}) async-start(bf16[32,16,512]{2,1,0:T(8,128)(2,1)} %project_last.1), calls=%async_computation.1 | async-start | bytes 1048576 | tf_op jit(solution)/shard_map/all_to_all | solution.py:521
  74.2 0.0 copy-start.8
  74.2 1.0 copy-done.8
  75.3 1.0 copy-done.10
  76.3 11.4 %exit_first.1 = (f32[2,256,512]{2,1,0:T(8,128)}, bf16[32,16,512]{2,1,0:T(8,128)(2,1)}, f32[2,256,256]{2,1,0:T(8,128)S(1)}) custom-call(s32[4,5]{1,0:T(4,128)S(1)} %pad_add_fusion.3.meta_ref, bf16[2,256,256]{2,1,0:T(8,128)(2,1)S(1)} %copy-done.1, bf16[512,512]{1,0:T(8,128)(2,1)S(1)} %copy-done.8, bf16[512,512]{1,0:T(8,128)(2,1)S(1)} %copy-done.10, ...), custom_call_target="tpu_custom_call" | custom-call | flops 11500000256 | bytes 1000000 | tf_op jit(solution)/shard_map/exit_first/pallas_call | solution.py:451
  87.7 0.8 copy-done.16
  88.5 0.9 all-to-all-done.1.last_ref
  89.4 4.9 %all-to-all-start.2 = ((bf16[32,16,512]{2,1,0:T(8,128)(2,1)}), bf16[32,16,512]{2,1,0:T(8,128)(2,1)S(1)}, u32[]{:S(2)}, u32[]{:S(2)}) async-start(bf16[32,16,512]{2,1,0:T(8,128)(2,1)} %get-tuple-element.42), calls=%async_computation.2 | async-start | bytes 1048576 | tf_op jit(solution)/shard_map/all_to_all | solution.py:521
  94.3 0.0 copy-start.9
  94.4 1.0 copy-done.9
  95.4 1.0 copy-done.11
  96.4 1.0 copy-done.17
  97.5 7.8 %exit_rest.1 = bf16[32,16,1536]{2,1,0:T(8,128)(2,1)} custom-call(s32[4,5]{1,0:T(4,128)S(1)} %pad_add_fusion.3.meta_ref, bf16[2,256,256]{2,1,0:T(8,128)(2,1)S(1)} %copy-done.1, bf16[512,512]{1,0:T(8,128)(2,1)S(1)} %copy-done.9, bf16[512,512]{1,0:T(8,128)(2,1)S(1)} %copy-done.11, bf16[32,16,1536]{2,1,0:T(8,128)(2,1)} %all-to-all-done.most_ref, ...), custom_call_target="tpu_custom_call" | custom-call | flops 11500000256 | bytes 1000000 | tf_op jit(solution)/shard_map/exit_rest/pallas_call | solution.py:472
  105.3 4.2 %all-to-all-done.2.grad_ref = bf16[32,16,512]{2,1,0:T(8,128)(2,1)S(1)} async-done(((bf16[32,16,512]{2,1,0:T(8,128)(2,1)}), bf16[32,16,512]{2,1,0:T(8,128)(2,1)S(1)}, u32[]{:S(2)}, u32[]{:S(2)}) %all-to-all-start.2) | async-done | bytes 524320 | tf_op jit(solution)/shard_map/all_to_all | solution.py:521
  109.5 4.8 %all-to-all-start.3 = ((bf16[32,16,1536]{2,1,0:T(8,128)(2,1)}), bf16[32,16,1536]{2,1,0:T(8,128)(2,1)}, u32[]{:S(2)}, u32[]{:S(2)}) async-start(bf16[32,16,1536]{2,1,0:T(8,128)(2,1)} %exit_rest.1), calls=%async_computation.3 | async-start | bytes 3145728 | tf_op jit(solution)/shard_map/all_to_all | solution.py:521
  114.4 0.3 copy.22
  114.6 0.2 reshape.192
  115.0 0.1 reshape.193.idx_ref
  115.1 1.7 collective-permute-start.12
  116.8 2.3 %fusion.9 = (bf16[32,16,512]{2,1,0:T(8,128)(2,1)}, bf16[32,16,512]{2,1,0:T(8,128)(2,1)}) fusion(bf16[32,16,1536]{2,1,0:T(8,128)(2,1)} %exit_rest.1), kind=kLoop, calls=%fused_computation.80 | loop fusion | bytes 2097152 | tf_op jit(solution)/shard_map/slice | solution.py:595
  119.1 0.0 collective-permute-start.13
  119.1 0.5 collective-permute-start.14
  119.6 5.8 %back_first.1 = (f32[16,8192]{1,0:T(8,128)S(1)}, f32[16,8192]{1,0:T(8,128)S(1)}, f32[16,8192]{1,0:T(8,128)S(1)}, f32[16,8192]{1,0:T(8,128)S(1)}) custom-call(s32[32,128]{1,0:T(8,128)S(1)} %reshape.193.idx_ref, bf16[32,64,256]{2,1,0:T(8,128)(2,1)S(1)} %copy-done, bf16[32,16,512]{2,1,0:T(8,128)(2,1)S(1)} %all-to-all-done.2.grad_ref), custom_call_target="tpu_custom_call" | custom-call | flops 5750000128 | bytes 500000 | tf_op jit(solution)/shard_map/back_first/pallas_call | solution.py:249
  125.4 0.8 copy-done.12
  126.2 0.8 copy-done.14
  127.0 24.6 %all-to-all-done.3.grad_ref = bf16[32,16,1536]{2,1,0:T(8,128)(2,1)} async-done(((bf16[32,16,1536]{2,1,0:T(8,128)(2,1)}), bf16[32,16,1536]{2,1,0:T(8,128)(2,1)}, u32[]{:S(2)}, u32[]{:S(2)}) %all-to-all-start.3) | async-done | bytes 1572896 | tf_op jit(solution)/shard_map/all_to_all | solution.py:521
  151.7 1.0 copy-done.13
  152.7 1.0 copy-done.15
  153.8 9.6 %back_rest.1 = (bf16[16,8192]{1,0:T(8,128)(2,1)S(1)}, bf16[16,8192]{1,0:T(8,128)(2,1)S(1)}, bf16[16,8192]{1,0:T(8,128)(2,1)S(1)}, bf16[16,8192]{1,0:T(8,128)(2,1)S(1)}) custom-call(s32[32,128]{1,0:T(8,128)S(1)} %reshape.193.idx_ref, bf16[32,64,256]{2,1,0:T(8,128)(2,1)} %radon_ref.7, bf16[32,16,1536]{2,1,0:T(8,128)(2,1)} %all-to-all-done.3.grad_ref, ...), custom_call_target="tpu_custom_call" | custom-call | flops 10350000128 | bytes 900000 | tf_op jit(solution)/shard_map/back_rest/pallas_call | solution.py:249
  163.4 1.6 collective-permute-start.9
  165.0 0.7 collective-permute-start.10
  165.6 1.7 select_bitcast_fusion.3
  167.5 0.3 maximum_convert_fusion
  167.9 4.7 %copy.37 = f32[2,256,4,512]{3,2,1,0:T(4,128)} copy(f32[2,256,4,512]{3,1,0,2:T(8,128)S(1)} %maximum_convert_fusion) | data formatting | bytes 8388608
  172.6 4.6 %collective-permute-done.10 = bf16[16,8192]{1,0:T(8,128)(2,1)S(1)} collective-permute-done((bf16[16,8192]{1,0:T(8,128)(2,1)S(1)}, bf16[16,8192]{1,0:T(8,128)(2,1)S(1)}, u32[]{:S(2)}, u32[]{:S(2)}) %collective-permute-start.10) | collective-permute-done | bytes 262176 | tf_op jit(solution)/shard_map/ppermute | solution.py:36
  177.2 0.6 collective-permute-done.11
  177.8 0.1 select_bitcast_fusion.7
  177.9 1.6 multiply_add_fusion
  (65 shorter events, 0.5 us)
Async XLA Ops:
  0.6 5.2 %copy-start.19 = (s32[32,32,4]{1,2,0:T(4,128)S(1)}, s32[32,32,4]{1,2,0:T(4,128)}, u32[]{:S(2)}) copy-start(s32[32,32,4]{1,2,0:T(4,128)} %param.11) | copy-start | bytes 49156
  0.7 16.5 %copy-start = (bf16[32,64,256]{2,1,0:T(8,128)(2,1)S(1)}, bf16[32,64,256]{2,1,0:T(8,128)(2,1)}, u32[]{:S(2)}) copy-start(bf16[32,64,256]{2,1,0:T(8,128)(2,1)} %radon_ref.7) | copy-start | bytes 3145732
  2.8 8.7 %collective-permute-start.3 = (bf16[16,8192]{1,0:T(8,128)(2,1)}, bf16[16,8192]{1,0:T(8,128)(2,1)S(1)}, u32[]{:S(2)}, u32[]{:S(2)}) collective-permute-start(bf16[16,8192]{1,0:T(8,128)(2,1)} %get-tuple-element.73), channel_id=1, source_target_pairs={{0,1},{1,2},{2,3},{3,0},{4,5},{5,6},{6,7},{7,4},{8,9},{9,10},{10,1... | collective-permute-start | bytes 786440 | tf_op jit(solution)/shard_map/ppermute | solution.py:36
  5.4 11.6 %collective-permute-start.4 = (bf16[16,8192]{1,0:T(8,128)(2,1)S(1)}, bf16[16,8192]{1,0:T(8,128)(2,1)S(1)}, u32[]{:S(2)}, u32[]{:S(2)}) collective-permute-start(bf16[16,8192]{1,0:T(8,128)(2,1)S(1)} %get-tuple-element.75), channel_id=1, source_target_pairs={{0,2},{1,3},{2,0},{3,1},{4,6},{5,7},{6,4},{7,5},{8,10},{9,11},{10,... | collective-permute-start | bytes 786440 | tf_op jit(solution)/shard_map/ppermute | solution.py:36
  5.4 11.8 %collective-permute-start.5 = (bf16[16,8192]{1,0:T(8,128)(2,1)S(1)}, bf16[16,8192]{1,0:T(8,128)(2,1)S(1)}, u32[]{:S(2)}, u32[]{:S(2)}) collective-permute-start(bf16[16,8192]{1,0:T(8,128)(2,1)S(1)} %get-tuple-element.72), channel_id=1, source_target_pairs={{0,3},{1,0},{2,1},{3,2},{4,7},{5,4},{6,5},{7,6},{8,11},{9,8},{10,9... | collective-permute-start | bytes 786440 | tf_op jit(solution)/shard_map/ppermute | solution.py:36
  11.5 14.5 %copy-start.2 = (bf16[16,8192]{1,0:T(8,128)(2,1)}, bf16[16,8192]{1,0:T(8,128)(2,1)S(1)}, u32[]{:S(2)}) copy-start(bf16[16,8192]{1,0:T(8,128)(2,1)S(1)} %collective-permute-done.3.refs_1_) | copy-start | bytes 786436
  17.0 9.0 %copy-start.4 = (bf16[16,8192]{1,0:T(8,128)(2,1)}, bf16[16,8192]{1,0:T(8,128)(2,1)S(1)}, u32[]{:S(2)}) copy-start(bf16[16,8192]{1,0:T(8,128)(2,1)S(1)} %collective-permute-done.4.refs_2_) | copy-start | bytes 786436
  17.2 8.8 %copy-start.6 = (bf16[16,8192]{1,0:T(8,128)(2,1)}, bf16[16,8192]{1,0:T(8,128)(2,1)S(1)}, u32[]{:S(2)}) copy-start(bf16[16,8192]{1,0:T(8,128)(2,1)S(1)} %collective-permute-done.5.refs_3_) | copy-start | bytes 786436
  26.0 6.7 %copy-start.21 = (s32[4,1]{0,1:T(1,128)S(1)}, s32[4,1]{0,1:T(1,128)}, u32[]{:S(2)}) copy-start(s32[4,1]{0,1:T(1,128)} %param.15) | copy-start | bytes 52
  26.0 6.8 %copy-start.20 = (s32[4,4]{1,0:T(4,128)S(1)}, s32[4,4]{1,0:T(4,128)}, u32[]{:S(2)}) copy-start(s32[4,4]{1,0:T(4,128)} %param.14) | copy-start | bytes 196
  26.0 43.9 %all-to-all-start = ((bf16[32,16,1536]{2,1,0:T(8,128)(2,1)}), bf16[32,16,1536]{2,1,0:T(8,128)(2,1)}, u32[]{:S(2)}, u32[]{:S(2)}) async-start(bf16[32,16,1536]{2,1,0:T(8,128)(2,1)} %project_most.1), calls=%async_computation | async-start | bytes 3145728 | tf_op jit(solution)/shard_map/all_to_all | solution.py:521
  32.8 4.7 %collective-permute-start.2 = (s32[1,5]{1,0:T(1,128)S(1)}, s32[1,5]{1,0:T(1,128)S(1)}, u32[]{:S(2)}, u32[]{:S(2)}) collective-permute-start(s32[1,5]{1,0:T(1,128)S(1)} %get-tuple-element.91), channel_id=1, source_target_pairs={{0,1},{1,2},{2,3},{3,0},{4,5},{5,6},{6,7},{7,4},{8,9},{9,10},{10,1... | collective-permute-start | bytes 68 | tf_op jit(solution)/shard_map/ppermute | solution.py:36
  34.5 4.6 %collective-permute-start.1 = (s32[1,5]{1,0:T(1,128)S(1)}, s32[1,5]{1,0:T(1,128)S(1)}, u32[]{:S(2)}, u32[]{:S(2)}) collective-permute-start(s32[1,5]{1,0:T(1,128)S(1)} %get-tuple-element.92), channel_id=1, source_target_pairs={{0,2},{1,3},{2,0},{3,1},{4,6},{5,7},{6,4},{7,5},{8,10},{9,11},{10,... | collective-permute-start | bytes 68 | tf_op jit(solution)/shard_map/ppermute | solution.py:36
  34.6 5.3 %collective-permute-start = (s32[1,5]{1,0:T(1,128)S(1)}, s32[1,5]{1,0:T(1,128)S(1)}, u32[]{:S(2)}, u32[]{:S(2)}) collective-permute-start(s32[1,5]{1,0:T(1,128)S(1)} %get-tuple-element.93), channel_id=1, source_target_pairs={{0,3},{1,0},{2,1},{3,2},{4,7},{5,4},{6,5},{7,6},{8,11},{9,8},{10,9... | collective-permute-start | bytes 68 | tf_op jit(solution)/shard_map/ppermute | solution.py:36
  39.8 6.1 %copy-start.3 = (bf16[16,8192]{1,0:T(8,128)(2,1)S(1)}, bf16[16,8192]{1,0:T(8,128)(2,1)}, u32[]{:S(2)}) copy-start(bf16[16,8192]{1,0:T(8,128)(2,1)} %copy-done.2) | copy-start | bytes 786436
  39.8 6.1 %copy-start.5 = (bf16[16,8192]{1,0:T(8,128)(2,1)S(1)}, bf16[16,8192]{1,0:T(8,128)(2,1)}, u32[]{:S(2)}) copy-start(bf16[16,8192]{1,0:T(8,128)(2,1)} %copy-done.4) | copy-start | bytes 786436
  39.8 6.1 %copy-start.7 = (bf16[16,8192]{1,0:T(8,128)(2,1)S(1)}, bf16[16,8192]{1,0:T(8,128)(2,1)}, u32[]{:S(2)}) copy-start(bf16[16,8192]{1,0:T(8,128)(2,1)} %copy-done.6) | copy-start | bytes 786436
  42.6 31.6 %collective-permute-start.6 = (bf16[4,256,256]{2,1,0:T(8,128)(2,1)}, bf16[4,256,256]{2,1,0:T(8,128)(2,1)}, u32[]{:S(2)}, u32[]{:S(2)}) collective-permute-start(bf16[4,256,256]{2,1,0:T(8,128)(2,1)} %get-tuple-element.64), channel_id=1, source_target_pairs={{0,3},{1,0},{2,1},{3,2},{4,7},{5,4},{6,5},{7,6},{8,11},{9,8},{10,9... | collective-permute-start | bytes 1572872 | tf_op jit(solution)/shard_map/ppermute | solution.py:36
  42.7 51.7 %collective-permute-start.7 = (bf16[4,256,256]{2,1,0:T(8,128)(2,1)}, bf16[4,256,256]{2,1,0:T(8,128)(2,1)S(1)}, u32[]{:S(2)}, u32[]{:S(2)}) collective-permute-start(bf16[4,256,256]{2,1,0:T(8,128)(2,1)} %get-tuple-element.63), channel_id=1, source_target_pairs={{0,2},{1,3},{2,0},{3,1},{4,6},{5,7},{6,4},{7,5},{8,10},{9,11},{10,... | collective-permute-start | bytes 1572872 | tf_op jit(solution)/shard_map/ppermute | solution.py:36
  44.2 30.0 %copy-start.1 = (bf16[2,256,256]{2,1,0:T(8,128)(2,1)S(1)}, bf16[2,256,256]{2,1,0:T(8,128)(2,1)}, u32[]{:S(2)}) copy-start(bf16[2,256,256]{2,1,0:T(8,128)(2,1)} %probe_ref.3) | copy-start | bytes 786436
  44.2 50.1 %collective-permute-start.8 = (bf16[4,256,256]{2,1,0:T(8,128)(2,1)}, bf16[4,256,256]{2,1,0:T(8,128)(2,1)S(1)}, u32[]{:S(2)}, u32[]{:S(2)}) collective-permute-start(bf16[4,256,256]{2,1,0:T(8,128)(2,1)} %get-tuple-element.62), channel_id=1, source_target_pairs={{0,1},{1,2},{2,3},{3,0},{4,5},{5,6},{6,7},{7,4},{8,9},{9,10},{10,1... | collective-permute-start | bytes 1572872 | tf_op jit(solution)/shard_map/ppermute | solution.py:36
  69.9 19.5 %all-to-all-start.1 = ((bf16[32,16,512]{2,1,0:T(8,128)(2,1)}), bf16[32,16,512]{2,1,0:T(8,128)(2,1)S(1)}, u32[]{:S(2)}, u32[]{:S(2)}) async-start(bf16[32,16,512]{2,1,0:T(8,128)(2,1)} %project_last.1), calls=%async_computation.1 | async-start | bytes 1048576 | tf_op jit(solution)/shard_map/all_to_all | solution.py:521
  74.2 1.0 copy-start.8
  75.3 1.0 copy-start.10
  87.7 0.8 copy-start.16
  89.4 20.1 %all-to-all-start.2 = ((bf16[32,16,512]{2,1,0:T(8,128)(2,1)}), bf16[32,16,512]{2,1,0:T(8,128)(2,1)S(1)}, u32[]{:S(2)}, u32[]{:S(2)}) async-start(bf16[32,16,512]{2,1,0:T(8,128)(2,1)} %get-tuple-element.42), calls=%async_computation.2 | async-start | bytes 1048576 | tf_op jit(solution)/shard_map/all_to_all | solution.py:521
  94.3 1.0 copy-start.9
  95.4 1.0 copy-start.11
  96.4 1.0 copy-start.17
  109.5 42.2 %all-to-all-start.3 = ((bf16[32,16,1536]{2,1,0:T(8,128)(2,1)}), bf16[32,16,1536]{2,1,0:T(8,128)(2,1)}, u32[]{:S(2)}, u32[]{:S(2)}) async-start(bf16[32,16,1536]{2,1,0:T(8,128)(2,1)} %exit_rest.1), calls=%async_computation.3 | async-start | bytes 3145728 | tf_op jit(solution)/shard_map/all_to_all | solution.py:521
  115.1 50.5 %collective-permute-start.12 = (bf16[32,16,512]{2,1,0:T(8,128)(2,1)}, bf16[32,16,512]{2,1,0:T(8,128)(2,1)}, u32[]{:S(2)}, u32[]{:S(2)}) collective-permute-start(bf16[32,16,512]{2,1,0:T(8,128)(2,1)} %get-tuple-element.42), channel_id=1, source_target_pairs={{0,1},{1,2},{2,3},{3,0},{4,5},{5,6},{6,7},{7,4},{8,9},{9,10},{10,1... | collective-permute-start | bytes 1572872 | tf_op jit(solution)/shard_map/ppermute | solution.py:36
  119.1 46.6 %collective-permute-start.13 = (bf16[32,16,512]{2,1,0:T(8,128)(2,1)}, bf16[32,16,512]{2,1,0:T(8,128)(2,1)}, u32[]{:S(2)}, u32[]{:S(2)}) collective-permute-start(bf16[32,16,512]{2,1,0:T(8,128)(2,1)} %get-tuple-element.67), channel_id=1, source_target_pairs={{0,2},{1,3},{2,0},{3,1},{4,6},{5,7},{6,4},{7,5},{8,10},{9,11},{10,... | collective-permute-start | bytes 1572872 | tf_op jit(solution)/shard_map/ppermute | solution.py:36
  119.1 46.5 %collective-permute-start.14 = (bf16[32,16,512]{2,1,0:T(8,128)(2,1)}, bf16[32,16,512]{2,1,0:T(8,128)(2,1)}, u32[]{:S(2)}, u32[]{:S(2)}) collective-permute-start(bf16[32,16,512]{2,1,0:T(8,128)(2,1)} %get-tuple-element.66), channel_id=1, source_target_pairs={{0,3},{1,0},{2,1},{3,2},{4,7},{5,4},{6,5},{7,6},{8,11},{9,8},{10,9... | collective-permute-start | bytes 1572872 | tf_op jit(solution)/shard_map/ppermute | solution.py:36
  125.4 0.8 copy-start.12
  126.2 0.8 copy-start.14
  151.7 1.0 copy-start.13
  152.7 1.0 copy-start.15
  163.4 9.2 %collective-permute-start.9 = (bf16[16,8192]{1,0:T(8,128)(2,1)S(1)}, bf16[16,8192]{1,0:T(8,128)(2,1)S(1)}, u32[]{:S(2)}, u32[]{:S(2)}) collective-permute-start(bf16[16,8192]{1,0:T(8,128)(2,1)S(1)} %get-tuple-element.52), channel_id=1, source_target_pairs={{0,1},{1,2},{2,3},{3,0},{4,5},{5,6},{6,7},{7,4},{8,9},{9,10},{10,1... | collective-permute-start | bytes 786440 | tf_op jit(solution)/shard_map/ppermute | solution.py:36
  165.0 12.2 %collective-permute-start.10 = (bf16[16,8192]{1,0:T(8,128)(2,1)S(1)}, bf16[16,8192]{1,0:T(8,128)(2,1)S(1)}, u32[]{:S(2)}, u32[]{:S(2)}) collective-permute-start(bf16[16,8192]{1,0:T(8,128)(2,1)S(1)} %get-tuple-element.53), channel_id=1, source_target_pairs={{0,2},{1,3},{2,0},{3,1},{4,6},{5,7},{6,4},{7,5},{8,10},{9,11},{10,... | collective-permute-start | bytes 786440 | tf_op jit(solution)/shard_map/ppermute | solution.py:36
  165.6 12.2 %collective-permute-start.11 = (bf16[16,8192]{1,0:T(8,128)(2,1)S(1)}, bf16[16,8192]{1,0:T(8,128)(2,1)S(1)}, u32[]{:S(2)}, u32[]{:S(2)}) collective-permute-start(bf16[16,8192]{1,0:T(8,128)(2,1)S(1)} %get-tuple-element.54), channel_id=1, source_target_pairs={{0,3},{1,0},{2,1},{3,2},{4,7},{5,4},{6,5},{7,6},{8,11},{9,8},{10,9... | collective-permute-start | bytes 786440 | tf_op jit(solution)/shard_map/ppermute | solution.py:36
  172.6 5.3 %copy-start.18 = (bf16[2,32,8192]{2,1,0:T(8,128)(2,1)S(1)}, bf16[2,32,8192]{2,1,0:T(8,128)(2,1)}, u32[]{:S(2)}) copy-start(bf16[2,32,8192]{2,1,0:T(8,128)(2,1)} %param.9) | copy-start | bytes 3145732

commit v6 on v5

--- a/solution.py
+++ b/solution.py
@@ -13,10 +13,10 @@
 LANES = 128
 ROWS = 16
 GROUP = 8
-VMEM_LIMIT = 50 * 1024 * 1024
+MEBI = 1024 * 1024
 everywhere = pl.BlockSpec(memory_space=pltpu.VMEM)
 scalars = pl.BlockSpec(memory_space=pltpu.SMEM)
-CHAINS = 4
+CHAINS = 8
 BATCH = 4
 
 
@@ -81,9 +81,8 @@
                 vv_ref[tiles + k * per_piece + t] = swapped[i * ROWS : (i + 1) * ROWS]
 
 
-def project_chunk(chunks, idx_ref, radon_ref, vv_ref, out_ref, lhs_refs):
+def project_blocks(blocks, idx_ref, radon_ref, vv_ref, out_ref, lhs_refs):
     angles, block, span = radon_ref.shape
-    blocks = out_ref.shape[2] // block // len(chunks)
     feeds = span // block
     low = lower_half((ROWS, LANES))
     batch = lhs_refs[0].shape[0]
@@ -91,16 +90,15 @@
     def gather(start, lhs_ref):
         for n in range(batch):
             a = start + n
-            for i, chunk in enumerate(chunks):
-                for b in range(blocks):
-                    row = (i * blocks + b) * ROWS
-                    for jp in range(feeds // 2):
-                        at = (chunk * blocks + b) * feeds + 2 * jp
-                        first = vv_ref[idx_ref[a, at]]
-                        second = vv_ref[idx_ref[a, at + 1]]
-                        lhs_ref[n, row : row + ROWS, jp * LANES : (jp + 1) * LANES] = jnp.where(
-                            low, first, second
-                        )
+            for i, b in enumerate(blocks):
+                row = i * ROWS
+                for jp in range(feeds // 2):
+                    at = b * feeds + 2 * jp
+                    first = vv_ref[idx_ref[a, at]]
+                    second = vv_ref[idx_ref[a, at + 1]]
+                    lhs_ref[n, row : row + ROWS, jp * LANES : (jp + 1) * LANES] = jnp.where(
+                        low, first, second
+                    )
 
     def multiply(start, lhs_ref):
         for n in range(batch):
@@ -108,7 +106,7 @@
             product = lax.dot_general(
                 lhs_ref[n], radon_ref[a], (((1,), (1,)), ((), ())), preferred_element_type=jnp.float32
             )
-            for pair in range(len(chunks) * blocks // 2):
+            for pair in range(len(blocks) // 2):
                 row = 2 * pair * ROWS
                 tile = jnp.concatenate(
                     [product[row : row + ROWS], product[row + ROWS : row + 2 * ROWS]], axis=1
@@ -126,11 +124,11 @@
         gather(jnp.minimum(start + 2 * batch, angles - batch), lhs_refs[0])
 
 
-def project_kernel(chunks, pieces, idx_ref, radon_ref, *refs):
+def project_kernel(blocks, pieces, idx_ref, radon_ref, *refs):
     vol_refs = refs[:pieces]
     out_ref, vv_ref, *lhs_refs = refs[pieces:]
     arrange(vol_refs, vv_ref)
-    project_chunk(chunks, idx_ref, radon_ref, vv_ref, out_ref, lhs_refs)
+    project_blocks(blocks, idx_ref, radon_ref, vv_ref, out_ref, lhs_refs)
 
 
 def guess(microseconds):
@@ -139,38 +137,42 @@
     )
 
 
-def project(idx, radon_tiles, vol_pieces, tile_width, chunks, name):
+def project(idx, radon_tiles, vol_pieces, blocks, name):
     angles, block, span = radon_tiles.shape
     pieces = len(vol_pieces)
     tiles = pieces * vol_pieces[0].shape[1] // LANES
-    rows = len(chunks) * tile_width // block * ROWS
+    out_shape = (angles, ROWS, len(blocks) * block)
     return pl.pallas_call(
-        functools.partial(project_kernel, chunks, pieces),
-        out_shape=jax.ShapeDtypeStruct((angles, ROWS, len(chunks) * tile_width), jnp.bfloat16),
+        functools.partial(project_kernel, blocks, pieces),
+        out_shape=jax.ShapeDtypeStruct(out_shape, jnp.bfloat16),
         in_specs=[scalars, everywhere] + [everywhere] * pieces,
         out_specs=everywhere,
         scratch_shapes=[pltpu.VMEM((2 * tiles, ROWS, LANES), jnp.bfloat16)]
-        + [pltpu.VMEM((BATCH, rows, span), jnp.bfloat16)] * 2,
-        compiler_params=pltpu.CompilerParams(vmem_limit_bytes=VMEM_LIMIT),
-        cost_estimate=guess(4 + 2 * len(chunks)),
+        + [pltpu.VMEM((BATCH, len(blocks) * ROWS, span), jnp.bfloat16)] * 2,
+        compiler_params=pltpu.CompilerParams(
+            vmem_limit_bytes=14 * MEBI + 2 * radon_tiles.size + 2 * math.prod(out_shape)
+        ),
+        cost_estimate=guess(4 + len(blocks) // 4),
         name=name,
     )(idx, radon_tiles, *vol_pieces)
 
 
-def back_project_kernel(chunks, pieces, has_start, idx_ref, radon_ref, grad_ref, *refs):
-    start_refs, refs = (refs[:pieces], refs[pieces:]) if has_start else (None, refs)
-    out_refs, refs = refs[:pieces], refs[pieces:]
+def back_project_kernel(blocks, has_start, outs, idx_ref, radon_ref, grad_ref, *refs):
+    start_ref, refs = (refs[0], refs[1:]) if has_start else (None, refs)
+    out_refs, refs = refs[:outs], refs[outs:]
     acc_refs, (w_ref, *contrib_refs) = refs[:CHAINS], refs[CHAINS:]
     angles, block, span = radon_ref.shape
-    per_piece = out_refs[0].shape[1] // LANES
-    blocks = grad_ref.shape[2] // block // len(chunks)
-    pairs = len(chunks) * blocks // 2
+    pairs = len(blocks) // 2
     feeds = span // block
-
-    @pl.loop(0, acc_refs[0].shape[0], unroll=16)
+    coef_blocks = acc_refs[0].shape[0]
+
+    @pl.loop(0, coef_blocks, unroll=16)
     def _(t):
-        for acc_ref in acc_refs:
-            acc_ref[t] = jnp.zeros((GROUP, LANES), jnp.float32)
+        for n, acc_ref in enumerate(acc_refs):
+            if n == 0 and has_start:
+                acc_ref[t] = start_ref[t]
+            else:
+                acc_ref[t] = jnp.zeros((GROUP, LANES), jnp.float32)
 
     low = lower_half((GROUP, LANES))
     low_rows = lower_half((block, LANES))
@@ -203,14 +205,12 @@
             )
 
     def scatter(start, contrib_ref):
-        for i, chunk in enumerate(chunks):
-            for b in range(blocks):
-                row = (i * blocks + b) * GROUP
-                for j in range(feeds):
-                    at = (chunk * blocks + b) * feeds + j
-                    for n in range(CHAINS):
-                        tile = contrib_ref[n, row : row + GROUP, j * LANES : (j + 1) * LANES]
-                        acc_refs[n][idx_ref[start + n, at]] += tile
+        for i, b in enumerate(blocks):
+            row = i * GROUP
+            for j in range(feeds):
+                for n in range(CHAINS):
+                    tile = contrib_ref[n, row : row + GROUP, j * LANES : (j + 1) * LANES]
+                    acc_refs[n][idx_ref[start + n, b * feeds + j]] += tile
 
     multiply(0, 0, contrib_refs[0])
 
@@ -222,40 +222,54 @@
         multiply(jnp.minimum(start + 2 * CHAINS, angles - CHAINS), 0, contrib_refs[0])
         scatter(start + CHAINS, contrib_refs[1])
 
-    for k in range(pieces):
-
-        @pl.loop(0, per_piece, unroll=16)
+    def total(t):
+        sums = [acc_ref[t] for acc_ref in acc_refs]
+        while len(sums) > 1:
+            sums = [sums[i] + sums[i + 1] for i in range(0, len(sums), 2)]
+        return sums[0]
+
+    if outs == 1:
+
+        @pl.loop(0, coef_blocks, unroll=16)
         def _(t):
-            lanes = pl.ds(pl.multiple_of(t * LANES, LANES), LANES)
-            at = 2 * (k * per_piece + t)
-            even, odd = acc_refs[0][at], acc_refs[0][at + 1]
-            for acc_ref in acc_refs[1:]:
-                even += acc_ref[at]
-                odd += acc_ref[at + 1]
-            real = jnp.where(low, even, swap_halves(odd))
-            imag = jnp.where(low, swap_halves(even), odd)
-            total = jnp.concatenate([real, imag], axis=0)
-            if has_start:
-                total += start_refs[k][:, lanes]
-            out_refs[k][:, lanes] = total.astype(out_refs[k].dtype)
-
-
-def back_project(idx, radon_tiles, grads, chunks, start, pieces, piece_width, out_type, name):
+            out_refs[0][t] = total(t)
+
+    else:
+        per_piece = out_refs[0].shape[1] // LANES
+        for k, out_ref in enumerate(out_refs):
+
+            @pl.loop(0, per_piece, unroll=16)
+            def _(t):
+                lanes = pl.ds(pl.multiple_of(t * LANES, LANES), LANES)
+                even = total(2 * (k * per_piece + t))
+                odd = total(2 * (k * per_piece + t) + 1)
+                real = jnp.where(low, even, swap_halves(odd))
+                imag = jnp.where(low, swap_halves(even), odd)
+                out_ref[:, lanes] = jnp.concatenate([real, imag], axis=0).astype(out_ref.dtype)
+
+
+def back_project(idx, radon_tiles, grads, blocks, start, pieces, piece_width, name):
     angles, block, span = radon_tiles.shape
     coef_blocks = pieces * piece_width // block
-    rows = grads.shape[2] // block * GROUP
+    rows = len(blocks) * GROUP
     has_start = start is not None
-    operands = [idx, radon_tiles, grads] + (list(start) if has_start else [])
+    if has_start:
+        out_shape = [jax.ShapeDtypeStruct((ROWS, piece_width), jnp.bfloat16)] * pieces
+    else:
+        out_shape = [jax.ShapeDtypeStruct((coef_blocks, GROUP, LANES), jnp.float32)]
+    operands = [idx, radon_tiles, grads] + ([start] if has_start else [])
     return pl.pallas_call(
-        functools.partial(back_project_kernel, chunks, pieces, has_start),
-        out_shape=[jax.ShapeDtypeStruct((ROWS, piece_width), out_type)] * pieces,
+        functools.partial(back_project_kernel, blocks, has_start, len(out_shape)),
+        out_shape=out_shape,
         in_specs=[scalars] + [everywhere] * (len(operands) - 1),
-        out_specs=[everywhere] * pieces,
+        out_specs=[everywhere] * len(out_shape),
         scratch_shapes=[pltpu.VMEM((coef_blocks, GROUP, LANES), jnp.float32)] * CHAINS
         + [pltpu.VMEM((2 * CHAINS, 2 * block, 2 * span), jnp.bfloat16)]
         + [pltpu.VMEM((CHAINS, rows, 2 * span), jnp.float32)] * 2,
-        compiler_params=pltpu.CompilerParams(vmem_limit_bytes=VMEM_LIMIT),
-        cost_estimate=guess(3 + 2 * len(chunks)),
+        compiler_params=pltpu.CompilerParams(
+            vmem_limit_bytes=34 * MEBI + 2 * radon_tiles.size + 2 * grads.size
+        ),
+        cost_estimate=guess(4 + len(blocks) // 4),
         name=name,
     )(*operands)
 
@@ -369,14 +383,12 @@
                             acc_ref[here] += jnp.where(past, ahead, behind)
 
 
-def exit_first_kernel(
-    tiles, meta_ref, probe_ref, forward_ref, inverse_ref, most_ref, *refs
-):
+def exit_first_kernel(tiles, meta_ref, probe_ref, forward_ref, inverse_ref, sino_ref, *refs):
     amp_refs, refs = refs[:tiles], refs[tiles:]
     partial_ref, grad_ref, spill_ref, acc_ref, *scratch = refs
-    groups = most_ref.shape[0]
-    tile_width = partial_ref.shape[2]
-    done = tiles * tile_width
+    groups = sino_ref.shape[0]
+    width = probe_ref.shape[1]
+    done = sino_ref.shape[2] - width
 
     @pl.loop(0, groups)
     def _(g):
@@ -385,35 +397,33 @@
             acc_ref[c, rows, :] = jnp.zeros((GROUP, acc_ref.shape[2]), jnp.float32)
 
     add_slots(
-        meta_ref, probe_ref, forward_ref, inverse_ref, most_ref, acc_ref, amp_refs, scratch, 0
+        meta_ref, probe_ref, forward_ref, inverse_ref, sino_ref, acc_ref, amp_refs, scratch, 0
     )
 
     @pl.loop(0, groups)
     def _(g):
         rows = pl.ds(pl.multiple_of(g * GROUP, GROUP), GROUP)
-        whole = [acc_ref[c, rows, tile_width:done] for c in range(2)]
+        whole = [acc_ref[c, rows, width:done] for c in range(2)]
         grad_ref[g] = jnp.concatenate(whole, axis=0).astype(jnp.bfloat16)
         for c in range(2):
-            partial_ref[c, rows, :] = acc_ref[c, rows, :tile_width]
+            partial_ref[c, rows, :] = acc_ref[c, rows, :width]
             spill_ref[c, rows, :] = acc_ref[c, rows, done:]
 
 
 def exit_rest_kernel(
-    tiles, meta_ref, probe_ref, forward_ref, inverse_ref, most_ref, last_ref, partial_ref, spill_ref, *refs
+    tiles, meta_ref, probe_ref, forward_ref, inverse_ref, early_ref, late_ref, partial_ref, spill_ref, *refs
 ):
     amp_refs, refs = refs[:tiles], refs[tiles:]
     out_ref, ext_ref, acc_ref, *scratch = refs
-    groups = most_ref.shape[0]
+    groups = early_ref.shape[0]
     width = probe_ref.shape[1]
-    tile_width = partial_ref.shape[2]
-    done = tiles * tile_width
-    kept = done - tile_width
+    done = width + late_ref.shape[2]
 
     @pl.loop(0, groups)
     def _(g):
-        ext_ref[g, :, :kept] = most_ref[g, :, most_ref.shape[2] - kept :]
-        ext_ref[g, :, kept:done] = last_ref[g]
-        ext_ref[g, :, done:] = most_ref[g, :, :width]
+        ext_ref[g, :, :width] = early_ref[g, :, early_ref.shape[2] - width :]
+        ext_ref[g, :, width:done] = late_ref[g]
+        ext_ref[g, :, done:] = early_ref[g, :, :width]
         rows = pl.ds(pl.multiple_of(g * GROUP, GROUP), GROUP)
         for c in range(2):
             acc_ref[c, rows, :width] = spill_ref[c, rows, :]
@@ -427,12 +437,8 @@
     @pl.loop(0, groups)
     def _(g):
         rows = pl.ds(pl.multiple_of(g * GROUP, GROUP), GROUP)
-        here, wrapped = [], []
-        for c in range(2):
-            here.append(acc_ref[c, rows, :done])
-            whole = partial_ref[c, rows, :]
-            spilled = whole[:, :width] + acc_ref[c, rows, done:]
-            wrapped.append(jnp.concatenate([spilled, whole[:, width:]], axis=1))
+        here = [acc_ref[c, rows, :done] for c in range(2)]
+        wrapped = [acc_ref[c, rows, done:] + partial_ref[c, rows, :] for c in range(2)]
         out_ref[g, :, :done] = jnp.concatenate(here, axis=0).astype(jnp.bfloat16)
         out_ref[g, :, done:] = jnp.concatenate(wrapped, axis=0).astype(jnp.bfloat16)
 
@@ -443,43 +449,39 @@
     ] * 4
 
 
-def exit_first(meta, probe_field, tables, most, amps, tile_width):
-    groups, rows = most.shape[:2]
+def exit_first(meta, probe_field, tables, sino, amps):
+    groups, rows, reach = sino.shape
     width = probe_field.shape[1]
-    tiles = len(amps)
     slices = groups * GROUP
+    edge = jax.ShapeDtypeStruct((2, slices, width), jnp.float32)
+    grad = jax.ShapeDtypeStruct((groups, rows, reach - 2 * width), jnp.bfloat16)
     return pl.pallas_call(
-        functools.partial(exit_first_kernel, tiles),
-        out_shape=[
-            jax.ShapeDtypeStruct((2, slices, tile_width), jnp.float32),
-            jax.ShapeDtypeStruct((groups, rows, (tiles - 1) * tile_width), jnp.bfloat16),
-            jax.ShapeDtypeStruct((2, slices, width), jnp.float32),
-        ],
-        in_specs=[scalars] + [everywhere] * (4 + tiles),
+        functools.partial(exit_first_kernel, len(amps)),
+        out_shape=[edge, grad, edge],
+        in_specs=[scalars] + [everywhere] * (4 + len(amps)),
         out_specs=[everywhere] * 3,
-        scratch_shapes=exit_scratch(groups, width, tiles * tile_width + width),
-        compiler_params=pltpu.CompilerParams(vmem_limit_bytes=VMEM_LIMIT),
+        scratch_shapes=exit_scratch(groups, width, reach),
+        compiler_params=pltpu.CompilerParams(vmem_limit_bytes=28 * MEBI),
         cost_estimate=guess(10),
         name="exit_first",
-    )(meta, probe_field, *tables, most, *amps)
-
-
-def exit_rest(meta, probe_field, tables, most, final, partial, spill, amps):
-    groups, rows, tile_width = final.shape
+    )(meta, probe_field, *tables, sino, *amps)
+
+
+def exit_rest(meta, probe_field, tables, early, late, partial, spill, amps):
+    groups, rows = late.shape[:2]
     width = probe_field.shape[1]
-    tiles = len(amps)
-    reach = tiles * tile_width + width
+    reach = late.shape[2] + 2 * width
     return pl.pallas_call(
-        functools.partial(exit_rest_kernel, tiles),
-        out_shape=jax.ShapeDtypeStruct((groups, rows, (tiles + 1) * tile_width), jnp.bfloat16),
-        in_specs=[scalars] + [everywhere] * (7 + tiles),
+        functools.partial(exit_rest_kernel, len(amps)),
+        out_shape=jax.ShapeDtypeStruct((groups, rows, reach), jnp.bfloat16),
+        in_specs=[scalars] + [everywhere] * (7 + len(amps)),
         out_specs=everywhere,
         scratch_shapes=[pltpu.VMEM((groups, rows, reach), jnp.bfloat16)]
         + exit_scratch(groups, width, reach),
-        compiler_params=pltpu.CompilerParams(vmem_limit_bytes=VMEM_LIMIT),
+        compiler_params=pltpu.CompilerParams(vmem_limit_bytes=30 * MEBI),
         cost_estimate=guess(10),
         name="exit_rest",
-    )(meta, probe_field, *tables, most, final, partial, spill, *amps)
+    )(meta, probe_field, *tables, early, late, partial, spill, *amps)
 
 
 def to_groups(received, own_slices):
@@ -533,7 +535,6 @@
     own = slab // n_pos
     rows = 2 * own
     blocks_each = width // block_size
-    last = n_pos - 1
 
     def slices_for(j):
         start = (pos + j) % n_pos * own
@@ -568,37 +569,44 @@
     tile_idx = by_chunk(crossed * (n_pos * tiles_each) + piece * tiles_each + within // 2)
     block_idx = by_chunk(piece * blocks_each + within)
     padded = [pad_rows(piece, own) for piece in vol_pieces]
-    most = list(range(last))
-    sino_most = project(tile_idx, radon_tiles, padded, tile_width, most, "project_most")
-    sino_most, padded = lax.optimization_barrier((sino_most, padded))
-    sino_last = project(tile_idx, radon_tiles, padded, tile_width, [last], "project_last")
-    got_most = everyone(cut_rows(sino_most, own))
-    got_most, sino_last = lax.optimization_barrier((got_most, sino_last))
-    got_last = everyone(cut_rows(sino_last, own))
-    got_most, got_last = to_groups(got_most, own), to_groups(got_last, own)
-    tables = dft_tables(probe_field.shape[1])
-    partial, first_grad, spill = exit_first(
-        meta, probe_field, tables, got_most, amp_pieces[:2], tile_width
-    )
-    own_grad = first_grad
-    first_grad, got_last = lax.optimization_barrier((first_grad, got_last))
-    joined = exit_rest(
-        meta, probe_field, tables, got_most, got_last, partial, spill, amp_pieces[2:]
-    )
-    back_first = everyone(from_groups(first_grad, own))
-    back_first, joined_sent = lax.optimization_barrier((back_first, joined))
-    back_rest = everyone(from_groups(joined_sent, own))
-    partial_grad = back_project(
-        block_idx, radon_tiles, pad_rows(back_first, own), [1], None, n_pos, width, jnp.float32, "back_first"
-    )
-    order = list(range(2, n_pos)) + [0]
-    joined_tiles = {j: joined[:, :, i * tile_width : (i + 1) * tile_width] for i, j in enumerate(order)}
-    joined_tiles[1] = own_grad
-    tile_pieces = rotate_pos([joined_tiles[j] for j in range(n_pos)], 1)
+    probe_width = probe_field.shape[1]
+    tables = dft_tables(probe_width)
+    half = n_pos // 2
+    reach = (half * tile_width + probe_width) // block_size
+    edge = probe_width // block_size
+    early_blocks = list(range(reach))
+    late_blocks = list(range(reach, det_blocks))
+    first_blocks = list(range(edge, half * tile_width // block_size))
+    rest_blocks = list(range(half * tile_width // block_size, det_blocks)) + list(range(edge))
+
+    sino_early = project(tile_idx, radon_tiles, padded, early_blocks, "project_early")
+    sino_early, padded = lax.optimization_barrier((sino_early, padded))
+    sino_late = project(tile_idx, radon_tiles, padded, late_blocks, "project_late")
+    got_early = everyone(cut_rows(sino_early, own))
+    got_early, sino_late = lax.optimization_barrier((got_early, sino_late))
+    got_late = everyone(cut_rows(sino_late, own))
+    got_early, got_late = to_groups(got_early, own), to_groups(got_late, own)
+    partial, first_grad, spill = exit_first(meta, probe_field, tables, got_early, amp_pieces[:half])
+    first_sent, got_late = lax.optimization_barrier((first_grad, got_late))
+    rest_grad = exit_rest(
+        meta, probe_field, tables, got_early, got_late, partial, spill, amp_pieces[half:]
+    )
+    back_first = everyone(from_groups(first_sent, own))
+    back_first, rest_sent = lax.optimization_barrier((back_first, rest_grad))
+    back_rest = everyone(from_groups(rest_sent, own))
+    first_sum = back_project(
+        block_idx, radon_tiles, pad_rows(back_first, own), first_blocks, None, n_pos, width, "back_first"
+    )[0]
+    wrapped = rest_grad.shape[2] - probe_width
+    tile_pieces = [jnp.concatenate([rest_grad[:, :, wrapped:], first_grad[:, :, : tile_width - probe_width]], axis=2)]
+    for j in range(1, n_pos):
+        source, begin = (first_grad, j * tile_width - probe_width) if j < half else (rest_grad, (j - half) * tile_width)
+        tile_pieces.append(source[:, :, begin : begin + tile_width])
+    tile_pieces = rotate_pos(tile_pieces, 1)
     obj_pieces = back_project(
-        block_idx, radon_tiles, pad_rows(back_rest, own), order, partial_grad, n_pos, width, jnp.bfloat16, "back_rest"
-    )
-    groups = joined.shape[0]
+        block_idx, radon_tiles, pad_rows(back_rest, own), rest_blocks, first_sum, n_pos, width, "back_rest"
+    )
+    groups = rest_grad.shape[0]
     tile_pieces = [tile_pieces[-j % n_pos] for j in range(n_pos)]
     tile_pieces = [
         piece.reshape(groups, 2, GROUP, tile_width).transpose(1, 0, 2, 3).reshape(2, groups * GROUP, tile_width)

time: 181 us -> 178 us (0.983)
  waiting for transfers between devices: 68.5 us -> 58.9 us
  local copies, waits for them, and re-layouts: 23 us -> 29.9 us
    all_to_all x4, waiting for transfers between devices: 48.2 us -> 41.2 us  [everyone(): return lax.all_to_all(chunk, ('ang', 'pos'), 0, 0, tiled=True)]
    slice x1 -> x4, local copies, waits for them, and re-layouts: 2.29 us -> 6.82 us  [the longest x2 4.21 us: on_device(): tile_pieces.append(source[:, :, begin:begin + tile_width])]
    unnamed x48 -> x50, local copies, waits for them, and re-layouts: 14.6 us -> 17.5 us
    ppermute x15, waiting for transfers between devices: 20.3 us -> 17.7 us  [rotate_pos(): lax.ppermute(pieces[j], 'pos', [(i, (i + sign * j) % count) for i in rang...]
  transfers between devices with their start and end apart: 19 -> 19, of which waited for: 12 -> 11; matrix products, arithmetic and copies ran while one was open for 8% -> 11% of each run, Pallas kernels for 22% -> 23%
where the time goes in v6:
time: 178 us; the launch traced here: 177 us
  waiting for transfers between devices  58.9 us (33%)
  Pallas kernels  47.8 us (27%)
  starting transfers between devices  34.8 us (20%)
  local copies, waits for them, and re-layouts  29.9 us (17%)
  other arithmetic  4.47 us (3%)
    all_to_all x4, waiting for transfers between devices, everyone(): return lax.all_to_all(chunk, ('ang', 'pos'), 0, 0, tiled=True)  41.2 us
    all_to_all x4, starting transfers between devices, everyone(): return lax.all_to_all(chunk, ('ang', 'pos'), 0, 0, tiled=True)  22 us
    ppermute x15, waiting for transfers between devices, rotate_pos(): lax.ppermute(pieces[j], 'pos', [(i, (i + sign * j) % count) for i in rang...  17.7 us
    unnamed x50, local copies, waits for them, and re-layouts  17.5 us
    pallas_call x2, Pallas kernels, back_project(): pl.pallas_call(functools.partial(back_project_kernel, blocks, has_start,...  15.8 us
    pallas_call x2, Pallas kernels, project(): pl.pallas_call(functools.partial(project_kernel, blocks, pieces), out_sha...  14.2 us
    ppermute x15, starting transfers between devices, rotate_pos(): lax.ppermute(pieces[j], 'pos', [(i, (i + sign * j) % count) for i in rang...  12.8 us
    pallas_call x1, Pallas kernels, exit_rest(): pl.pallas_call(functools.partial(exit_rest_kernel, len(amps)), out_shape=...  9.22 us
  transfers between devices with their start and end apart: 19, of which 11 were waited for; matrix products, arithmetic and copies ran while one was open for 11% of the time, Pallas kernels for 23%

profile of v6, /device:TPU:1, one launch (start us, length us, event | category | flops | bytes accessed | tf_op | source)
XLA Modules:
  0.0 176.9 jit_solution(3127196068315498973)
XLA Ops:
  0.7 1.3 dynamic-slice_bitcast_fusion.4
  2.1 2.7 %collective-permute-start.3 = (bf16[16,8192]{1,0:T(8,128)(2,1)S(1)}, bf16[16,8192]{1,0:T(8,128)(2,1)S(1)}, u32[]{:S(2)}, u32[]{:S(2)}) collective-permute-start(bf16[16,8192]{1,0:T(8,128)(2,1)S(1)} %get-tuple-element.65), channel_id=1, source_target_pairs={{0,1},{1,2},{2,3},{3,0},{4,5},{5,6},{6,7},{7,4},{8,9},{9,10},{10,1... | collective-permute-start | bytes 786440 | tf_op jit(solution)/shard_map/ppermute | solution.py:36
  4.7 0.5 collective-permute-start.5
  5.2 0.3 fusion.5
  5.5 0.3 copy.28
  5.8 0.2 reshape.194
  6.2 0.1 reshape.195.idx_ref
  6.3 4.0 %collective-permute-done.3.refs_1_ = bf16[16,8192]{1,0:T(8,128)(2,1)S(1)} collective-permute-done((bf16[16,8192]{1,0:T(8,128)(2,1)S(1)}, bf16[16,8192]{1,0:T(8,128)(2,1)S(1)}, u32[]{:S(2)}, u32[]{:S(2)}) %collective-permute-start.3) | collective-permute-done | bytes 262176 | tf_op jit(solution)/shard_map/ppermute | solution.py:36
  10.2 5.6 %collective-permute-done.4.refs_2_ = bf16[16,8192]{1,0:T(8,128)(2,1)S(1)} collective-permute-done((bf16[16,8192]{1,0:T(8,128)(2,1)S(1)}, bf16[16,8192]{1,0:T(8,128)(2,1)S(1)}, u32[]{:S(2)}, u32[]{:S(2)}) %collective-permute-start.4) | collective-permute-done | bytes 262176 | tf_op jit(solution)/shard_map/ppermute | solution.py:36
  15.8 0.5 collective-permute-done.5.refs_3_
  16.3 8.0 %project_early.1 = bf16[32,16,1280]{2,1,0:T(8,128)(2,1)} custom-call(s32[32,128]{1,0:T(8,128)S(1)} %reshape.195.idx_ref, bf16[32,64,256]{2,1,0:T(8,128)(2,1)S(1)} %copy-done, bf16[16,8192]{1,0:T(8,128)(2,1)S(1)} %get-tuple-element.30.refs_0_, bf16[16,8192]{1,0:T(8,128)(2,1)S(1)} %collective-permute-done.3.refs_1_, ...), custom_call_target="tpu_custom_call" | custom-call | flops 10350000128 | bytes 900000 | tf_op jit(solution)/shard_map/project_early/pallas_call | solution.py:145
  24.3 6.5 %all-to-all-start = ((bf16[32,16,1280]{2,1,0:T(8,128)(2,1)}), bf16[32,16,1280]{2,1,0:T(8,128)(2,1)S(1)}, u32[]{:S(2)}, u32[]{:S(2)}) async-start(bf16[32,16,1280]{2,1,0:T(8,128)(2,1)} %project_early.1), calls=%async_computation | async-start | bytes 2621440 | tf_op jit(solution)/shard_map/all_to_all | solution.py:523
  30.9 2.8 %dynamic-slice_bitcast_fusion = (bf16[4,256,256]{2,1,0:T(8,128)(2,1)}, bf16[4,256,256]{2,1,0:T(8,128)(2,1)}, bf16[4,256,256]{2,1,0:T(8,128)(2,1)}, bf16[4,256,256]{2,1,0:T(8,128)(2,1)S(1)}) fusion(bf16[4,4,256,256]{3,2,1,0:T(8,128)(2,1)} %param.13, s32[]{:T(128)S(6)} %select_n.307, s32[]{:T(128)S(6)} %select_n.305, s32[]{:T(128)S(6)} %select_n.303, ...), kind=kLoop, calls=%fused_computation.11 | loop fusion | bytes 4194320 | tf_op jit(solution)/shard_map/jit(dynamic_index_in_dim)/squeeze | solution.py:552
  33.7 0.3 collective-permute-start.6
  34.0 6.3 %project_late.1 = bf16[32,16,768]{2,1,0:T(8,128)(2,1)} custom-call(s32[32,128]{1,0:T(8,128)S(1)} %reshape.195.idx_ref, bf16[32,64,256]{2,1,0:T(8,128)(2,1)S(1)} %copy-done, bf16[16,8192]{1,0:T(8,128)(2,1)S(1)} %get-tuple-element.30.refs_0_, bf16[16,8192]{1,0:T(8,128)(2,1)S(1)} %collective-permute-done.3.refs_1_, bf16[16,8192]{1,0:T(8,128)(2,1)S(1)} %copy-done.5, ...), custom_call_target="tpu_custom_call" | custom-call | flops 8049999872 | bytes 700000 | tf_op jit(solution)/shard_map/project_late/pallas_call | solution.py:145
  40.3 21.8 %all-to-all-done.sino_ref.early_ref = bf16[32,16,1280]{2,1,0:T(8,128)(2,1)S(1)} async-done(((bf16[32,16,1280]{2,1,0:T(8,128)(2,1)}), bf16[32,16,1280]{2,1,0:T(8,128)(2,1)S(1)}, u32[]{:S(2)}, u32[]{:S(2)}) %all-to-all-start) | async-done | bytes 1310752 | tf_op jit(solution)/shard_map/all_to_all | solution.py:523
  62.1 4.5 %all-to-all-start.1 = ((bf16[32,16,768]{2,1,0:T(8,128)(2,1)}), bf16[32,16,768]{2,1,0:T(8,128)(2,1)S(1)}, u32[]{:S(2)}, u32[]{:S(2)}) async-start(bf16[32,16,768]{2,1,0:T(8,128)(2,1)} %project_late.1), calls=%async_computation.1 | async-start | bytes 1572864 | tf_op jit(solution)/shard_map/all_to_all | solution.py:523
  66.6 0.1 copy.27
  66.7 0.1 pad_add_fusion.2
  66.8 1.7 collective-permute-start.2
  68.5 0.5 collective-permute-start
  69.0 0.2 collective-permute-done.2
  69.2 2.1 %collective-permute-done.1 = s32[1,5]{1,0:T(1,128)S(1)} collective-permute-done((s32[1,5]{1,0:T(1,128)S(1)}, s32[1,5]{1,0:T(1,128)S(1)}, u32[]{:S(2)}, u32[]{:S(2)}) %collective-permute-start.1) | collective-permute-done | bytes 52 | tf_op jit(solution)/shard_map/ppermute | solution.py:36
  71.2 0.3 collective-permute-done
  71.6 1.7 collective-permute-start.7
  73.3 0.7 collective-permute-start.8
  74.0 0.9 copy-done.2
  74.9 1.0 copy-done.8
  76.0 1.0 copy-done.10
  77.0 8.6 %exit_first.1 = (f32[2,256,256]{2,1,0:T(8,128)S(1)}, bf16[32,16,768]{2,1,0:T(8,128)(2,1)}, f32[2,256,256]{2,1,0:T(8,128)S(1)}) custom-call(s32[4,5]{1,0:T(4,128)S(1)} %pad_add_fusion.3.meta_ref, bf16[2,256,256]{2,1,0:T(8,128)(2,1)S(1)} %copy-done.2, bf16[512,512]{1,0:T(8,128)(2,1)S(1)} %copy-done.8, bf16[512,512]{1,0:T(8,128)(2,1)S(1)} %copy-done.10, ...), custom_call_target="tpu_custom_call" | custom-call | flops 11500000256 | bytes 1000000 | tf_op jit(solution)/shard_map/exit_first/pallas_call | solution.py:458
  85.6 0.8 copy-done.14
  86.4 0.8 copy-done.16
  87.2 6.9 %all-to-all-start.2 = ((bf16[32,16,768]{2,1,0:T(8,128)(2,1)}), bf16[32,16,768]{2,1,0:T(8,128)(2,1)S(1)}, u32[]{:S(2)}, u32[]{:S(2)}) async-start(bf16[32,16,768]{2,1,0:T(8,128)(2,1)} %get-tuple-element.38), calls=%async_computation.2 | async-start | bytes 1572864 | tf_op jit(solution)/shard_map/all_to_all | solution.py:523
  94.1 0.9 copy-done.3
  95.1 1.0 copy-done.9
  96.1 1.0 copy-done.11
  97.1 1.0 copy-done.15
  98.2 1.0 copy-done.17
  99.2 9.2 %exit_rest.1 = bf16[32,16,1280]{2,1,0:T(8,128)(2,1)} custom-call(s32[4,5]{1,0:T(4,128)S(1)} %pad_add_fusion.3.meta_ref, bf16[2,256,256]{2,1,0:T(8,128)(2,1)S(1)} %copy-done.3, bf16[512,512]{1,0:T(8,128)(2,1)S(1)} %copy-done.9, bf16[512,512]{1,0:T(8,128)(2,1)S(1)} %copy-done.11, bf16[32,16,1280]{2,1,0:T(8,128)(2,1)S(1)} %all-to-all-done.sino_ref.early_ref, ...), custom_call_target="tpu_custom_call" | custom-call | flops 11500000256 | bytes 1000000 | tf_op jit(solution)/shard_map/exit_rest/pallas_call | solution.py:474
  108.4 5.8 %all-to-all-done.2.grad_ref = bf16[32,16,768]{2,1,0:T(8,128)(2,1)S(1)} async-done(((bf16[32,16,768]{2,1,0:T(8,128)(2,1)}), bf16[32,16,768]{2,1,0:T(8,128)(2,1)S(1)}, u32[]{:S(2)}, u32[]{:S(2)}) %all-to-all-start.2) | async-done | bytes 786464 | tf_op jit(solution)/shard_map/all_to_all | solution.py:523
  114.2 4.1 %all-to-all-start.3 = ((bf16[32,16,1280]{2,1,0:T(8,128)(2,1)}), bf16[32,16,1280]{2,1,0:T(8,128)(2,1)S(1)}, u32[]{:S(2)}, u32[]{:S(2)}) async-start(bf16[32,16,1280]{2,1,0:T(8,128)(2,1)} %exit_rest.1), calls=%async_computation.3 | async-start | bytes 2621440 | tf_op jit(solution)/shard_map/all_to_all | solution.py:523
  118.3 0.3 copy.22
  118.6 0.2 reshape.192
  119.0 0.1 reshape.193.idx_ref
  119.1 2.0 %slice.101 = bf16[32,16,512]{2,1,0:T(8,128)(2,1)} slice(bf16[32,16,768]{2,1,0:T(8,128)(2,1)} %get-tuple-element.38), slice={[0:32], [0:16], [256:768]} | slice | bytes 1048576 | tf_op jit(solution)/shard_map/slice | solution.py:604
  121.1 1.0 slice.105
  122.0 1.7 collective-permute-start.12
  123.7 1.7 slice.128
  125.4 2.2 %fusion.9 = (bf16[32,16,512]{2,1,0:T(8,128)(2,1)}, bf16[32,16,512]{2,1,0:T(8,128)(2,1)}) fusion(bf16[32,16,1280]{2,1,0:T(8,128)(2,1)} %exit_rest.1), kind=kLoop, calls=%fused_computation.81 | loop fusion | bytes 2097152 | tf_op jit(solution)/shard_map/slice | solution.py:604
  127.6 0.5 collective-permute-start.14
  128.2 6.5 %back_first.1.refs_0_ = f32[512,8,128]{2,1,0:T(8,128)S(1)} custom-call(s32[32,128]{1,0:T(8,128)S(1)} %reshape.193.idx_ref, bf16[32,64,256]{2,1,0:T(8,128)(2,1)S(1)} %copy-done.1, bf16[32,16,768]{2,1,0:T(8,128)(2,1)S(1)} %all-to-all-done.2.grad_ref), custom_call_target="tpu_custom_call" | custom-call | flops 8049999872 | bytes 700000 | tf_op jit(solution)/shard_map/back_first/pallas_call | solution.py:261
  134.7 1.3 copy-done.12
  136.0 13.6 %all-to-all-done.3.grad_ref = bf16[32,16,1280]{2,1,0:T(8,128)(2,1)S(1)} async-done(((bf16[32,16,1280]{2,1,0:T(8,128)(2,1)}), bf16[32,16,1280]{2,1,0:T(8,128)(2,1)S(1)}, u32[]{:S(2)}, u32[]{:S(2)}) %all-to-all-start.3) | async-done | bytes 1310752 | tf_op jit(solution)/shard_map/all_to_all | solution.py:523
  149.7 1.6 copy-done.13
  151.2 9.2 %back_rest.1 = (bf16[16,8192]{1,0:T(8,128)(2,1)S(1)}, bf16[16,8192]{1,0:T(8,128)(2,1)S(1)}, bf16[16,8192]{1,0:T(8,128)(2,1)S(1)}, bf16[16,8192]{1,0:T(8,128)(2,1)S(1)}) custom-call(s32[32,128]{1,0:T(8,128)S(1)} %reshape.193.idx_ref, bf16[32,64,256]{2,1,0:T(8,128)(2,1)S(1)} %copy-done.1, bf16[32,16,1280]{2,1,0:T(8,128)(2,1)S(1)} %all-to-all-done.3.grad_ref, ...), custom_call_target="tpu_custom_call" | custom-call | flops 10350000128 | bytes 900000 | tf_op jit(solution)/shard_map/back_rest/pallas_call | solution.py:261
  160.5 1.9 %collective-permute-start.9 = (bf16[16,8192]{1,0:T(8,128)(2,1)S(1)}, bf16[16,8192]{1,0:T(8,128)(2,1)S(1)}, u32[]{:S(2)}, u32[]{:S(2)}) collective-permute-start(bf16[16,8192]{1,0:T(8,128)(2,1)S(1)} %get-tuple-element.44), channel_id=1, source_target_pairs={{0,1},{1,2},{2,3},{3,0},{4,5},{5,6},{6,7},{7,4},{8,9},{9,10},{10,1... | collective-permute-start | bytes 786440 | tf_op jit(solution)/shard_map/ppermute | solution.py:36
  162.4 0.7 collective-permute-start.10
  163.1 1.9 %select_bitcast_fusion.3 = (bf16[32,2,8,512]{3,2,1,0:T(8,128)(2,1)S(1)}, bf16[32,2,8,512]{3,2,1,0:T(8,128)(2,1)S(1)}, bf16[32,2,8,512]{3,2,1,0:T(8,128)(2,1)S(1)}, bf16[32,2,8,512]{3,2,1,0:T(8,128)(2,1)S(1)}) fusion(pred[]{:T(512)S(6)} %ne.93, bf16[32,16,512]{2,1,0:T(8,128)(2,1)} %collective-permute-done.12, ...), kind=kLoop, calls=%fused_computation.10 | loop fusion | flops 3145728 | bytes 4194306 | tf_op jit(solution)/shard_map/jit(_where)/select_n | solution.py:46
  165.2 0.3 maximum_convert_fusion
  165.5 4.7 %copy.37 = f32[2,256,4,512]{3,2,1,0:T(4,128)} copy(f32[2,256,4,512]{3,1,0,2:T(8,128)S(1)} %maximum_convert_fusion) | data formatting | bytes 8388608
  170.3 4.4 %collective-permute-done.10 = bf16[16,8192]{1,0:T(8,128)(2,1)S(1)} collective-permute-done((bf16[16,8192]{1,0:T(8,128)(2,1)S(1)}, bf16[16,8192]{1,0:T(8,128)(2,1)S(1)}, u32[]{:S(2)}, u32[]{:S(2)}) %collective-permute-start.10) | collective-permute-done | bytes 262176 | tf_op jit(solution)/shard_map/ppermute | solution.py:36
  174.6 0.6 collective-permute-done.11
  175.2 0.1 select_bitcast_fusion.7
  175.3 1.6 multiply_add_fusion
  (70 shorter events, 0.5 us)
Async XLA Ops:
  0.6 4.6 %copy-start.20 = (s32[32,32,4]{1,2,0:T(4,128)S(1)}, s32[32,32,4]{1,2,0:T(4,128)}, u32[]{:S(2)}) copy-start(s32[32,32,4]{1,2,0:T(4,128)} %param.11) | copy-start | bytes 49156
  0.7 15.7 %copy-start = (bf16[32,64,256]{2,1,0:T(8,128)(2,1)S(1)}, bf16[32,64,256]{2,1,0:T(8,128)(2,1)}, u32[]{:S(2)}) copy-start(bf16[32,64,256]{2,1,0:T(8,128)(2,1)} %radon_ref.7) | copy-start | bytes 3145732
  2.1 8.2 %collective-permute-start.3 = (bf16[16,8192]{1,0:T(8,128)(2,1)S(1)}, bf16[16,8192]{1,0:T(8,128)(2,1)S(1)}, u32[]{:S(2)}, u32[]{:S(2)}) collective-permute-start(bf16[16,8192]{1,0:T(8,128)(2,1)S(1)} %get-tuple-element.65), channel_id=1, source_target_pairs={{0,1},{1,2},{2,3},{3,0},{4,5},{5,6},{6,7},{7,4},{8,9},{9,10},{10,1... | collective-permute-start | bytes 786440 | tf_op jit(solution)/shard_map/ppermute | solution.py:36
  4.7 11.1 %collective-permute-start.4 = (bf16[16,8192]{1,0:T(8,128)(2,1)S(1)}, bf16[16,8192]{1,0:T(8,128)(2,1)S(1)}, u32[]{:S(2)}, u32[]{:S(2)}) collective-permute-start(bf16[16,8192]{1,0:T(8,128)(2,1)S(1)} %get-tuple-element.67), channel_id=1, source_target_pairs={{0,2},{1,3},{2,0},{3,1},{4,6},{5,7},{6,4},{7,5},{8,10},{9,11},{10,... | collective-permute-start | bytes 786440 | tf_op jit(solution)/shard_map/ppermute | solution.py:36
  4.7 11.6 %collective-permute-start.5 = (bf16[16,8192]{1,0:T(8,128)(2,1)S(1)}, bf16[16,8192]{1,0:T(8,128)(2,1)S(1)}, u32[]{:S(2)}, u32[]{:S(2)}) collective-permute-start(bf16[16,8192]{1,0:T(8,128)(2,1)S(1)} %get-tuple-element.64), channel_id=1, source_target_pairs={{0,3},{1,0},{2,1},{3,2},{4,7},{5,4},{6,5},{7,6},{8,11},{9,8},{10,9... | collective-permute-start | bytes 786440 | tf_op jit(solution)/shard_map/ppermute | solution.py:36
  15.8 8.5 %copy-start.4 = (bf16[16,8192]{1,0:T(8,128)(2,1)}, bf16[16,8192]{1,0:T(8,128)(2,1)S(1)}, u32[]{:S(2)}) copy-start(bf16[16,8192]{1,0:T(8,128)(2,1)S(1)} %collective-permute-done.4.refs_2_) | copy-start | bytes 786436
  16.3 8.0 %copy-start.6 = (bf16[16,8192]{1,0:T(8,128)(2,1)}, bf16[16,8192]{1,0:T(8,128)(2,1)S(1)}, u32[]{:S(2)}) copy-start(bf16[16,8192]{1,0:T(8,128)(2,1)S(1)} %collective-permute-done.5.refs_3_) | copy-start | bytes 786436
  24.3 37.8 %all-to-all-start = ((bf16[32,16,1280]{2,1,0:T(8,128)(2,1)}), bf16[32,16,1280]{2,1,0:T(8,128)(2,1)S(1)}, u32[]{:S(2)}, u32[]{:S(2)}) async-start(bf16[32,16,1280]{2,1,0:T(8,128)(2,1)} %project_early.1), calls=%async_computation | async-start | bytes 2621440 | tf_op jit(solution)/shard_map/all_to_all | solution.py:523
  30.9 3.1 %copy-start.5 = (bf16[16,8192]{1,0:T(8,128)(2,1)S(1)}, bf16[16,8192]{1,0:T(8,128)(2,1)}, u32[]{:S(2)}) copy-start(bf16[16,8192]{1,0:T(8,128)(2,1)} %copy-done.4) | copy-start | bytes 786436
  30.9 3.1 %copy-start.7 = (bf16[16,8192]{1,0:T(8,128)(2,1)S(1)}, bf16[16,8192]{1,0:T(8,128)(2,1)}, u32[]{:S(2)}) copy-start(bf16[16,8192]{1,0:T(8,128)(2,1)} %copy-done.6) | copy-start | bytes 786436
  33.7 32.8 %copy-start.22 = (s32[4,1]{0,1:T(1,128)S(1)}, s32[4,1]{0,1:T(1,128)}, u32[]{:S(2)}) copy-start(s32[4,1]{0,1:T(1,128)} %param.15) | copy-start | bytes 52
  33.7 33.0 %copy-start.21 = (s32[4,4]{1,0:T(4,128)S(1)}, s32[4,4]{1,0:T(4,128)}, u32[]{:S(2)}) copy-start(s32[4,4]{1,0:T(4,128)} %param.14) | copy-start | bytes 196
  33.7 40.2 %collective-permute-start.6 = (bf16[4,256,256]{2,1,0:T(8,128)(2,1)}, bf16[4,256,256]{2,1,0:T(8,128)(2,1)}, u32[]{:S(2)}, u32[]{:S(2)}) collective-permute-start(bf16[4,256,256]{2,1,0:T(8,128)(2,1)} %get-tuple-element.56), channel_id=1, source_target_pairs={{0,3},{1,0},{2,1},{3,2},{4,7},{5,4},{6,5},{7,6},{8,11},{9,8},{10,9... | collective-permute-start | bytes 1572872 | tf_op jit(solution)/shard_map/ppermute | solution.py:36
  62.1 25.1 %all-to-all-start.1 = ((bf16[32,16,768]{2,1,0:T(8,128)(2,1)}), bf16[32,16,768]{2,1,0:T(8,128)(2,1)S(1)}, u32[]{:S(2)}, u32[]{:S(2)}) async-start(bf16[32,16,768]{2,1,0:T(8,128)(2,1)} %project_late.1), calls=%async_computation.1 | async-start | bytes 1572864 | tf_op jit(solution)/shard_map/all_to_all | solution.py:523
  66.8 2.4 %collective-permute-start.2 = (s32[1,5]{1,0:T(1,128)S(1)}, s32[1,5]{1,0:T(1,128)S(1)}, u32[]{:S(2)}, u32[]{:S(2)}) collective-permute-start(s32[1,5]{1,0:T(1,128)S(1)} %get-tuple-element.83), channel_id=1, source_target_pairs={{0,1},{1,2},{2,3},{3,0},{4,5},{5,6},{6,7},{7,4},{8,9},{9,10},{10,1... | collective-permute-start | bytes 68 | tf_op jit(solution)/shard_map/ppermute | solution.py:36
  68.5 2.8 %collective-permute-start.1 = (s32[1,5]{1,0:T(1,128)S(1)}, s32[1,5]{1,0:T(1,128)S(1)}, u32[]{:S(2)}, u32[]{:S(2)}) collective-permute-start(s32[1,5]{1,0:T(1,128)S(1)} %get-tuple-element.84), channel_id=1, source_target_pairs={{0,2},{1,3},{2,0},{3,1},{4,6},{5,7},{6,4},{7,5},{8,10},{9,11},{10,... | collective-permute-start | bytes 68 | tf_op jit(solution)/shard_map/ppermute | solution.py:36
  68.5 3.1 %collective-permute-start = (s32[1,5]{1,0:T(1,128)S(1)}, s32[1,5]{1,0:T(1,128)S(1)}, u32[]{:S(2)}, u32[]{:S(2)}) collective-permute-start(s32[1,5]{1,0:T(1,128)S(1)} %get-tuple-element.85), channel_id=1, source_target_pairs={{0,3},{1,0},{2,1},{3,2},{4,7},{5,4},{6,5},{7,6},{8,11},{9,8},{10,9... | collective-permute-start | bytes 68 | tf_op jit(solution)/shard_map/ppermute | solution.py:36
  71.6 22.5 %collective-permute-start.7 = (bf16[4,256,256]{2,1,0:T(8,128)(2,1)}, bf16[4,256,256]{2,1,0:T(8,128)(2,1)S(1)}, u32[]{:S(2)}, u32[]{:S(2)}) collective-permute-start(bf16[4,256,256]{2,1,0:T(8,128)(2,1)} %get-tuple-element.55), channel_id=1, source_target_pairs={{0,2},{1,3},{2,0},{3,1},{4,6},{5,7},{6,4},{7,5},{8,10},{9,11},{10,... | collective-permute-start | bytes 1572872 | tf_op jit(solution)/shard_map/ppermute | solution.py:36
  73.3 20.8 %collective-permute-start.8 = (bf16[4,256,256]{2,1,0:T(8,128)(2,1)}, bf16[4,256,256]{2,1,0:T(8,128)(2,1)}, u32[]{:S(2)}, u32[]{:S(2)}) collective-permute-start(bf16[4,256,256]{2,1,0:T(8,128)(2,1)} %get-tuple-element.54), channel_id=1, source_target_pairs={{0,1},{1,2},{2,3},{3,0},{4,5},{5,6},{6,7},{7,4},{8,9},{9,10},{10,1... | collective-permute-start | bytes 1572872 | tf_op jit(solution)/shard_map/ppermute | solution.py:36
  74.0 1.0 copy-start.2
  74.9 1.0 copy-start.8
  76.0 1.0 copy-start.10
  85.6 0.8 copy-start.14
  86.4 0.8 copy-start.16
  87.2 27.1 %all-to-all-start.2 = ((bf16[32,16,768]{2,1,0:T(8,128)(2,1)}), bf16[32,16,768]{2,1,0:T(8,128)(2,1)S(1)}, u32[]{:S(2)}, u32[]{:S(2)}) async-start(bf16[32,16,768]{2,1,0:T(8,128)(2,1)} %get-tuple-element.38), calls=%async_computation.2 | async-start | bytes 1572864 | tf_op jit(solution)/shard_map/all_to_all | solution.py:523
  94.1 1.0 copy-start.3
  95.1 1.0 copy-start.9
  96.1 1.0 copy-start.11
  97.1 1.0 copy-start.15
  98.2 1.0 copy-start.17
  114.2 35.4 %all-to-all-start.3 = ((bf16[32,16,1280]{2,1,0:T(8,128)(2,1)}), bf16[32,16,1280]{2,1,0:T(8,128)(2,1)S(1)}, u32[]{:S(2)}, u32[]{:S(2)}) async-start(bf16[32,16,1280]{2,1,0:T(8,128)(2,1)} %exit_rest.1), calls=%async_computation.3 | async-start | bytes 2621440 | tf_op jit(solution)/shard_map/all_to_all | solution.py:523
  119.1 9.1 %copy-start.1 = (bf16[32,64,256]{2,1,0:T(8,128)(2,1)S(1)}, bf16[32,64,256]{2,1,0:T(8,128)(2,1)}, u32[]{:S(2)}) copy-start(bf16[32,64,256]{2,1,0:T(8,128)(2,1)} %radon_ref.7) | copy-start | bytes 3145732
  122.0 41.0 %collective-permute-start.12 = (bf16[32,16,512]{2,1,0:T(8,128)(2,1)}, bf16[32,16,512]{2,1,0:T(8,128)(2,1)}, u32[]{:S(2)}, u32[]{:S(2)}) collective-permute-start(bf16[32,16,512]{2,1,0:T(8,128)(2,1)} %slice.101), channel_id=1, source_target_pairs={{0,1},{1,2},{2,3},{3,0},{4,5},{5,6},{6,7},{7,4},{8,9},{9,10},{10,1... | collective-permute-start | bytes 1572872 | tf_op jit(solution)/shard_map/ppermute | solution.py:36
  127.6 35.4 %collective-permute-start.13 = (bf16[32,16,512]{2,1,0:T(8,128)(2,1)}, bf16[32,16,512]{2,1,0:T(8,128)(2,1)}, u32[]{:S(2)}, u32[]{:S(2)}) collective-permute-start(bf16[32,16,512]{2,1,0:T(8,128)(2,1)} %get-tuple-element.59), channel_id=1, source_target_pairs={{0,2},{1,3},{2,0},{3,1},{4,6},{5,7},{6,4},{7,5},{8,10},{9,11},{10,... | collective-permute-start | bytes 1572872 | tf_op jit(solution)/shard_map/ppermute | solution.py:36
  127.6 35.4 %collective-permute-start.14 = (bf16[32,16,512]{2,1,0:T(8,128)(2,1)}, bf16[32,16,512]{2,1,0:T(8,128)(2,1)}, u32[]{:S(2)}, u32[]{:S(2)}) collective-permute-start(bf16[32,16,512]{2,1,0:T(8,128)(2,1)} %get-tuple-element.58), channel_id=1, source_target_pairs={{0,3},{1,0},{2,1},{3,2},{4,7},{5,4},{6,5},{7,6},{8,11},{9,8},{10,9... | collective-permute-start | bytes 1572872 | tf_op jit(solution)/shard_map/ppermute | solution.py:36
  134.7 1.3 copy-start.12
  149.7 1.6 copy-start.13
  151.2 11.8 %copy-start.19 = (bf16[32,16,256]{2,1,0:T(8,128)(2,1)S(1)}, bf16[32,16,256]{2,1,0:T(8,128)(2,1)}, u32[]{:S(2)}) copy-start(bf16[32,16,256]{2,1,0:T(8,128)(2,1)} %slice.128) | copy-start | bytes 786436
  160.5 9.8 %collective-permute-start.9 = (bf16[16,8192]{1,0:T(8,128)(2,1)S(1)}, bf16[16,8192]{1,0:T(8,128)(2,1)S(1)}, u32[]{:S(2)}, u32[]{:S(2)}) collective-permute-start(bf16[16,8192]{1,0:T(8,128)(2,1)S(1)} %get-tuple-element.44), channel_id=1, source_target_pairs={{0,1},{1,2},{2,3},{3,0},{4,5},{5,6},{6,7},{7,4},{8,9},{9,10},{10,1... | collective-permute-start | bytes 786440 | tf_op jit(solution)/shard_map/ppermute | solution.py:36
  162.4 12.2 %collective-permute-start.10 = (bf16[16,8192]{1,0:T(8,128)(2,1)S(1)}, bf16[16,8192]{1,0:T(8,128)(2,1)S(1)}, u32[]{:S(2)}, u32[]{:S(2)}) collective-permute-start(bf16[16,8192]{1,0:T(8,128)(2,1)S(1)} %get-tuple-element.45), channel_id=1, source_target_pairs={{0,2},{1,3},{2,0},{3,1},{4,6},{5,7},{6,4},{7,5},{8,10},{9,11},{10,... | collective-permute-start | bytes 786440 | tf_op jit(solution)/shard_map/ppermute | solution.py:36
  163.0 12.2 %collective-permute-start.11 = (bf16[16,8192]{1,0:T(8,128)(2,1)S(1)}, bf16[16,8192]{1,0:T(8,128)(2,1)S(1)}, u32[]{:S(2)}, u32[]{:S(2)}) collective-permute-start(bf16[16,8192]{1,0:T(8,128)(2,1)S(1)} %get-tuple-element.46), channel_id=1, source_target_pairs={{0,3},{1,0},{2,1},{3,2},{4,7},{5,4},{6,5},{7,6},{8,11},{9,8},{10,9... | collective-permute-start | bytes 786440 | tf_op jit(solution)/shard_map/ppermute | solution.py:36
  170.3 5.1 %copy-start.18 = (bf16[2,32,8192]{2,1,0:T(8,128)(2,1)S(1)}, bf16[2,32,8192]{2,1,0:T(8,128)(2,1)}, u32[]{:S(2)}) copy-start(bf16[2,32,8192]{2,1,0:T(8,128)(2,1)} %param.9) | copy-start | bytes 3145732

commit v7 on v6

--- a/solution.py
+++ b/solution.py
@@ -16,7 +16,7 @@
 MEBI = 1024 * 1024
 everywhere = pl.BlockSpec(memory_space=pltpu.VMEM)
 scalars = pl.BlockSpec(memory_space=pltpu.SMEM)
-CHAINS = 8
+CHAINS = 4
 BATCH = 4
 
 
@@ -161,6 +161,10 @@
     start_ref, refs = (refs[0], refs[1:]) if has_start else (None, refs)
     out_refs, refs = refs[:outs], refs[outs:]
     acc_refs, (w_ref, *contrib_refs) = refs[:CHAINS], refs[CHAINS:]
+    if has_start:
+        contrib_refs, start_sem = contrib_refs[:-1], contrib_refs[-1]
+        start_copy = pltpu.make_async_copy(start_ref, acc_refs[0], start_sem)
+        start_copy.start()
     angles, block, span = radon_ref.shape
     pairs = len(blocks) // 2
     feeds = span // block
@@ -168,11 +172,8 @@
 
     @pl.loop(0, coef_blocks, unroll=16)
     def _(t):
-        for n, acc_ref in enumerate(acc_refs):
-            if n == 0 and has_start:
-                acc_ref[t] = start_ref[t]
-            else:
-                acc_ref[t] = jnp.zeros((GROUP, LANES), jnp.float32)
+        for acc_ref in acc_refs[1:] if has_start else acc_refs:
+            acc_ref[t] = jnp.zeros((GROUP, LANES), jnp.float32)
 
     low = lower_half((GROUP, LANES))
     low_rows = lower_half((block, LANES))
@@ -213,6 +214,8 @@
                     acc_refs[n][idx_ref[start + n, b * feeds + j]] += tile
 
     multiply(0, 0, contrib_refs[0])
+    if has_start:
+        start_copy.wait()
 
     @pl.loop(0, angles // (2 * CHAINS))
     def _(step):
@@ -261,14 +264,13 @@
     return pl.pallas_call(
         functools.partial(back_project_kernel, blocks, has_start, len(out_shape)),
         out_shape=out_shape,
-        in_specs=[scalars] + [everywhere] * (len(operands) - 1),
+        in_specs=[scalars] + [everywhere] * 2 + [pl.BlockSpec(memory_space=pl.ANY)] * has_start,
         out_specs=[everywhere] * len(out_shape),
         scratch_shapes=[pltpu.VMEM((coef_blocks, GROUP, LANES), jnp.float32)] * CHAINS
         + [pltpu.VMEM((2 * CHAINS, 2 * block, 2 * span), jnp.bfloat16)]
-        + [pltpu.VMEM((CHAINS, rows, 2 * span), jnp.float32)] * 2,
-        compiler_params=pltpu.CompilerParams(
-            vmem_limit_bytes=34 * MEBI + 2 * radon_tiles.size + 2 * grads.size
-        ),
+        + [pltpu.VMEM((CHAINS, rows, 2 * span), jnp.float32)] * 2
+        + [pltpu.SemaphoreType.DMA] * has_start,
+        compiler_params=pltpu.CompilerParams(vmem_limit_bytes=60 * MEBI),
         cost_estimate=guess(4 + len(blocks) // 4),
         name=name,
     )(*operands)
@@ -461,7 +463,7 @@
         in_specs=[scalars] + [everywhere] * (4 + len(amps)),
         out_specs=[everywhere] * 3,
         scratch_shapes=exit_scratch(groups, width, reach),
-        compiler_params=pltpu.CompilerParams(vmem_limit_bytes=28 * MEBI),
+        compiler_params=pltpu.CompilerParams(vmem_limit_bytes=60 * MEBI),
         cost_estimate=guess(10),
         name="exit_first",
     )(meta, probe_field, *tables, sino, *amps)
@@ -478,7 +480,7 @@
         out_specs=everywhere,
         scratch_shapes=[pltpu.VMEM((groups, rows, reach), jnp.bfloat16)]
         + exit_scratch(groups, width, reach),
-        compiler_params=pltpu.CompilerParams(vmem_limit_bytes=30 * MEBI),
+        compiler_params=pltpu.CompilerParams(vmem_limit_bytes=60 * MEBI),
         cost_estimate=guess(10),
         name="exit_rest",
     )(meta, probe_field, *tables, early, late, partial, spill, *amps)
@@ -541,11 +543,6 @@
         return lax.dynamic_slice_in_dim(volume, start, own, 1).reshape(rows, width)
 
     vol_pieces = rotate_pos([slices_for(j) for j in range(n_pos)], 1)
-    meta = jnp.concatenate([offsets, counts], axis=1)
-    meta = rotate_pos(
-        [lax.dynamic_slice_in_dim(meta, (pos - j) % n_pos, 1, 0) for j in range(n_pos)], -1
-    )
-    meta = jnp.concatenate(meta, axis=0)
     vol_pieces, amplitudes = lax.optimization_barrier((vol_pieces, amplitudes))
     amp_pieces = rotate_pos(
         [
@@ -580,12 +577,21 @@
     rest_blocks = list(range(half * tile_width // block_size, det_blocks)) + list(range(edge))
 
     sino_early = project(tile_idx, radon_tiles, padded, early_blocks, "project_early")
-    sino_early, padded = lax.optimization_barrier((sino_early, padded))
+    sino_early, padded, offsets, counts = lax.optimization_barrier(
+        (sino_early, padded, offsets, counts)
+    )
+    meta = jnp.concatenate([offsets, counts], axis=1)
+    meta = rotate_pos(
+        [lax.dynamic_slice_in_dim(meta, (pos - j) % n_pos, 1, 0) for j in range(n_pos)], -1
+    )
+    meta = jnp.concatenate(meta, axis=0)
+    padded, meta = lax.optimization_barrier((padded, meta))
     sino_late = project(tile_idx, radon_tiles, padded, late_blocks, "project_late")
     got_early = everyone(cut_rows(sino_early, own))
     got_early, sino_late = lax.optimization_barrier((got_early, sino_late))
     got_late = everyone(cut_rows(sino_late, own))
     got_early, got_late = to_groups(got_early, own), to_groups(got_late, own)
+    got_early, amp_pieces = lax.optimization_barrier((got_early, amp_pieces))
     partial, first_grad, spill = exit_first(meta, probe_field, tables, got_early, amp_pieces[:half])
     first_sent, got_late = lax.optimization_barrier((first_grad, got_late))
     rest_grad = exit_rest(

time: 178 us -> 174 us (0.978)
  local copies, waits for them, and re-layouts: 29.9 us -> 12.2 us
  waiting for transfers between devices: 58.9 us -> 72 us
  Pallas kernels: 47.8 us -> 51.9 us
  starting transfers between devices: 34.8 us -> 32.2 us
    unnamed x50 -> x25, local copies, waits for them, and re-layouts: 17.5 us -> 4.79 us
    all_to_all x4, waiting for transfers between devices: 41.2 us -> 53.6 us  [everyone(): return lax.all_to_all(chunk, ('ang', 'pos'), 0, 0, tiled=True)]
    slice x2, local copies, waits for them, and re-layouts: 4.21 us -> 0.99 us  [on_device(): tile_pieces.append(source[:, :, begin:begin + tile_width])]
    all_to_all x4, starting transfers between devices: 22 us -> 19.1 us  [everyone(): return lax.all_to_all(chunk, ('ang', 'pos'), 0, 0, tiled=True)]
  transfers between devices with their start and end apart: 19 -> 19, of which waited for: 11 -> 10; matrix products, arithmetic and copies ran while one was open for 11% -> 7% of each run, Pallas kernels for 23% -> 25%
where the time goes in v7:
time: 174 us; the launch traced here: 173 us
  waiting for transfers between devices  72 us (41%)
  Pallas kernels  51.9 us (30%)
  starting transfers between devices  32.2 us (19%)
  local copies, waits for them, and re-layouts  12.2 us (7%)
  other arithmetic  3.67 us (2%)
    all_to_all x4, waiting for transfers between devices, everyone(): return lax.all_to_all(chunk, ('ang', 'pos'), 0, 0, tiled=True)  53.6 us
    all_to_all x4, starting transfers between devices, everyone(): return lax.all_to_all(chunk, ('ang', 'pos'), 0, 0, tiled=True)  19.1 us
    ppermute x15, waiting for transfers between devices, rotate_pos(): lax.ppermute(pieces[j], 'pos', [(i, (i + sign * j) % count) for i in rang...  18.4 us
    pallas_call x2, Pallas kernels, back_project(): pl.pallas_call(functools.partial(back_project_kernel, blocks, has_start,...  17.1 us
    pallas_call x2, Pallas kernels, project(): pl.pallas_call(functools.partial(project_kernel, blocks, pieces), out_sha...  14.3 us
    ppermute x15, starting transfers between devices, rotate_pos(): lax.ppermute(pieces[j], 'pos', [(i, (i + sign * j) % count) for i in rang...  13.1 us
    pallas_call x1, Pallas kernels, exit_rest(): pl.pallas_call(functools.partial(exit_rest_kernel, len(amps)), out_shape=...  10.6 us
    pallas_call x1, Pallas kernels, exit_first(): pl.pallas_call(functools.partial(exit_first_kernel, len(amps)), out_shape...  9.89 us
  transfers between devices with their start and end apart: 19, of which 10 were waited for; matrix products, arithmetic and copies ran while one was open for 7% of the time, Pallas kernels for 25%

profile of v7, /device:TPU:1, one launch (start us, length us, event | category | flops | bytes accessed | tf_op | source)
XLA Modules:
  0.0 173.1 jit_solution(12186342301077834449)
XLA Ops:
  0.7 0.0 copy-start
  0.7 1.3 dynamic-slice_bitcast_fusion.4
  2.1 2.7 %collective-permute-start = (bf16[16,8192]{1,0:T(8,128)(2,1)S(1)}, bf16[16,8192]{1,0:T(8,128)(2,1)S(1)}, u32[]{:S(2)}, u32[]{:S(2)}) collective-permute-start(bf16[16,8192]{1,0:T(8,128)(2,1)S(1)} %get-tuple-element.89), channel_id=1, source_target_pairs={{0,1},{1,2},{2,3},{3,0},{4,5},{5,6},{6,7},{7,4},{8,9},{9,10},{10,1... | collective-permute-start | bytes 786440 | tf_op jit(solution)/shard_map/ppermute | solution.py:36
  4.7 0.0 collective-permute-start.1
  4.7 0.5 collective-permute-start.2
  5.2 0.3 fusion.5
  5.5 0.3 copy.27
  5.8 0.2 reshape.194
  6.2 0.1 reshape.195.idx_ref
  6.3 4.0 %collective-permute-done.refs_1_ = bf16[16,8192]{1,0:T(8,128)(2,1)S(1)} collective-permute-done((bf16[16,8192]{1,0:T(8,128)(2,1)S(1)}, bf16[16,8192]{1,0:T(8,128)(2,1)S(1)}, u32[]{:S(2)}, u32[]{:S(2)}) %collective-permute-start) | collective-permute-done | bytes 262176 | tf_op jit(solution)/shard_map/ppermute | solution.py:36
  10.2 5.6 %collective-permute-done.1.refs_2_ = bf16[16,8192]{1,0:T(8,128)(2,1)S(1)} collective-permute-done((bf16[16,8192]{1,0:T(8,128)(2,1)S(1)}, bf16[16,8192]{1,0:T(8,128)(2,1)S(1)}, u32[]{:S(2)}, u32[]{:S(2)}) %collective-permute-start.1) | collective-permute-done | bytes 262176 | tf_op jit(solution)/shard_map/ppermute | solution.py:36
  15.8 0.5 collective-permute-done.2.refs_3_
  16.3 8.0 %project_early.1 = bf16[32,16,1280]{2,1,0:T(8,128)(2,1)} custom-call(s32[32,128]{1,0:T(8,128)S(1)} %reshape.195.idx_ref, bf16[32,64,256]{2,1,0:T(8,128)(2,1)S(1)} %copy-done, bf16[16,8192]{1,0:T(8,128)(2,1)S(1)} %get-tuple-element.49.refs_0_, bf16[16,8192]{1,0:T(8,128)(2,1)S(1)} %collective-permute-done.refs_1_, ...), custom_call_target="tpu_custom_call" | custom-call | flops 10350000128 | bytes 900000 | tf_op jit(solution)/shard_map/project_early/pallas_call | solution.py:145
  24.3 6.5 %all-to-all-start = ((bf16[32,16,1280]{2,1,0:T(8,128)(2,1)}), bf16[32,16,1280]{2,1,0:T(8,128)(2,1)S(1)}, u32[]{:S(2)}, u32[]{:S(2)}) async-start(bf16[32,16,1280]{2,1,0:T(8,128)(2,1)} %project_early.1), calls=%async_computation | async-start | bytes 2621440 | tf_op jit(solution)/shard_map/all_to_all | solution.py:525
  30.9 0.1 copy.32
  31.0 0.1 pad_add_fusion.2
  31.1 1.7 collective-permute-start.5
  32.8 0.0 collective-permute-start.4
  32.8 0.5 collective-permute-start.3
  33.3 2.9 %dynamic-slice_bitcast_fusion = (bf16[4,256,256]{2,1,0:T(8,128)(2,1)}, bf16[4,256,256]{2,1,0:T(8,128)(2,1)}, bf16[4,256,256]{2,1,0:T(8,128)(2,1)}, bf16[4,256,256]{2,1,0:T(8,128)(2,1)}) fusion(bf16[4,4,256,256]{3,2,1,0:T(8,128)(2,1)} %param.13, s32[]{:T(128)S(6)} %select_n.316, s32[]{:T(128)S(6)} %select_n.314, s32[]{:T(128)S(6)} %select_n.312, s32[]{:T(128)S(6)} %select_n.310), kind=kLoop, calls=%fused_computation.11 | loop fusion | bytes 4194320 | tf_op jit(solution)/shard_map/jit(dynamic_index_in_dim)/squeeze | solution.py:549
  36.3 1.3 collective-permute-start.6
  37.6 0.0 collective-permute-start.7
  37.6 0.0 collective-permute-done.5
  37.6 1.6 collective-permute-start.8
  39.2 0.0 collective-permute-done.4
  39.2 0.0 collective-permute-done.3
  39.2 0.6 pad_add_fusion.3.meta_ref
  39.8 6.3 %project_late.1 = bf16[32,16,768]{2,1,0:T(8,128)(2,1)} custom-call(s32[32,128]{1,0:T(8,128)S(1)} %reshape.195.idx_ref, bf16[32,64,256]{2,1,0:T(8,128)(2,1)S(1)} %copy-done, bf16[16,8192]{1,0:T(8,128)(2,1)S(1)} %get-tuple-element.49.refs_0_, bf16[16,8192]{1,0:T(8,128)(2,1)S(1)} %collective-permute-done.refs_1_, ...), custom_call_target="tpu_custom_call" | custom-call | flops 8049999872 | bytes 700000 | tf_op jit(solution)/shard_map/project_late/pallas_call | solution.py:145
  46.1 16.1 %all-to-all-done.sino_ref.early_ref = bf16[32,16,1280]{2,1,0:T(8,128)(2,1)S(1)} async-done(((bf16[32,16,1280]{2,1,0:T(8,128)(2,1)}), bf16[32,16,1280]{2,1,0:T(8,128)(2,1)S(1)}, u32[]{:S(2)}, u32[]{:S(2)}) %all-to-all-start) | async-done | bytes 1310752 | tf_op jit(solution)/shard_map/all_to_all | solution.py:525
  62.2 4.4 %all-to-all-start.1 = ((bf16[32,16,768]{2,1,0:T(8,128)(2,1)}), bf16[32,16,768]{2,1,0:T(8,128)(2,1)S(1)}, u32[]{:S(2)}, u32[]{:S(2)}) async-start(bf16[32,16,768]{2,1,0:T(8,128)(2,1)} %project_late.1), calls=%async_computation.1 | async-start | bytes 1572864 | tf_op jit(solution)/shard_map/all_to_all | solution.py:525
  66.6 0.0 collective-permute-done.6.refs_1_
  66.6 0.0 collective-permute-done.7.refs_0_
  66.6 1.7 collective-permute-done.8.refs_1_
  68.3 9.9 %exit_first.1 = (f32[2,256,256]{2,1,0:T(8,128)}, bf16[32,16,768]{2,1,0:T(8,128)(2,1)}, f32[2,256,256]{2,1,0:T(8,128)}) custom-call(s32[4,5]{1,0:T(4,128)} %pad_add_fusion.3.meta_ref, bf16[2,256,256]{2,1,0:T(8,128)(2,1)} %probe_ref.3, bf16[512,512]{1,0:T(8,128)(2,1)} %constant.148.forward_ref, bf16[512,512]{1,0:T(8,128)(2,1)} %constant.151.inverse_ref, ...), custom_call_target="tpu_custom_call" | custom-call | flops 11500000256 | bytes 1000000 | tf_op jit(solution)/shard_map/exit_first/pallas_call | solution.py:460
  78.2 8.5 %all-to-all-done.1.late_ref = bf16[32,16,768]{2,1,0:T(8,128)(2,1)S(1)} async-done(((bf16[32,16,768]{2,1,0:T(8,128)(2,1)}), bf16[32,16,768]{2,1,0:T(8,128)(2,1)S(1)}, u32[]{:S(2)}, u32[]{:S(2)}) %all-to-all-start.1) | async-done | bytes 786464 | tf_op jit(solution)/shard_map/all_to_all | solution.py:525
  86.7 4.1 %all-to-all-start.2 = ((bf16[32,16,768]{2,1,0:T(8,128)(2,1)}), bf16[32,16,768]{2,1,0:T(8,128)(2,1)S(1)}, u32[]{:S(2)}, u32[]{:S(2)}) async-start(bf16[32,16,768]{2,1,0:T(8,128)(2,1)} %get-tuple-element.60), calls=%async_computation.2 | async-start | bytes 1572864 | tf_op jit(solution)/shard_map/all_to_all | solution.py:525
  90.8 10.6 %exit_rest.1 = bf16[32,16,1280]{2,1,0:T(8,128)(2,1)} custom-call(s32[4,5]{1,0:T(4,128)} %pad_add_fusion.3.meta_ref, bf16[2,256,256]{2,1,0:T(8,128)(2,1)} %probe_ref.3, bf16[512,512]{1,0:T(8,128)(2,1)} %constant.148.forward_ref, bf16[512,512]{1,0:T(8,128)(2,1)} %constant.151.inverse_ref, bf16[32,16,1280]{2,1,0:T(8,128)(2,1)} %copy-done.4, ...), custom_call_target="tpu_custom_call" | custom-call | flops 11500000256 | bytes 1000000 | tf_op jit(solution)/shard_map/exit_rest/pallas_call | solution.py:476
  101.4 9.6 %all-to-all-done.2.grad_ref = bf16[32,16,768]{2,1,0:T(8,128)(2,1)S(1)} async-done(((bf16[32,16,768]{2,1,0:T(8,128)(2,1)}), bf16[32,16,768]{2,1,0:T(8,128)(2,1)S(1)}, u32[]{:S(2)}, u32[]{:S(2)}) %all-to-all-start.2) | async-done | bytes 786464 | tf_op jit(solution)/shard_map/all_to_all | solution.py:525
  111.0 4.1 %all-to-all-start.3 = ((bf16[32,16,1280]{2,1,0:T(8,128)(2,1)}), bf16[32,16,1280]{2,1,0:T(8,128)(2,1)}, u32[]{:S(2)}, u32[]{:S(2)}) async-start(bf16[32,16,1280]{2,1,0:T(8,128)(2,1)} %exit_rest.1), calls=%async_computation.3 | async-start | bytes 2621440 | tf_op jit(solution)/shard_map/all_to_all | solution.py:525
  115.1 0.0 copy-start.1
  115.1 0.3 copy.22
  115.4 0.2 reshape.192
  115.8 0.7 reshape.193.idx_ref
  116.5 0.1 slice.101
  116.6 1.7 collective-permute-start.12
  118.3 0.9 fusion.9
  119.2 0.0 collective-permute-start.13
  119.3 0.5 collective-permute-start.14
  119.8 7.2 %back_first.1.refs_0_ = f32[512,8,128]{2,1,0:T(8,128)} custom-call(s32[32,128]{1,0:T(8,128)} %reshape.193.idx_ref, bf16[32,64,256]{2,1,0:T(8,128)(2,1)} %radon_ref.7, bf16[32,16,768]{2,1,0:T(8,128)(2,1)} %copy-done.5), custom_call_target="tpu_custom_call" | custom-call | flops 8049999872 | bytes 700000 | tf_op jit(solution)/shard_map/back_first/pallas_call | solution.py:264
  127.0 19.5 %all-to-all-done.3.grad_ref = bf16[32,16,1280]{2,1,0:T(8,128)(2,1)} async-done(((bf16[32,16,1280]{2,1,0:T(8,128)(2,1)}), bf16[32,16,1280]{2,1,0:T(8,128)(2,1)}, u32[]{:S(2)}, u32[]{:S(2)}) %all-to-all-start.3) | async-done | bytes 1310752 | tf_op jit(solution)/shard_map/all_to_all | solution.py:525
  146.5 9.9 %back_rest.1 = (bf16[16,8192]{1,0:T(8,128)(2,1)}, bf16[16,8192]{1,0:T(8,128)(2,1)}, bf16[16,8192]{1,0:T(8,128)(2,1)}, bf16[16,8192]{1,0:T(8,128)(2,1)}) custom-call(s32[32,128]{1,0:T(8,128)} %reshape.193.idx_ref, bf16[32,64,256]{2,1,0:T(8,128)(2,1)} %radon_ref.7, bf16[32,16,1280]{2,1,0:T(8,128)(2,1)} %all-to-all-done.3.grad_ref, ...), custom_call_target="tpu_custom_call" | custom-call | flops 10350000128 | bytes 900000 | tf_op jit(solution)/shard_map/back_rest/pallas_call | solution.py:264
  156.4 1.9 %collective-permute-start.9 = (bf16[16,8192]{1,0:T(8,128)(2,1)}, bf16[16,8192]{1,0:T(8,128)(2,1)S(1)}, u32[]{:S(2)}, u32[]{:S(2)}) collective-permute-start(bf16[16,8192]{1,0:T(8,128)(2,1)} %get-tuple-element.68), channel_id=1, source_target_pairs={{0,1},{1,2},{2,3},{3,0},{4,5},{5,6},{6,7},{7,4},{8,9},{9,10},{10,1... | collective-permute-start | bytes 786440 | tf_op jit(solution)/shard_map/ppermute | solution.py:36
  158.3 0.7 collective-permute-start.10
  159.0 0.0 collective-permute-done.12
  159.0 0.0 collective-permute-start.11
  159.0 0.0 collective-permute-done.13
  159.0 0.6 select_bitcast_fusion.3
  159.8 0.3 maximum_convert_fusion
  160.1 4.7 %copy.37 = f32[2,256,4,512]{3,2,1,0:T(4,128)} copy(f32[2,256,4,512]{3,1,0,2:T(8,128)S(1)} %maximum_convert_fusion) | data formatting | bytes 8388608
  164.8 0.0 collective-permute-done.9
  164.8 5.9 %collective-permute-done.10 = bf16[16,8192]{1,0:T(8,128)(2,1)S(1)} collective-permute-done((bf16[16,8192]{1,0:T(8,128)(2,1)}, bf16[16,8192]{1,0:T(8,128)(2,1)S(1)}, u32[]{:S(2)}, u32[]{:S(2)}) %collective-permute-start.10) | collective-permute-done | bytes 262176 | tf_op jit(solution)/shard_map/ppermute | solution.py:36
  170.8 0.6 collective-permute-done.11
  171.4 0.1 select_bitcast_fusion.7
  171.5 1.6 multiply_add_fusion
  (46 shorter events, 0.4 us)
Async XLA Ops:
  0.6 4.6 %copy-start.8 = (s32[32,32,4]{1,2,0:T(4,128)S(1)}, s32[32,32,4]{1,2,0:T(4,128)}, u32[]{:S(2)}) copy-start(s32[32,32,4]{1,2,0:T(4,128)} %param.11) | copy-start | bytes 49156
  0.7 15.7 %copy-start = (bf16[32,64,256]{2,1,0:T(8,128)(2,1)S(1)}, bf16[32,64,256]{2,1,0:T(8,128)(2,1)}, u32[]{:S(2)}) copy-start(bf16[32,64,256]{2,1,0:T(8,128)(2,1)} %radon_ref.7) | copy-start | bytes 3145732
  2.1 8.2 %collective-permute-start = (bf16[16,8192]{1,0:T(8,128)(2,1)S(1)}, bf16[16,8192]{1,0:T(8,128)(2,1)S(1)}, u32[]{:S(2)}, u32[]{:S(2)}) collective-permute-start(bf16[16,8192]{1,0:T(8,128)(2,1)S(1)} %get-tuple-element.89), channel_id=1, source_target_pairs={{0,1},{1,2},{2,3},{3,0},{4,5},{5,6},{6,7},{7,4},{8,9},{9,10},{10,1... | collective-permute-start | bytes 786440 | tf_op jit(solution)/shard_map/ppermute | solution.py:36
  4.7 11.1 %collective-permute-start.1 = (bf16[16,8192]{1,0:T(8,128)(2,1)S(1)}, bf16[16,8192]{1,0:T(8,128)(2,1)S(1)}, u32[]{:S(2)}, u32[]{:S(2)}) collective-permute-start(bf16[16,8192]{1,0:T(8,128)(2,1)S(1)} %get-tuple-element.91), channel_id=1, source_target_pairs={{0,2},{1,3},{2,0},{3,1},{4,6},{5,7},{6,4},{7,5},{8,10},{9,11},{10,... | collective-permute-start | bytes 786440 | tf_op jit(solution)/shard_map/ppermute | solution.py:36
  4.7 11.6 %collective-permute-start.2 = (bf16[16,8192]{1,0:T(8,128)(2,1)S(1)}, bf16[16,8192]{1,0:T(8,128)(2,1)S(1)}, u32[]{:S(2)}, u32[]{:S(2)}) collective-permute-start(bf16[16,8192]{1,0:T(8,128)(2,1)S(1)} %get-tuple-element.88), channel_id=1, source_target_pairs={{0,3},{1,0},{2,1},{3,2},{4,7},{5,4},{6,5},{7,6},{8,11},{9,8},{10,9... | collective-permute-start | bytes 786440 | tf_op jit(solution)/shard_map/ppermute | solution.py:36
  24.3 6.6 %copy-start.10 = (s32[4,1]{0,1:T(1,128)S(1)}, s32[4,1]{0,1:T(1,128)}, u32[]{:S(2)}) copy-start(s32[4,1]{0,1:T(1,128)} %param.15) | copy-start | bytes 52
  24.3 6.7 %copy-start.9 = (s32[4,4]{1,0:T(4,128)S(1)}, s32[4,4]{1,0:T(4,128)}, u32[]{:S(2)}) copy-start(s32[4,4]{1,0:T(4,128)} %param.14) | copy-start | bytes 196
  24.3 37.9 %all-to-all-start = ((bf16[32,16,1280]{2,1,0:T(8,128)(2,1)}), bf16[32,16,1280]{2,1,0:T(8,128)(2,1)S(1)}, u32[]{:S(2)}, u32[]{:S(2)}) async-start(bf16[32,16,1280]{2,1,0:T(8,128)(2,1)} %project_early.1), calls=%async_computation | async-start | bytes 2621440 | tf_op jit(solution)/shard_map/all_to_all | solution.py:525
  31.1 6.5 %collective-permute-start.5 = (s32[1,5]{1,0:T(1,128)S(1)}, s32[1,5]{1,0:T(1,128)S(1)}, u32[]{:S(2)}, u32[]{:S(2)}) collective-permute-start(s32[1,5]{1,0:T(1,128)S(1)} %get-tuple-element.107), channel_id=1, source_target_pairs={{0,1},{1,2},{2,3},{3,0},{4,5},{5,6},{6,7},{7,4},{8,9},{9,10},{10,1... | collective-permute-start | bytes 68 | tf_op jit(solution)/shard_map/ppermute | solution.py:36
  32.8 6.4 %collective-permute-start.4 = (s32[1,5]{1,0:T(1,128)S(1)}, s32[1,5]{1,0:T(1,128)S(1)}, u32[]{:S(2)}, u32[]{:S(2)}) collective-permute-start(s32[1,5]{1,0:T(1,128)S(1)} %get-tuple-element.108), channel_id=1, source_target_pairs={{0,2},{1,3},{2,0},{3,1},{4,6},{5,7},{6,4},{7,5},{8,10},{9,11},{10,... | collective-permute-start | bytes 68 | tf_op jit(solution)/shard_map/ppermute | solution.py:36
  32.8 6.4 %collective-permute-start.3 = (s32[1,5]{1,0:T(1,128)S(1)}, s32[1,5]{1,0:T(1,128)S(1)}, u32[]{:S(2)}, u32[]{:S(2)}) collective-permute-start(s32[1,5]{1,0:T(1,128)S(1)} %get-tuple-element.109), channel_id=1, source_target_pairs={{0,3},{1,0},{2,1},{3,2},{4,7},{5,4},{6,5},{7,6},{8,11},{9,8},{10,9... | collective-permute-start | bytes 68 | tf_op jit(solution)/shard_map/ppermute | solution.py:36
  36.3 30.3 %collective-permute-start.6 = (bf16[4,256,256]{2,1,0:T(8,128)(2,1)}, bf16[4,256,256]{2,1,0:T(8,128)(2,1)}, u32[]{:S(2)}, u32[]{:S(2)}) collective-permute-start(bf16[4,256,256]{2,1,0:T(8,128)(2,1)} %get-tuple-element.80), channel_id=1, source_target_pairs={{0,3},{1,0},{2,1},{3,2},{4,7},{5,4},{6,5},{7,6},{8,11},{9,8},{10,9... | collective-permute-start | bytes 1572872 | tf_op jit(solution)/shard_map/ppermute | solution.py:36
  37.6 29.0 %collective-permute-start.7 = (bf16[4,256,256]{2,1,0:T(8,128)(2,1)}, bf16[4,256,256]{2,1,0:T(8,128)(2,1)}, u32[]{:S(2)}, u32[]{:S(2)}) collective-permute-start(bf16[4,256,256]{2,1,0:T(8,128)(2,1)} %get-tuple-element.79), channel_id=1, source_target_pairs={{0,2},{1,3},{2,0},{3,1},{4,6},{5,7},{6,4},{7,5},{8,10},{9,11},{10,... | collective-permute-start | bytes 1572872 | tf_op jit(solution)/shard_map/ppermute | solution.py:36
  37.6 30.7 %collective-permute-start.8 = (bf16[4,256,256]{2,1,0:T(8,128)(2,1)}, bf16[4,256,256]{2,1,0:T(8,128)(2,1)}, u32[]{:S(2)}, u32[]{:S(2)}) collective-permute-start(bf16[4,256,256]{2,1,0:T(8,128)(2,1)} %get-tuple-element.78), channel_id=1, source_target_pairs={{0,1},{1,2},{2,3},{3,0},{4,5},{5,6},{6,7},{7,4},{8,9},{9,10},{10,1... | collective-permute-start | bytes 1572872 | tf_op jit(solution)/shard_map/ppermute | solution.py:36
  62.2 6.1 %copy-start.4 = (bf16[32,16,1280]{2,1,0:T(8,128)(2,1)}, bf16[32,16,1280]{2,1,0:T(8,128)(2,1)S(1)}, u32[]{:S(2)}) copy-start(bf16[32,16,1280]{2,1,0:T(8,128)(2,1)S(1)} %all-to-all-done.sino_ref.early_ref) | copy-start | bytes 3932164
  62.2 24.5 %all-to-all-start.1 = ((bf16[32,16,768]{2,1,0:T(8,128)(2,1)}), bf16[32,16,768]{2,1,0:T(8,128)(2,1)S(1)}, u32[]{:S(2)}, u32[]{:S(2)}) async-start(bf16[32,16,768]{2,1,0:T(8,128)(2,1)} %project_late.1), calls=%async_computation.1 | async-start | bytes 1572864 | tf_op jit(solution)/shard_map/all_to_all | solution.py:525
  86.7 4.1 %copy-start.6 = (bf16[32,16,768]{2,1,0:T(8,128)(2,1)}, bf16[32,16,768]{2,1,0:T(8,128)(2,1)S(1)}, u32[]{:S(2)}) copy-start(bf16[32,16,768]{2,1,0:T(8,128)(2,1)S(1)} %all-to-all-done.1.late_ref) | copy-start | bytes 2359300
  86.7 24.2 %all-to-all-start.2 = ((bf16[32,16,768]{2,1,0:T(8,128)(2,1)}), bf16[32,16,768]{2,1,0:T(8,128)(2,1)S(1)}, u32[]{:S(2)}, u32[]{:S(2)}) async-start(bf16[32,16,768]{2,1,0:T(8,128)(2,1)} %get-tuple-element.60), calls=%async_computation.2 | async-start | bytes 1572864 | tf_op jit(solution)/shard_map/all_to_all | solution.py:525
  101.4 15.1 %copy-start.3 = (bf16[32,16,768]{2,1,0:T(8,128)(2,1)S(1)}, bf16[32,16,768]{2,1,0:T(8,128)(2,1)}, u32[]{:S(2)}) copy-start(bf16[32,16,768]{2,1,0:T(8,128)(2,1)} %get-tuple-element.60) | copy-start | bytes 2359300
  111.0 4.8 %copy-start.5 = (bf16[32,16,768]{2,1,0:T(8,128)(2,1)}, bf16[32,16,768]{2,1,0:T(8,128)(2,1)S(1)}, u32[]{:S(2)}) copy-start(bf16[32,16,768]{2,1,0:T(8,128)(2,1)S(1)} %all-to-all-done.2.grad_ref) | copy-start | bytes 2359300
  111.0 35.5 %all-to-all-start.3 = ((bf16[32,16,1280]{2,1,0:T(8,128)(2,1)}), bf16[32,16,1280]{2,1,0:T(8,128)(2,1)}, u32[]{:S(2)}, u32[]{:S(2)}) async-start(bf16[32,16,1280]{2,1,0:T(8,128)(2,1)} %exit_rest.1), calls=%async_computation.3 | async-start | bytes 2621440 | tf_op jit(solution)/shard_map/all_to_all | solution.py:525
  115.1 3.2 %copy-start.1 = (bf16[32,16,1280]{2,1,0:T(8,128)(2,1)S(1)}, bf16[32,16,1280]{2,1,0:T(8,128)(2,1)}, u32[]{:S(2)}) copy-start(bf16[32,16,1280]{2,1,0:T(8,128)(2,1)} %exit_rest.1) | copy-start | bytes 3932164
  116.6 42.4 %collective-permute-start.12 = (bf16[32,16,512]{2,1,0:T(8,128)(2,1)S(1)}, bf16[32,16,512]{2,1,0:T(8,128)(2,1)S(1)}, u32[]{:S(2)}, u32[]{:S(2)}) collective-permute-start(bf16[32,16,512]{2,1,0:T(8,128)(2,1)S(1)} %slice.101), channel_id=1, source_target_pairs={{0,1},{1,2},{2,3},{3,0},{4,5},{5,6},{6,7},{7,4},{8,9},{9,10},{10,1... | collective-permute-start | bytes 1572872 | tf_op jit(solution)/shard_map/ppermute | solution.py:36
  119.2 39.8 %collective-permute-start.13 = (bf16[32,16,512]{2,1,0:T(8,128)(2,1)}, bf16[32,16,512]{2,1,0:T(8,128)(2,1)S(1)}, u32[]{:S(2)}, u32[]{:S(2)}) collective-permute-start(bf16[32,16,512]{2,1,0:T(8,128)(2,1)} %get-tuple-element.83), channel_id=1, source_target_pairs={{0,2},{1,3},{2,0},{3,1},{4,6},{5,7},{6,4},{7,5},{8,10},{9,11},{10,... | collective-permute-start | bytes 1572872 | tf_op jit(solution)/shard_map/ppermute | solution.py:36
  119.3 39.7 %collective-permute-start.14 = (bf16[32,16,512]{2,1,0:T(8,128)(2,1)S(1)}, bf16[32,16,512]{2,1,0:T(8,128)(2,1)S(1)}, u32[]{:S(2)}, u32[]{:S(2)}) collective-permute-start(bf16[32,16,512]{2,1,0:T(8,128)(2,1)S(1)} %get-tuple-element.82), channel_id=1, source_target_pairs={{0,3},{1,0},{2,1},{3,2},{4,7},{5,4},{6,5},{7,6},{8,11},{9,8},{10,9... | collective-permute-start | bytes 1572872 | tf_op jit(solution)/shard_map/ppermute | solution.py:36
  156.4 8.4 %collective-permute-start.9 = (bf16[16,8192]{1,0:T(8,128)(2,1)}, bf16[16,8192]{1,0:T(8,128)(2,1)S(1)}, u32[]{:S(2)}, u32[]{:S(2)}) collective-permute-start(bf16[16,8192]{1,0:T(8,128)(2,1)} %get-tuple-element.68), channel_id=1, source_target_pairs={{0,1},{1,2},{2,3},{3,0},{4,5},{5,6},{6,7},{7,4},{8,9},{9,10},{10,1... | collective-permute-start | bytes 786440 | tf_op jit(solution)/shard_map/ppermute | solution.py:36
  158.3 12.4 %collective-permute-start.10 = (bf16[16,8192]{1,0:T(8,128)(2,1)}, bf16[16,8192]{1,0:T(8,128)(2,1)S(1)}, u32[]{:S(2)}, u32[]{:S(2)}) collective-permute-start(bf16[16,8192]{1,0:T(8,128)(2,1)} %get-tuple-element.69), channel_id=1, source_target_pairs={{0,2},{1,3},{2,0},{3,1},{4,6},{5,7},{6,4},{7,5},{8,10},{9,11},{10,... | collective-permute-start | bytes 786440 | tf_op jit(solution)/shard_map/ppermute | solution.py:36
  159.0 12.4 %collective-permute-start.11 = (bf16[16,8192]{1,0:T(8,128)(2,1)}, bf16[16,8192]{1,0:T(8,128)(2,1)S(1)}, u32[]{:S(2)}, u32[]{:S(2)}) collective-permute-start(bf16[16,8192]{1,0:T(8,128)(2,1)} %get-tuple-element.70), channel_id=1, source_target_pairs={{0,3},{1,0},{2,1},{3,2},{4,7},{5,4},{6,5},{7,6},{8,11},{9,8},{10,9... | collective-permute-start | bytes 786440 | tf_op jit(solution)/shard_map/ppermute | solution.py:36
  160.1 11.3 %copy-start.7 = (bf16[16,8192]{1,0:T(8,128)(2,1)S(1)}, bf16[16,8192]{1,0:T(8,128)(2,1)}, u32[]{:S(2)}) copy-start(bf16[16,8192]{1,0:T(8,128)(2,1)} %get-tuple-element.71) | copy-start | bytes 786436
  164.8 6.7 %copy-start.2 = (bf16[2,32,8192]{2,1,0:T(8,128)(2,1)S(1)}, bf16[2,32,8192]{2,1,0:T(8,128)(2,1)}, u32[]{:S(2)}) copy-start(bf16[2,32,8192]{2,1,0:T(8,128)(2,1)} %param.9) | copy-start | bytes 3145732

commit v8 on v7

--- a/solution.py
+++ b/solution.py
@@ -18,6 +18,7 @@
 scalars = pl.BlockSpec(memory_space=pltpu.SMEM)
 CHAINS = 4
 BATCH = 4
+AHEAD = 16
 
 
 def dft_tables(width):
@@ -90,15 +91,15 @@
     def gather(start, lhs_ref):
         for n in range(batch):
             a = start + n
-            for i, b in enumerate(blocks):
-                row = i * ROWS
-                for jp in range(feeds // 2):
+            places = [(i, b, jp) for i, b in enumerate(blocks) for jp in range(feeds // 2)]
+            for group in range(0, len(places), AHEAD):
+                tiles = []
+                for i, b, jp in places[group : group + AHEAD]:
                     at = b * feeds + 2 * jp
-                    first = vv_ref[idx_ref[a, at]]
-                    second = vv_ref[idx_ref[a, at + 1]]
-                    lhs_ref[n, row : row + ROWS, jp * LANES : (jp + 1) * LANES] = jnp.where(
-                        low, first, second
-                    )
+                    tiles.append((vv_ref[idx_ref[a, at]], vv_ref[idx_ref[a, at + 1]]))
+                for (i, b, jp), (first, second) in zip(places[group : group + AHEAD], tiles):
+                    rows = slice(i * ROWS, (i + 1) * ROWS)
+                    lhs_ref[n, rows, jp * LANES : (jp + 1) * LANES] = jnp.where(low, first, second)
 
     def multiply(start, lhs_ref):
         for n in range(batch):
@@ -208,10 +209,20 @@
     def scatter(start, contrib_ref):
         for i, b in enumerate(blocks):
             row = i * GROUP
-            for j in range(feeds):
+            for j in range(0, feeds, 2):
+                sums = []
                 for n in range(CHAINS):
-                    tile = contrib_ref[n, row : row + GROUP, j * LANES : (j + 1) * LANES]
-                    acc_refs[n][idx_ref[start + n, b * feeds + j]] += tile
+                    here, there = (idx_ref[start + n, b * feeds + j + i] for i in range(2))
+                    one, two = (
+                        contrib_ref[n, row : row + GROUP, (j + i) * LANES : (j + i + 1) * LANES]
+                        for i in range(2)
+                    )
+                    first = acc_refs[n][here] + one
+                    second = jnp.where(here == there, first, acc_refs[n][there]) + two
+                    sums.append((here, first, there, second))
+                for n, (here, first, there, second) in enumerate(sums):
+                    acc_refs[n][here] = first
+                    acc_refs[n][there] = second
 
     multiply(0, 0, contrib_refs[0])
     if has_start:

time: 174 us -> 175 us (level)
  Pallas kernels: 51.9 us -> 56.2 us
  waiting for transfers between devices: 72 us -> 69.1 us
    all_to_all x4, waiting for transfers between devices: 53.6 us -> 50.8 us  [everyone(): return lax.all_to_all(chunk, ('ang', 'pos'), 0, 0, tiled=True)]
    pallas_call x2, Pallas kernels: 17.1 us -> 19.5 us  [back_project(): pl.pallas_call(functools.partial(back_project_kernel, blocks, has_start,...]
    pallas_call x1, Pallas kernels: 9.89 us -> 11.9 us  [exit_first(): pl.pallas_call(functools.partial(exit_first_kernel, len(amps)), out_shape...]
  transfers between devices with their start and end apart: 19 -> 19, of which waited for: 10 -> 10; matrix products, arithmetic and copies ran while one was open for 7% -> 7% of each run, Pallas kernels for 25% -> 28%
where the time goes in v8:
time: 175 us
  waiting for transfers between devices  69.1 us (39%)
  Pallas kernels  56.2 us (32%)
  starting transfers between devices  32.2 us (18%)
  local copies, waits for them, and re-layouts  12.2 us (7%)
  other arithmetic  3.67 us (2%)
    all_to_all x4, waiting for transfers between devices, everyone(): return lax.all_to_all(chunk, ('ang', 'pos'), 0, 0, tiled=True)  50.8 us
    pallas_call x2, Pallas kernels, back_project(): pl.pallas_call(functools.partial(back_project_kernel, blocks, has_start,...  19.5 us
    all_to_all x4, starting transfers between devices, everyone(): return lax.all_to_all(chunk, ('ang', 'pos'), 0, 0, tiled=True)  19.1 us
    ppermute x15, waiting for transfers between devices, rotate_pos(): lax.ppermute(pieces[j], 'pos', [(i, (i + sign * j) % count) for i in rang...  18.4 us
    pallas_call x2, Pallas kernels, project(): pl.pallas_call(functools.partial(project_kernel, blocks, pieces), out_sha...  14.2 us
    ppermute x15, starting transfers between devices, rotate_pos(): lax.ppermute(pieces[j], 'pos', [(i, (i + sign * j) % count) for i in rang...  13.1 us
    pallas_call x1, Pallas kernels, exit_first(): pl.pallas_call(functools.partial(exit_first_kernel, len(amps)), out_shape...  11.9 us
    pallas_call x1, Pallas kernels, exit_rest(): pl.pallas_call(functools.partial(exit_rest_kernel, len(amps)), out_shape=...  10.6 us
  transfers between devices with their start and end apart: 19, of which 10 were waited for; matrix products, arithmetic and copies ran while one was open for 7% of the time, Pallas kernels for 28%

profile of v8, /device:TPU:1, one launch (start us, length us, event | category | flops | bytes accessed | tf_op | source)
XLA Modules:
  0.0 174.6 jit_solution(13747943672605507950)
XLA Ops:
  0.7 0.0 copy-start
  0.7 1.3 dynamic-slice_bitcast_fusion.4
  2.1 2.7 %collective-permute-start = (bf16[16,8192]{1,0:T(8,128)(2,1)S(1)}, bf16[16,8192]{1,0:T(8,128)(2,1)S(1)}, u32[]{:S(2)}, u32[]{:S(2)}) collective-permute-start(bf16[16,8192]{1,0:T(8,128)(2,1)S(1)} %get-tuple-element.89), channel_id=1, source_target_pairs={{0,1},{1,2},{2,3},{3,0},{4,5},{5,6},{6,7},{7,4},{8,9},{9,10},{10,1... | collective-permute-start | bytes 786440 | tf_op jit(solution)/shard_map/ppermute | solution.py:37
  4.7 0.0 collective-permute-start.1
  4.7 0.5 collective-permute-start.2
  5.2 0.3 fusion.5
  5.5 0.3 copy.27
  5.8 0.2 reshape.194
  6.2 0.1 reshape.195.idx_ref
  6.3 4.0 %collective-permute-done.refs_1_ = bf16[16,8192]{1,0:T(8,128)(2,1)S(1)} collective-permute-done((bf16[16,8192]{1,0:T(8,128)(2,1)S(1)}, bf16[16,8192]{1,0:T(8,128)(2,1)S(1)}, u32[]{:S(2)}, u32[]{:S(2)}) %collective-permute-start) | collective-permute-done | bytes 262176 | tf_op jit(solution)/shard_map/ppermute | solution.py:37
  10.2 5.6 %collective-permute-done.1.refs_2_ = bf16[16,8192]{1,0:T(8,128)(2,1)S(1)} collective-permute-done((bf16[16,8192]{1,0:T(8,128)(2,1)S(1)}, bf16[16,8192]{1,0:T(8,128)(2,1)S(1)}, u32[]{:S(2)}, u32[]{:S(2)}) %collective-permute-start.1) | collective-permute-done | bytes 262176 | tf_op jit(solution)/shard_map/ppermute | solution.py:37
  15.8 0.5 collective-permute-done.2.refs_3_
  16.3 7.9 %project_early.1 = bf16[32,16,1280]{2,1,0:T(8,128)(2,1)} custom-call(s32[32,128]{1,0:T(8,128)S(1)} %reshape.195.idx_ref, bf16[32,64,256]{2,1,0:T(8,128)(2,1)S(1)} %copy-done, bf16[16,8192]{1,0:T(8,128)(2,1)S(1)} %get-tuple-element.49.refs_0_, bf16[16,8192]{1,0:T(8,128)(2,1)S(1)} %collective-permute-done.refs_1_, ...), custom_call_target="tpu_custom_call" | custom-call | flops 10350000128 | bytes 900000 | tf_op jit(solution)/shard_map/project_early/pallas_call | solution.py:146
  24.3 6.5 %all-to-all-start = ((bf16[32,16,1280]{2,1,0:T(8,128)(2,1)}), bf16[32,16,1280]{2,1,0:T(8,128)(2,1)S(1)}, u32[]{:S(2)}, u32[]{:S(2)}) async-start(bf16[32,16,1280]{2,1,0:T(8,128)(2,1)} %project_early.1), calls=%async_computation | async-start | bytes 2621440 | tf_op jit(solution)/shard_map/all_to_all | solution.py:536
  30.9 0.1 copy.32
  31.0 0.1 pad_add_fusion.2
  31.1 1.7 collective-permute-start.5
  32.8 0.0 collective-permute-start.4
  32.8 0.5 collective-permute-start.3
  33.3 2.9 %dynamic-slice_bitcast_fusion = (bf16[4,256,256]{2,1,0:T(8,128)(2,1)}, bf16[4,256,256]{2,1,0:T(8,128)(2,1)}, bf16[4,256,256]{2,1,0:T(8,128)(2,1)}, bf16[4,256,256]{2,1,0:T(8,128)(2,1)}) fusion(bf16[4,4,256,256]{3,2,1,0:T(8,128)(2,1)} %param.13, s32[]{:T(128)S(6)} %select_n.316, s32[]{:T(128)S(6)} %select_n.314, s32[]{:T(128)S(6)} %select_n.312, s32[]{:T(128)S(6)} %select_n.310), kind=kLoop, calls=%fused_computation.11 | loop fusion | bytes 4194320 | tf_op jit(solution)/shard_map/jit(dynamic_index_in_dim)/squeeze | solution.py:560
  36.2 1.3 collective-permute-start.6
  37.6 0.0 collective-permute-start.7
  37.6 0.0 collective-permute-done.5
  37.6 1.6 collective-permute-start.8
  39.2 0.0 collective-permute-done.4
  39.2 0.0 collective-permute-done.3
  39.2 0.6 pad_add_fusion.3.meta_ref
  39.8 6.3 %project_late.1 = bf16[32,16,768]{2,1,0:T(8,128)(2,1)} custom-call(s32[32,128]{1,0:T(8,128)S(1)} %reshape.195.idx_ref, bf16[32,64,256]{2,1,0:T(8,128)(2,1)S(1)} %copy-done, bf16[16,8192]{1,0:T(8,128)(2,1)S(1)} %get-tuple-element.49.refs_0_, bf16[16,8192]{1,0:T(8,128)(2,1)S(1)} %collective-permute-done.refs_1_, ...), custom_call_target="tpu_custom_call" | custom-call | flops 8049999872 | bytes 700000 | tf_op jit(solution)/shard_map/project_late/pallas_call | solution.py:146
  46.0 16.1 %all-to-all-done.sino_ref.early_ref = bf16[32,16,1280]{2,1,0:T(8,128)(2,1)S(1)} async-done(((bf16[32,16,1280]{2,1,0:T(8,128)(2,1)}), bf16[32,16,1280]{2,1,0:T(8,128)(2,1)S(1)}, u32[]{:S(2)}, u32[]{:S(2)}) %all-to-all-start) | async-done | bytes 1310752 | tf_op jit(solution)/shard_map/all_to_all | solution.py:536
  62.1 4.4 %all-to-all-start.1 = ((bf16[32,16,768]{2,1,0:T(8,128)(2,1)}), bf16[32,16,768]{2,1,0:T(8,128)(2,1)S(1)}, u32[]{:S(2)}, u32[]{:S(2)}) async-start(bf16[32,16,768]{2,1,0:T(8,128)(2,1)} %project_late.1), calls=%async_computation.1 | async-start | bytes 1572864 | tf_op jit(solution)/shard_map/all_to_all | solution.py:536
  66.5 0.0 collective-permute-done.6.refs_1_
  66.5 0.0 collective-permute-done.7.refs_0_
  66.5 1.7 collective-permute-done.8.refs_1_
  68.3 11.9 %exit_first.1 = (f32[2,256,256]{2,1,0:T(8,128)}, bf16[32,16,768]{2,1,0:T(8,128)(2,1)}, f32[2,256,256]{2,1,0:T(8,128)}) custom-call(s32[4,5]{1,0:T(4,128)} %pad_add_fusion.3.meta_ref, bf16[2,256,256]{2,1,0:T(8,128)(2,1)} %probe_ref.3, bf16[512,512]{1,0:T(8,128)(2,1)} %constant.148.forward_ref, bf16[512,512]{1,0:T(8,128)(2,1)} %constant.151.inverse_ref, ...), custom_call_target="tpu_custom_call" | custom-call | flops 11500000256 | bytes 1000000 | tf_op jit(solution)/shard_map/exit_first/pallas_call | solution.py:471
  80.2 6.5 %all-to-all-done.1.late_ref = bf16[32,16,768]{2,1,0:T(8,128)(2,1)S(1)} async-done(((bf16[32,16,768]{2,1,0:T(8,128)(2,1)}), bf16[32,16,768]{2,1,0:T(8,128)(2,1)S(1)}, u32[]{:S(2)}, u32[]{:S(2)}) %all-to-all-start.1) | async-done | bytes 786464 | tf_op jit(solution)/shard_map/all_to_all | solution.py:536
  86.7 4.1 %all-to-all-start.2 = ((bf16[32,16,768]{2,1,0:T(8,128)(2,1)}), bf16[32,16,768]{2,1,0:T(8,128)(2,1)S(1)}, u32[]{:S(2)}, u32[]{:S(2)}) async-start(bf16[32,16,768]{2,1,0:T(8,128)(2,1)} %get-tuple-element.60), calls=%async_computation.2 | async-start | bytes 1572864 | tf_op jit(solution)/shard_map/all_to_all | solution.py:536
  90.8 10.6 %exit_rest.1 = bf16[32,16,1280]{2,1,0:T(8,128)(2,1)} custom-call(s32[4,5]{1,0:T(4,128)} %pad_add_fusion.3.meta_ref, bf16[2,256,256]{2,1,0:T(8,128)(2,1)} %probe_ref.3, bf16[512,512]{1,0:T(8,128)(2,1)} %constant.148.forward_ref, bf16[512,512]{1,0:T(8,128)(2,1)} %constant.151.inverse_ref, bf16[32,16,1280]{2,1,0:T(8,128)(2,1)} %copy-done.4, ...), custom_call_target="tpu_custom_call" | custom-call | flops 11500000256 | bytes 1000000 | tf_op jit(solution)/shard_map/exit_rest/pallas_call | solution.py:487
  101.4 9.6 %all-to-all-done.2.grad_ref = bf16[32,16,768]{2,1,0:T(8,128)(2,1)S(1)} async-done(((bf16[32,16,768]{2,1,0:T(8,128)(2,1)}), bf16[32,16,768]{2,1,0:T(8,128)(2,1)S(1)}, u32[]{:S(2)}, u32[]{:S(2)}) %all-to-all-start.2) | async-done | bytes 786464 | tf_op jit(solution)/shard_map/all_to_all | solution.py:536
  110.9 4.1 %all-to-all-start.3 = ((bf16[32,16,1280]{2,1,0:T(8,128)(2,1)}), bf16[32,16,1280]{2,1,0:T(8,128)(2,1)}, u32[]{:S(2)}, u32[]{:S(2)}) async-start(bf16[32,16,1280]{2,1,0:T(8,128)(2,1)} %exit_rest.1), calls=%async_computation.3 | async-start | bytes 2621440 | tf_op jit(solution)/shard_map/all_to_all | solution.py:536
  115.1 0.0 copy-start.1
  115.1 0.3 copy.22
  115.4 0.2 reshape.192
  115.8 0.7 reshape.193.idx_ref
  116.5 0.1 slice.101
  116.6 1.7 collective-permute-start.12
  118.3 0.9 fusion.9
  119.2 0.0 collective-permute-start.13
  119.3 0.5 collective-permute-start.14
  119.8 8.1 %back_first.1.refs_0_ = f32[512,8,128]{2,1,0:T(8,128)} custom-call(s32[32,128]{1,0:T(8,128)} %reshape.193.idx_ref, bf16[32,64,256]{2,1,0:T(8,128)(2,1)} %radon_ref.7, bf16[32,16,768]{2,1,0:T(8,128)(2,1)} %copy-done.5), custom_call_target="tpu_custom_call" | custom-call | flops 8049999872 | bytes 700000 | tf_op jit(solution)/shard_map/back_first/pallas_call | solution.py:275
  127.8 18.6 %all-to-all-done.3.grad_ref = bf16[32,16,1280]{2,1,0:T(8,128)(2,1)} async-done(((bf16[32,16,1280]{2,1,0:T(8,128)(2,1)}), bf16[32,16,1280]{2,1,0:T(8,128)(2,1)}, u32[]{:S(2)}, u32[]{:S(2)}) %all-to-all-start.3) | async-done | bytes 1310752 | tf_op jit(solution)/shard_map/all_to_all | solution.py:536
  146.5 11.4 %back_rest.1 = (bf16[16,8192]{1,0:T(8,128)(2,1)}, bf16[16,8192]{1,0:T(8,128)(2,1)}, bf16[16,8192]{1,0:T(8,128)(2,1)}, bf16[16,8192]{1,0:T(8,128)(2,1)}) custom-call(s32[32,128]{1,0:T(8,128)} %reshape.193.idx_ref, bf16[32,64,256]{2,1,0:T(8,128)(2,1)} %radon_ref.7, bf16[32,16,1280]{2,1,0:T(8,128)(2,1)} %all-to-all-done.3.grad_ref, ...), custom_call_target="tpu_custom_call" | custom-call | flops 10350000128 | bytes 900000 | tf_op jit(solution)/shard_map/back_rest/pallas_call | solution.py:275
  157.9 1.9 %collective-permute-start.9 = (bf16[16,8192]{1,0:T(8,128)(2,1)}, bf16[16,8192]{1,0:T(8,128)(2,1)S(1)}, u32[]{:S(2)}, u32[]{:S(2)}) collective-permute-start(bf16[16,8192]{1,0:T(8,128)(2,1)} %get-tuple-element.68), channel_id=1, source_target_pairs={{0,1},{1,2},{2,3},{3,0},{4,5},{5,6},{6,7},{7,4},{8,9},{9,10},{10,1... | collective-permute-start | bytes 786440 | tf_op jit(solution)/shard_map/ppermute | solution.py:37
  159.8 0.7 collective-permute-start.10
  160.5 0.0 collective-permute-done.12
  160.5 0.0 collective-permute-start.11
  160.5 0.0 collective-permute-done.13
  160.5 0.0 collective-permute-done.14
  160.5 0.6 select_bitcast_fusion.3
  161.2 0.3 maximum_convert_fusion
  161.6 4.7 %copy.37 = f32[2,256,4,512]{3,2,1,0:T(4,128)} copy(f32[2,256,4,512]{3,1,0,2:T(8,128)S(1)} %maximum_convert_fusion) | data formatting | bytes 8388608
  166.3 5.9 %collective-permute-done.10 = bf16[16,8192]{1,0:T(8,128)(2,1)S(1)} collective-permute-done((bf16[16,8192]{1,0:T(8,128)(2,1)}, bf16[16,8192]{1,0:T(8,128)(2,1)S(1)}, u32[]{:S(2)}, u32[]{:S(2)}) %collective-permute-start.10) | collective-permute-done | bytes 262176 | tf_op jit(solution)/shard_map/ppermute | solution.py:37
  172.2 0.6 collective-permute-done.11
  172.9 0.1 select_bitcast_fusion.7
  173.0 1.6 multiply_add_fusion
  (46 shorter events, 0.4 us)
Async XLA Ops:
  0.6 4.6 %copy-start.8 = (s32[32,32,4]{1,2,0:T(4,128)S(1)}, s32[32,32,4]{1,2,0:T(4,128)}, u32[]{:S(2)}) copy-start(s32[32,32,4]{1,2,0:T(4,128)} %param.11) | copy-start | bytes 49156
  0.7 15.7 %copy-start = (bf16[32,64,256]{2,1,0:T(8,128)(2,1)S(1)}, bf16[32,64,256]{2,1,0:T(8,128)(2,1)}, u32[]{:S(2)}) copy-start(bf16[32,64,256]{2,1,0:T(8,128)(2,1)} %radon_ref.7) | copy-start | bytes 3145732
  2.1 8.2 %collective-permute-start = (bf16[16,8192]{1,0:T(8,128)(2,1)S(1)}, bf16[16,8192]{1,0:T(8,128)(2,1)S(1)}, u32[]{:S(2)}, u32[]{:S(2)}) collective-permute-start(bf16[16,8192]{1,0:T(8,128)(2,1)S(1)} %get-tuple-element.89), channel_id=1, source_target_pairs={{0,1},{1,2},{2,3},{3,0},{4,5},{5,6},{6,7},{7,4},{8,9},{9,10},{10,1... | collective-permute-start | bytes 786440 | tf_op jit(solution)/shard_map/ppermute | solution.py:37
  4.7 11.1 %collective-permute-start.1 = (bf16[16,8192]{1,0:T(8,128)(2,1)S(1)}, bf16[16,8192]{1,0:T(8,128)(2,1)S(1)}, u32[]{:S(2)}, u32[]{:S(2)}) collective-permute-start(bf16[16,8192]{1,0:T(8,128)(2,1)S(1)} %get-tuple-element.91), channel_id=1, source_target_pairs={{0,2},{1,3},{2,0},{3,1},{4,6},{5,7},{6,4},{7,5},{8,10},{9,11},{10,... | collective-permute-start | bytes 786440 | tf_op jit(solution)/shard_map/ppermute | solution.py:37
  4.7 11.6 %collective-permute-start.2 = (bf16[16,8192]{1,0:T(8,128)(2,1)S(1)}, bf16[16,8192]{1,0:T(8,128)(2,1)S(1)}, u32[]{:S(2)}, u32[]{:S(2)}) collective-permute-start(bf16[16,8192]{1,0:T(8,128)(2,1)S(1)} %get-tuple-element.88), channel_id=1, source_target_pairs={{0,3},{1,0},{2,1},{3,2},{4,7},{5,4},{6,5},{7,6},{8,11},{9,8},{10,9... | collective-permute-start | bytes 786440 | tf_op jit(solution)/shard_map/ppermute | solution.py:37
  24.3 6.6 %copy-start.10 = (s32[4,1]{0,1:T(1,128)S(1)}, s32[4,1]{0,1:T(1,128)}, u32[]{:S(2)}) copy-start(s32[4,1]{0,1:T(1,128)} %param.15) | copy-start | bytes 52
  24.3 6.7 %copy-start.9 = (s32[4,4]{1,0:T(4,128)S(1)}, s32[4,4]{1,0:T(4,128)}, u32[]{:S(2)}) copy-start(s32[4,4]{1,0:T(4,128)} %param.14) | copy-start | bytes 196
  24.3 37.9 %all-to-all-start = ((bf16[32,16,1280]{2,1,0:T(8,128)(2,1)}), bf16[32,16,1280]{2,1,0:T(8,128)(2,1)S(1)}, u32[]{:S(2)}, u32[]{:S(2)}) async-start(bf16[32,16,1280]{2,1,0:T(8,128)(2,1)} %project_early.1), calls=%async_computation | async-start | bytes 2621440 | tf_op jit(solution)/shard_map/all_to_all | solution.py:536
  31.1 6.5 %collective-permute-start.5 = (s32[1,5]{1,0:T(1,128)S(1)}, s32[1,5]{1,0:T(1,128)S(1)}, u32[]{:S(2)}, u32[]{:S(2)}) collective-permute-start(s32[1,5]{1,0:T(1,128)S(1)} %get-tuple-element.107), channel_id=1, source_target_pairs={{0,1},{1,2},{2,3},{3,0},{4,5},{5,6},{6,7},{7,4},{8,9},{9,10},{10,1... | collective-permute-start | bytes 68 | tf_op jit(solution)/shard_map/ppermute | solution.py:37
  32.8 6.4 %collective-permute-start.4 = (s32[1,5]{1,0:T(1,128)S(1)}, s32[1,5]{1,0:T(1,128)S(1)}, u32[]{:S(2)}, u32[]{:S(2)}) collective-permute-start(s32[1,5]{1,0:T(1,128)S(1)} %get-tuple-element.108), channel_id=1, source_target_pairs={{0,2},{1,3},{2,0},{3,1},{4,6},{5,7},{6,4},{7,5},{8,10},{9,11},{10,... | collective-permute-start | bytes 68 | tf_op jit(solution)/shard_map/ppermute | solution.py:37
  32.8 6.4 %collective-permute-start.3 = (s32[1,5]{1,0:T(1,128)S(1)}, s32[1,5]{1,0:T(1,128)S(1)}, u32[]{:S(2)}, u32[]{:S(2)}) collective-permute-start(s32[1,5]{1,0:T(1,128)S(1)} %get-tuple-element.109), channel_id=1, source_target_pairs={{0,3},{1,0},{2,1},{3,2},{4,7},{5,4},{6,5},{7,6},{8,11},{9,8},{10,9... | collective-permute-start | bytes 68 | tf_op jit(solution)/shard_map/ppermute | solution.py:37
  36.2 30.3 %collective-permute-start.6 = (bf16[4,256,256]{2,1,0:T(8,128)(2,1)}, bf16[4,256,256]{2,1,0:T(8,128)(2,1)}, u32[]{:S(2)}, u32[]{:S(2)}) collective-permute-start(bf16[4,256,256]{2,1,0:T(8,128)(2,1)} %get-tuple-element.80), channel_id=1, source_target_pairs={{0,3},{1,0},{2,1},{3,2},{4,7},{5,4},{6,5},{7,6},{8,11},{9,8},{10,9... | collective-permute-start | bytes 1572872 | tf_op jit(solution)/shard_map/ppermute | solution.py:37
  37.6 29.0 %collective-permute-start.7 = (bf16[4,256,256]{2,1,0:T(8,128)(2,1)}, bf16[4,256,256]{2,1,0:T(8,128)(2,1)}, u32[]{:S(2)}, u32[]{:S(2)}) collective-permute-start(bf16[4,256,256]{2,1,0:T(8,128)(2,1)} %get-tuple-element.79), channel_id=1, source_target_pairs={{0,2},{1,3},{2,0},{3,1},{4,6},{5,7},{6,4},{7,5},{8,10},{9,11},{10,... | collective-permute-start | bytes 1572872 | tf_op jit(solution)/shard_map/ppermute | solution.py:37
  37.6 30.7 %collective-permute-start.8 = (bf16[4,256,256]{2,1,0:T(8,128)(2,1)}, bf16[4,256,256]{2,1,0:T(8,128)(2,1)}, u32[]{:S(2)}, u32[]{:S(2)}) collective-permute-start(bf16[4,256,256]{2,1,0:T(8,128)(2,1)} %get-tuple-element.78), channel_id=1, source_target_pairs={{0,1},{1,2},{2,3},{3,0},{4,5},{5,6},{6,7},{7,4},{8,9},{9,10},{10,1... | collective-permute-start | bytes 1572872 | tf_op jit(solution)/shard_map/ppermute | solution.py:37
  62.1 6.1 %copy-start.4 = (bf16[32,16,1280]{2,1,0:T(8,128)(2,1)}, bf16[32,16,1280]{2,1,0:T(8,128)(2,1)S(1)}, u32[]{:S(2)}) copy-start(bf16[32,16,1280]{2,1,0:T(8,128)(2,1)S(1)} %all-to-all-done.sino_ref.early_ref) | copy-start | bytes 3932164
  62.1 24.5 %all-to-all-start.1 = ((bf16[32,16,768]{2,1,0:T(8,128)(2,1)}), bf16[32,16,768]{2,1,0:T(8,128)(2,1)S(1)}, u32[]{:S(2)}, u32[]{:S(2)}) async-start(bf16[32,16,768]{2,1,0:T(8,128)(2,1)} %project_late.1), calls=%async_computation.1 | async-start | bytes 1572864 | tf_op jit(solution)/shard_map/all_to_all | solution.py:536
  86.7 4.1 %copy-start.6 = (bf16[32,16,768]{2,1,0:T(8,128)(2,1)}, bf16[32,16,768]{2,1,0:T(8,128)(2,1)S(1)}, u32[]{:S(2)}) copy-start(bf16[32,16,768]{2,1,0:T(8,128)(2,1)S(1)} %all-to-all-done.1.late_ref) | copy-start | bytes 2359300
  86.7 24.2 %all-to-all-start.2 = ((bf16[32,16,768]{2,1,0:T(8,128)(2,1)}), bf16[32,16,768]{2,1,0:T(8,128)(2,1)S(1)}, u32[]{:S(2)}, u32[]{:S(2)}) async-start(bf16[32,16,768]{2,1,0:T(8,128)(2,1)} %get-tuple-element.60), calls=%async_computation.2 | async-start | bytes 1572864 | tf_op jit(solution)/shard_map/all_to_all | solution.py:536
  101.4 15.1 %copy-start.3 = (bf16[32,16,768]{2,1,0:T(8,128)(2,1)S(1)}, bf16[32,16,768]{2,1,0:T(8,128)(2,1)}, u32[]{:S(2)}) copy-start(bf16[32,16,768]{2,1,0:T(8,128)(2,1)} %get-tuple-element.60) | copy-start | bytes 2359300
  110.9 4.8 %copy-start.5 = (bf16[32,16,768]{2,1,0:T(8,128)(2,1)}, bf16[32,16,768]{2,1,0:T(8,128)(2,1)S(1)}, u32[]{:S(2)}) copy-start(bf16[32,16,768]{2,1,0:T(8,128)(2,1)S(1)} %all-to-all-done.2.grad_ref) | copy-start | bytes 2359300
  110.9 35.5 %all-to-all-start.3 = ((bf16[32,16,1280]{2,1,0:T(8,128)(2,1)}), bf16[32,16,1280]{2,1,0:T(8,128)(2,1)}, u32[]{:S(2)}, u32[]{:S(2)}) async-start(bf16[32,16,1280]{2,1,0:T(8,128)(2,1)} %exit_rest.1), calls=%async_computation.3 | async-start | bytes 2621440 | tf_op jit(solution)/shard_map/all_to_all | solution.py:536
  115.1 3.2 %copy-start.1 = (bf16[32,16,1280]{2,1,0:T(8,128)(2,1)S(1)}, bf16[32,16,1280]{2,1,0:T(8,128)(2,1)}, u32[]{:S(2)}) copy-start(bf16[32,16,1280]{2,1,0:T(8,128)(2,1)} %exit_rest.1) | copy-start | bytes 3932164
  116.6 43.9 %collective-permute-start.12 = (bf16[32,16,512]{2,1,0:T(8,128)(2,1)S(1)}, bf16[32,16,512]{2,1,0:T(8,128)(2,1)S(1)}, u32[]{:S(2)}, u32[]{:S(2)}) collective-permute-start(bf16[32,16,512]{2,1,0:T(8,128)(2,1)S(1)} %slice.101), channel_id=1, source_target_pairs={{0,1},{1,2},{2,3},{3,0},{4,5},{5,6},{6,7},{7,4},{8,9},{9,10},{10,1... | collective-permute-start | bytes 1572872 | tf_op jit(solution)/shard_map/ppermute | solution.py:37
  119.2 41.3 %collective-permute-start.13 = (bf16[32,16,512]{2,1,0:T(8,128)(2,1)}, bf16[32,16,512]{2,1,0:T(8,128)(2,1)S(1)}, u32[]{:S(2)}, u32[]{:S(2)}) collective-permute-start(bf16[32,16,512]{2,1,0:T(8,128)(2,1)} %get-tuple-element.83), channel_id=1, source_target_pairs={{0,2},{1,3},{2,0},{3,1},{4,6},{5,7},{6,4},{7,5},{8,10},{9,11},{10,... | collective-permute-start | bytes 1572872 | tf_op jit(solution)/shard_map/ppermute | solution.py:37
  119.3 41.2 %collective-permute-start.14 = (bf16[32,16,512]{2,1,0:T(8,128)(2,1)S(1)}, bf16[32,16,512]{2,1,0:T(8,128)(2,1)S(1)}, u32[]{:S(2)}, u32[]{:S(2)}) collective-permute-start(bf16[32,16,512]{2,1,0:T(8,128)(2,1)S(1)} %get-tuple-element.82), channel_id=1, source_target_pairs={{0,3},{1,0},{2,1},{3,2},{4,7},{5,4},{6,5},{7,6},{8,11},{9,8},{10,9... | collective-permute-start | bytes 1572872 | tf_op jit(solution)/shard_map/ppermute | solution.py:37
  157.9 8.4 %collective-permute-start.9 = (bf16[16,8192]{1,0:T(8,128)(2,1)}, bf16[16,8192]{1,0:T(8,128)(2,1)S(1)}, u32[]{:S(2)}, u32[]{:S(2)}) collective-permute-start(bf16[16,8192]{1,0:T(8,128)(2,1)} %get-tuple-element.68), channel_id=1, source_target_pairs={{0,1},{1,2},{2,3},{3,0},{4,5},{5,6},{6,7},{7,4},{8,9},{9,10},{10,1... | collective-permute-start | bytes 786440 | tf_op jit(solution)/shard_map/ppermute | solution.py:37
  159.8 12.4 %collective-permute-start.10 = (bf16[16,8192]{1,0:T(8,128)(2,1)}, bf16[16,8192]{1,0:T(8,128)(2,1)S(1)}, u32[]{:S(2)}, u32[]{:S(2)}) collective-permute-start(bf16[16,8192]{1,0:T(8,128)(2,1)} %get-tuple-element.69), channel_id=1, source_target_pairs={{0,2},{1,3},{2,0},{3,1},{4,6},{5,7},{6,4},{7,5},{8,10},{9,11},{10,... | collective-permute-start | bytes 786440 | tf_op jit(solution)/shard_map/ppermute | solution.py:37
  160.5 12.4 %collective-permute-start.11 = (bf16[16,8192]{1,0:T(8,128)(2,1)}, bf16[16,8192]{1,0:T(8,128)(2,1)S(1)}, u32[]{:S(2)}, u32[]{:S(2)}) collective-permute-start(bf16[16,8192]{1,0:T(8,128)(2,1)} %get-tuple-element.70), channel_id=1, source_target_pairs={{0,3},{1,0},{2,1},{3,2},{4,7},{5,4},{6,5},{7,6},{8,11},{9,8},{10,9... | collective-permute-start | bytes 786440 | tf_op jit(solution)/shard_map/ppermute | solution.py:37
  161.6 11.3 %copy-start.7 = (bf16[16,8192]{1,0:T(8,128)(2,1)S(1)}, bf16[16,8192]{1,0:T(8,128)(2,1)}, u32[]{:S(2)}) copy-start(bf16[16,8192]{1,0:T(8,128)(2,1)} %get-tuple-element.71) | copy-start | bytes 786436
  166.3 6.7 %copy-start.2 = (bf16[2,32,8192]{2,1,0:T(8,128)(2,1)S(1)}, bf16[2,32,8192]{2,1,0:T(8,128)(2,1)}, u32[]{:S(2)}) copy-start(bf16[2,32,8192]{2,1,0:T(8,128)(2,1)} %param.9) | copy-start | bytes 3145732

commit v9 on v7

--- a/solution.py
+++ b/solution.py
@@ -588,17 +588,16 @@
     padded, meta = lax.optimization_barrier((padded, meta))
     sino_late = project(tile_idx, radon_tiles, padded, late_blocks, "project_late")
     got_early = everyone(cut_rows(sino_early, own))
-    got_early, sino_late = lax.optimization_barrier((got_early, sino_late))
     got_late = everyone(cut_rows(sino_late, own))
     got_early, got_late = to_groups(got_early, own), to_groups(got_late, own)
     got_early, amp_pieces = lax.optimization_barrier((got_early, amp_pieces))
     partial, first_grad, spill = exit_first(meta, probe_field, tables, got_early, amp_pieces[:half])
-    first_sent, got_late = lax.optimization_barrier((first_grad, got_late))
+    first_sent = first_grad
     rest_grad = exit_rest(
         meta, probe_field, tables, got_early, got_late, partial, spill, amp_pieces[half:]
     )
     back_first = everyone(from_groups(first_sent, own))
-    back_first, rest_sent = lax.optimization_barrier((back_first, rest_grad))
+    rest_sent = rest_grad
     back_rest = everyone(from_groups(rest_sent, own))
     first_sum = back_project(
         block_idx, radon_tiles, pad_rows(back_first, own), first_blocks, None, n_pos, width, "back_first"

time: 174 us -> 174 us (level)
    ppermute x15, waiting for transfers between devices: 18.4 us -> 20.7 us  [rotate_pos(): lax.ppermute(pieces[j], 'pos', [(i, (i + sign * j) % count) for i in rang...]
    all_to_all x4, waiting for transfers between devices: 53.6 us -> 51.8 us  [everyone(): return lax.all_to_all(chunk, ('ang', 'pos'), 0, 0, tiled=True)]
where the time goes in v9:
time: 174 us
  waiting for transfers between devices  72.5 us (42%)
  Pallas kernels  51.9 us (30%)
  starting transfers between devices  32.1 us (18%)
  local copies, waits for them, and re-layouts  12.3 us (7%)
  other arithmetic  3.67 us (2%)
    all_to_all x4, waiting for transfers between devices, everyone(): return lax.all_to_all(chunk, ('ang', 'pos'), 0, 0, tiled=True)  51.8 us
    ppermute x15, waiting for transfers between devices, rotate_pos(): lax.ppermute(pieces[j], 'pos', [(i, (i + sign * j) % count) for i in rang...  20.7 us
    all_to_all x4, starting transfers between devices, everyone(): return lax.all_to_all(chunk, ('ang', 'pos'), 0, 0, tiled=True)  18.8 us
    pallas_call x2, Pallas kernels, back_project(): pl.pallas_call(functools.partial(back_project_kernel, blocks, has_start,...  17.1 us
    pallas_call x2, Pallas kernels, project(): pl.pallas_call(functools.partial(project_kernel, blocks, pieces), out_sha...  14.3 us
    ppermute x15, starting transfers between devices, rotate_pos(): lax.ppermute(pieces[j], 'pos', [(i, (i + sign * j) % count) for i in rang...  13.3 us
    pallas_call x1, Pallas kernels, exit_rest(): pl.pallas_call(functools.partial(exit_rest_kernel, len(amps)), out_shape=...  10.6 us
    pallas_call x1, Pallas kernels, exit_first(): pl.pallas_call(functools.partial(exit_first_kernel, len(amps)), out_shape...  9.89 us
  transfers between devices with their start and end apart: 19, of which 10 were waited for; matrix products, arithmetic and copies ran while one was open for 7% of the time, Pallas kernels for 25%

profile of v9, /device:TPU:1, one launch (start us, length us, event | category | flops | bytes accessed | tf_op | source)
XLA Modules:
  0.0 173.6 jit_solution(3270333165430482930)
XLA Ops:
  0.7 0.0 copy-start
  0.7 1.3 dynamic-slice_bitcast_fusion.4
  2.1 0.1 collective-permute-start.2
  2.2 2.6 %collective-permute-start = (bf16[16,8192]{1,0:T(8,128)(2,1)S(1)}, bf16[16,8192]{1,0:T(8,128)(2,1)S(1)}, u32[]{:S(2)}, u32[]{:S(2)}) collective-permute-start(bf16[16,8192]{1,0:T(8,128)(2,1)S(1)} %get-tuple-element.77), channel_id=1, source_target_pairs={{0,1},{1,2},{2,3},{3,0},{4,5},{5,6},{6,7},{7,4},{8,9},{9,10},{10,1... | collective-permute-start | bytes 786440 | tf_op jit(solution)/shard_map/ppermute | solution.py:36
  4.8 1.1 collective-permute-start.1
  5.9 0.3 fusion.5
  6.2 0.3 copy.27
  6.5 0.2 reshape.194
  6.9 0.1 reshape.195.idx_ref
  7.0 4.0 %collective-permute-done.2.refs_3_ = bf16[16,8192]{1,0:T(8,128)(2,1)S(1)} collective-permute-done((bf16[16,8192]{1,0:T(8,128)(2,1)S(1)}, bf16[16,8192]{1,0:T(8,128)(2,1)S(1)}, u32[]{:S(2)}, u32[]{:S(2)}) %collective-permute-start.2) | collective-permute-done | bytes 262176 | tf_op jit(solution)/shard_map/ppermute | solution.py:36
  11.0 0.0 collective-permute-done.refs_1_
  11.0 6.2 %collective-permute-done.1.refs_2_ = bf16[16,8192]{1,0:T(8,128)(2,1)S(1)} collective-permute-done((bf16[16,8192]{1,0:T(8,128)(2,1)S(1)}, bf16[16,8192]{1,0:T(8,128)(2,1)S(1)}, u32[]{:S(2)}, u32[]{:S(2)}) %collective-permute-start.1) | collective-permute-done | bytes 262176 | tf_op jit(solution)/shard_map/ppermute | solution.py:36
  17.2 8.0 %project_early.1 = bf16[32,16,1280]{2,1,0:T(8,128)(2,1)} custom-call(s32[32,128]{1,0:T(8,128)S(1)} %reshape.195.idx_ref, bf16[32,64,256]{2,1,0:T(8,128)(2,1)S(1)} %copy-done, bf16[16,8192]{1,0:T(8,128)(2,1)S(1)} %get-tuple-element.45.refs_0_, bf16[16,8192]{1,0:T(8,128)(2,1)S(1)} %collective-permute-done.refs_1_, ...), custom_call_target="tpu_custom_call" | custom-call | flops 10350000128 | bytes 900000 | tf_op jit(solution)/shard_map/project_early/pallas_call | solution.py:145
  25.2 6.2 %all-to-all-start = ((bf16[32,16,1280]{2,1,0:T(8,128)(2,1)}), bf16[32,16,1280]{2,1,0:T(8,128)(2,1)S(1)}, u32[]{:S(2)}, u32[]{:S(2)}) async-start(bf16[32,16,1280]{2,1,0:T(8,128)(2,1)} %project_early.1), calls=%async_computation | async-start | bytes 2621440 | tf_op jit(solution)/shard_map/all_to_all | solution.py:525
  31.5 0.1 copy.32
  31.6 0.1 pad_add_fusion.2
  31.6 1.7 collective-permute-start.5
  33.3 0.0 collective-permute-start.4
  33.3 0.5 collective-permute-start.3
  33.9 2.9 %dynamic-slice_bitcast_fusion = (bf16[4,256,256]{2,1,0:T(8,128)(2,1)}, bf16[4,256,256]{2,1,0:T(8,128)(2,1)}, bf16[4,256,256]{2,1,0:T(8,128)(2,1)}, bf16[4,256,256]{2,1,0:T(8,128)(2,1)}) fusion(bf16[4,4,256,256]{3,2,1,0:T(8,128)(2,1)} %param.13, s32[]{:T(128)S(6)} %select_n.316, s32[]{:T(128)S(6)} %select_n.314, s32[]{:T(128)S(6)} %select_n.312, s32[]{:T(128)S(6)} %select_n.310), kind=kLoop, calls=%fused_computation.11 | loop fusion | bytes 4194320 | tf_op jit(solution)/shard_map/jit(dynamic_index_in_dim)/squeeze | solution.py:549
  36.8 1.2 collective-permute-start.8
  38.0 1.4 collective-permute-start.7
  39.5 0.0 collective-permute-done.5
  39.5 0.0 collective-permute-start.6
  39.5 0.0 collective-permute-done.4
  39.5 0.0 collective-permute-done.3
  39.5 0.6 pad_add_fusion.3.meta_ref
  40.1 6.3 %project_late.1 = bf16[32,16,768]{2,1,0:T(8,128)(2,1)} custom-call(s32[32,128]{1,0:T(8,128)S(1)} %reshape.195.idx_ref, bf16[32,64,256]{2,1,0:T(8,128)(2,1)S(1)} %copy-done, bf16[16,8192]{1,0:T(8,128)(2,1)S(1)} %get-tuple-element.45.refs_0_, bf16[16,8192]{1,0:T(8,128)(2,1)S(1)} %collective-permute-done.refs_1_, ...), custom_call_target="tpu_custom_call" | custom-call | flops 8049999872 | bytes 700000 | tf_op jit(solution)/shard_map/project_late/pallas_call | solution.py:145
  46.4 16.3 %all-to-all-done.sino_ref.early_ref = bf16[32,16,1280]{2,1,0:T(8,128)(2,1)S(1)} async-done(((bf16[32,16,1280]{2,1,0:T(8,128)(2,1)}), bf16[32,16,1280]{2,1,0:T(8,128)(2,1)S(1)}, u32[]{:S(2)}, u32[]{:S(2)}) %all-to-all-start) | async-done | bytes 1310752 | tf_op jit(solution)/shard_map/all_to_all | solution.py:525
  62.7 4.4 %all-to-all-start.1 = ((bf16[32,16,768]{2,1,0:T(8,128)(2,1)}), bf16[32,16,768]{2,1,0:T(8,128)(2,1)S(1)}, u32[]{:S(2)}, u32[]{:S(2)}) async-start(bf16[32,16,768]{2,1,0:T(8,128)(2,1)} %project_late.1), calls=%async_computation.1 | async-start | bytes 1572864 | tf_op jit(solution)/shard_map/all_to_all | solution.py:525
  67.1 0.0 collective-permute-done.8.refs_1_
  67.1 3.2 %collective-permute-done.7.refs_0_ = bf16[4,256,256]{2,1,0:T(8,128)(2,1)} collective-permute-done((bf16[4,256,256]{2,1,0:T(8,128)(2,1)}, bf16[4,256,256]{2,1,0:T(8,128)(2,1)}, u32[]{:S(2)}, u32[]{:S(2)}) %collective-permute-start.7) | collective-permute-done | bytes 524320 | tf_op jit(solution)/shard_map/ppermute | solution.py:36
  70.3 0.6 collective-permute-done.6.refs_1_
  71.0 9.9 %exit_first.1 = (f32[2,256,256]{2,1,0:T(8,128)}, bf16[32,16,768]{2,1,0:T(8,128)(2,1)}, f32[2,256,256]{2,1,0:T(8,128)}) custom-call(s32[4,5]{1,0:T(4,128)} %pad_add_fusion.3.meta_ref, bf16[2,256,256]{2,1,0:T(8,128)(2,1)} %probe_ref.3, bf16[512,512]{1,0:T(8,128)(2,1)} %constant.148.forward_ref, bf16[512,512]{1,0:T(8,128)(2,1)} %constant.151.inverse_ref, ...), custom_call_target="tpu_custom_call" | custom-call | flops 11500000256 | bytes 1000000 | tf_op jit(solution)/shard_map/exit_first/pallas_call | solution.py:460
  80.9 6.4 %all-to-all-done.1.late_ref = bf16[32,16,768]{2,1,0:T(8,128)(2,1)S(1)} async-done(((bf16[32,16,768]{2,1,0:T(8,128)(2,1)}), bf16[32,16,768]{2,1,0:T(8,128)(2,1)S(1)}, u32[]{:S(2)}, u32[]{:S(2)}) %all-to-all-start.1) | async-done | bytes 786464 | tf_op jit(solution)/shard_map/all_to_all | solution.py:525
  87.2 4.1 %all-to-all-start.3 = ((bf16[32,16,768]{2,1,0:T(8,128)(2,1)}), bf16[32,16,768]{2,1,0:T(8,128)(2,1)S(1)}, u32[]{:S(2)}, u32[]{:S(2)}) async-start(bf16[32,16,768]{2,1,0:T(8,128)(2,1)} %get-tuple-element.55), calls=%async_computation.3 | async-start | bytes 1572864 | tf_op jit(solution)/shard_map/all_to_all | solution.py:525
  91.4 10.6 %exit_rest.1 = bf16[32,16,1280]{2,1,0:T(8,128)(2,1)} custom-call(s32[4,5]{1,0:T(4,128)} %pad_add_fusion.3.meta_ref, bf16[2,256,256]{2,1,0:T(8,128)(2,1)} %probe_ref.3, bf16[512,512]{1,0:T(8,128)(2,1)} %constant.148.forward_ref, bf16[512,512]{1,0:T(8,128)(2,1)} %constant.151.inverse_ref, bf16[32,16,1280]{2,1,0:T(8,128)(2,1)} %copy-done.4, ...), custom_call_target="tpu_custom_call" | custom-call | flops 11500000256 | bytes 1000000 | tf_op jit(solution)/shard_map/exit_rest/pallas_call | solution.py:476
  101.9 9.6 %all-to-all-done.3.grad_ref = bf16[32,16,768]{2,1,0:T(8,128)(2,1)S(1)} async-done(((bf16[32,16,768]{2,1,0:T(8,128)(2,1)}), bf16[32,16,768]{2,1,0:T(8,128)(2,1)S(1)}, u32[]{:S(2)}, u32[]{:S(2)}) %all-to-all-start.3) | async-done | bytes 786464 | tf_op jit(solution)/shard_map/all_to_all | solution.py:525
  111.5 4.1 %all-to-all-start.2 = ((bf16[32,16,1280]{2,1,0:T(8,128)(2,1)}), bf16[32,16,1280]{2,1,0:T(8,128)(2,1)}, u32[]{:S(2)}, u32[]{:S(2)}) async-start(bf16[32,16,1280]{2,1,0:T(8,128)(2,1)} %exit_rest.1), calls=%async_computation.2 | async-start | bytes 2621440 | tf_op jit(solution)/shard_map/all_to_all | solution.py:525
  115.7 0.3 copy.22
  115.9 0.2 reshape.192
  116.3 0.7 reshape.193.idx_ref
  117.1 0.1 slice.101
  117.1 1.7 collective-permute-start.12
  118.8 1.1 fusion.9
  119.9 0.0 collective-permute-start.14
  119.9 0.3 collective-permute-start.13
  120.2 7.2 %back_first.1.refs_0_ = f32[512,8,128]{2,1,0:T(8,128)} custom-call(s32[32,128]{1,0:T(8,128)} %reshape.193.idx_ref, bf16[32,64,256]{2,1,0:T(8,128)(2,1)} %radon_ref.7, bf16[32,16,768]{2,1,0:T(8,128)(2,1)} %copy-done.5), custom_call_target="tpu_custom_call" | custom-call | flops 8049999872 | bytes 700000 | tf_op jit(solution)/shard_map/back_first/pallas_call | solution.py:264
  127.4 19.6 %all-to-all-done.2.grad_ref = bf16[32,16,1280]{2,1,0:T(8,128)(2,1)} async-done(((bf16[32,16,1280]{2,1,0:T(8,128)(2,1)}), bf16[32,16,1280]{2,1,0:T(8,128)(2,1)}, u32[]{:S(2)}, u32[]{:S(2)}) %all-to-all-start.2) | async-done | bytes 1310752 | tf_op jit(solution)/shard_map/all_to_all | solution.py:525
  147.0 9.9 %back_rest.1 = (bf16[16,8192]{1,0:T(8,128)(2,1)}, bf16[16,8192]{1,0:T(8,128)(2,1)}, bf16[16,8192]{1,0:T(8,128)(2,1)}, bf16[16,8192]{1,0:T(8,128)(2,1)}) custom-call(s32[32,128]{1,0:T(8,128)} %reshape.193.idx_ref, bf16[32,64,256]{2,1,0:T(8,128)(2,1)} %radon_ref.7, bf16[32,16,1280]{2,1,0:T(8,128)(2,1)} %all-to-all-done.2.grad_ref, ...), custom_call_target="tpu_custom_call" | custom-call | flops 10350000128 | bytes 900000 | tf_op jit(solution)/shard_map/back_rest/pallas_call | solution.py:264
  156.9 1.9 %collective-permute-start.9 = (bf16[16,8192]{1,0:T(8,128)(2,1)}, bf16[16,8192]{1,0:T(8,128)(2,1)S(1)}, u32[]{:S(2)}, u32[]{:S(2)}) collective-permute-start(bf16[16,8192]{1,0:T(8,128)(2,1)} %get-tuple-element.56), channel_id=1, source_target_pairs={{0,1},{1,2},{2,3},{3,0},{4,5},{5,6},{6,7},{7,4},{8,9},{9,10},{10,1... | collective-permute-start | bytes 786440 | tf_op jit(solution)/shard_map/ppermute | solution.py:36
  158.8 0.7 collective-permute-start.10
  159.5 0.0 collective-permute-done.12
  159.5 0.0 collective-permute-start.11
  159.5 0.0 collective-permute-done.14
  159.5 0.0 collective-permute-done.13
  159.5 0.6 select_bitcast_fusion.3
  160.3 0.3 maximum_convert_fusion
  160.6 4.7 %copy.37 = f32[2,256,4,512]{3,2,1,0:T(4,128)} copy(f32[2,256,4,512]{3,1,0,2:T(8,128)S(1)} %maximum_convert_fusion) | data formatting | bytes 8388608
  165.3 0.0 collective-permute-done.9
  165.3 5.9 %collective-permute-done.10 = bf16[16,8192]{1,0:T(8,128)(2,1)S(1)} collective-permute-done((bf16[16,8192]{1,0:T(8,128)(2,1)}, bf16[16,8192]{1,0:T(8,128)(2,1)S(1)}, u32[]{:S(2)}, u32[]{:S(2)}) %collective-permute-start.10) | collective-permute-done | bytes 262176 | tf_op jit(solution)/shard_map/ppermute | solution.py:36
  171.3 0.6 collective-permute-done.11
  171.9 0.1 select_bitcast_fusion.7
  172.0 1.6 multiply_add_fusion
  (46 shorter events, 0.4 us)
Async XLA Ops:
  0.6 5.3 %copy-start.8 = (s32[32,32,4]{1,2,0:T(4,128)S(1)}, s32[32,32,4]{1,2,0:T(4,128)}, u32[]{:S(2)}) copy-start(s32[32,32,4]{1,2,0:T(4,128)} %param.11) | copy-start | bytes 49156
  0.7 16.5 %copy-start = (bf16[32,64,256]{2,1,0:T(8,128)(2,1)S(1)}, bf16[32,64,256]{2,1,0:T(8,128)(2,1)}, u32[]{:S(2)}) copy-start(bf16[32,64,256]{2,1,0:T(8,128)(2,1)} %radon_ref.7) | copy-start | bytes 3145732
  2.1 8.9 %collective-permute-start.2 = (bf16[16,8192]{1,0:T(8,128)(2,1)S(1)}, bf16[16,8192]{1,0:T(8,128)(2,1)S(1)}, u32[]{:S(2)}, u32[]{:S(2)}) collective-permute-start(bf16[16,8192]{1,0:T(8,128)(2,1)S(1)} %get-tuple-element.76), channel_id=1, source_target_pairs={{0,3},{1,0},{2,1},{3,2},{4,7},{5,4},{6,5},{7,6},{8,11},{9,8},{10,9... | collective-permute-start | bytes 786440 | tf_op jit(solution)/shard_map/ppermute | solution.py:36
  2.2 8.8 %collective-permute-start = (bf16[16,8192]{1,0:T(8,128)(2,1)S(1)}, bf16[16,8192]{1,0:T(8,128)(2,1)S(1)}, u32[]{:S(2)}, u32[]{:S(2)}) collective-permute-start(bf16[16,8192]{1,0:T(8,128)(2,1)S(1)} %get-tuple-element.77), channel_id=1, source_target_pairs={{0,1},{1,2},{2,3},{3,0},{4,5},{5,6},{6,7},{7,4},{8,9},{9,10},{10,1... | collective-permute-start | bytes 786440 | tf_op jit(solution)/shard_map/ppermute | solution.py:36
  4.8 12.4 %collective-permute-start.1 = (bf16[16,8192]{1,0:T(8,128)(2,1)S(1)}, bf16[16,8192]{1,0:T(8,128)(2,1)S(1)}, u32[]{:S(2)}, u32[]{:S(2)}) collective-permute-start(bf16[16,8192]{1,0:T(8,128)(2,1)S(1)} %get-tuple-element.79), channel_id=1, source_target_pairs={{0,2},{1,3},{2,0},{3,1},{4,6},{5,7},{6,4},{7,5},{8,10},{9,11},{10,... | collective-permute-start | bytes 786440 | tf_op jit(solution)/shard_map/ppermute | solution.py:36
  25.2 6.3 %copy-start.10 = (s32[4,1]{0,1:T(1,128)S(1)}, s32[4,1]{0,1:T(1,128)}, u32[]{:S(2)}) copy-start(s32[4,1]{0,1:T(1,128)} %param.15) | copy-start | bytes 52
  25.2 6.4 %copy-start.9 = (s32[4,4]{1,0:T(4,128)S(1)}, s32[4,4]{1,0:T(4,128)}, u32[]{:S(2)}) copy-start(s32[4,4]{1,0:T(4,128)} %param.14) | copy-start | bytes 196
  25.2 37.5 %all-to-all-start = ((bf16[32,16,1280]{2,1,0:T(8,128)(2,1)}), bf16[32,16,1280]{2,1,0:T(8,128)(2,1)S(1)}, u32[]{:S(2)}, u32[]{:S(2)}) async-start(bf16[32,16,1280]{2,1,0:T(8,128)(2,1)} %project_early.1), calls=%async_computation | async-start | bytes 2621440 | tf_op jit(solution)/shard_map/all_to_all | solution.py:525
  31.6 7.8 %collective-permute-start.5 = (s32[1,5]{1,0:T(1,128)S(1)}, s32[1,5]{1,0:T(1,128)S(1)}, u32[]{:S(2)}, u32[]{:S(2)}) collective-permute-start(s32[1,5]{1,0:T(1,128)S(1)} %get-tuple-element.95), channel_id=1, source_target_pairs={{0,1},{1,2},{2,3},{3,0},{4,5},{5,6},{6,7},{7,4},{8,9},{9,10},{10,1... | collective-permute-start | bytes 68 | tf_op jit(solution)/shard_map/ppermute | solution.py:36
  33.3 6.1 %collective-permute-start.4 = (s32[1,5]{1,0:T(1,128)S(1)}, s32[1,5]{1,0:T(1,128)S(1)}, u32[]{:S(2)}, u32[]{:S(2)}) collective-permute-start(s32[1,5]{1,0:T(1,128)S(1)} %get-tuple-element.96), channel_id=1, source_target_pairs={{0,2},{1,3},{2,0},{3,1},{4,6},{5,7},{6,4},{7,5},{8,10},{9,11},{10,... | collective-permute-start | bytes 68 | tf_op jit(solution)/shard_map/ppermute | solution.py:36
  33.3 6.2 %collective-permute-start.3 = (s32[1,5]{1,0:T(1,128)S(1)}, s32[1,5]{1,0:T(1,128)S(1)}, u32[]{:S(2)}, u32[]{:S(2)}) collective-permute-start(s32[1,5]{1,0:T(1,128)S(1)} %get-tuple-element.97), channel_id=1, source_target_pairs={{0,3},{1,0},{2,1},{3,2},{4,7},{5,4},{6,5},{7,6},{8,11},{9,8},{10,9... | collective-permute-start | bytes 68 | tf_op jit(solution)/shard_map/ppermute | solution.py:36
  36.8 30.3 %collective-permute-start.8 = (bf16[4,256,256]{2,1,0:T(8,128)(2,1)}, bf16[4,256,256]{2,1,0:T(8,128)(2,1)}, u32[]{:S(2)}, u32[]{:S(2)}) collective-permute-start(bf16[4,256,256]{2,1,0:T(8,128)(2,1)} %get-tuple-element.66), channel_id=1, source_target_pairs={{0,1},{1,2},{2,3},{3,0},{4,5},{5,6},{6,7},{7,4},{8,9},{9,10},{10,1... | collective-permute-start | bytes 1572872 | tf_op jit(solution)/shard_map/ppermute | solution.py:36
  38.0 32.3 %collective-permute-start.7 = (bf16[4,256,256]{2,1,0:T(8,128)(2,1)}, bf16[4,256,256]{2,1,0:T(8,128)(2,1)}, u32[]{:S(2)}, u32[]{:S(2)}) collective-permute-start(bf16[4,256,256]{2,1,0:T(8,128)(2,1)} %get-tuple-element.67), channel_id=1, source_target_pairs={{0,2},{1,3},{2,0},{3,1},{4,6},{5,7},{6,4},{7,5},{8,10},{9,11},{10,... | collective-permute-start | bytes 1572872 | tf_op jit(solution)/shard_map/ppermute | solution.py:36
  39.5 31.5 %collective-permute-start.6 = (bf16[4,256,256]{2,1,0:T(8,128)(2,1)}, bf16[4,256,256]{2,1,0:T(8,128)(2,1)}, u32[]{:S(2)}, u32[]{:S(2)}) collective-permute-start(bf16[4,256,256]{2,1,0:T(8,128)(2,1)} %get-tuple-element.68), channel_id=1, source_target_pairs={{0,3},{1,0},{2,1},{3,2},{4,7},{5,4},{6,5},{7,6},{8,11},{9,8},{10,9... | collective-permute-start | bytes 1572872 | tf_op jit(solution)/shard_map/ppermute | solution.py:36
  62.7 8.3 %copy-start.4 = (bf16[32,16,1280]{2,1,0:T(8,128)(2,1)}, bf16[32,16,1280]{2,1,0:T(8,128)(2,1)S(1)}, u32[]{:S(2)}) copy-start(bf16[32,16,1280]{2,1,0:T(8,128)(2,1)S(1)} %all-to-all-done.sino_ref.early_ref) | copy-start | bytes 3932164
  62.7 24.5 %all-to-all-start.1 = ((bf16[32,16,768]{2,1,0:T(8,128)(2,1)}), bf16[32,16,768]{2,1,0:T(8,128)(2,1)S(1)}, u32[]{:S(2)}, u32[]{:S(2)}) async-start(bf16[32,16,768]{2,1,0:T(8,128)(2,1)} %project_late.1), calls=%async_computation.1 | async-start | bytes 1572864 | tf_op jit(solution)/shard_map/all_to_all | solution.py:525
  87.2 4.1 %copy-start.6 = (bf16[32,16,768]{2,1,0:T(8,128)(2,1)}, bf16[32,16,768]{2,1,0:T(8,128)(2,1)S(1)}, u32[]{:S(2)}) copy-start(bf16[32,16,768]{2,1,0:T(8,128)(2,1)S(1)} %all-to-all-done.1.late_ref) | copy-start | bytes 2359300
  87.2 24.2 %all-to-all-start.3 = ((bf16[32,16,768]{2,1,0:T(8,128)(2,1)}), bf16[32,16,768]{2,1,0:T(8,128)(2,1)S(1)}, u32[]{:S(2)}, u32[]{:S(2)}) async-start(bf16[32,16,768]{2,1,0:T(8,128)(2,1)} %get-tuple-element.55), calls=%async_computation.3 | async-start | bytes 1572864 | tf_op jit(solution)/shard_map/all_to_all | solution.py:525
  101.9 15.1 %copy-start.1 = (bf16[32,16,1280]{2,1,0:T(8,128)(2,1)S(1)}, bf16[32,16,1280]{2,1,0:T(8,128)(2,1)}, u32[]{:S(2)}) copy-start(bf16[32,16,1280]{2,1,0:T(8,128)(2,1)} %exit_rest.1) | copy-start | bytes 3932164
  101.9 15.1 %copy-start.3 = (bf16[32,16,768]{2,1,0:T(8,128)(2,1)S(1)}, bf16[32,16,768]{2,1,0:T(8,128)(2,1)}, u32[]{:S(2)}) copy-start(bf16[32,16,768]{2,1,0:T(8,128)(2,1)} %get-tuple-element.55) | copy-start | bytes 2359300
  111.5 4.8 %copy-start.5 = (bf16[32,16,768]{2,1,0:T(8,128)(2,1)}, bf16[32,16,768]{2,1,0:T(8,128)(2,1)S(1)}, u32[]{:S(2)}) copy-start(bf16[32,16,768]{2,1,0:T(8,128)(2,1)S(1)} %all-to-all-done.3.grad_ref) | copy-start | bytes 2359300
  111.5 35.5 %all-to-all-start.2 = ((bf16[32,16,1280]{2,1,0:T(8,128)(2,1)}), bf16[32,16,1280]{2,1,0:T(8,128)(2,1)}, u32[]{:S(2)}, u32[]{:S(2)}) async-start(bf16[32,16,1280]{2,1,0:T(8,128)(2,1)} %exit_rest.1), calls=%async_computation.2 | async-start | bytes 2621440 | tf_op jit(solution)/shard_map/all_to_all | solution.py:525
  117.1 42.4 %collective-permute-start.12 = (bf16[32,16,512]{2,1,0:T(8,128)(2,1)S(1)}, bf16[32,16,512]{2,1,0:T(8,128)(2,1)S(1)}, u32[]{:S(2)}, u32[]{:S(2)}) collective-permute-start(bf16[32,16,512]{2,1,0:T(8,128)(2,1)S(1)} %slice.101), channel_id=1, source_target_pairs={{0,1},{1,2},{2,3},{3,0},{4,5},{5,6},{6,7},{7,4},{8,9},{9,10},{10,1... | collective-permute-start | bytes 1572872 | tf_op jit(solution)/shard_map/ppermute | solution.py:36
  119.9 39.6 %collective-permute-start.14 = (bf16[32,16,512]{2,1,0:T(8,128)(2,1)}, bf16[32,16,512]{2,1,0:T(8,128)(2,1)S(1)}, u32[]{:S(2)}, u32[]{:S(2)}) collective-permute-start(bf16[32,16,512]{2,1,0:T(8,128)(2,1)} %get-tuple-element.70), channel_id=1, source_target_pairs={{0,3},{1,0},{2,1},{3,2},{4,7},{5,4},{6,5},{7,6},{8,11},{9,8},{10,9... | collective-permute-start | bytes 1572872 | tf_op jit(solution)/shard_map/ppermute | solution.py:36
  119.9 39.6 %collective-permute-start.13 = (bf16[32,16,512]{2,1,0:T(8,128)(2,1)}, bf16[32,16,512]{2,1,0:T(8,128)(2,1)S(1)}, u32[]{:S(2)}, u32[]{:S(2)}) collective-permute-start(bf16[32,16,512]{2,1,0:T(8,128)(2,1)} %get-tuple-element.71), channel_id=1, source_target_pairs={{0,2},{1,3},{2,0},{3,1},{4,6},{5,7},{6,4},{7,5},{8,10},{9,11},{10,... | collective-permute-start | bytes 1572872 | tf_op jit(solution)/shard_map/ppermute | solution.py:36
  156.9 8.4 %collective-permute-start.9 = (bf16[16,8192]{1,0:T(8,128)(2,1)}, bf16[16,8192]{1,0:T(8,128)(2,1)S(1)}, u32[]{:S(2)}, u32[]{:S(2)}) collective-permute-start(bf16[16,8192]{1,0:T(8,128)(2,1)} %get-tuple-element.56), channel_id=1, source_target_pairs={{0,1},{1,2},{2,3},{3,0},{4,5},{5,6},{6,7},{7,4},{8,9},{9,10},{10,1... | collective-permute-start | bytes 786440 | tf_op jit(solution)/shard_map/ppermute | solution.py:36
  158.8 12.4 %collective-permute-start.10 = (bf16[16,8192]{1,0:T(8,128)(2,1)}, bf16[16,8192]{1,0:T(8,128)(2,1)S(1)}, u32[]{:S(2)}, u32[]{:S(2)}) collective-permute-start(bf16[16,8192]{1,0:T(8,128)(2,1)} %get-tuple-element.57), channel_id=1, source_target_pairs={{0,2},{1,3},{2,0},{3,1},{4,6},{5,7},{6,4},{7,5},{8,10},{9,11},{10,... | collective-permute-start | bytes 786440 | tf_op jit(solution)/shard_map/ppermute | solution.py:36
  159.5 12.4 %collective-permute-start.11 = (bf16[16,8192]{1,0:T(8,128)(2,1)}, bf16[16,8192]{1,0:T(8,128)(2,1)S(1)}, u32[]{:S(2)}, u32[]{:S(2)}) collective-permute-start(bf16[16,8192]{1,0:T(8,128)(2,1)} %get-tuple-element.58), channel_id=1, source_target_pairs={{0,3},{1,0},{2,1},{3,2},{4,7},{5,4},{6,5},{7,6},{8,11},{9,8},{10,9... | collective-permute-start | bytes 786440 | tf_op jit(solution)/shard_map/ppermute | solution.py:36
  160.6 11.3 %copy-start.7 = (bf16[16,8192]{1,0:T(8,128)(2,1)S(1)}, bf16[16,8192]{1,0:T(8,128)(2,1)}, u32[]{:S(2)}) copy-start(bf16[16,8192]{1,0:T(8,128)(2,1)} %get-tuple-element.59) | copy-start | bytes 786436
  165.3 6.7 %copy-start.2 = (bf16[2,32,8192]{2,1,0:T(8,128)(2,1)S(1)}, bf16[2,32,8192]{2,1,0:T(8,128)(2,1)}, u32[]{:S(2)}) copy-start(bf16[2,32,8192]{2,1,0:T(8,128)(2,1)} %param.9) | copy-start | bytes 3145732

commit v10 on v7

--- a/solution.py
+++ b/solution.py
@@ -82,8 +82,8 @@
 
 
 def project_blocks(blocks, idx_ref, radon_ref, vv_ref, out_ref, lhs_refs):
-    angles, block, span = radon_ref.shape
-    feeds = span // block
+    angles, span, twice = radon_ref.shape
+    feeds = 2 * span // twice
     low = lower_half((ROWS, LANES))
     batch = lhs_refs[0].shape[0]
 
@@ -103,13 +103,11 @@
     def multiply(start, lhs_ref):
         for n in range(batch):
             a = start + n
-            product = lax.dot_general(
-                lhs_ref[n], radon_ref[a], (((1,), (1,)), ((), ())), preferred_element_type=jnp.float32
-            )
+            product = jnp.dot(lhs_ref[n], radon_ref[a], preferred_element_type=jnp.float32)
             for pair in range(len(blocks) // 2):
                 row = 2 * pair * ROWS
-                tile = jnp.concatenate(
-                    [product[row : row + ROWS], product[row + ROWS : row + 2 * ROWS]], axis=1
+                tile = jnp.where(
+                    low, product[row : row + ROWS], product[row + ROWS : row + 2 * ROWS]
                 )
                 out_ref[a, :, pair * LANES : (pair + 1) * LANES] = tile.astype(jnp.bfloat16)
 
@@ -137,8 +135,9 @@
     )
 
 
-def project(idx, radon_tiles, vol_pieces, blocks, name):
-    angles, block, span = radon_tiles.shape
+def project(idx, radon_twice, vol_pieces, blocks, name):
+    angles, span, twice = radon_twice.shape
+    block = twice // 2
     pieces = len(vol_pieces)
     tiles = pieces * vol_pieces[0].shape[1] // LANES
     out_shape = (angles, ROWS, len(blocks) * block)
@@ -150,48 +149,49 @@
         scratch_shapes=[pltpu.VMEM((2 * tiles, ROWS, LANES), jnp.bfloat16)]
         + [pltpu.VMEM((BATCH, len(blocks) * ROWS, span), jnp.bfloat16)] * 2,
         compiler_params=pltpu.CompilerParams(
-            vmem_limit_bytes=14 * MEBI + 2 * radon_tiles.size + 2 * math.prod(out_shape)
+            vmem_limit_bytes=14 * MEBI + 2 * radon_twice.size + 2 * math.prod(out_shape)
         ),
         cost_estimate=guess(4 + len(blocks) // 4),
         name=name,
-    )(idx, radon_tiles, *vol_pieces)
-
-
-def back_project_kernel(blocks, has_start, outs, idx_ref, radon_ref, grad_ref, *refs):
+    )(idx, radon_twice, *vol_pieces)
+
+
+def back_project_kernel(blocks, has_start, outs, idx_ref, wide_hbm, grad_hbm, *refs):
     start_ref, refs = (refs[0], refs[1:]) if has_start else (None, refs)
     out_refs, refs = refs[:outs], refs[outs:]
-    acc_refs, (w_ref, *contrib_refs) = refs[:CHAINS], refs[CHAINS:]
+    acc_refs, refs = refs[:CHAINS], refs[CHAINS:]
+    wide_ref, grad_ref, wide_sems, grad_sems, *refs = refs
+    contrib_refs = refs[:2]
+    angles, both, span = wide_ref.shape
+    pairs = len(blocks) // 2
+    feeds = span // both
+    coef_blocks = acc_refs[0].shape[0]
+    low = lower_half((GROUP, LANES))
+
+    def copies(step):
+        here = pl.ds(step * CHAINS, CHAINS)
+        return (
+            pltpu.make_async_copy(wide_hbm.at[here], wide_ref.at[here], wide_sems.at[step]),
+            pltpu.make_async_copy(grad_hbm.at[here], grad_ref.at[here], grad_sems.at[step]),
+        )
+
+    @pl.loop(0, angles // CHAINS)
+    def _(step):
+        for copy in copies(step):
+            copy.start()
+
     if has_start:
-        contrib_refs, start_sem = contrib_refs[:-1], contrib_refs[-1]
-        start_copy = pltpu.make_async_copy(start_ref, acc_refs[0], start_sem)
+        start_copy = pltpu.make_async_copy(start_ref, acc_refs[0], refs[2])
         start_copy.start()
-    angles, block, span = radon_ref.shape
-    pairs = len(blocks) // 2
-    feeds = span // block
-    coef_blocks = acc_refs[0].shape[0]
 
     @pl.loop(0, coef_blocks, unroll=16)
     def _(t):
         for acc_ref in acc_refs[1:] if has_start else acc_refs:
             acc_ref[t] = jnp.zeros((GROUP, LANES), jnp.float32)
 
-    low = lower_half((GROUP, LANES))
-    low_rows = lower_half((block, LANES))
-    w_ref[...] = jnp.zeros_like(w_ref)
-
-    def widen(slot, a):
-        for jp in range(feeds // 2):
-            tile = radon_ref[a, :, jp * LANES : (jp + 1) * LANES].astype(jnp.float32)
-            turned = swap_halves(tile)
-            for side, (first, second) in enumerate(((tile, turned), (turned, tile))):
-                lanes = slice((2 * jp + side) * LANES, (2 * jp + side + 1) * LANES)
-                w_ref[slot, :block, lanes] = jnp.where(low_rows, first, 0.0).astype(jnp.bfloat16)
-                w_ref[slot, block:, lanes] = jnp.where(low_rows, 0.0, second).astype(jnp.bfloat16)
-
-    def multiply(start, half, contrib_ref):
+    def multiply(step, contrib_ref):
         for n in range(CHAINS):
-            a = start + n
-            widen(half * CHAINS + n, a)
+            a = step * CHAINS + n
             lhs = []
             for pair in range(pairs):
                 tile = grad_ref[a, :, pair * LANES : (pair + 1) * LANES].astype(jnp.float32)
@@ -200,10 +200,12 @@
                 odd = jnp.where(low, swap_halves(real), imag)
                 lhs.append(jnp.concatenate([even, odd], axis=0).astype(jnp.bfloat16))
             contrib_ref[n] = jnp.dot(
-                jnp.concatenate(lhs, axis=0),
-                w_ref[half * CHAINS + n],
-                preferred_element_type=jnp.float32,
+                jnp.concatenate(lhs, axis=0), wide_ref[a], preferred_element_type=jnp.float32
             )
+
+    def arrived(step):
+        for copy in copies(step):
+            copy.wait()
 
     def scatter(start, contrib_ref):
         for i, b in enumerate(blocks):
@@ -213,17 +215,26 @@
                     tile = contrib_ref[n, row : row + GROUP, j * LANES : (j + 1) * LANES]
                     acc_refs[n][idx_ref[start + n, b * feeds + j]] += tile
 
-    multiply(0, 0, contrib_refs[0])
+    arrived(0)
+    multiply(0, contrib_refs[0])
     if has_start:
         start_copy.wait()
 
-    @pl.loop(0, angles // (2 * CHAINS))
-    def _(step):
-        start = step * 2 * CHAINS
-        multiply(start + CHAINS, 1, contrib_refs[1])
-        scatter(start, contrib_refs[0])
-        multiply(jnp.minimum(start + 2 * CHAINS, angles - CHAINS), 0, contrib_refs[0])
-        scatter(start + CHAINS, contrib_refs[1])
+    steps = angles // CHAINS
+
+    @pl.loop(0, steps // 2)
+    def _(half):
+        step = 2 * half
+        arrived(step + 1)
+        multiply(step + 1, contrib_refs[1])
+        scatter(step * CHAINS, contrib_refs[0])
+
+        @pl.when(step + 2 < steps)
+        def _():
+            arrived(step + 2)
+
+        multiply(jnp.minimum(step + 2, steps - 1), contrib_refs[0])
+        scatter((step + 1) * CHAINS, contrib_refs[1])
 
     def total(t):
         sums = [acc_ref[t] for acc_ref in acc_refs]
@@ -251,24 +262,25 @@
                 out_ref[:, lanes] = jnp.concatenate([real, imag], axis=0).astype(out_ref.dtype)
 
 
-def back_project(idx, radon_tiles, grads, blocks, start, pieces, piece_width, name):
-    angles, block, span = radon_tiles.shape
-    coef_blocks = pieces * piece_width // block
-    rows = len(blocks) * GROUP
+def back_project(idx, radon_wide, grads, blocks, start, pieces, piece_width, name):
+    angles, both, span = radon_wide.shape
+    coef_blocks = pieces * piece_width // (both // 2)
+    contrib = (CHAINS, len(blocks) * GROUP, span)
     has_start = start is not None
     if has_start:
         out_shape = [jax.ShapeDtypeStruct((ROWS, piece_width), jnp.bfloat16)] * pieces
     else:
         out_shape = [jax.ShapeDtypeStruct((coef_blocks, GROUP, LANES), jnp.float32)]
-    operands = [idx, radon_tiles, grads] + ([start] if has_start else [])
+    operands = [idx, radon_wide, grads] + ([start] if has_start else [])
     return pl.pallas_call(
         functools.partial(back_project_kernel, blocks, has_start, len(out_shape)),
         out_shape=out_shape,
-        in_specs=[scalars] + [everywhere] * 2 + [pl.BlockSpec(memory_space=pl.ANY)] * has_start,
+        in_specs=[scalars] + [pl.BlockSpec(memory_space=pl.ANY)] * (len(operands) - 1),
         out_specs=[everywhere] * len(out_shape),
         scratch_shapes=[pltpu.VMEM((coef_blocks, GROUP, LANES), jnp.float32)] * CHAINS
-        + [pltpu.VMEM((2 * CHAINS, 2 * block, 2 * span), jnp.bfloat16)]
-        + [pltpu.VMEM((CHAINS, rows, 2 * span), jnp.float32)] * 2
+        + [pltpu.VMEM(radon_wide.shape, jnp.bfloat16), pltpu.VMEM(grads.shape, jnp.bfloat16)]
+        + [pltpu.SemaphoreType.DMA((angles // CHAINS,))] * 2
+        + [pltpu.VMEM(contrib, jnp.float32)] * 2
         + [pltpu.SemaphoreType.DMA] * has_start,
         compiler_params=pltpu.CompilerParams(vmem_limit_bytes=60 * MEBI),
         cost_estimate=guess(4 + len(blocks) // 4),
@@ -566,6 +578,8 @@
     tile_idx = by_chunk(crossed * (n_pos * tiles_each) + piece * tiles_each + within // 2)
     block_idx = by_chunk(piece * blocks_each + within)
     padded = [pad_rows(piece, own) for piece in vol_pieces]
+    turned = jnp.transpose(radon_tiles, (0, 2, 1))
+    radon_twice = jnp.concatenate([turned, turned], axis=2)
     probe_width = probe_field.shape[1]
     tables = dft_tables(probe_width)
     half = n_pos // 2
@@ -576,7 +590,7 @@
     first_blocks = list(range(edge, half * tile_width // block_size))
     rest_blocks = list(range(half * tile_width // block_size, det_blocks)) + list(range(edge))
 
-    sino_early = project(tile_idx, radon_tiles, padded, early_blocks, "project_early")
+    sino_early = project(tile_idx, radon_twice, padded, early_blocks, "project_early")
     sino_early, padded, offsets, counts = lax.optimization_barrier(
         (sino_early, padded, offsets, counts)
     )
@@ -586,8 +600,12 @@
     )
     meta = jnp.concatenate(meta, axis=0)
     padded, meta = lax.optimization_barrier((padded, meta))
-    sino_late = project(tile_idx, radon_tiles, padded, late_blocks, "project_late")
+    sino_late = project(tile_idx, radon_twice, padded, late_blocks, "project_late")
     got_early = everyone(cut_rows(sino_early, own))
+    sino_late, radon_tiles = lax.optimization_barrier((sino_late, radon_tiles))
+    split = radon_tiles.reshape(angles, 1, block_size, feeds, 1, block_size)
+    same = jnp.eye(2, dtype=jnp.bfloat16).reshape(1, 2, 1, 1, 2, 1)
+    radon_wide = (split * same).reshape(angles, 2 * block_size, 2 * feeds * block_size)
     got_early, sino_late = lax.optimization_barrier((got_early, sino_late))
     got_late = everyone(cut_rows(sino_late, own))
     got_early, got_late = to_groups(got_early, own), to_groups(got_late, own)
@@ -601,7 +619,7 @@
     back_first, rest_sent = lax.optimization_barrier((back_first, rest_grad))
     back_rest = everyone(from_groups(rest_sent, own))
     first_sum = back_project(
-        block_idx, radon_tiles, pad_rows(back_first, own), first_blocks, None, n_pos, width, "back_first"
+        block_idx, radon_wide, pad_rows(back_first, own), first_blocks, None, n_pos, width, "back_first"
     )[0]
     wrapped = rest_grad.shape[2] - probe_width
     tile_pieces = [jnp.concatenate([rest_grad[:, :, wrapped:], first_grad[:, :, : tile_width - probe_width]], axis=2)]
@@ -610,7 +628,7 @@
         tile_pieces.append(source[:, :, begin : begin + tile_width])
     tile_pieces = rotate_pos(tile_pieces, 1)
     obj_pieces = back_project(
-        block_idx, radon_tiles, pad_rows(back_rest, own), rest_blocks, first_sum, n_pos, width, "back_rest"
+        block_idx, radon_wide, pad_rows(back_rest, own), rest_blocks, first_sum, n_pos, width, "back_rest"
     )
     groups = rest_grad.shape[0]
     tile_pieces = [tile_pieces[-j % n_pos] for j in range(n_pos)]

time: 174 us -> 189 us (1.086)
  local copies, waits for them, and re-layouts: 12.2 us -> 40 us
  waiting for transfers between devices: 72 us -> 47.9 us
  other arithmetic: 3.67 us -> 11.7 us
  Pallas kernels: 51.9 us -> 54.8 us
    mul x0 -> x5, local copies, waits for them, and re-layouts: none -> 25.3 us  [on_device(): split * same]
    all_to_all x4, waiting for transfers between devices: 53.6 us -> 34.6 us  [everyone(): return lax.all_to_all(chunk, ('ang', 'pos'), 0, 0, tiled=True)]
    ppermute x15, waiting for transfers between devices: 18.4 us -> 13.3 us  [rotate_pos(): lax.ppermute(pieces[j], 'pos', [(i, (i + sign * j) % count) for i in rang...]
    mul x0 -> x1, other arithmetic: none -> 4.66 us  [on_device(): split * same]
    concatenate x0 -> x1, other arithmetic: none -> 3.38 us  [on_device(): radon_twice = jnp.concatenate([turned, turned], axis=2)]
    pallas_call x2, Pallas kernels: 17.1 us -> 20.5 us  [back_project(): pl.pallas_call(functools.partial(back_project_kernel, blocks, has_start,...]
    unnamed x25 -> x26, local copies, waits for them, and re-layouts: 4.79 us -> 6.55 us
  transfers between devices with their start and end apart: 19 -> 19, of which waited for: 10 -> 8; matrix products, arithmetic and copies ran while one was open for 7% -> 25% of each run, Pallas kernels for 25% -> 25%
where the time goes in v10:
time: 189 us; the launch traced here: 188 us
  Pallas kernels  54.8 us (29%)
  waiting for transfers between devices  47.9 us (25%)
  local copies, waits for them, and re-layouts  40 us (21%)
  starting transfers between devices  32.3 us (17%)
  other arithmetic  11.7 us (6%)
    all_to_all x4, waiting for transfers between devices, everyone(): return lax.all_to_all(chunk, ('ang', 'pos'), 0, 0, tiled=True)  34.6 us
    mul x5, local copies, waits for them, and re-layouts, on_device(): split * same  25.3 us
    pallas_call x2, Pallas kernels, back_project(): pl.pallas_call(functools.partial(back_project_kernel, blocks, has_start,...  20.5 us
    all_to_all x4, starting transfers between devices, everyone(): return lax.all_to_all(chunk, ('ang', 'pos'), 0, 0, tiled=True)  19.2 us
    pallas_call x2, Pallas kernels, project(): pl.pallas_call(functools.partial(project_kernel, blocks, pieces), out_sha...  13.8 us
    ppermute x15, waiting for transfers between devices, rotate_pos(): lax.ppermute(pieces[j], 'pos', [(i, (i + sign * j) % count) for i in rang...  13.3 us
    ppermute x15, starting transfers between devices, rotate_pos(): lax.ppermute(pieces[j], 'pos', [(i, (i + sign * j) % count) for i in rang...  13.2 us
    pallas_call x1, Pallas kernels, exit_rest(): pl.pallas_call(functools.partial(exit_rest_kernel, len(amps)), out_shape=...  10.6 us
  transfers between devices with their start and end apart: 19, of which 8 were waited for; matrix products, arithmetic and copies ran while one was open for 25% of the time, Pallas kernels for 25%

profile of v10, /device:TPU:1, one launch (start us, length us, event | category | flops | bytes accessed | tf_op | source)
XLA Modules:
  0.0 188.0 jit_solution(11597221734073643140)
XLA Ops:
  0.7 0.0 copy-start.1
  0.7 2.1 %dynamic-slice_bitcast_fusion.4 = (bf16[16,8192]{1,0:T(8,128)(2,1)S(1)}, bf16[16,8192]{1,0:T(8,128)(2,1)}, bf16[16,8192]{1,0:T(8,128)(2,1)S(1)}, bf16[16,8192]{1,0:T(8,128)(2,1)}) fusion(bf16[2,32,8192]{2,1,0:T(8,128)(2,1)} %param.9, s32[]{:T(128)S(6)} %select_n.309, s32[]{:T(128)S(6)} %select_n.305, s32[]{:T(128)S(6)} %select_n.303, s32[]{:T(128)S(6)} %select_n.307), kind=kLoop, calls=%fused_computation.25 | loop fusion | bytes 2097168 | tf_op jit(solution)/shard_map/reshape | solution.py:555
  2.8 2.6 %collective-permute-start = (bf16[16,8192]{1,0:T(8,128)(2,1)}, bf16[16,8192]{1,0:T(8,128)(2,1)S(1)}, u32[]{:S(2)}, u32[]{:S(2)}) collective-permute-start(bf16[16,8192]{1,0:T(8,128)(2,1)} %get-tuple-element.93), channel_id=1, source_target_pairs={{0,1},{1,2},{2,3},{3,0},{4,5},{5,6},{6,7},{7,4},{8,9},{9,10},{10,1... | collective-permute-start | bytes 786440 | tf_op jit(solution)/shard_map/ppermute | solution.py:36
  5.5 0.0 collective-permute-start.1
  5.5 0.4 collective-permute-start.2
  5.9 0.3 fusion.5
  6.2 0.3 copy.28
  6.5 0.2 reshape.208
  6.9 0.1 reshape.209.idx_ref
  7.0 1.8 copy.33
  8.7 3.4 %pad_maximum_fusion.radon_ref = bf16[32,256,128]{2,1,0:T(8,128)(2,1)S(1)} fusion(bf16[32,256,64]{2,1,0:T(8,128)(2,1)} %bitcast.91), kind=kLoop, calls=%fused_computation | loop fusion | flops 4194304 | bytes 3145728 | tf_op jit(solution)/shard_map/concatenate | solution.py:582
  12.1 4.8 %collective-permute-done.1.refs_2_ = bf16[16,8192]{1,0:T(8,128)(2,1)S(1)} collective-permute-done((bf16[16,8192]{1,0:T(8,128)(2,1)}, bf16[16,8192]{1,0:T(8,128)(2,1)S(1)}, u32[]{:S(2)}, u32[]{:S(2)}) %collective-permute-start.1) | collective-permute-done | bytes 262176 | tf_op jit(solution)/shard_map/ppermute | solution.py:36
  17.0 0.3 collective-permute-done.2.refs_3_
  17.3 7.8 %project_early.1 = bf16[32,16,1280]{2,1,0:T(8,128)(2,1)} custom-call(s32[32,128]{1,0:T(8,128)S(1)} %reshape.209.idx_ref, bf16[32,256,128]{2,1,0:T(8,128)(2,1)S(1)} %pad_maximum_fusion.radon_ref, bf16[16,8192]{1,0:T(8,128)(2,1)S(1)} %get-tuple-element.49.refs_0_, bf16[16,8192]{1,0:T(8,128)(2,1)S(1)} %collective-permute-done.refs_1_, ...), custom_call_target="tpu_custom_call" | custom-call | flops 10350000128 | bytes 900000 | tf_op jit(solution)/shard_map/project_early/pallas_call | solution.py:144
  25.1 6.6 %all-to-all-start = ((bf16[32,16,1280]{2,1,0:T(8,128)(2,1)}), bf16[32,16,1280]{2,1,0:T(8,128)(2,1)}, u32[]{:S(2)}, u32[]{:S(2)}) async-start(bf16[32,16,1280]{2,1,0:T(8,128)(2,1)} %project_early.1), calls=%async_computation | async-start | bytes 2621440 | tf_op jit(solution)/shard_map/all_to_all | solution.py:537
  31.7 0.1 copy.34
  31.8 0.1 pad_add_fusion.2
  31.9 1.7 collective-permute-start.5
  33.6 0.0 collective-permute-start.4
  33.7 0.5 collective-permute-start.3
  34.2 2.9 %dynamic-slice_bitcast_fusion = (bf16[4,256,256]{2,1,0:T(8,128)(2,1)}, bf16[4,256,256]{2,1,0:T(8,128)(2,1)}, bf16[4,256,256]{2,1,0:T(8,128)(2,1)}, bf16[4,256,256]{2,1,0:T(8,128)(2,1)}) fusion(bf16[4,4,256,256]{3,2,1,0:T(8,128)(2,1)} %param.13, s32[]{:T(128)S(6)} %select_n.316, s32[]{:T(128)S(6)} %select_n.314, s32[]{:T(128)S(6)} %select_n.312, s32[]{:T(128)S(6)} %select_n.310), kind=kLoop, calls=%fused_computation.13 | loop fusion | bytes 4194320 | tf_op jit(solution)/shard_map/jit(dynamic_index_in_dim)/squeeze | solution.py:561
  37.1 1.3 collective-permute-start.6
  38.4 0.0 collective-permute-start.7
  38.4 1.6 collective-permute-start.8
  40.0 0.0 collective-permute-done.4
  40.0 0.0 collective-permute-done.3
  40.0 0.6 pad_add_fusion.3.meta_ref
  40.6 6.0 %project_late.1 = bf16[32,16,768]{2,1,0:T(8,128)(2,1)} custom-call(s32[32,128]{1,0:T(8,128)S(1)} %reshape.209.idx_ref, bf16[32,256,128]{2,1,0:T(8,128)(2,1)S(1)} %pad_maximum_fusion.radon_ref, bf16[16,8192]{1,0:T(8,128)(2,1)S(1)} %get-tuple-element.49.refs_0_, bf16[16,8192]{1,0:T(8,128)(2,1)S(1)} %collective-permute-done.refs_1_, ...), custom_call_target="tpu_custom_call" | custom-call | flops 8049999872 | bytes 700000 | tf_op jit(solution)/shard_map/project_late/pallas_call | solution.py:144
  46.6 16.4 %all-to-all-done.sino_ref.early_ref = bf16[32,16,1280]{2,1,0:T(8,128)(2,1)} async-done(((bf16[32,16,1280]{2,1,0:T(8,128)(2,1)}), bf16[32,16,1280]{2,1,0:T(8,128)(2,1)}, u32[]{:S(2)}, u32[]{:S(2)}) %all-to-all-start) | async-done | bytes 1310752 | tf_op jit(solution)/shard_map/all_to_all | solution.py:537
  63.0 4.4 %all-to-all-start.1 = ((bf16[32,16,768]{2,1,0:T(8,128)(2,1)}), bf16[32,16,768]{2,1,0:T(8,128)(2,1)S(1)}, u32[]{:S(2)}, u32[]{:S(2)}) async-start(bf16[32,16,768]{2,1,0:T(8,128)(2,1)} %project_late.1), calls=%async_computation.1 | async-start | bytes 1572864 | tf_op jit(solution)/shard_map/all_to_all | solution.py:537
  67.4 0.0 collective-permute-done.6.refs_1_
  67.5 1.6 collective-permute-done.8.refs_1_
  69.1 9.9 %exit_first.1 = (f32[2,256,256]{2,1,0:T(8,128)}, bf16[32,16,768]{2,1,0:T(8,128)(2,1)}, f32[2,256,256]{2,1,0:T(8,128)}) custom-call(s32[4,5]{1,0:T(4,128)} %pad_add_fusion.3.meta_ref, bf16[2,256,256]{2,1,0:T(8,128)(2,1)} %probe_ref.3, bf16[512,512]{1,0:T(8,128)(2,1)} %constant.148.forward_ref, bf16[512,512]{1,0:T(8,128)(2,1)} %constant.151.inverse_ref, ...), custom_call_target="tpu_custom_call" | custom-call | flops 11500000256 | bytes 1000000 | tf_op jit(solution)/shard_map/exit_first/pallas_call | solution.py:472
  78.9 8.7 %all-to-all-done.1.late_ref = bf16[32,16,768]{2,1,0:T(8,128)(2,1)S(1)} async-done(((bf16[32,16,768]{2,1,0:T(8,128)(2,1)}), bf16[32,16,768]{2,1,0:T(8,128)(2,1)S(1)}, u32[]{:S(2)}, u32[]{:S(2)}) %all-to-all-start.1) | async-done | bytes 786464 | tf_op jit(solution)/shard_map/all_to_all | solution.py:537
  87.6 4.1 %all-to-all-start.2 = ((bf16[32,16,768]{2,1,0:T(8,128)(2,1)}), bf16[32,16,768]{2,1,0:T(8,128)(2,1)S(1)}, u32[]{:S(2)}, u32[]{:S(2)}) async-start(bf16[32,16,768]{2,1,0:T(8,128)(2,1)} %get-tuple-element.64), calls=%async_computation.2 | async-start | bytes 1572864 | tf_op jit(solution)/shard_map/all_to_all | solution.py:537
  91.7 10.6 %exit_rest.1 = bf16[32,16,1280]{2,1,0:T(8,128)(2,1)} custom-call(s32[4,5]{1,0:T(4,128)} %pad_add_fusion.3.meta_ref, bf16[2,256,256]{2,1,0:T(8,128)(2,1)} %probe_ref.3, bf16[512,512]{1,0:T(8,128)(2,1)} %constant.148.forward_ref, bf16[512,512]{1,0:T(8,128)(2,1)} %constant.151.inverse_ref, bf16[32,16,1280]{2,1,0:T(8,128)(2,1)} %all-to-all-done.sino_ref.early_ref, ...), custom_call_target="tpu_custom_call" | custom-call | flops 11500000256 | bytes 1000000 | tf_op jit(solution)/shard_map/exit_rest/pallas_call | solution.py:488
  102.3 9.5 %all-to-all-done.2.grad_hbm = bf16[32,16,768]{2,1,0:T(8,128)(2,1)S(1)} async-done(((bf16[32,16,768]{2,1,0:T(8,128)(2,1)}), bf16[32,16,768]{2,1,0:T(8,128)(2,1)S(1)}, u32[]{:S(2)}, u32[]{:S(2)}) %all-to-all-start.2) | async-done | bytes 786464 | tf_op jit(solution)/shard_map/all_to_all | solution.py:537
  111.8 4.1 %all-to-all-start.3 = ((bf16[32,16,1280]{2,1,0:T(8,128)(2,1)}), bf16[32,16,1280]{2,1,0:T(8,128)(2,1)}, u32[]{:S(2)}, u32[]{:S(2)}) async-start(bf16[32,16,1280]{2,1,0:T(8,128)(2,1)} %exit_rest.1), calls=%async_computation.3 | async-start | bytes 2621440 | tf_op jit(solution)/shard_map/all_to_all | solution.py:537
  116.0 0.3 copy.23
  116.3 0.2 reshape.206
  116.7 0.7 reshape.207.idx_ref
  117.4 0.2 mul.68
  117.6 0.2 mul.69
  117.8 0.9 mul.65
  118.7 5.6 %mul.66 = bf16[32,2,64,4,2,64]{5,4,3,2,1,0:T(2,128)(2,1)} broadcast(bf16[32,64,4,64]{3,2,1,0:T(4,128)(2,1)S(1)} %mul.65), dimensions={0,2,3,5} | broadcast | bytes 5242880 | tf_op jit(solution)/shard_map/mul | solution.py:608
  124.3 18.4 %mul.67 = bf16[32,128,512]{2,1,0:T(8,128)(2,1)} reshape(bf16[32,2,64,4,2,64]{5,4,3,2,1,0:T(2,128)(2,1)} %mul.66) | data formatting | bytes 8388608 | tf_op jit(solution)/shard_map/mul | solution.py:608
  142.7 4.7 %broadcast_multiply_fusion.wide_hbm = bf16[32,128,512]{2,1,0:T(8,128)(2,1)} fusion(bf16[32,128,512]{2,1,0:T(8,128)(2,1)} %mul.67, bf16[128,512]{1,0:T(8,128)(2,1)S(1)} %mul.69), kind=kLoop, calls=%fused_computation.3 | loop fusion | flops 2097152 | bytes 8519680 | tf_op jit(solution)/shard_map/mul | solution.py:608
  147.3 0.1 slice.101
  147.4 1.7 collective-permute-start.12
  149.1 0.9 fusion.9
  150.1 0.0 collective-permute-start.13
  150.1 0.5 collective-permute-start.14
  150.6 8.4 %back_first.1.refs_0_ = f32[512,8,128]{2,1,0:T(8,128)} custom-call(s32[32,128]{1,0:T(8,128)} %reshape.207.idx_ref, bf16[32,128,512]{2,1,0:T(8,128)(2,1)} %broadcast_multiply_fusion.wide_hbm, bf16[32,16,768]{2,1,0:T(8,128)(2,1)} %copy-done.5), custom_call_target="tpu_custom_call" | custom-call | flops 8049999872 | bytes 700000 | tf_op jit(solution)/shard_map/back_first/pallas_call | solution.py:275
  159.1 12.1 %back_rest.1 = (bf16[16,8192]{1,0:T(8,128)(2,1)}, bf16[16,8192]{1,0:T(8,128)(2,1)}, bf16[16,8192]{1,0:T(8,128)(2,1)}, bf16[16,8192]{1,0:T(8,128)(2,1)}) custom-call(s32[32,128]{1,0:T(8,128)} %reshape.207.idx_ref, bf16[32,128,512]{2,1,0:T(8,128)(2,1)} %broadcast_multiply_fusion.wide_hbm, bf16[32,16,1280]{2,1,0:T(8,128)(2,1)} %all-to-all-done.3.grad_hbm, ...), custom_call_target="tpu_custom_call" | custom-call | flops 10350000128 | bytes 900000 | tf_op jit(solution)/shard_map/back_rest/pallas_call | solution.py:275
  171.1 1.3 collective-permute-start.9
  172.4 1.4 collective-permute-start.10
  173.9 0.0 collective-permute-start.11
  173.9 0.6 select_bitcast_fusion.3
  174.6 0.3 maximum_convert_fusion
  175.0 4.7 %copy.39 = f32[2,256,4,512]{3,2,1,0:T(4,128)} copy(f32[2,256,4,512]{3,1,0,2:T(8,128)S(1)} %maximum_convert_fusion) | data formatting | bytes 8388608
  179.7 5.9 %collective-permute-done.10 = bf16[16,8192]{1,0:T(8,128)(2,1)S(1)} collective-permute-done((bf16[16,8192]{1,0:T(8,128)(2,1)}, bf16[16,8192]{1,0:T(8,128)(2,1)S(1)}, u32[]{:S(2)}, u32[]{:S(2)}) %collective-permute-start.10) | collective-permute-done | bytes 262176 | tf_op jit(solution)/shard_map/ppermute | solution.py:36
  185.6 0.6 collective-permute-done.11
  186.3 0.1 select_bitcast_fusion.7
  186.4 1.6 multiply_add_fusion
  (55 shorter events, 0.5 us)
Async XLA Ops:
  0.6 5.3 %copy-start.8 = (s32[32,32,4]{1,2,0:T(4,128)S(1)}, s32[32,32,4]{1,2,0:T(4,128)}, u32[]{:S(2)}) copy-start(s32[32,32,4]{1,2,0:T(4,128)} %param.11) | copy-start | bytes 49156
  0.7 6.3 %copy-start.1 = (bf16[32,64,256]{2,1,0:T(8,128)(2,1)S(1)}, bf16[32,64,256]{2,1,0:T(8,128)(2,1)}, u32[]{:S(2)}) copy-start(bf16[32,64,256]{2,1,0:T(8,128)(2,1)} %param.10) | copy-start | bytes 3145732
  2.8 9.3 %collective-permute-start = (bf16[16,8192]{1,0:T(8,128)(2,1)}, bf16[16,8192]{1,0:T(8,128)(2,1)S(1)}, u32[]{:S(2)}, u32[]{:S(2)}) collective-permute-start(bf16[16,8192]{1,0:T(8,128)(2,1)} %get-tuple-element.93), channel_id=1, source_target_pairs={{0,1},{1,2},{2,3},{3,0},{4,5},{5,6},{6,7},{7,4},{8,9},{9,10},{10,1... | collective-permute-start | bytes 786440 | tf_op jit(solution)/shard_map/ppermute | solution.py:36
  5.5 11.5 %collective-permute-start.1 = (bf16[16,8192]{1,0:T(8,128)(2,1)}, bf16[16,8192]{1,0:T(8,128)(2,1)S(1)}, u32[]{:S(2)}, u32[]{:S(2)}) collective-permute-start(bf16[16,8192]{1,0:T(8,128)(2,1)} %get-tuple-element.95), channel_id=1, source_target_pairs={{0,2},{1,3},{2,0},{3,1},{4,6},{5,7},{6,4},{7,5},{8,10},{9,11},{10,... | collective-permute-start | bytes 786440 | tf_op jit(solution)/shard_map/ppermute | solution.py:36
  5.5 11.8 %collective-permute-start.2 = (bf16[16,8192]{1,0:T(8,128)(2,1)S(1)}, bf16[16,8192]{1,0:T(8,128)(2,1)S(1)}, u32[]{:S(2)}, u32[]{:S(2)}) collective-permute-start(bf16[16,8192]{1,0:T(8,128)(2,1)S(1)} %get-tuple-element.92), channel_id=1, source_target_pairs={{0,3},{1,0},{2,1},{3,2},{4,7},{5,4},{6,5},{7,6},{8,11},{9,8},{10,9... | collective-permute-start | bytes 786440 | tf_op jit(solution)/shard_map/ppermute | solution.py:36
  25.1 6.7 %copy-start.10 = (s32[4,1]{0,1:T(1,128)S(1)}, s32[4,1]{0,1:T(1,128)}, u32[]{:S(2)}) copy-start(s32[4,1]{0,1:T(1,128)} %param.15) | copy-start | bytes 52
  25.1 6.8 %copy-start.9 = (s32[4,4]{1,0:T(4,128)S(1)}, s32[4,4]{1,0:T(4,128)}, u32[]{:S(2)}) copy-start(s32[4,4]{1,0:T(4,128)} %param.14) | copy-start | bytes 196
  25.1 38.0 %all-to-all-start = ((bf16[32,16,1280]{2,1,0:T(8,128)(2,1)}), bf16[32,16,1280]{2,1,0:T(8,128)(2,1)}, u32[]{:S(2)}, u32[]{:S(2)}) async-start(bf16[32,16,1280]{2,1,0:T(8,128)(2,1)} %project_early.1), calls=%async_computation | async-start | bytes 2621440 | tf_op jit(solution)/shard_map/all_to_all | solution.py:537
  31.9 6.5 %collective-permute-start.5 = (s32[1,5]{1,0:T(1,128)S(1)}, s32[1,5]{1,0:T(1,128)S(1)}, u32[]{:S(2)}, u32[]{:S(2)}) collective-permute-start(s32[1,5]{1,0:T(1,128)S(1)} %get-tuple-element.111), channel_id=1, source_target_pairs={{0,1},{1,2},{2,3},{3,0},{4,5},{5,6},{6,7},{7,4},{8,9},{9,10},{10,1... | collective-permute-start | bytes 68 | tf_op jit(solution)/shard_map/ppermute | solution.py:36
  33.6 6.4 %collective-permute-start.4 = (s32[1,5]{1,0:T(1,128)S(1)}, s32[1,5]{1,0:T(1,128)S(1)}, u32[]{:S(2)}, u32[]{:S(2)}) collective-permute-start(s32[1,5]{1,0:T(1,128)S(1)} %get-tuple-element.112), channel_id=1, source_target_pairs={{0,2},{1,3},{2,0},{3,1},{4,6},{5,7},{6,4},{7,5},{8,10},{9,11},{10,... | collective-permute-start | bytes 68 | tf_op jit(solution)/shard_map/ppermute | solution.py:36
  33.7 6.4 %collective-permute-start.3 = (s32[1,5]{1,0:T(1,128)S(1)}, s32[1,5]{1,0:T(1,128)S(1)}, u32[]{:S(2)}, u32[]{:S(2)}) collective-permute-start(s32[1,5]{1,0:T(1,128)S(1)} %get-tuple-element.113), channel_id=1, source_target_pairs={{0,3},{1,0},{2,1},{3,2},{4,7},{5,4},{6,5},{7,6},{8,11},{9,8},{10,9... | collective-permute-start | bytes 68 | tf_op jit(solution)/shard_map/ppermute | solution.py:36
  37.1 30.4 %collective-permute-start.6 = (bf16[4,256,256]{2,1,0:T(8,128)(2,1)}, bf16[4,256,256]{2,1,0:T(8,128)(2,1)}, u32[]{:S(2)}, u32[]{:S(2)}) collective-permute-start(bf16[4,256,256]{2,1,0:T(8,128)(2,1)} %get-tuple-element.84), channel_id=1, source_target_pairs={{0,3},{1,0},{2,1},{3,2},{4,7},{5,4},{6,5},{7,6},{8,11},{9,8},{10,9... | collective-permute-start | bytes 1572872 | tf_op jit(solution)/shard_map/ppermute | solution.py:36
  38.4 29.1 %collective-permute-start.7 = (bf16[4,256,256]{2,1,0:T(8,128)(2,1)}, bf16[4,256,256]{2,1,0:T(8,128)(2,1)}, u32[]{:S(2)}, u32[]{:S(2)}) collective-permute-start(bf16[4,256,256]{2,1,0:T(8,128)(2,1)} %get-tuple-element.83), channel_id=1, source_target_pairs={{0,2},{1,3},{2,0},{3,1},{4,6},{5,7},{6,4},{7,5},{8,10},{9,11},{10,... | collective-permute-start | bytes 1572872 | tf_op jit(solution)/shard_map/ppermute | solution.py:36
  38.4 30.6 %collective-permute-start.8 = (bf16[4,256,256]{2,1,0:T(8,128)(2,1)}, bf16[4,256,256]{2,1,0:T(8,128)(2,1)}, u32[]{:S(2)}, u32[]{:S(2)}) collective-permute-start(bf16[4,256,256]{2,1,0:T(8,128)(2,1)} %get-tuple-element.82), channel_id=1, source_target_pairs={{0,1},{1,2},{2,3},{3,0},{4,5},{5,6},{6,7},{7,4},{8,9},{9,10},{10,1... | collective-permute-start | bytes 1572872 | tf_op jit(solution)/shard_map/ppermute | solution.py:36
  63.0 24.5 %all-to-all-start.1 = ((bf16[32,16,768]{2,1,0:T(8,128)(2,1)}), bf16[32,16,768]{2,1,0:T(8,128)(2,1)S(1)}, u32[]{:S(2)}, u32[]{:S(2)}) async-start(bf16[32,16,768]{2,1,0:T(8,128)(2,1)} %project_late.1), calls=%async_computation.1 | async-start | bytes 1572864 | tf_op jit(solution)/shard_map/all_to_all | solution.py:537
  87.6 4.1 %copy-start.6 = (bf16[32,16,768]{2,1,0:T(8,128)(2,1)}, bf16[32,16,768]{2,1,0:T(8,128)(2,1)S(1)}, u32[]{:S(2)}) copy-start(bf16[32,16,768]{2,1,0:T(8,128)(2,1)S(1)} %all-to-all-done.1.late_ref) | copy-start | bytes 2359300
  87.6 24.2 %all-to-all-start.2 = ((bf16[32,16,768]{2,1,0:T(8,128)(2,1)}), bf16[32,16,768]{2,1,0:T(8,128)(2,1)S(1)}, u32[]{:S(2)}, u32[]{:S(2)}) async-start(bf16[32,16,768]{2,1,0:T(8,128)(2,1)} %get-tuple-element.64), calls=%async_computation.2 | async-start | bytes 1572864 | tf_op jit(solution)/shard_map/all_to_all | solution.py:537
  102.3 15.5 %copy-start.2 = (bf16[32,64,256]{2,1,0:T(8,128)(2,1)S(1)}, bf16[32,64,256]{2,1,0:T(8,128)(2,1)}, u32[]{:S(2)}) copy-start(bf16[32,64,256]{2,1,0:T(8,128)(2,1)} %param.10) | copy-start | bytes 3145732
  111.8 4.2 %copy-start.5 = (bf16[32,16,768]{2,1,0:T(8,128)(2,1)}, bf16[32,16,768]{2,1,0:T(8,128)(2,1)S(1)}, u32[]{:S(2)}) copy-start(bf16[32,16,768]{2,1,0:T(8,128)(2,1)S(1)} %all-to-all-done.2.grad_hbm) | copy-start | bytes 2359300
  111.8 47.2 %all-to-all-start.3 = ((bf16[32,16,1280]{2,1,0:T(8,128)(2,1)}), bf16[32,16,1280]{2,1,0:T(8,128)(2,1)}, u32[]{:S(2)}, u32[]{:S(2)}) async-start(bf16[32,16,1280]{2,1,0:T(8,128)(2,1)} %exit_rest.1), calls=%async_computation.3 | async-start | bytes 2621440 | tf_op jit(solution)/shard_map/all_to_all | solution.py:537
  142.7 4.7 %copy-start.4 = (bf16[32,16,768]{2,1,0:T(8,128)(2,1)S(1)}, bf16[32,16,768]{2,1,0:T(8,128)(2,1)}, u32[]{:S(2)}) copy-start(bf16[32,16,768]{2,1,0:T(8,128)(2,1)} %get-tuple-element.64) | copy-start | bytes 2359300
  142.7 6.4 %copy-start = (bf16[32,16,1280]{2,1,0:T(8,128)(2,1)S(1)}, bf16[32,16,1280]{2,1,0:T(8,128)(2,1)}, u32[]{:S(2)}) copy-start(bf16[32,16,1280]{2,1,0:T(8,128)(2,1)} %exit_rest.1) | copy-start | bytes 3932164
  147.4 26.4 %collective-permute-start.12 = (bf16[32,16,512]{2,1,0:T(8,128)(2,1)S(1)}, bf16[32,16,512]{2,1,0:T(8,128)(2,1)S(1)}, u32[]{:S(2)}, u32[]{:S(2)}) collective-permute-start(bf16[32,16,512]{2,1,0:T(8,128)(2,1)S(1)} %slice.101), channel_id=1, source_target_pairs={{0,1},{1,2},{2,3},{3,0},{4,5},{5,6},{6,7},{7,4},{8,9},{9,10},{10,1... | collective-permute-start | bytes 1572872 | tf_op jit(solution)/shard_map/ppermute | solution.py:36
  150.1 23.8 %collective-permute-start.13 = (bf16[32,16,512]{2,1,0:T(8,128)(2,1)}, bf16[32,16,512]{2,1,0:T(8,128)(2,1)S(1)}, u32[]{:S(2)}, u32[]{:S(2)}) collective-permute-start(bf16[32,16,512]{2,1,0:T(8,128)(2,1)} %get-tuple-element.87), channel_id=1, source_target_pairs={{0,2},{1,3},{2,0},{3,1},{4,6},{5,7},{6,4},{7,5},{8,10},{9,11},{10,... | collective-permute-start | bytes 1572872 | tf_op jit(solution)/shard_map/ppermute | solution.py:36
  150.1 23.7 %collective-permute-start.14 = (bf16[32,16,512]{2,1,0:T(8,128)(2,1)S(1)}, bf16[32,16,512]{2,1,0:T(8,128)(2,1)S(1)}, u32[]{:S(2)}, u32[]{:S(2)}) collective-permute-start(bf16[32,16,512]{2,1,0:T(8,128)(2,1)S(1)} %get-tuple-element.86), channel_id=1, source_target_pairs={{0,3},{1,0},{2,1},{3,2},{4,7},{5,4},{6,5},{7,6},{8,11},{9,8},{10,9... | collective-permute-start | bytes 1572872 | tf_op jit(solution)/shard_map/ppermute | solution.py:36
  171.1 8.6 %collective-permute-start.9 = (bf16[16,8192]{1,0:T(8,128)(2,1)}, bf16[16,8192]{1,0:T(8,128)(2,1)S(1)}, u32[]{:S(2)}, u32[]{:S(2)}) collective-permute-start(bf16[16,8192]{1,0:T(8,128)(2,1)} %get-tuple-element.72), channel_id=1, source_target_pairs={{0,1},{1,2},{2,3},{3,0},{4,5},{5,6},{6,7},{7,4},{8,9},{9,10},{10,1... | collective-permute-start | bytes 786440 | tf_op jit(solution)/shard_map/ppermute | solution.py:36
  172.4 13.2 %collective-permute-start.10 = (bf16[16,8192]{1,0:T(8,128)(2,1)}, bf16[16,8192]{1,0:T(8,128)(2,1)S(1)}, u32[]{:S(2)}, u32[]{:S(2)}) collective-permute-start(bf16[16,8192]{1,0:T(8,128)(2,1)} %get-tuple-element.73), channel_id=1, source_target_pairs={{0,2},{1,3},{2,0},{3,1},{4,6},{5,7},{6,4},{7,5},{8,10},{9,11},{10,... | collective-permute-start | bytes 786440 | tf_op jit(solution)/shard_map/ppermute | solution.py:36
  173.9 12.4 %collective-permute-start.11 = (bf16[16,8192]{1,0:T(8,128)(2,1)}, bf16[16,8192]{1,0:T(8,128)(2,1)S(1)}, u32[]{:S(2)}, u32[]{:S(2)}) collective-permute-start(bf16[16,8192]{1,0:T(8,128)(2,1)} %get-tuple-element.74), channel_id=1, source_target_pairs={{0,3},{1,0},{2,1},{3,2},{4,7},{5,4},{6,5},{7,6},{8,11},{9,8},{10,9... | collective-permute-start | bytes 786440 | tf_op jit(solution)/shard_map/ppermute | solution.py:36
  175.0 11.3 %copy-start.7 = (bf16[16,8192]{1,0:T(8,128)(2,1)S(1)}, bf16[16,8192]{1,0:T(8,128)(2,1)}, u32[]{:S(2)}) copy-start(bf16[16,8192]{1,0:T(8,128)(2,1)} %get-tuple-element.75) | copy-start | bytes 786436
  179.7 6.7 %copy-start.3 = (bf16[2,32,8192]{2,1,0:T(8,128)(2,1)S(1)}, bf16[2,32,8192]{2,1,0:T(8,128)(2,1)}, u32[]{:S(2)}) copy-start(bf16[2,32,8192]{2,1,0:T(8,128)(2,1)} %param.9) | copy-start | bytes 3145732

commit v11 on v7

--- a/solution.py
+++ b/solution.py
@@ -15,6 +15,7 @@
 GROUP = 8
 MEBI = 1024 * 1024
 everywhere = pl.BlockSpec(memory_space=pltpu.VMEM)
+anywhere = pl.BlockSpec(memory_space=pl.ANY)
 scalars = pl.BlockSpec(memory_space=pltpu.SMEM)
 CHAINS = 4
 BATCH = 4
@@ -81,7 +82,7 @@
                 vv_ref[tiles + k * per_piece + t] = swapped[i * ROWS : (i + 1) * ROWS]
 
 
-def project_blocks(blocks, idx_ref, radon_ref, vv_ref, out_ref, lhs_refs):
+def project_blocks(blocks, idx_ref, radon_ref, vv_ref, out_hbm, out_ref, out_sems, lhs_refs):
     angles, block, span = radon_ref.shape
     feeds = span // block
     low = lower_half((ROWS, LANES))
@@ -113,6 +114,10 @@
                 )
                 out_ref[a, :, pair * LANES : (pair + 1) * LANES] = tile.astype(jnp.bfloat16)
 
+    def leave(step):
+        here = pl.ds(step * 2 * batch, 2 * batch)
+        return pltpu.make_async_copy(out_ref.at[here], out_hbm.at[here], out_sems.at[step])
+
     gather(0, lhs_refs[0])
 
     @pl.loop(0, angles // (2 * batch))
@@ -121,14 +126,19 @@
         multiply(start, lhs_refs[0])
         gather(start + batch, lhs_refs[1])
         multiply(start + batch, lhs_refs[1])
+        leave(step).start()
         gather(jnp.minimum(start + 2 * batch, angles - batch), lhs_refs[0])
+
+    @pl.loop(0, angles // (2 * batch))
+    def _(step):
+        leave(step).wait()
 
 
 def project_kernel(blocks, pieces, idx_ref, radon_ref, *refs):
     vol_refs = refs[:pieces]
-    out_ref, vv_ref, *lhs_refs = refs[pieces:]
+    out_hbm, vv_ref, out_ref, out_sems, *lhs_refs = refs[pieces:]
     arrange(vol_refs, vv_ref)
-    project_blocks(blocks, idx_ref, radon_ref, vv_ref, out_ref, lhs_refs)
+    project_blocks(blocks, idx_ref, radon_ref, vv_ref, out_hbm, out_ref, out_sems, lhs_refs)
 
 
 def guess(microseconds):
@@ -146,8 +156,9 @@
         functools.partial(project_kernel, blocks, pieces),
         out_shape=jax.ShapeDtypeStruct(out_shape, jnp.bfloat16),
         in_specs=[scalars, everywhere] + [everywhere] * pieces,
-        out_specs=everywhere,
+        out_specs=anywhere,
         scratch_shapes=[pltpu.VMEM((2 * tiles, ROWS, LANES), jnp.bfloat16)]
+        + [pltpu.VMEM(out_shape, jnp.bfloat16), pltpu.SemaphoreType.DMA((angles // (2 * BATCH),))]
         + [pltpu.VMEM((BATCH, len(blocks) * ROWS, span), jnp.bfloat16)] * 2,
         compiler_params=pltpu.CompilerParams(
             vmem_limit_bytes=14 * MEBI + 2 * radon_tiles.size + 2 * math.prod(out_shape)
@@ -157,18 +168,37 @@
     )(idx, radon_tiles, *vol_pieces)
 
 
-def back_project_kernel(blocks, has_start, outs, idx_ref, radon_ref, grad_ref, *refs):
+def back_project_kernel(blocks, has_start, outs, idx_ref, radon_hbm, grad_hbm, *refs):
     start_ref, refs = (refs[0], refs[1:]) if has_start else (None, refs)
     out_refs, refs = refs[:outs], refs[outs:]
-    acc_refs, (w_ref, *contrib_refs) = refs[:CHAINS], refs[CHAINS:]
-    if has_start:
-        contrib_refs, start_sem = contrib_refs[:-1], contrib_refs[-1]
-        start_copy = pltpu.make_async_copy(start_ref, acc_refs[0], start_sem)
-        start_copy.start()
+    acc_refs, refs = refs[:CHAINS], refs[CHAINS:]
+    radon_ref, grad_ref, radon_sems, grad_sems, w_ref, *refs = refs
+    contrib_refs = refs[:2]
     angles, block, span = radon_ref.shape
     pairs = len(blocks) // 2
     feeds = span // block
     coef_blocks = acc_refs[0].shape[0]
+    steps = angles // CHAINS
+
+    def copies(step):
+        here = pl.ds(step * CHAINS, CHAINS)
+        return (
+            pltpu.make_async_copy(radon_hbm.at[here], radon_ref.at[here], radon_sems.at[step]),
+            pltpu.make_async_copy(grad_hbm.at[here], grad_ref.at[here], grad_sems.at[step]),
+        )
+
+    def arrived(step):
+        for copy in copies(step):
+            copy.wait()
+
+    @pl.loop(0, steps)
+    def _(step):
+        for copy in copies(step):
+            copy.start()
+
+    if has_start:
+        start_copy = pltpu.make_async_copy(start_ref, acc_refs[0], refs[2])
+        start_copy.start()
 
     @pl.loop(0, coef_blocks, unroll=16)
     def _(t):
@@ -177,7 +207,6 @@
 
     low = lower_half((GROUP, LANES))
     low_rows = lower_half((block, LANES))
-    w_ref[...] = jnp.zeros_like(w_ref)
 
     def widen(slot, a):
         for jp in range(feeds // 2):
@@ -213,15 +242,23 @@
                     tile = contrib_ref[n, row : row + GROUP, j * LANES : (j + 1) * LANES]
                     acc_refs[n][idx_ref[start + n, b * feeds + j]] += tile
 
+    arrived(0)
     multiply(0, 0, contrib_refs[0])
     if has_start:
         start_copy.wait()
 
-    @pl.loop(0, angles // (2 * CHAINS))
-    def _(step):
-        start = step * 2 * CHAINS
+    @pl.loop(0, steps // 2)
+    def _(half):
+        step = 2 * half
+        start = step * CHAINS
+        arrived(step + 1)
         multiply(start + CHAINS, 1, contrib_refs[1])
         scatter(start, contrib_refs[0])
+
+        @pl.when(step + 2 < steps)
+        def _():
+            arrived(step + 2)
+
         multiply(jnp.minimum(start + 2 * CHAINS, angles - CHAINS), 0, contrib_refs[0])
         scatter(start + CHAINS, contrib_refs[1])
 
@@ -264,9 +301,11 @@
     return pl.pallas_call(
         functools.partial(back_project_kernel, blocks, has_start, len(out_shape)),
         out_shape=out_shape,
-        in_specs=[scalars] + [everywhere] * 2 + [pl.BlockSpec(memory_space=pl.ANY)] * has_start,
+        in_specs=[scalars] + [anywhere] * (len(operands) - 1),
         out_specs=[everywhere] * len(out_shape),
         scratch_shapes=[pltpu.VMEM((coef_blocks, GROUP, LANES), jnp.float32)] * CHAINS
+        + [pltpu.VMEM(radon_tiles.shape, jnp.bfloat16), pltpu.VMEM(grads.shape, jnp.bfloat16)]
+        + [pltpu.SemaphoreType.DMA((angles // CHAINS,))] * 2
         + [pltpu.VMEM((2 * CHAINS, 2 * block, 2 * span), jnp.bfloat16)]
         + [pltpu.VMEM((CHAINS, rows, 2 * span), jnp.float32)] * 2
         + [pltpu.SemaphoreType.DMA] * has_start,

time: 174 us -> 175 us (level)
  Pallas kernels: 51.9 us -> 54.5 us
    pallas_call x2, Pallas kernels: 17.1 us -> 20.2 us  [back_project(): pl.pallas_call(functools.partial(back_project_kernel, blocks, has_start,...]
    pallas_call x1, Pallas kernels: 9.89 us -> 7.86 us  [exit_first(): pl.pallas_call(functools.partial(exit_first_kernel, len(amps)), out_shape...]
    pallas_call x1, Pallas kernels: 10.6 us -> 12.6 us  [exit_rest(): pl.pallas_call(functools.partial(exit_rest_kernel, len(amps)), out_shape=...]
  transfers between devices with their start and end apart: 19 -> 19, of which waited for: 10 -> 10; matrix products, arithmetic and copies ran while one was open for 7% -> 7% of each run, Pallas kernels for 25% -> 27%
where the time goes in v11:
time: 175 us
  waiting for transfers between devices  70.7 us (40%)
  Pallas kernels  54.5 us (31%)
  starting transfers between devices  32.3 us (18%)
  local copies, waits for them, and re-layouts  12.2 us (7%)
  other arithmetic  3.67 us (2%)
    all_to_all x4, waiting for transfers between devices, everyone(): return lax.all_to_all(chunk, ('ang', 'pos'), 0, 0, tiled=True)  52.4 us
    pallas_call x2, Pallas kernels, back_project(): pl.pallas_call(functools.partial(back_project_kernel, blocks, has_start,...  20.2 us
    all_to_all x4, starting transfers between devices, everyone(): return lax.all_to_all(chunk, ('ang', 'pos'), 0, 0, tiled=True)  19.1 us
    ppermute x15, waiting for transfers between devices, rotate_pos(): lax.ppermute(pieces[j], 'pos', [(i, (i + sign * j) % count) for i in rang...  18.4 us
    pallas_call x2, Pallas kernels, project(): pl.pallas_call(functools.partial(project_kernel, blocks, pieces), out_sha...  13.8 us
    ppermute x15, starting transfers between devices, rotate_pos(): lax.ppermute(pieces[j], 'pos', [(i, (i + sign * j) % count) for i in rang...  13.1 us
    pallas_call x1, Pallas kernels, exit_rest(): pl.pallas_call(functools.partial(exit_rest_kernel, len(amps)), out_shape=...  12.6 us
    pallas_call x1, Pallas kernels, exit_first(): pl.pallas_call(functools.partial(exit_first_kernel, len(amps)), out_shape...  7.86 us
  transfers between devices with their start and end apart: 19, of which 10 were waited for; matrix products, arithmetic and copies ran while one was open for 7% of the time, Pallas kernels for 27%

profile of v11, /device:TPU:1, one launch (start us, length us, event | category | flops | bytes accessed | tf_op | source)
XLA Modules:
  0.0 174.6 jit_solution(10263435298688843014)
XLA Ops:
  0.7 0.0 copy-start
  0.7 1.3 dynamic-slice_bitcast_fusion.4
  2.1 2.7 %collective-permute-start = (bf16[16,8192]{1,0:T(8,128)(2,1)S(1)}, bf16[16,8192]{1,0:T(8,128)(2,1)S(1)}, u32[]{:S(2)}, u32[]{:S(2)}) collective-permute-start(bf16[16,8192]{1,0:T(8,128)(2,1)S(1)} %get-tuple-element.89), channel_id=1, source_target_pairs={{0,1},{1,2},{2,3},{3,0},{4,5},{5,6},{6,7},{7,4},{8,9},{9,10},{10,1... | collective-permute-start | bytes 786440 | tf_op jit(solution)/shard_map/ppermute | solution.py:37
  4.7 0.0 collective-permute-start.1
  4.7 0.5 collective-permute-start.2
  5.2 0.3 fusion.5
  5.5 0.3 copy.27
  5.8 0.2 reshape.194
  6.2 0.1 reshape.195.idx_ref
  6.3 4.0 %collective-permute-done.refs_1_ = bf16[16,8192]{1,0:T(8,128)(2,1)S(1)} collective-permute-done((bf16[16,8192]{1,0:T(8,128)(2,1)S(1)}, bf16[16,8192]{1,0:T(8,128)(2,1)S(1)}, u32[]{:S(2)}, u32[]{:S(2)}) %collective-permute-start) | collective-permute-done | bytes 262176 | tf_op jit(solution)/shard_map/ppermute | solution.py:37
  10.2 5.6 %collective-permute-done.1.refs_2_ = bf16[16,8192]{1,0:T(8,128)(2,1)S(1)} collective-permute-done((bf16[16,8192]{1,0:T(8,128)(2,1)S(1)}, bf16[16,8192]{1,0:T(8,128)(2,1)S(1)}, u32[]{:S(2)}, u32[]{:S(2)}) %collective-permute-start.1) | collective-permute-done | bytes 262176 | tf_op jit(solution)/shard_map/ppermute | solution.py:37
  15.8 0.5 collective-permute-done.2.refs_3_
  16.3 7.7 %project_early.1 = bf16[32,16,1280]{2,1,0:T(8,128)(2,1)} custom-call(s32[32,128]{1,0:T(8,128)S(1)} %reshape.195.idx_ref, bf16[32,64,256]{2,1,0:T(8,128)(2,1)S(1)} %copy-done, bf16[16,8192]{1,0:T(8,128)(2,1)S(1)} %get-tuple-element.49.refs_0_, bf16[16,8192]{1,0:T(8,128)(2,1)S(1)} %collective-permute-done.refs_1_, ...), custom_call_target="tpu_custom_call" | custom-call | flops 10350000128 | bytes 900000 | tf_op jit(solution)/shard_map/project_early/pallas_call | solution.py:155
  24.1 0.0 copy-start.10
  24.1 0.0 copy-start.9
  24.1 6.5 %all-to-all-start = ((bf16[32,16,1280]{2,1,0:T(8,128)(2,1)}), bf16[32,16,1280]{2,1,0:T(8,128)(2,1)S(1)}, u32[]{:S(2)}, u32[]{:S(2)}) async-start(bf16[32,16,1280]{2,1,0:T(8,128)(2,1)} %project_early.1), calls=%async_computation | async-start | bytes 2621440 | tf_op jit(solution)/shard_map/all_to_all | solution.py:564
  30.7 0.1 copy.32
  30.8 0.1 pad_add_fusion.2
  30.9 1.7 collective-permute-start.5
  32.6 0.0 collective-permute-start.4
  32.6 0.5 collective-permute-start.3
  33.1 2.9 %dynamic-slice_bitcast_fusion = (bf16[4,256,256]{2,1,0:T(8,128)(2,1)}, bf16[4,256,256]{2,1,0:T(8,128)(2,1)}, bf16[4,256,256]{2,1,0:T(8,128)(2,1)}, bf16[4,256,256]{2,1,0:T(8,128)(2,1)}) fusion(bf16[4,4,256,256]{3,2,1,0:T(8,128)(2,1)} %param.13, s32[]{:T(128)S(6)} %select_n.316, s32[]{:T(128)S(6)} %select_n.314, s32[]{:T(128)S(6)} %select_n.312, s32[]{:T(128)S(6)} %select_n.310), kind=kLoop, calls=%fused_computation.11 | loop fusion | bytes 4194320 | tf_op jit(solution)/shard_map/jit(dynamic_index_in_dim)/squeeze | solution.py:588
  36.0 1.3 collective-permute-start.6
  37.4 0.0 collective-permute-start.7
  37.4 0.0 collective-permute-done.5
  37.4 1.6 collective-permute-start.8
  39.0 0.0 collective-permute-done.4
  39.0 0.6 pad_add_fusion.3.meta_ref
  39.6 6.1 %project_late.1 = bf16[32,16,768]{2,1,0:T(8,128)(2,1)} custom-call(s32[32,128]{1,0:T(8,128)S(1)} %reshape.195.idx_ref, bf16[32,64,256]{2,1,0:T(8,128)(2,1)S(1)} %copy-done, bf16[16,8192]{1,0:T(8,128)(2,1)S(1)} %get-tuple-element.49.refs_0_, bf16[16,8192]{1,0:T(8,128)(2,1)S(1)} %collective-permute-done.refs_1_, ...), custom_call_target="tpu_custom_call" | custom-call | flops 8049999872 | bytes 700000 | tf_op jit(solution)/shard_map/project_late/pallas_call | solution.py:155
  45.8 16.2 %all-to-all-done.sino_ref.early_ref = bf16[32,16,1280]{2,1,0:T(8,128)(2,1)S(1)} async-done(((bf16[32,16,1280]{2,1,0:T(8,128)(2,1)}), bf16[32,16,1280]{2,1,0:T(8,128)(2,1)S(1)}, u32[]{:S(2)}, u32[]{:S(2)}) %all-to-all-start) | async-done | bytes 1310752 | tf_op jit(solution)/shard_map/all_to_all | solution.py:564
  62.0 4.4 %all-to-all-start.1 = ((bf16[32,16,768]{2,1,0:T(8,128)(2,1)}), bf16[32,16,768]{2,1,0:T(8,128)(2,1)S(1)}, u32[]{:S(2)}, u32[]{:S(2)}) async-start(bf16[32,16,768]{2,1,0:T(8,128)(2,1)} %project_late.1), calls=%async_computation.1 | async-start | bytes 1572864 | tf_op jit(solution)/shard_map/all_to_all | solution.py:564
  66.3 0.0 collective-permute-done.6.refs_1_
  66.3 0.0 collective-permute-done.7.refs_0_
  66.4 1.7 collective-permute-done.8.refs_1_
  68.1 7.9 %exit_first.1 = (f32[2,256,256]{2,1,0:T(8,128)}, bf16[32,16,768]{2,1,0:T(8,128)(2,1)}, f32[2,256,256]{2,1,0:T(8,128)}) custom-call(s32[4,5]{1,0:T(4,128)} %pad_add_fusion.3.meta_ref, bf16[2,256,256]{2,1,0:T(8,128)(2,1)} %probe_ref.3, bf16[512,512]{1,0:T(8,128)(2,1)} %constant.148.forward_ref, bf16[512,512]{1,0:T(8,128)(2,1)} %constant.151.inverse_ref, ...), custom_call_target="tpu_custom_call" | custom-call | flops 11500000256 | bytes 1000000 | tf_op jit(solution)/shard_map/exit_first/pallas_call | solution.py:499
  75.9 10.6 %all-to-all-done.1.late_ref = bf16[32,16,768]{2,1,0:T(8,128)(2,1)S(1)} async-done(((bf16[32,16,768]{2,1,0:T(8,128)(2,1)}), bf16[32,16,768]{2,1,0:T(8,128)(2,1)S(1)}, u32[]{:S(2)}, u32[]{:S(2)}) %all-to-all-start.1) | async-done | bytes 786464 | tf_op jit(solution)/shard_map/all_to_all | solution.py:564
  86.5 4.1 %all-to-all-start.2 = ((bf16[32,16,768]{2,1,0:T(8,128)(2,1)}), bf16[32,16,768]{2,1,0:T(8,128)(2,1)S(1)}, u32[]{:S(2)}, u32[]{:S(2)}) async-start(bf16[32,16,768]{2,1,0:T(8,128)(2,1)} %get-tuple-element.60), calls=%async_computation.2 | async-start | bytes 1572864 | tf_op jit(solution)/shard_map/all_to_all | solution.py:564
  90.6 12.6 %exit_rest.1 = bf16[32,16,1280]{2,1,0:T(8,128)(2,1)} custom-call(s32[4,5]{1,0:T(4,128)} %pad_add_fusion.3.meta_ref, bf16[2,256,256]{2,1,0:T(8,128)(2,1)} %probe_ref.3, bf16[512,512]{1,0:T(8,128)(2,1)} %constant.148.forward_ref, bf16[512,512]{1,0:T(8,128)(2,1)} %constant.151.inverse_ref, bf16[32,16,1280]{2,1,0:T(8,128)(2,1)} %copy-done.4, ...), custom_call_target="tpu_custom_call" | custom-call | flops 11500000256 | bytes 1000000 | tf_op jit(solution)/shard_map/exit_rest/pallas_call | solution.py:515
  103.2 7.5 %all-to-all-done.2.grad_hbm = bf16[32,16,768]{2,1,0:T(8,128)(2,1)S(1)} async-done(((bf16[32,16,768]{2,1,0:T(8,128)(2,1)}), bf16[32,16,768]{2,1,0:T(8,128)(2,1)S(1)}, u32[]{:S(2)}, u32[]{:S(2)}) %all-to-all-start.2) | async-done | bytes 786464 | tf_op jit(solution)/shard_map/all_to_all | solution.py:564
  110.7 4.1 %all-to-all-start.3 = ((bf16[32,16,1280]{2,1,0:T(8,128)(2,1)}), bf16[32,16,1280]{2,1,0:T(8,128)(2,1)}, u32[]{:S(2)}, u32[]{:S(2)}) async-start(bf16[32,16,1280]{2,1,0:T(8,128)(2,1)} %exit_rest.1), calls=%async_computation.3 | async-start | bytes 2621440 | tf_op jit(solution)/shard_map/all_to_all | solution.py:564
  114.9 0.0 copy-start.1
  114.9 0.3 copy.22
  115.2 0.2 reshape.192
  115.6 0.7 reshape.193.idx_ref
  116.3 0.1 slice.101
  116.4 1.7 collective-permute-start.12
  118.1 0.9 fusion.9
  119.0 0.0 collective-permute-start.13
  119.1 0.5 collective-permute-start.14
  119.6 8.6 %back_first.1.refs_0_ = f32[512,8,128]{2,1,0:T(8,128)} custom-call(s32[32,128]{1,0:T(8,128)} %reshape.193.idx_ref, bf16[32,64,256]{2,1,0:T(8,128)(2,1)} %radon_hbm.3, bf16[32,16,768]{2,1,0:T(8,128)(2,1)} %copy-done.5), custom_call_target="tpu_custom_call" | custom-call | flops 8049999872 | bytes 700000 | tf_op jit(solution)/shard_map/back_first/pallas_call | solution.py:301
  128.2 18.1 %all-to-all-done.3.grad_hbm = bf16[32,16,1280]{2,1,0:T(8,128)(2,1)} async-done(((bf16[32,16,1280]{2,1,0:T(8,128)(2,1)}), bf16[32,16,1280]{2,1,0:T(8,128)(2,1)}, u32[]{:S(2)}, u32[]{:S(2)}) %all-to-all-start.3) | async-done | bytes 1310752 | tf_op jit(solution)/shard_map/all_to_all | solution.py:564
  146.3 11.6 %back_rest.1 = (bf16[16,8192]{1,0:T(8,128)(2,1)}, bf16[16,8192]{1,0:T(8,128)(2,1)}, bf16[16,8192]{1,0:T(8,128)(2,1)}, bf16[16,8192]{1,0:T(8,128)(2,1)}) custom-call(s32[32,128]{1,0:T(8,128)} %reshape.193.idx_ref, bf16[32,64,256]{2,1,0:T(8,128)(2,1)} %radon_hbm.3, bf16[32,16,1280]{2,1,0:T(8,128)(2,1)} %all-to-all-done.3.grad_hbm, ...), custom_call_target="tpu_custom_call" | custom-call | flops 10350000128 | bytes 900000 | tf_op jit(solution)/shard_map/back_rest/pallas_call | solution.py:301
  157.9 1.9 %collective-permute-start.9 = (bf16[16,8192]{1,0:T(8,128)(2,1)}, bf16[16,8192]{1,0:T(8,128)(2,1)S(1)}, u32[]{:S(2)}, u32[]{:S(2)}) collective-permute-start(bf16[16,8192]{1,0:T(8,128)(2,1)} %get-tuple-element.68), channel_id=1, source_target_pairs={{0,1},{1,2},{2,3},{3,0},{4,5},{5,6},{6,7},{7,4},{8,9},{9,10},{10,1... | collective-permute-start | bytes 786440 | tf_op jit(solution)/shard_map/ppermute | solution.py:37
  159.8 0.7 collective-permute-start.10
  160.5 0.0 collective-permute-done.12
  160.5 0.0 collective-permute-done.14
  160.5 0.6 select_bitcast_fusion.3
  161.2 0.3 maximum_convert_fusion
  161.6 4.7 %copy.37 = f32[2,256,4,512]{3,2,1,0:T(4,128)} copy(f32[2,256,4,512]{3,1,0,2:T(8,128)S(1)} %maximum_convert_fusion) | data formatting | bytes 8388608
  166.3 0.0 collective-permute-done.9
  166.3 5.9 %collective-permute-done.10 = bf16[16,8192]{1,0:T(8,128)(2,1)S(1)} collective-permute-done((bf16[16,8192]{1,0:T(8,128)(2,1)}, bf16[16,8192]{1,0:T(8,128)(2,1)S(1)}, u32[]{:S(2)}, u32[]{:S(2)}) %collective-permute-start.10) | collective-permute-done | bytes 262176 | tf_op jit(solution)/shard_map/ppermute | solution.py:37
  172.3 0.6 collective-permute-done.11
  172.9 0.1 select_bitcast_fusion.7
  173.0 1.6 multiply_add_fusion
  (46 shorter events, 0.5 us)
Async XLA Ops:
  0.6 4.6 %copy-start.8 = (s32[32,32,4]{1,2,0:T(4,128)S(1)}, s32[32,32,4]{1,2,0:T(4,128)}, u32[]{:S(2)}) copy-start(s32[32,32,4]{1,2,0:T(4,128)} %param.11) | copy-start | bytes 49156
  0.7 15.7 %copy-start = (bf16[32,64,256]{2,1,0:T(8,128)(2,1)S(1)}, bf16[32,64,256]{2,1,0:T(8,128)(2,1)}, u32[]{:S(2)}) copy-start(bf16[32,64,256]{2,1,0:T(8,128)(2,1)} %radon_hbm.3) | copy-start | bytes 3145732
  2.1 8.2 %collective-permute-start = (bf16[16,8192]{1,0:T(8,128)(2,1)S(1)}, bf16[16,8192]{1,0:T(8,128)(2,1)S(1)}, u32[]{:S(2)}, u32[]{:S(2)}) collective-permute-start(bf16[16,8192]{1,0:T(8,128)(2,1)S(1)} %get-tuple-element.89), channel_id=1, source_target_pairs={{0,1},{1,2},{2,3},{3,0},{4,5},{5,6},{6,7},{7,4},{8,9},{9,10},{10,1... | collective-permute-start | bytes 786440 | tf_op jit(solution)/shard_map/ppermute | solution.py:37
  4.7 11.1 %collective-permute-start.1 = (bf16[16,8192]{1,0:T(8,128)(2,1)S(1)}, bf16[16,8192]{1,0:T(8,128)(2,1)S(1)}, u32[]{:S(2)}, u32[]{:S(2)}) collective-permute-start(bf16[16,8192]{1,0:T(8,128)(2,1)S(1)} %get-tuple-element.91), channel_id=1, source_target_pairs={{0,2},{1,3},{2,0},{3,1},{4,6},{5,7},{6,4},{7,5},{8,10},{9,11},{10,... | collective-permute-start | bytes 786440 | tf_op jit(solution)/shard_map/ppermute | solution.py:37
  4.7 11.6 %collective-permute-start.2 = (bf16[16,8192]{1,0:T(8,128)(2,1)S(1)}, bf16[16,8192]{1,0:T(8,128)(2,1)S(1)}, u32[]{:S(2)}, u32[]{:S(2)}) collective-permute-start(bf16[16,8192]{1,0:T(8,128)(2,1)S(1)} %get-tuple-element.88), channel_id=1, source_target_pairs={{0,3},{1,0},{2,1},{3,2},{4,7},{5,4},{6,5},{7,6},{8,11},{9,8},{10,9... | collective-permute-start | bytes 786440 | tf_op jit(solution)/shard_map/ppermute | solution.py:37
  24.1 6.6 %copy-start.10 = (s32[4,1]{0,1:T(1,128)S(1)}, s32[4,1]{0,1:T(1,128)}, u32[]{:S(2)}) copy-start(s32[4,1]{0,1:T(1,128)} %param.15) | copy-start | bytes 52
  24.1 6.7 %copy-start.9 = (s32[4,4]{1,0:T(4,128)S(1)}, s32[4,4]{1,0:T(4,128)}, u32[]{:S(2)}) copy-start(s32[4,4]{1,0:T(4,128)} %param.14) | copy-start | bytes 196
  24.1 37.9 %all-to-all-start = ((bf16[32,16,1280]{2,1,0:T(8,128)(2,1)}), bf16[32,16,1280]{2,1,0:T(8,128)(2,1)S(1)}, u32[]{:S(2)}, u32[]{:S(2)}) async-start(bf16[32,16,1280]{2,1,0:T(8,128)(2,1)} %project_early.1), calls=%async_computation | async-start | bytes 2621440 | tf_op jit(solution)/shard_map/all_to_all | solution.py:564
  30.9 6.5 %collective-permute-start.5 = (s32[1,5]{1,0:T(1,128)S(1)}, s32[1,5]{1,0:T(1,128)S(1)}, u32[]{:S(2)}, u32[]{:S(2)}) collective-permute-start(s32[1,5]{1,0:T(1,128)S(1)} %get-tuple-element.107), channel_id=1, source_target_pairs={{0,1},{1,2},{2,3},{3,0},{4,5},{5,6},{6,7},{7,4},{8,9},{9,10},{10,1... | collective-permute-start | bytes 68 | tf_op jit(solution)/shard_map/ppermute | solution.py:37
  32.6 6.4 %collective-permute-start.4 = (s32[1,5]{1,0:T(1,128)S(1)}, s32[1,5]{1,0:T(1,128)S(1)}, u32[]{:S(2)}, u32[]{:S(2)}) collective-permute-start(s32[1,5]{1,0:T(1,128)S(1)} %get-tuple-element.108), channel_id=1, source_target_pairs={{0,2},{1,3},{2,0},{3,1},{4,6},{5,7},{6,4},{7,5},{8,10},{9,11},{10,... | collective-permute-start | bytes 68 | tf_op jit(solution)/shard_map/ppermute | solution.py:37
  32.6 6.4 %collective-permute-start.3 = (s32[1,5]{1,0:T(1,128)S(1)}, s32[1,5]{1,0:T(1,128)S(1)}, u32[]{:S(2)}, u32[]{:S(2)}) collective-permute-start(s32[1,5]{1,0:T(1,128)S(1)} %get-tuple-element.109), channel_id=1, source_target_pairs={{0,3},{1,0},{2,1},{3,2},{4,7},{5,4},{6,5},{7,6},{8,11},{9,8},{10,9... | collective-permute-start | bytes 68 | tf_op jit(solution)/shard_map/ppermute | solution.py:37
  36.0 30.3 %collective-permute-start.6 = (bf16[4,256,256]{2,1,0:T(8,128)(2,1)}, bf16[4,256,256]{2,1,0:T(8,128)(2,1)}, u32[]{:S(2)}, u32[]{:S(2)}) collective-permute-start(bf16[4,256,256]{2,1,0:T(8,128)(2,1)} %get-tuple-element.80), channel_id=1, source_target_pairs={{0,3},{1,0},{2,1},{3,2},{4,7},{5,4},{6,5},{7,6},{8,11},{9,8},{10,9... | collective-permute-start | bytes 1572872 | tf_op jit(solution)/shard_map/ppermute | solution.py:37
  37.4 29.0 %collective-permute-start.7 = (bf16[4,256,256]{2,1,0:T(8,128)(2,1)}, bf16[4,256,256]{2,1,0:T(8,128)(2,1)}, u32[]{:S(2)}, u32[]{:S(2)}) collective-permute-start(bf16[4,256,256]{2,1,0:T(8,128)(2,1)} %get-tuple-element.79), channel_id=1, source_target_pairs={{0,2},{1,3},{2,0},{3,1},{4,6},{5,7},{6,4},{7,5},{8,10},{9,11},{10,... | collective-permute-start | bytes 1572872 | tf_op jit(solution)/shard_map/ppermute | solution.py:37
  37.4 30.7 %collective-permute-start.8 = (bf16[4,256,256]{2,1,0:T(8,128)(2,1)}, bf16[4,256,256]{2,1,0:T(8,128)(2,1)}, u32[]{:S(2)}, u32[]{:S(2)}) collective-permute-start(bf16[4,256,256]{2,1,0:T(8,128)(2,1)} %get-tuple-element.78), channel_id=1, source_target_pairs={{0,1},{1,2},{2,3},{3,0},{4,5},{5,6},{6,7},{7,4},{8,9},{9,10},{10,1... | collective-permute-start | bytes 1572872 | tf_op jit(solution)/shard_map/ppermute | solution.py:37
  62.0 6.1 %copy-start.4 = (bf16[32,16,1280]{2,1,0:T(8,128)(2,1)}, bf16[32,16,1280]{2,1,0:T(8,128)(2,1)S(1)}, u32[]{:S(2)}) copy-start(bf16[32,16,1280]{2,1,0:T(8,128)(2,1)S(1)} %all-to-all-done.sino_ref.early_ref) | copy-start | bytes 3932164
  62.0 24.5 %all-to-all-start.1 = ((bf16[32,16,768]{2,1,0:T(8,128)(2,1)}), bf16[32,16,768]{2,1,0:T(8,128)(2,1)S(1)}, u32[]{:S(2)}, u32[]{:S(2)}) async-start(bf16[32,16,768]{2,1,0:T(8,128)(2,1)} %project_late.1), calls=%async_computation.1 | async-start | bytes 1572864 | tf_op jit(solution)/shard_map/all_to_all | solution.py:564
  86.5 4.1 %copy-start.6 = (bf16[32,16,768]{2,1,0:T(8,128)(2,1)}, bf16[32,16,768]{2,1,0:T(8,128)(2,1)S(1)}, u32[]{:S(2)}) copy-start(bf16[32,16,768]{2,1,0:T(8,128)(2,1)S(1)} %all-to-all-done.1.late_ref) | copy-start | bytes 2359300
  86.5 24.2 %all-to-all-start.2 = ((bf16[32,16,768]{2,1,0:T(8,128)(2,1)}), bf16[32,16,768]{2,1,0:T(8,128)(2,1)S(1)}, u32[]{:S(2)}, u32[]{:S(2)}) async-start(bf16[32,16,768]{2,1,0:T(8,128)(2,1)} %get-tuple-element.60), calls=%async_computation.2 | async-start | bytes 1572864 | tf_op jit(solution)/shard_map/all_to_all | solution.py:564
  103.2 13.1 %copy-start.3 = (bf16[32,16,768]{2,1,0:T(8,128)(2,1)S(1)}, bf16[32,16,768]{2,1,0:T(8,128)(2,1)}, u32[]{:S(2)}) copy-start(bf16[32,16,768]{2,1,0:T(8,128)(2,1)} %get-tuple-element.60) | copy-start | bytes 2359300
  110.7 4.8 %copy-start.5 = (bf16[32,16,768]{2,1,0:T(8,128)(2,1)}, bf16[32,16,768]{2,1,0:T(8,128)(2,1)S(1)}, u32[]{:S(2)}) copy-start(bf16[32,16,768]{2,1,0:T(8,128)(2,1)S(1)} %all-to-all-done.2.grad_hbm) | copy-start | bytes 2359300
  110.7 35.5 %all-to-all-start.3 = ((bf16[32,16,1280]{2,1,0:T(8,128)(2,1)}), bf16[32,16,1280]{2,1,0:T(8,128)(2,1)}, u32[]{:S(2)}, u32[]{:S(2)}) async-start(bf16[32,16,1280]{2,1,0:T(8,128)(2,1)} %exit_rest.1), calls=%async_computation.3 | async-start | bytes 2621440 | tf_op jit(solution)/shard_map/all_to_all | solution.py:564
  114.9 3.2 %copy-start.1 = (bf16[32,16,1280]{2,1,0:T(8,128)(2,1)S(1)}, bf16[32,16,1280]{2,1,0:T(8,128)(2,1)}, u32[]{:S(2)}) copy-start(bf16[32,16,1280]{2,1,0:T(8,128)(2,1)} %exit_rest.1) | copy-start | bytes 3932164
  116.4 44.1 %collective-permute-start.12 = (bf16[32,16,512]{2,1,0:T(8,128)(2,1)S(1)}, bf16[32,16,512]{2,1,0:T(8,128)(2,1)S(1)}, u32[]{:S(2)}, u32[]{:S(2)}) collective-permute-start(bf16[32,16,512]{2,1,0:T(8,128)(2,1)S(1)} %slice.101), channel_id=1, source_target_pairs={{0,1},{1,2},{2,3},{3,0},{4,5},{5,6},{6,7},{7,4},{8,9},{9,10},{10,1... | collective-permute-start | bytes 1572872 | tf_op jit(solution)/shard_map/ppermute | solution.py:37
  119.0 41.5 %collective-permute-start.13 = (bf16[32,16,512]{2,1,0:T(8,128)(2,1)}, bf16[32,16,512]{2,1,0:T(8,128)(2,1)S(1)}, u32[]{:S(2)}, u32[]{:S(2)}) collective-permute-start(bf16[32,16,512]{2,1,0:T(8,128)(2,1)} %get-tuple-element.83), channel_id=1, source_target_pairs={{0,2},{1,3},{2,0},{3,1},{4,6},{5,7},{6,4},{7,5},{8,10},{9,11},{10,... | collective-permute-start | bytes 1572872 | tf_op jit(solution)/shard_map/ppermute | solution.py:37
  119.1 41.4 %collective-permute-start.14 = (bf16[32,16,512]{2,1,0:T(8,128)(2,1)S(1)}, bf16[32,16,512]{2,1,0:T(8,128)(2,1)S(1)}, u32[]{:S(2)}, u32[]{:S(2)}) collective-permute-start(bf16[32,16,512]{2,1,0:T(8,128)(2,1)S(1)} %get-tuple-element.82), channel_id=1, source_target_pairs={{0,3},{1,0},{2,1},{3,2},{4,7},{5,4},{6,5},{7,6},{8,11},{9,8},{10,9... | collective-permute-start | bytes 1572872 | tf_op jit(solution)/shard_map/ppermute | solution.py:37
  157.9 8.4 %collective-permute-start.9 = (bf16[16,8192]{1,0:T(8,128)(2,1)}, bf16[16,8192]{1,0:T(8,128)(2,1)S(1)}, u32[]{:S(2)}, u32[]{:S(2)}) collective-permute-start(bf16[16,8192]{1,0:T(8,128)(2,1)} %get-tuple-element.68), channel_id=1, source_target_pairs={{0,1},{1,2},{2,3},{3,0},{4,5},{5,6},{6,7},{7,4},{8,9},{9,10},{10,1... | collective-permute-start | bytes 786440 | tf_op jit(solution)/shard_map/ppermute | solution.py:37
  159.8 12.5 %collective-permute-start.10 = (bf16[16,8192]{1,0:T(8,128)(2,1)}, bf16[16,8192]{1,0:T(8,128)(2,1)S(1)}, u32[]{:S(2)}, u32[]{:S(2)}) collective-permute-start(bf16[16,8192]{1,0:T(8,128)(2,1)} %get-tuple-element.69), channel_id=1, source_target_pairs={{0,2},{1,3},{2,0},{3,1},{4,6},{5,7},{6,4},{7,5},{8,10},{9,11},{10,... | collective-permute-start | bytes 786440 | tf_op jit(solution)/shard_map/ppermute | solution.py:37
  160.5 12.4 %collective-permute-start.11 = (bf16[16,8192]{1,0:T(8,128)(2,1)}, bf16[16,8192]{1,0:T(8,128)(2,1)S(1)}, u32[]{:S(2)}, u32[]{:S(2)}) collective-permute-start(bf16[16,8192]{1,0:T(8,128)(2,1)} %get-tuple-element.70), channel_id=1, source_target_pairs={{0,3},{1,0},{2,1},{3,2},{4,7},{5,4},{6,5},{7,6},{8,11},{9,8},{10,9... | collective-permute-start | bytes 786440 | tf_op jit(solution)/shard_map/ppermute | solution.py:37
  161.6 11.3 %copy-start.7 = (bf16[16,8192]{1,0:T(8,128)(2,1)S(1)}, bf16[16,8192]{1,0:T(8,128)(2,1)}, u32[]{:S(2)}) copy-start(bf16[16,8192]{1,0:T(8,128)(2,1)} %get-tuple-element.71) | copy-start | bytes 786436
  166.3 6.7 %copy-start.2 = (bf16[2,32,8192]{2,1,0:T(8,128)(2,1)S(1)}, bf16[2,32,8192]{2,1,0:T(8,128)(2,1)}, u32[]{:S(2)}) copy-start(bf16[2,32,8192]{2,1,0:T(8,128)(2,1)} %param.9) | copy-start | bytes 3145732

commit v12 on v11

--- a/solution.py
+++ b/solution.py
@@ -123,11 +123,17 @@
     @pl.loop(0, angles // (2 * batch))
     def _(step):
         start = step * 2 * batch
+
+        @pl.when(step > 0)
+        def _():
+            leave(step - 1).start()
+
         multiply(start, lhs_refs[0])
         gather(start + batch, lhs_refs[1])
         multiply(start + batch, lhs_refs[1])
-        leave(step).start()
         gather(jnp.minimum(start + 2 * batch, angles - batch), lhs_refs[0])
+
+    leave(angles // (2 * batch) - 1).start()
 
     @pl.loop(0, angles // (2 * batch))
     def _(step):
@@ -172,30 +178,17 @@
     start_ref, refs = (refs[0], refs[1:]) if has_start else (None, refs)
     out_refs, refs = refs[:outs], refs[outs:]
     acc_refs, refs = refs[:CHAINS], refs[CHAINS:]
-    radon_ref, grad_ref, radon_sems, grad_sems, w_ref, *refs = refs
+    radon_ref, grad_ref, radon_sem, grad_sem, w_ref, *refs = refs
     contrib_refs = refs[:2]
     angles, block, span = radon_ref.shape
     pairs = len(blocks) // 2
     feeds = span // block
     coef_blocks = acc_refs[0].shape[0]
-    steps = angles // CHAINS
-
-    def copies(step):
-        here = pl.ds(step * CHAINS, CHAINS)
-        return (
-            pltpu.make_async_copy(radon_hbm.at[here], radon_ref.at[here], radon_sems.at[step]),
-            pltpu.make_async_copy(grad_hbm.at[here], grad_ref.at[here], grad_sems.at[step]),
-        )
-
-    def arrived(step):
-        for copy in copies(step):
-            copy.wait()
-
-    @pl.loop(0, steps)
-    def _(step):
-        for copy in copies(step):
-            copy.start()
-
+
+    radon_copy = pltpu.make_async_copy(radon_hbm, radon_ref, radon_sem)
+    grad_copy = pltpu.make_async_copy(grad_hbm, grad_ref, grad_sem)
+    radon_copy.start()
+    grad_copy.start()
     if has_start:
         start_copy = pltpu.make_async_copy(start_ref, acc_refs[0], refs[2])
         start_copy.start()
@@ -221,13 +214,7 @@
         for n in range(CHAINS):
             a = start + n
             widen(half * CHAINS + n, a)
-            lhs = []
-            for pair in range(pairs):
-                tile = grad_ref[a, :, pair * LANES : (pair + 1) * LANES].astype(jnp.float32)
-                real, imag = tile[:GROUP], tile[GROUP:]
-                even = jnp.where(low, real, swap_halves(imag))
-                odd = jnp.where(low, swap_halves(real), imag)
-                lhs.append(jnp.concatenate([even, odd], axis=0).astype(jnp.bfloat16))
+            lhs = [grad_ref[a, :, pair * LANES : (pair + 1) * LANES] for pair in range(pairs)]
             contrib_ref[n] = jnp.dot(
                 jnp.concatenate(lhs, axis=0),
                 w_ref[half * CHAINS + n],
@@ -242,23 +229,17 @@
                     tile = contrib_ref[n, row : row + GROUP, j * LANES : (j + 1) * LANES]
                     acc_refs[n][idx_ref[start + n, b * feeds + j]] += tile
 
-    arrived(0)
+    radon_copy.wait()
+    grad_copy.wait()
     multiply(0, 0, contrib_refs[0])
     if has_start:
         start_copy.wait()
 
-    @pl.loop(0, steps // 2)
-    def _(half):
-        step = 2 * half
-        start = step * CHAINS
-        arrived(step + 1)
+    @pl.loop(0, angles // (2 * CHAINS))
+    def _(step):
+        start = step * 2 * CHAINS
         multiply(start + CHAINS, 1, contrib_refs[1])
         scatter(start, contrib_refs[0])
-
-        @pl.when(step + 2 < steps)
-        def _():
-            arrived(step + 2)
-
         multiply(jnp.minimum(start + 2 * CHAINS, angles - CHAINS), 0, contrib_refs[0])
         scatter(start + CHAINS, contrib_refs[1])
 
@@ -305,7 +286,7 @@
         out_specs=[everywhere] * len(out_shape),
         scratch_shapes=[pltpu.VMEM((coef_blocks, GROUP, LANES), jnp.float32)] * CHAINS
         + [pltpu.VMEM(radon_tiles.shape, jnp.bfloat16), pltpu.VMEM(grads.shape, jnp.bfloat16)]
-        + [pltpu.SemaphoreType.DMA((angles // CHAINS,))] * 2
+        + [pltpu.SemaphoreType.DMA] * 2
         + [pltpu.VMEM((2 * CHAINS, 2 * block, 2 * span), jnp.bfloat16)]
         + [pltpu.VMEM((CHAINS, rows, 2 * span), jnp.float32)] * 2
         + [pltpu.SemaphoreType.DMA] * has_start,
@@ -424,9 +405,19 @@
                             acc_ref[here] += jnp.where(past, ahead, behind)
 
 
+def pack_blocks(packed_ref, g, real, imag, begin):
+    low = lower_half((GROUP, LANES))
+    for t in range(real.shape[1] // LANES):
+        lanes = slice(t * LANES, (t + 1) * LANES)
+        even = jnp.where(low, real[:, lanes], swap_halves(imag[:, lanes]))
+        odd = jnp.where(low, swap_halves(real[:, lanes]), imag[:, lanes])
+        put = slice(begin + t * LANES, begin + (t + 1) * LANES)
+        packed_ref[g, :, put] = jnp.concatenate([even, odd], axis=0).astype(jnp.bfloat16)
+
+
 def exit_first_kernel(tiles, meta_ref, probe_ref, forward_ref, inverse_ref, sino_ref, *refs):
     amp_refs, refs = refs[:tiles], refs[tiles:]
-    partial_ref, grad_ref, spill_ref, acc_ref, *scratch = refs
+    partial_ref, grad_ref, packed_ref, spill_ref, acc_ref, *scratch = refs
     groups = sino_ref.shape[0]
     width = probe_ref.shape[1]
     done = sino_ref.shape[2] - width
@@ -446,6 +437,7 @@
         rows = pl.ds(pl.multiple_of(g * GROUP, GROUP), GROUP)
         whole = [acc_ref[c, rows, width:done] for c in range(2)]
         grad_ref[g] = jnp.concatenate(whole, axis=0).astype(jnp.bfloat16)
+        pack_blocks(packed_ref, g, *whole, 0)
         for c in range(2):
             partial_ref[c, rows, :] = acc_ref[c, rows, :width]
             spill_ref[c, rows, :] = acc_ref[c, rows, done:]
@@ -455,7 +447,7 @@
     tiles, meta_ref, probe_ref, forward_ref, inverse_ref, early_ref, late_ref, partial_ref, spill_ref, *refs
 ):
     amp_refs, refs = refs[:tiles], refs[tiles:]
-    out_ref, ext_ref, acc_ref, *scratch = refs
+    out_ref, packed_ref, ext_ref, acc_ref, *scratch = refs
     groups = early_ref.shape[0]
     width = probe_ref.shape[1]
     done = width + late_ref.shape[2]
@@ -482,6 +474,8 @@
         wrapped = [acc_ref[c, rows, done:] + partial_ref[c, rows, :] for c in range(2)]
         out_ref[g, :, :done] = jnp.concatenate(here, axis=0).astype(jnp.bfloat16)
         out_ref[g, :, done:] = jnp.concatenate(wrapped, axis=0).astype(jnp.bfloat16)
+        pack_blocks(packed_ref, g, *here, 0)
+        pack_blocks(packed_ref, g, *wrapped, done)
 
 
 def exit_scratch(groups, width, reach):
@@ -498,9 +492,9 @@
     grad = jax.ShapeDtypeStruct((groups, rows, reach - 2 * width), jnp.bfloat16)
     return pl.pallas_call(
         functools.partial(exit_first_kernel, len(amps)),
-        out_shape=[edge, grad, edge],
+        out_shape=[edge, grad, grad, edge],
         in_specs=[scalars] + [everywhere] * (4 + len(amps)),
-        out_specs=[everywhere] * 3,
+        out_specs=[everywhere] * 4,
         scratch_shapes=exit_scratch(groups, width, reach),
         compiler_params=pltpu.CompilerParams(vmem_limit_bytes=60 * MEBI),
         cost_estimate=guess(10),
@@ -514,9 +508,9 @@
     reach = late.shape[2] + 2 * width
     return pl.pallas_call(
         functools.partial(exit_rest_kernel, len(amps)),
-        out_shape=jax.ShapeDtypeStruct((groups, rows, reach), jnp.bfloat16),
+        out_shape=[jax.ShapeDtypeStruct((groups, rows, reach), jnp.bfloat16)] * 2,
         in_specs=[scalars] + [everywhere] * (7 + len(amps)),
-        out_specs=everywhere,
+        out_specs=[everywhere] * 2,
         scratch_shapes=[pltpu.VMEM((groups, rows, reach), jnp.bfloat16)]
         + exit_scratch(groups, width, reach),
         compiler_params=pltpu.CompilerParams(vmem_limit_bytes=60 * MEBI),
@@ -631,13 +625,13 @@
     got_late = everyone(cut_rows(sino_late, own))
     got_early, got_late = to_groups(got_early, own), to_groups(got_late, own)
     got_early, amp_pieces = lax.optimization_barrier((got_early, amp_pieces))
-    partial, first_grad, spill = exit_first(meta, probe_field, tables, got_early, amp_pieces[:half])
-    first_sent, got_late = lax.optimization_barrier((first_grad, got_late))
-    rest_grad = exit_rest(
+    partial, first_grad, first_sent, spill = exit_first(meta, probe_field, tables, got_early, amp_pieces[:half])
+    first_sent, got_late = lax.optimization_barrier((first_sent, got_late))
+    rest_grad, rest_sent = exit_rest(
         meta, probe_field, tables, got_early, got_late, partial, spill, amp_pieces[half:]
     )
     back_first = everyone(from_groups(first_sent, own))
-    back_first, rest_sent = lax.optimization_barrier((back_first, rest_grad))
+    back_first, rest_sent = lax.optimization_barrier((back_first, rest_sent))
     back_rest = everyone(from_groups(rest_sent, own))
     first_sum = back_project(
         block_idx, radon_tiles, pad_rows(back_first, own), first_blocks, None, n_pos, width, "back_first"

time: 175 us -> 175 us (level)
  waiting for transfers between devices: 70.7 us -> 62.6 us
  local copies, waits for them, and re-layouts: 12.2 us -> 17 us
  Pallas kernels: 54.5 us -> 56.9 us
    all_to_all x4, waiting for transfers between devices: 52.4 us -> 45.3 us  [everyone(): return lax.all_to_all(chunk, ('ang', 'pos'), 0, 0, tiled=True)]
    pallas_call x1, Pallas kernels: 7.86 us -> 12.4 us  [exit_first(): pl.pallas_call(functools.partial(exit_first_kernel, len(amps)), out_shape...]
    pallas_call x2, Pallas kernels: 20.2 us -> 17.4 us  [back_project(): pl.pallas_call(functools.partial(back_project_kernel, blocks, has_start,...]
    slice x2, local copies, waits for them, and re-layouts: 0.99 us -> 2.98 us  [on_device(): tile_pieces.append(source[:, :, begin:begin + tile_width])]
    unnamed x25, local copies, waits for them, and re-layouts: 4.79 us -> 6.72 us
  transfers between devices with their start and end apart: 19 -> 19, of which waited for: 10 -> 10; matrix products, arithmetic and copies ran while one was open for 7% -> 10% of each run, Pallas kernels for 27% -> 28%
where the time goes in v12:
time: 175 us
  waiting for transfers between devices  62.6 us (36%)
  Pallas kernels  56.9 us (33%)
  starting transfers between devices  32.2 us (18%)
  local copies, waits for them, and re-layouts  17 us (10%)
  other arithmetic  4.73 us (3%)
    all_to_all x4, waiting for transfers between devices, everyone(): return lax.all_to_all(chunk, ('ang', 'pos'), 0, 0, tiled=True)  45.3 us
    all_to_all x4, starting transfers between devices, everyone(): return lax.all_to_all(chunk, ('ang', 'pos'), 0, 0, tiled=True)  19.1 us
    pallas_call x2, Pallas kernels, back_project(): pl.pallas_call(functools.partial(back_project_kernel, blocks, has_start,...  17.4 us
    ppermute x15, waiting for transfers between devices, rotate_pos(): lax.ppermute(pieces[j], 'pos', [(i, (i + sign * j) % count) for i in rang...  17.3 us
    pallas_call x2, Pallas kernels, project(): pl.pallas_call(functools.partial(project_kernel, blocks, pieces), out_sha...  13.8 us
    pallas_call x1, Pallas kernels, exit_rest(): pl.pallas_call(functools.partial(exit_rest_kernel, len(amps)), out_shape=...  13.3 us
    ppermute x15, starting transfers between devices, rotate_pos(): lax.ppermute(pieces[j], 'pos', [(i, (i + sign * j) % count) for i in rang...  13.1 us
    pallas_call x1, Pallas kernels, exit_first(): pl.pallas_call(functools.partial(exit_first_kernel, len(amps)), out_shape...  12.4 us
  transfers between devices with their start and end apart: 19, of which 10 were waited for; matrix products, arithmetic and copies ran while one was open for 10% of the time, Pallas kernels for 28%

profile of v12, /device:TPU:1, one launch (start us, length us, event | category | flops | bytes accessed | tf_op | source)
XLA Modules:
  0.0 174.6 jit_solution(11077006111065257390)
XLA Ops:
  0.7 0.0 copy-start
  0.7 1.3 dynamic-slice_bitcast_fusion.4
  2.1 2.7 %collective-permute-start = (bf16[16,8192]{1,0:T(8,128)(2,1)S(1)}, bf16[16,8192]{1,0:T(8,128)(2,1)S(1)}, u32[]{:S(2)}, u32[]{:S(2)}) collective-permute-start(bf16[16,8192]{1,0:T(8,128)(2,1)S(1)} %get-tuple-element.95), channel_id=1, source_target_pairs={{0,1},{1,2},{2,3},{3,0},{4,5},{5,6},{6,7},{7,4},{8,9},{9,10},{10,1... | collective-permute-start | bytes 786440 | tf_op jit(solution)/shard_map/ppermute | solution.py:37
  4.7 0.0 collective-permute-start.1
  4.7 0.5 collective-permute-start.2
  5.2 0.3 fusion.5
  5.5 0.3 copy.27
  5.8 0.2 reshape.194
  6.2 0.1 reshape.195.idx_ref
  6.3 4.0 %collective-permute-done.refs_1_ = bf16[16,8192]{1,0:T(8,128)(2,1)S(1)} collective-permute-done((bf16[16,8192]{1,0:T(8,128)(2,1)S(1)}, bf16[16,8192]{1,0:T(8,128)(2,1)S(1)}, u32[]{:S(2)}, u32[]{:S(2)}) %collective-permute-start) | collective-permute-done | bytes 262176 | tf_op jit(solution)/shard_map/ppermute | solution.py:37
  10.2 5.6 %collective-permute-done.1.refs_2_ = bf16[16,8192]{1,0:T(8,128)(2,1)S(1)} collective-permute-done((bf16[16,8192]{1,0:T(8,128)(2,1)S(1)}, bf16[16,8192]{1,0:T(8,128)(2,1)S(1)}, u32[]{:S(2)}, u32[]{:S(2)}) %collective-permute-start.1) | collective-permute-done | bytes 262176 | tf_op jit(solution)/shard_map/ppermute | solution.py:37
  15.8 0.5 collective-permute-done.2.refs_3_
  16.3 7.6 %project_early.1 = bf16[32,16,1280]{2,1,0:T(8,128)(2,1)} custom-call(s32[32,128]{1,0:T(8,128)S(1)} %reshape.195.idx_ref, bf16[32,64,256]{2,1,0:T(8,128)(2,1)S(1)} %copy-done, bf16[16,8192]{1,0:T(8,128)(2,1)S(1)} %get-tuple-element.52.refs_0_, bf16[16,8192]{1,0:T(8,128)(2,1)S(1)} %collective-permute-done.refs_1_, ...), custom_call_target="tpu_custom_call" | custom-call | flops 10350000128 | bytes 900000 | tf_op jit(solution)/shard_map/project_early/pallas_call | solution.py:161
  24.0 0.0 copy-start.10
  24.0 0.0 copy-start.9
  24.0 6.5 %all-to-all-start = ((bf16[32,16,1280]{2,1,0:T(8,128)(2,1)}), bf16[32,16,1280]{2,1,0:T(8,128)(2,1)S(1)}, u32[]{:S(2)}, u32[]{:S(2)}) async-start(bf16[32,16,1280]{2,1,0:T(8,128)(2,1)} %project_early.1), calls=%async_computation | async-start | bytes 2621440 | tf_op jit(solution)/shard_map/all_to_all | solution.py:558
  30.6 0.1 copy.32
  30.7 0.1 pad_add_fusion.2
  30.8 1.7 collective-permute-start.5
  32.5 0.0 collective-permute-start.4
  32.5 0.5 collective-permute-start.3
  33.0 2.9 %dynamic-slice_bitcast_fusion = (bf16[4,256,256]{2,1,0:T(8,128)(2,1)}, bf16[4,256,256]{2,1,0:T(8,128)(2,1)}, bf16[4,256,256]{2,1,0:T(8,128)(2,1)}, bf16[4,256,256]{2,1,0:T(8,128)(2,1)}) fusion(bf16[4,4,256,256]{3,2,1,0:T(8,128)(2,1)} %param.13, s32[]{:T(128)S(6)} %select_n.316, s32[]{:T(128)S(6)} %select_n.314, s32[]{:T(128)S(6)} %select_n.312, s32[]{:T(128)S(6)} %select_n.310), kind=kLoop, calls=%fused_computation.11 | loop fusion | bytes 4194320 | tf_op jit(solution)/shard_map/jit(dynamic_index_in_dim)/squeeze | solution.py:582
  35.9 1.3 collective-permute-start.6
  37.2 0.0 collective-permute-start.7
  37.3 1.6 collective-permute-start.8
  38.9 0.0 collective-permute-done.4
  38.9 0.6 pad_add_fusion.3.meta_ref
  39.5 6.2 %project_late.1 = bf16[32,16,768]{2,1,0:T(8,128)(2,1)} custom-call(s32[32,128]{1,0:T(8,128)S(1)} %reshape.195.idx_ref, bf16[32,64,256]{2,1,0:T(8,128)(2,1)S(1)} %copy-done, bf16[16,8192]{1,0:T(8,128)(2,1)S(1)} %get-tuple-element.52.refs_0_, bf16[16,8192]{1,0:T(8,128)(2,1)S(1)} %collective-permute-done.refs_1_, ...), custom_call_target="tpu_custom_call" | custom-call | flops 8049999872 | bytes 700000 | tf_op jit(solution)/shard_map/project_late/pallas_call | solution.py:161
  45.6 16.2 %all-to-all-done.sino_ref.early_ref = bf16[32,16,1280]{2,1,0:T(8,128)(2,1)S(1)} async-done(((bf16[32,16,1280]{2,1,0:T(8,128)(2,1)}), bf16[32,16,1280]{2,1,0:T(8,128)(2,1)S(1)}, u32[]{:S(2)}, u32[]{:S(2)}) %all-to-all-start) | async-done | bytes 1310752 | tf_op jit(solution)/shard_map/all_to_all | solution.py:558
  61.9 4.4 %all-to-all-start.1 = ((bf16[32,16,768]{2,1,0:T(8,128)(2,1)}), bf16[32,16,768]{2,1,0:T(8,128)(2,1)S(1)}, u32[]{:S(2)}, u32[]{:S(2)}) async-start(bf16[32,16,768]{2,1,0:T(8,128)(2,1)} %project_late.1), calls=%async_computation.1 | async-start | bytes 1572864 | tf_op jit(solution)/shard_map/all_to_all | solution.py:558
  66.3 0.0 collective-permute-done.6.refs_1_
  66.3 1.7 collective-permute-done.8.refs_1_
  68.0 12.4 %exit_first.1 = (f32[2,256,256]{2,1,0:T(8,128)}, bf16[32,16,768]{2,1,0:T(8,128)(2,1)}, bf16[32,16,768]{2,1,0:T(8,128)(2,1)}, f32[2,256,256]{2,1,0:T(8,128)}) custom-call(s32[4,5]{1,0:T(4,128)} %pad_add_fusion.3.meta_ref, bf16[2,256,256]{2,1,0:T(8,128)(2,1)} %probe_ref.3, bf16[512,512]{1,0:T(8,128)(2,1)} %constant.148.forward_ref, ...), custom_call_target="tpu_custom_call" | custom-call | flops 11500000256 | bytes 1000000 | tf_op jit(solution)/shard_map/exit_first/pallas_call | solution.py:493
  80.4 6.0 %all-to-all-done.1.late_ref = bf16[32,16,768]{2,1,0:T(8,128)(2,1)S(1)} async-done(((bf16[32,16,768]{2,1,0:T(8,128)(2,1)}), bf16[32,16,768]{2,1,0:T(8,128)(2,1)S(1)}, u32[]{:S(2)}, u32[]{:S(2)}) %all-to-all-start.1) | async-done | bytes 786464 | tf_op jit(solution)/shard_map/all_to_all | solution.py:558
  86.4 4.1 %all-to-all-start.2 = ((bf16[32,16,768]{2,1,0:T(8,128)(2,1)}), bf16[32,16,768]{2,1,0:T(8,128)(2,1)S(1)}, u32[]{:S(2)}, u32[]{:S(2)}) async-start(bf16[32,16,768]{2,1,0:T(8,128)(2,1)} %get-tuple-element.63), calls=%async_computation.2 | async-start | bytes 1572864 | tf_op jit(solution)/shard_map/all_to_all | solution.py:558
  90.5 13.3 %exit_rest.1 = (bf16[32,16,1280]{2,1,0:T(8,128)(2,1)}, bf16[32,16,1280]{2,1,0:T(8,128)(2,1)}) custom-call(s32[4,5]{1,0:T(4,128)} %pad_add_fusion.3.meta_ref, bf16[2,256,256]{2,1,0:T(8,128)(2,1)} %probe_ref.3, bf16[512,512]{1,0:T(8,128)(2,1)} %constant.148.forward_ref, bf16[512,512]{1,0:T(8,128)(2,1)} %constant.151.inverse_ref, ...), custom_call_target="tpu_custom_call" | custom-call | flops 11500000256 | bytes 1000000 | tf_op jit(solution)/shard_map/exit_rest/pallas_call | solution.py:509
  103.8 6.8 %all-to-all-done.2.grad_hbm = bf16[32,16,768]{2,1,0:T(8,128)(2,1)S(1)} async-done(((bf16[32,16,768]{2,1,0:T(8,128)(2,1)}), bf16[32,16,768]{2,1,0:T(8,128)(2,1)S(1)}, u32[]{:S(2)}, u32[]{:S(2)}) %all-to-all-start.2) | async-done | bytes 786464 | tf_op jit(solution)/shard_map/all_to_all | solution.py:558
  110.7 0.9 copy-done.5
  111.5 4.1 %all-to-all-start.3 = ((bf16[32,16,1280]{2,1,0:T(8,128)(2,1)}), bf16[32,16,1280]{2,1,0:T(8,128)(2,1)S(1)}, u32[]{:S(2)}, u32[]{:S(2)}) async-start(bf16[32,16,1280]{2,1,0:T(8,128)(2,1)} %get-tuple-element.70), calls=%async_computation.3 | async-start | bytes 2621440 | tf_op jit(solution)/shard_map/all_to_all | solution.py:558
  115.6 0.0 copy-start.4
  115.7 0.3 copy.22
  115.9 0.2 reshape.192
  116.3 0.7 reshape.193.idx_ref
  117.0 1.9 %slice.101 = bf16[32,16,512]{2,1,0:T(8,128)(2,1)} slice(bf16[32,16,768]{2,1,0:T(8,128)(2,1)} %get-tuple-element.76), slice={[0:32], [0:16], [256:768]} | slice | bytes 1048576 | tf_op jit(solution)/shard_map/slice | solution.py:643
  118.9 1.0 slice.105
  119.9 1.7 collective-permute-start.12
  121.6 1.1 fusion.9
  122.7 0.5 collective-permute-start.14
  123.2 7.5 %back_first.1.refs_0_ = f32[512,8,128]{2,1,0:T(8,128)} custom-call(s32[32,128]{1,0:T(8,128)} %reshape.193.idx_ref, bf16[32,64,256]{2,1,0:T(8,128)(2,1)} %radon_hbm.3, bf16[32,16,768]{2,1,0:T(8,128)(2,1)} %copy-done.5), custom_call_target="tpu_custom_call" | custom-call | flops 8049999872 | bytes 700000 | tf_op jit(solution)/shard_map/back_first/pallas_call | solution.py:282
  130.7 16.2 %all-to-all-done.3.grad_hbm = bf16[32,16,1280]{2,1,0:T(8,128)(2,1)S(1)} async-done(((bf16[32,16,1280]{2,1,0:T(8,128)(2,1)}), bf16[32,16,1280]{2,1,0:T(8,128)(2,1)S(1)}, u32[]{:S(2)}, u32[]{:S(2)}) %all-to-all-start.3) | async-done | bytes 1310752 | tf_op jit(solution)/shard_map/all_to_all | solution.py:558
  147.0 1.1 copy-done.3
  148.0 9.9 %back_rest.1 = (bf16[16,8192]{1,0:T(8,128)(2,1)}, bf16[16,8192]{1,0:T(8,128)(2,1)}, bf16[16,8192]{1,0:T(8,128)(2,1)}, bf16[16,8192]{1,0:T(8,128)(2,1)}) custom-call(s32[32,128]{1,0:T(8,128)} %reshape.193.idx_ref, bf16[32,64,256]{2,1,0:T(8,128)(2,1)} %radon_hbm.3, bf16[32,16,1280]{2,1,0:T(8,128)(2,1)} %copy-done.3, f32[512,8,128]{2,1,0:T(8,128)} %back_first.1.refs_0_), custom_call_target="tpu_custom_call" | custom-call | flops 10350000128 | bytes 900000 | tf_op jit(solution)/shard_map/back_rest/pallas_call | solution.py:282
  157.9 1.9 %collective-permute-start.9 = (bf16[16,8192]{1,0:T(8,128)(2,1)}, bf16[16,8192]{1,0:T(8,128)(2,1)S(1)}, u32[]{:S(2)}, u32[]{:S(2)}) collective-permute-start(bf16[16,8192]{1,0:T(8,128)(2,1)} %get-tuple-element.72), channel_id=1, source_target_pairs={{0,1},{1,2},{2,3},{3,0},{4,5},{5,6},{6,7},{7,4},{8,9},{9,10},{10,1... | collective-permute-start | bytes 786440 | tf_op jit(solution)/shard_map/ppermute | solution.py:37
  159.9 0.7 collective-permute-start.10
  160.5 0.0 collective-permute-done.13
  160.5 0.0 collective-permute-done.14
  160.5 1.6 select_bitcast_fusion.3
  162.3 0.3 maximum_convert_fusion
  162.7 4.7 %copy.37 = f32[2,256,4,512]{3,2,1,0:T(4,128)} copy(f32[2,256,4,512]{3,1,0,2:T(8,128)S(1)} %maximum_convert_fusion) | data formatting | bytes 8388608
  167.4 0.0 collective-permute-done.9
  167.4 4.9 %collective-permute-done.10 = bf16[16,8192]{1,0:T(8,128)(2,1)S(1)} collective-permute-done((bf16[16,8192]{1,0:T(8,128)(2,1)}, bf16[16,8192]{1,0:T(8,128)(2,1)S(1)}, u32[]{:S(2)}, u32[]{:S(2)}) %collective-permute-start.10) | collective-permute-done | bytes 262176 | tf_op jit(solution)/shard_map/ppermute | solution.py:37
  172.3 0.6 collective-permute-done.11
  172.9 0.1 select_bitcast_fusion.7
  173.0 1.6 multiply_add_fusion
  (46 shorter events, 0.4 us)
Async XLA Ops:
  0.6 4.6 %copy-start.8 = (s32[32,32,4]{1,2,0:T(4,128)S(1)}, s32[32,32,4]{1,2,0:T(4,128)}, u32[]{:S(2)}) copy-start(s32[32,32,4]{1,2,0:T(4,128)} %param.11) | copy-start | bytes 49156
  0.7 15.7 %copy-start = (bf16[32,64,256]{2,1,0:T(8,128)(2,1)S(1)}, bf16[32,64,256]{2,1,0:T(8,128)(2,1)}, u32[]{:S(2)}) copy-start(bf16[32,64,256]{2,1,0:T(8,128)(2,1)} %radon_hbm.3) | copy-start | bytes 3145732
  2.1 8.2 %collective-permute-start = (bf16[16,8192]{1,0:T(8,128)(2,1)S(1)}, bf16[16,8192]{1,0:T(8,128)(2,1)S(1)}, u32[]{:S(2)}, u32[]{:S(2)}) collective-permute-start(bf16[16,8192]{1,0:T(8,128)(2,1)S(1)} %get-tuple-element.95), channel_id=1, source_target_pairs={{0,1},{1,2},{2,3},{3,0},{4,5},{5,6},{6,7},{7,4},{8,9},{9,10},{10,1... | collective-permute-start | bytes 786440 | tf_op jit(solution)/shard_map/ppermute | solution.py:37
  4.7 11.1 %collective-permute-start.1 = (bf16[16,8192]{1,0:T(8,128)(2,1)S(1)}, bf16[16,8192]{1,0:T(8,128)(2,1)S(1)}, u32[]{:S(2)}, u32[]{:S(2)}) collective-permute-start(bf16[16,8192]{1,0:T(8,128)(2,1)S(1)} %get-tuple-element.97), channel_id=1, source_target_pairs={{0,2},{1,3},{2,0},{3,1},{4,6},{5,7},{6,4},{7,5},{8,10},{9,11},{10,... | collective-permute-start | bytes 786440 | tf_op jit(solution)/shard_map/ppermute | solution.py:37
  4.7 11.6 %collective-permute-start.2 = (bf16[16,8192]{1,0:T(8,128)(2,1)S(1)}, bf16[16,8192]{1,0:T(8,128)(2,1)S(1)}, u32[]{:S(2)}, u32[]{:S(2)}) collective-permute-start(bf16[16,8192]{1,0:T(8,128)(2,1)S(1)} %get-tuple-element.94), channel_id=1, source_target_pairs={{0,3},{1,0},{2,1},{3,2},{4,7},{5,4},{6,5},{7,6},{8,11},{9,8},{10,9... | collective-permute-start | bytes 786440 | tf_op jit(solution)/shard_map/ppermute | solution.py:37
  24.0 6.6 %copy-start.10 = (s32[4,1]{0,1:T(1,128)S(1)}, s32[4,1]{0,1:T(1,128)}, u32[]{:S(2)}) copy-start(s32[4,1]{0,1:T(1,128)} %param.15) | copy-start | bytes 52
  24.0 6.7 %copy-start.9 = (s32[4,4]{1,0:T(4,128)S(1)}, s32[4,4]{1,0:T(4,128)}, u32[]{:S(2)}) copy-start(s32[4,4]{1,0:T(4,128)} %param.14) | copy-start | bytes 196
  24.0 37.9 %all-to-all-start = ((bf16[32,16,1280]{2,1,0:T(8,128)(2,1)}), bf16[32,16,1280]{2,1,0:T(8,128)(2,1)S(1)}, u32[]{:S(2)}, u32[]{:S(2)}) async-start(bf16[32,16,1280]{2,1,0:T(8,128)(2,1)} %project_early.1), calls=%async_computation | async-start | bytes 2621440 | tf_op jit(solution)/shard_map/all_to_all | solution.py:558
  30.8 6.5 %collective-permute-start.5 = (s32[1,5]{1,0:T(1,128)S(1)}, s32[1,5]{1,0:T(1,128)S(1)}, u32[]{:S(2)}, u32[]{:S(2)}) collective-permute-start(s32[1,5]{1,0:T(1,128)S(1)} %get-tuple-element.113), channel_id=1, source_target_pairs={{0,1},{1,2},{2,3},{3,0},{4,5},{5,6},{6,7},{7,4},{8,9},{9,10},{10,1... | collective-permute-start | bytes 68 | tf_op jit(solution)/shard_map/ppermute | solution.py:37
  32.5 6.4 %collective-permute-start.4 = (s32[1,5]{1,0:T(1,128)S(1)}, s32[1,5]{1,0:T(1,128)S(1)}, u32[]{:S(2)}, u32[]{:S(2)}) collective-permute-start(s32[1,5]{1,0:T(1,128)S(1)} %get-tuple-element.114), channel_id=1, source_target_pairs={{0,2},{1,3},{2,0},{3,1},{4,6},{5,7},{6,4},{7,5},{8,10},{9,11},{10,... | collective-permute-start | bytes 68 | tf_op jit(solution)/shard_map/ppermute | solution.py:37
  32.5 6.4 %collective-permute-start.3 = (s32[1,5]{1,0:T(1,128)S(1)}, s32[1,5]{1,0:T(1,128)S(1)}, u32[]{:S(2)}, u32[]{:S(2)}) collective-permute-start(s32[1,5]{1,0:T(1,128)S(1)} %get-tuple-element.115), channel_id=1, source_target_pairs={{0,3},{1,0},{2,1},{3,2},{4,7},{5,4},{6,5},{7,6},{8,11},{9,8},{10,9... | collective-permute-start | bytes 68 | tf_op jit(solution)/shard_map/ppermute | solution.py:37
  35.9 30.3 %collective-permute-start.6 = (bf16[4,256,256]{2,1,0:T(8,128)(2,1)}, bf16[4,256,256]{2,1,0:T(8,128)(2,1)}, u32[]{:S(2)}, u32[]{:S(2)}) collective-permute-start(bf16[4,256,256]{2,1,0:T(8,128)(2,1)} %get-tuple-element.86), channel_id=1, source_target_pairs={{0,3},{1,0},{2,1},{3,2},{4,7},{5,4},{6,5},{7,6},{8,11},{9,8},{10,9... | collective-permute-start | bytes 1572872 | tf_op jit(solution)/shard_map/ppermute | solution.py:37
  37.2 29.0 %collective-permute-start.7 = (bf16[4,256,256]{2,1,0:T(8,128)(2,1)}, bf16[4,256,256]{2,1,0:T(8,128)(2,1)}, u32[]{:S(2)}, u32[]{:S(2)}) collective-permute-start(bf16[4,256,256]{2,1,0:T(8,128)(2,1)} %get-tuple-element.85), channel_id=1, source_target_pairs={{0,2},{1,3},{2,0},{3,1},{4,6},{5,7},{6,4},{7,5},{8,10},{9,11},{10,... | collective-permute-start | bytes 1572872 | tf_op jit(solution)/shard_map/ppermute | solution.py:37
  37.3 30.7 %collective-permute-start.8 = (bf16[4,256,256]{2,1,0:T(8,128)(2,1)}, bf16[4,256,256]{2,1,0:T(8,128)(2,1)}, u32[]{:S(2)}, u32[]{:S(2)}) collective-permute-start(bf16[4,256,256]{2,1,0:T(8,128)(2,1)} %get-tuple-element.84), channel_id=1, source_target_pairs={{0,1},{1,2},{2,3},{3,0},{4,5},{5,6},{6,7},{7,4},{8,9},{9,10},{10,1... | collective-permute-start | bytes 1572872 | tf_op jit(solution)/shard_map/ppermute | solution.py:37
  61.9 6.1 %copy-start.2 = (bf16[32,16,1280]{2,1,0:T(8,128)(2,1)}, bf16[32,16,1280]{2,1,0:T(8,128)(2,1)S(1)}, u32[]{:S(2)}) copy-start(bf16[32,16,1280]{2,1,0:T(8,128)(2,1)S(1)} %all-to-all-done.sino_ref.early_ref) | copy-start | bytes 3932164
  61.9 24.5 %all-to-all-start.1 = ((bf16[32,16,768]{2,1,0:T(8,128)(2,1)}), bf16[32,16,768]{2,1,0:T(8,128)(2,1)S(1)}, u32[]{:S(2)}, u32[]{:S(2)}) async-start(bf16[32,16,768]{2,1,0:T(8,128)(2,1)} %project_late.1), calls=%async_computation.1 | async-start | bytes 1572864 | tf_op jit(solution)/shard_map/all_to_all | solution.py:558
  86.4 4.1 %copy-start.6 = (bf16[32,16,768]{2,1,0:T(8,128)(2,1)}, bf16[32,16,768]{2,1,0:T(8,128)(2,1)S(1)}, u32[]{:S(2)}) copy-start(bf16[32,16,768]{2,1,0:T(8,128)(2,1)S(1)} %all-to-all-done.1.late_ref) | copy-start | bytes 2359300
  86.4 24.2 %all-to-all-start.2 = ((bf16[32,16,768]{2,1,0:T(8,128)(2,1)}), bf16[32,16,768]{2,1,0:T(8,128)(2,1)S(1)}, u32[]{:S(2)}, u32[]{:S(2)}) async-start(bf16[32,16,768]{2,1,0:T(8,128)(2,1)} %get-tuple-element.63), calls=%async_computation.2 | async-start | bytes 1572864 | tf_op jit(solution)/shard_map/all_to_all | solution.py:558
  110.7 0.9 copy-start.5
  111.5 35.4 %all-to-all-start.3 = ((bf16[32,16,1280]{2,1,0:T(8,128)(2,1)}), bf16[32,16,1280]{2,1,0:T(8,128)(2,1)S(1)}, u32[]{:S(2)}, u32[]{:S(2)}) async-start(bf16[32,16,1280]{2,1,0:T(8,128)(2,1)} %get-tuple-element.70), calls=%async_computation.3 | async-start | bytes 2621440 | tf_op jit(solution)/shard_map/all_to_all | solution.py:558
  115.6 5.9 %copy-start.4 = (bf16[32,16,1280]{2,1,0:T(8,128)(2,1)S(1)}, bf16[32,16,1280]{2,1,0:T(8,128)(2,1)}, u32[]{:S(2)}) copy-start(bf16[32,16,1280]{2,1,0:T(8,128)(2,1)} %get-tuple-element.77) | copy-start | bytes 3932164
  119.9 40.6 %collective-permute-start.12 = (bf16[32,16,512]{2,1,0:T(8,128)(2,1)}, bf16[32,16,512]{2,1,0:T(8,128)(2,1)}, u32[]{:S(2)}, u32[]{:S(2)}) collective-permute-start(bf16[32,16,512]{2,1,0:T(8,128)(2,1)} %slice.101), channel_id=1, source_target_pairs={{0,1},{1,2},{2,3},{3,0},{4,5},{5,6},{6,7},{7,4},{8,9},{9,10},{10,1... | collective-permute-start | bytes 1572872 | tf_op jit(solution)/shard_map/ppermute | solution.py:37
  122.7 37.8 %collective-permute-start.13 = (bf16[32,16,512]{2,1,0:T(8,128)(2,1)}, bf16[32,16,512]{2,1,0:T(8,128)(2,1)S(1)}, u32[]{:S(2)}, u32[]{:S(2)}) collective-permute-start(bf16[32,16,512]{2,1,0:T(8,128)(2,1)} %get-tuple-element.89), channel_id=1, source_target_pairs={{0,2},{1,3},{2,0},{3,1},{4,6},{5,7},{6,4},{7,5},{8,10},{9,11},{10,... | collective-permute-start | bytes 1572872 | tf_op jit(solution)/shard_map/ppermute | solution.py:37
  122.7 37.8 %collective-permute-start.14 = (bf16[32,16,512]{2,1,0:T(8,128)(2,1)}, bf16[32,16,512]{2,1,0:T(8,128)(2,1)S(1)}, u32[]{:S(2)}, u32[]{:S(2)}) collective-permute-start(bf16[32,16,512]{2,1,0:T(8,128)(2,1)} %get-tuple-element.88), channel_id=1, source_target_pairs={{0,3},{1,0},{2,1},{3,2},{4,7},{5,4},{6,5},{7,6},{8,11},{9,8},{10,9... | collective-permute-start | bytes 1572872 | tf_op jit(solution)/shard_map/ppermute | solution.py:37
  147.0 1.1 copy-start.3
  157.9 9.5 %collective-permute-start.9 = (bf16[16,8192]{1,0:T(8,128)(2,1)}, bf16[16,8192]{1,0:T(8,128)(2,1)S(1)}, u32[]{:S(2)}, u32[]{:S(2)}) collective-permute-start(bf16[16,8192]{1,0:T(8,128)(2,1)} %get-tuple-element.72), channel_id=1, source_target_pairs={{0,1},{1,2},{2,3},{3,0},{4,5},{5,6},{6,7},{7,4},{8,9},{9,10},{10,1... | collective-permute-start | bytes 786440 | tf_op jit(solution)/shard_map/ppermute | solution.py:37
  159.9 12.4 %collective-permute-start.10 = (bf16[16,8192]{1,0:T(8,128)(2,1)}, bf16[16,8192]{1,0:T(8,128)(2,1)S(1)}, u32[]{:S(2)}, u32[]{:S(2)}) collective-permute-start(bf16[16,8192]{1,0:T(8,128)(2,1)} %get-tuple-element.73), channel_id=1, source_target_pairs={{0,2},{1,3},{2,0},{3,1},{4,6},{5,7},{6,4},{7,5},{8,10},{9,11},{10,... | collective-permute-start | bytes 786440 | tf_op jit(solution)/shard_map/ppermute | solution.py:37
  160.5 12.4 %collective-permute-start.11 = (bf16[16,8192]{1,0:T(8,128)(2,1)}, bf16[16,8192]{1,0:T(8,128)(2,1)S(1)}, u32[]{:S(2)}, u32[]{:S(2)}) collective-permute-start(bf16[16,8192]{1,0:T(8,128)(2,1)} %get-tuple-element.74), channel_id=1, source_target_pairs={{0,3},{1,0},{2,1},{3,2},{4,7},{5,4},{6,5},{7,6},{8,11},{9,8},{10,9... | collective-permute-start | bytes 786440 | tf_op jit(solution)/shard_map/ppermute | solution.py:37
  162.7 10.2 %copy-start.7 = (bf16[16,8192]{1,0:T(8,128)(2,1)S(1)}, bf16[16,8192]{1,0:T(8,128)(2,1)}, u32[]{:S(2)}) copy-start(bf16[16,8192]{1,0:T(8,128)(2,1)} %get-tuple-element.75) | copy-start | bytes 786436
  167.4 5.6 %copy-start.1 = (bf16[2,32,8192]{2,1,0:T(8,128)(2,1)S(1)}, bf16[2,32,8192]{2,1,0:T(8,128)(2,1)}, u32[]{:S(2)}) copy-start(bf16[2,32,8192]{2,1,0:T(8,128)(2,1)} %param.9) | copy-start | bytes 3145732

commit v13 on v7

--- a/solution.py
+++ b/solution.py
@@ -15,6 +15,7 @@
 GROUP = 8
 MEBI = 1024 * 1024
 everywhere = pl.BlockSpec(memory_space=pltpu.VMEM)
+anywhere = pl.BlockSpec(memory_space=pl.ANY)
 scalars = pl.BlockSpec(memory_space=pltpu.SMEM)
 CHAINS = 4
 BATCH = 4
@@ -81,21 +82,23 @@
                 vv_ref[tiles + k * per_piece + t] = swapped[i * ROWS : (i + 1) * ROWS]
 
 
-def project_blocks(blocks, idx_ref, radon_ref, vv_ref, out_ref, lhs_refs):
+def project_blocks(blocks, idx_ref, radon_ref, vv_ref, out_hbm, out_ref, out_sems, lhs_refs):
     angles, block, span = radon_ref.shape
     feeds = span // block
     low = lower_half((ROWS, LANES))
     batch = lhs_refs[0].shape[0]
 
+    per_angle = idx_ref.shape[0] // angles
+
     def gather(start, lhs_ref):
         for n in range(batch):
-            a = start + n
+            base = (start + n) * per_angle
             for i, b in enumerate(blocks):
                 row = i * ROWS
                 for jp in range(feeds // 2):
                     at = b * feeds + 2 * jp
-                    first = vv_ref[idx_ref[a, at]]
-                    second = vv_ref[idx_ref[a, at + 1]]
+                    first = vv_ref[idx_ref[base + at]]
+                    second = vv_ref[idx_ref[base + at + 1]]
                     lhs_ref[n, row : row + ROWS, jp * LANES : (jp + 1) * LANES] = jnp.where(
                         low, first, second
                     )
@@ -113,22 +116,37 @@
                 )
                 out_ref[a, :, pair * LANES : (pair + 1) * LANES] = tile.astype(jnp.bfloat16)
 
+    def leave(step):
+        here = pl.ds(step * 2 * batch, 2 * batch)
+        return pltpu.make_async_copy(out_ref.at[here], out_hbm.at[here], out_sems.at[step])
+
     gather(0, lhs_refs[0])
 
     @pl.loop(0, angles // (2 * batch))
     def _(step):
         start = step * 2 * batch
+
+        @pl.when(step > 0)
+        def _():
+            leave(step - 1).start()
+
         multiply(start, lhs_refs[0])
         gather(start + batch, lhs_refs[1])
         multiply(start + batch, lhs_refs[1])
         gather(jnp.minimum(start + 2 * batch, angles - batch), lhs_refs[0])
 
+    leave(angles // (2 * batch) - 1).start()
+
+    @pl.loop(0, angles // (2 * batch))
+    def _(step):
+        leave(step).wait()
+
 
 def project_kernel(blocks, pieces, idx_ref, radon_ref, *refs):
     vol_refs = refs[:pieces]
-    out_ref, vv_ref, *lhs_refs = refs[pieces:]
+    out_hbm, vv_ref, out_ref, out_sems, *lhs_refs = refs[pieces:]
     arrange(vol_refs, vv_ref)
-    project_blocks(blocks, idx_ref, radon_ref, vv_ref, out_ref, lhs_refs)
+    project_blocks(blocks, idx_ref, radon_ref, vv_ref, out_hbm, out_ref, out_sems, lhs_refs)
 
 
 def guess(microseconds):
@@ -146,8 +164,9 @@
         functools.partial(project_kernel, blocks, pieces),
         out_shape=jax.ShapeDtypeStruct(out_shape, jnp.bfloat16),
         in_specs=[scalars, everywhere] + [everywhere] * pieces,
-        out_specs=everywhere,
+        out_specs=anywhere,
         scratch_shapes=[pltpu.VMEM((2 * tiles, ROWS, LANES), jnp.bfloat16)]
+        + [pltpu.VMEM(out_shape, jnp.bfloat16), pltpu.SemaphoreType.DMA((angles // (2 * BATCH),))]
         + [pltpu.VMEM((BATCH, len(blocks) * ROWS, span), jnp.bfloat16)] * 2,
         compiler_params=pltpu.CompilerParams(
             vmem_limit_bytes=14 * MEBI + 2 * radon_tiles.size + 2 * math.prod(out_shape)
@@ -205,13 +224,16 @@
                 preferred_element_type=jnp.float32,
             )
 
+    per_angle = idx_ref.shape[0] // angles
+
     def scatter(start, contrib_ref):
+        bases = [(start + n) * per_angle for n in range(CHAINS)]
         for i, b in enumerate(blocks):
             row = i * GROUP
             for j in range(feeds):
                 for n in range(CHAINS):
                     tile = contrib_ref[n, row : row + GROUP, j * LANES : (j + 1) * LANES]
-                    acc_refs[n][idx_ref[start + n, b * feeds + j]] += tile
+                    acc_refs[n][idx_ref[bases[n] + (b * feeds + j)]] += tile
 
     multiply(0, 0, contrib_refs[0])
     if has_start:
@@ -561,7 +583,7 @@
     def by_chunk(idx):
         idx = idx.reshape(angles // n_pos, n_pos, n_pos, det_blocks // n_pos * feeds)
         idx = jnp.stack([jnp.roll(idx[:, p], -p, axis=1) for p in range(n_pos)], axis=1)
-        return idx.reshape(angles, det_blocks * feeds)
+        return idx.reshape(angles * det_blocks * feeds)
 
     tile_idx = by_chunk(crossed * (n_pos * tiles_each) + piece * tiles_each + within // 2)
     block_idx = by_chunk(piece * blocks_each + within)

time: 174 us -> 173 us (level)
  no operation moved by 1% of the time
where the time goes in v13:
time: 173 us
  waiting for transfers between devices  72.2 us (42%)
  Pallas kernels  51.4 us (30%)
  starting transfers between devices  32.2 us (19%)
  local copies, waits for them, and re-layouts  12.2 us (7%)
  other arithmetic  3.67 us (2%)
    all_to_all x4, waiting for transfers between devices, everyone(): return lax.all_to_all(chunk, ('ang', 'pos'), 0, 0, tiled=True)  53.8 us
    all_to_all x4, starting transfers between devices, everyone(): return lax.all_to_all(chunk, ('ang', 'pos'), 0, 0, tiled=True)  19.1 us
    ppermute x15, waiting for transfers between devices, rotate_pos(): lax.ppermute(pieces[j], 'pos', [(i, (i + sign * j) % count) for i in rang...  18.4 us
    pallas_call x2, Pallas kernels, back_project(): pl.pallas_call(functools.partial(back_project_kernel, blocks, has_start,...  17.1 us
    pallas_call x2, Pallas kernels, project(): pl.pallas_call(functools.partial(project_kernel, blocks, pieces), out_sha...  13.8 us
    ppermute x15, starting transfers between devices, rotate_pos(): lax.ppermute(pieces[j], 'pos', [(i, (i + sign * j) % count) for i in rang...  13.1 us
    pallas_call x1, Pallas kernels, exit_rest(): pl.pallas_call(functools.partial(exit_rest_kernel, len(amps)), out_shape=...  10.6 us
    pallas_call x1, Pallas kernels, exit_first(): pl.pallas_call(functools.partial(exit_first_kernel, len(amps)), out_shape...  9.88 us
  transfers between devices with their start and end apart: 19, of which 10 were waited for; matrix products, arithmetic and copies ran while one was open for 7% of the time, Pallas kernels for 25%

profile of v13, /device:TPU:1, one launch (start us, length us, event | category | flops | bytes accessed | tf_op | source)
XLA Modules:
  0.0 172.8 jit_solution(13011768498353137629)
XLA Ops:
  0.7 0.0 copy-start
  0.7 1.3 dynamic-slice_bitcast_fusion.4
  2.1 2.7 %collective-permute-start = (bf16[16,8192]{1,0:T(8,128)(2,1)S(1)}, bf16[16,8192]{1,0:T(8,128)(2,1)S(1)}, u32[]{:S(2)}, u32[]{:S(2)}) collective-permute-start(bf16[16,8192]{1,0:T(8,128)(2,1)S(1)} %get-tuple-element.89), channel_id=1, source_target_pairs={{0,1},{1,2},{2,3},{3,0},{4,5},{5,6},{6,7},{7,4},{8,9},{9,10},{10,1... | collective-permute-start | bytes 786440 | tf_op jit(solution)/shard_map/ppermute | solution.py:37
  4.7 0.0 collective-permute-start.1
  4.7 0.5 collective-permute-start.2
  5.2 0.3 fusion.5
  5.5 0.3 copy.27
  5.8 0.2 reshape.194
  6.2 0.1 reshape.195.idx_ref
  6.3 4.0 %collective-permute-done.refs_1_ = bf16[16,8192]{1,0:T(8,128)(2,1)S(1)} collective-permute-done((bf16[16,8192]{1,0:T(8,128)(2,1)S(1)}, bf16[16,8192]{1,0:T(8,128)(2,1)S(1)}, u32[]{:S(2)}, u32[]{:S(2)}) %collective-permute-start) | collective-permute-done | bytes 262176 | tf_op jit(solution)/shard_map/ppermute | solution.py:37
  10.2 5.6 %collective-permute-done.1.refs_2_ = bf16[16,8192]{1,0:T(8,128)(2,1)S(1)} collective-permute-done((bf16[16,8192]{1,0:T(8,128)(2,1)S(1)}, bf16[16,8192]{1,0:T(8,128)(2,1)S(1)}, u32[]{:S(2)}, u32[]{:S(2)}) %collective-permute-start.1) | collective-permute-done | bytes 262176 | tf_op jit(solution)/shard_map/ppermute | solution.py:37
  15.8 0.5 collective-permute-done.2.refs_3_
  16.3 7.6 %project_early.1 = bf16[32,16,1280]{2,1,0:T(8,128)(2,1)} custom-call(s32[4096]{0:T(1024)S(1)} %reshape.195.idx_ref, bf16[32,64,256]{2,1,0:T(8,128)(2,1)S(1)} %copy-done, bf16[16,8192]{1,0:T(8,128)(2,1)S(1)} %get-tuple-element.49.refs_0_, bf16[16,8192]{1,0:T(8,128)(2,1)S(1)} %collective-permute-done.refs_1_, ...), custom_call_target="tpu_custom_call" | custom-call | flops 10350000128 | bytes 900000 | tf_op jit(solution)/shard_map/project_early/pallas_call | solution.py:163
  24.0 0.0 copy-start.10
  24.0 0.0 copy-start.9
  24.0 6.5 %all-to-all-start = ((bf16[32,16,1280]{2,1,0:T(8,128)(2,1)}), bf16[32,16,1280]{2,1,0:T(8,128)(2,1)S(1)}, u32[]{:S(2)}, u32[]{:S(2)}) async-start(bf16[32,16,1280]{2,1,0:T(8,128)(2,1)} %project_early.1), calls=%async_computation | async-start | bytes 2621440 | tf_op jit(solution)/shard_map/all_to_all | solution.py:547
  30.6 0.1 copy.32
  30.7 0.1 pad_add_fusion.2
  30.8 1.7 collective-permute-start.5
  32.5 0.5 collective-permute-start.3
  33.0 2.9 %dynamic-slice_bitcast_fusion = (bf16[4,256,256]{2,1,0:T(8,128)(2,1)}, bf16[4,256,256]{2,1,0:T(8,128)(2,1)}, bf16[4,256,256]{2,1,0:T(8,128)(2,1)}, bf16[4,256,256]{2,1,0:T(8,128)(2,1)}) fusion(bf16[4,4,256,256]{3,2,1,0:T(8,128)(2,1)} %param.13, s32[]{:T(128)S(6)} %select_n.316, s32[]{:T(128)S(6)} %select_n.314, s32[]{:T(128)S(6)} %select_n.312, s32[]{:T(128)S(6)} %select_n.310), kind=kLoop, calls=%fused_computation.11 | loop fusion | bytes 4194320 | tf_op jit(solution)/shard_map/jit(dynamic_index_in_dim)/squeeze | solution.py:571
  36.0 1.3 collective-permute-start.6
  37.3 0.0 collective-permute-start.7
  37.3 0.0 collective-permute-done.5
  37.3 1.6 collective-permute-start.8
  38.9 0.0 collective-permute-done.4
  38.9 0.0 collective-permute-done.3
  38.9 0.6 pad_add_fusion.3.meta_ref
  39.5 6.2 %project_late.1 = bf16[32,16,768]{2,1,0:T(8,128)(2,1)} custom-call(s32[4096]{0:T(1024)S(1)} %reshape.195.idx_ref, bf16[32,64,256]{2,1,0:T(8,128)(2,1)S(1)} %copy-done, bf16[16,8192]{1,0:T(8,128)(2,1)S(1)} %get-tuple-element.49.refs_0_, bf16[16,8192]{1,0:T(8,128)(2,1)S(1)} %collective-permute-done.refs_1_, ...), custom_call_target="tpu_custom_call" | custom-call | flops 8049999872 | bytes 700000 | tf_op jit(solution)/shard_map/project_late/pallas_call | solution.py:163
  45.7 16.2 %all-to-all-done.sino_ref.early_ref = bf16[32,16,1280]{2,1,0:T(8,128)(2,1)S(1)} async-done(((bf16[32,16,1280]{2,1,0:T(8,128)(2,1)}), bf16[32,16,1280]{2,1,0:T(8,128)(2,1)S(1)}, u32[]{:S(2)}, u32[]{:S(2)}) %all-to-all-start) | async-done | bytes 1310752 | tf_op jit(solution)/shard_map/all_to_all | solution.py:547
  61.9 4.4 %all-to-all-start.1 = ((bf16[32,16,768]{2,1,0:T(8,128)(2,1)}), bf16[32,16,768]{2,1,0:T(8,128)(2,1)S(1)}, u32[]{:S(2)}, u32[]{:S(2)}) async-start(bf16[32,16,768]{2,1,0:T(8,128)(2,1)} %project_late.1), calls=%async_computation.1 | async-start | bytes 1572864 | tf_op jit(solution)/shard_map/all_to_all | solution.py:547
  66.3 0.0 collective-permute-done.6.refs_1_
  66.3 1.7 collective-permute-done.8.refs_1_
  68.0 9.9 %exit_first.1 = (f32[2,256,256]{2,1,0:T(8,128)}, bf16[32,16,768]{2,1,0:T(8,128)(2,1)}, f32[2,256,256]{2,1,0:T(8,128)}) custom-call(s32[4,5]{1,0:T(4,128)} %pad_add_fusion.3.meta_ref, bf16[2,256,256]{2,1,0:T(8,128)(2,1)} %probe_ref.3, bf16[512,512]{1,0:T(8,128)(2,1)} %constant.148.forward_ref, bf16[512,512]{1,0:T(8,128)(2,1)} %constant.151.inverse_ref, ...), custom_call_target="tpu_custom_call" | custom-call | flops 11500000256 | bytes 1000000 | tf_op jit(solution)/shard_map/exit_first/pallas_call | solution.py:482
  77.9 8.5 %all-to-all-done.1.late_ref = bf16[32,16,768]{2,1,0:T(8,128)(2,1)S(1)} async-done(((bf16[32,16,768]{2,1,0:T(8,128)(2,1)}), bf16[32,16,768]{2,1,0:T(8,128)(2,1)S(1)}, u32[]{:S(2)}, u32[]{:S(2)}) %all-to-all-start.1) | async-done | bytes 786464 | tf_op jit(solution)/shard_map/all_to_all | solution.py:547
  86.4 4.1 %all-to-all-start.2 = ((bf16[32,16,768]{2,1,0:T(8,128)(2,1)}), bf16[32,16,768]{2,1,0:T(8,128)(2,1)S(1)}, u32[]{:S(2)}, u32[]{:S(2)}) async-start(bf16[32,16,768]{2,1,0:T(8,128)(2,1)} %get-tuple-element.60), calls=%async_computation.2 | async-start | bytes 1572864 | tf_op jit(solution)/shard_map/all_to_all | solution.py:547
  90.5 10.6 %exit_rest.1 = bf16[32,16,1280]{2,1,0:T(8,128)(2,1)} custom-call(s32[4,5]{1,0:T(4,128)} %pad_add_fusion.3.meta_ref, bf16[2,256,256]{2,1,0:T(8,128)(2,1)} %probe_ref.3, bf16[512,512]{1,0:T(8,128)(2,1)} %constant.148.forward_ref, bf16[512,512]{1,0:T(8,128)(2,1)} %constant.151.inverse_ref, bf16[32,16,1280]{2,1,0:T(8,128)(2,1)} %copy-done.4, ...), custom_call_target="tpu_custom_call" | custom-call | flops 11500000256 | bytes 1000000 | tf_op jit(solution)/shard_map/exit_rest/pallas_call | solution.py:498
  101.1 9.6 %all-to-all-done.2.grad_ref = bf16[32,16,768]{2,1,0:T(8,128)(2,1)S(1)} async-done(((bf16[32,16,768]{2,1,0:T(8,128)(2,1)}), bf16[32,16,768]{2,1,0:T(8,128)(2,1)S(1)}, u32[]{:S(2)}, u32[]{:S(2)}) %all-to-all-start.2) | async-done | bytes 786464 | tf_op jit(solution)/shard_map/all_to_all | solution.py:547
  110.7 4.1 %all-to-all-start.3 = ((bf16[32,16,1280]{2,1,0:T(8,128)(2,1)}), bf16[32,16,1280]{2,1,0:T(8,128)(2,1)}, u32[]{:S(2)}, u32[]{:S(2)}) async-start(bf16[32,16,1280]{2,1,0:T(8,128)(2,1)} %exit_rest.1), calls=%async_computation.3 | async-start | bytes 2621440 | tf_op jit(solution)/shard_map/all_to_all | solution.py:547
  114.8 0.0 copy-start.1
  114.8 0.3 copy.22
  115.1 0.2 reshape.192
  115.5 0.7 reshape.193.idx_ref
  116.2 0.1 slice.101
  116.3 1.7 collective-permute-start.12
  118.0 0.9 fusion.9
  118.9 0.0 collective-permute-start.13
  119.0 0.5 collective-permute-start.14
  119.5 7.2 %back_first.1.refs_0_ = f32[512,8,128]{2,1,0:T(8,128)} custom-call(s32[4096]{0:T(1024)} %reshape.193.idx_ref, bf16[32,64,256]{2,1,0:T(8,128)(2,1)} %radon_ref.7, bf16[32,16,768]{2,1,0:T(8,128)(2,1)} %copy-done.5), custom_call_target="tpu_custom_call" | custom-call | flops 8049999872 | bytes 700000 | tf_op jit(solution)/shard_map/back_first/pallas_call | solution.py:286
  126.7 19.5 %all-to-all-done.3.grad_ref = bf16[32,16,1280]{2,1,0:T(8,128)(2,1)} async-done(((bf16[32,16,1280]{2,1,0:T(8,128)(2,1)}), bf16[32,16,1280]{2,1,0:T(8,128)(2,1)}, u32[]{:S(2)}, u32[]{:S(2)}) %all-to-all-start.3) | async-done | bytes 1310752 | tf_op jit(solution)/shard_map/all_to_all | solution.py:547
  146.2 9.9 %back_rest.1 = (bf16[16,8192]{1,0:T(8,128)(2,1)}, bf16[16,8192]{1,0:T(8,128)(2,1)}, bf16[16,8192]{1,0:T(8,128)(2,1)}, bf16[16,8192]{1,0:T(8,128)(2,1)}) custom-call(s32[4096]{0:T(1024)} %reshape.193.idx_ref, bf16[32,64,256]{2,1,0:T(8,128)(2,1)} %radon_ref.7, bf16[32,16,1280]{2,1,0:T(8,128)(2,1)} %all-to-all-done.3.grad_ref, f32[512,8,128]{2,1,0:T(8,128)} %back_first.1.refs_0_), custom_call_target="tpu_custom_call" | custom-call | flops 10350000128 | bytes 900000 | tf_op jit(solution)/shard_map/back_rest/pallas_call | solution.py:286
  156.1 1.9 %collective-permute-start.9 = (bf16[16,8192]{1,0:T(8,128)(2,1)}, bf16[16,8192]{1,0:T(8,128)(2,1)S(1)}, u32[]{:S(2)}, u32[]{:S(2)}) collective-permute-start(bf16[16,8192]{1,0:T(8,128)(2,1)} %get-tuple-element.68), channel_id=1, source_target_pairs={{0,1},{1,2},{2,3},{3,0},{4,5},{5,6},{6,7},{7,4},{8,9},{9,10},{10,1... | collective-permute-start | bytes 786440 | tf_op jit(solution)/shard_map/ppermute | solution.py:37
  158.1 0.7 collective-permute-start.10
  158.7 0.0 collective-permute-done.12
  158.7 0.0 collective-permute-start.11
  158.7 0.0 collective-permute-done.14
  158.7 0.6 select_bitcast_fusion.3
  159.5 0.3 maximum_convert_fusion
  159.8 4.7 %copy.37 = f32[2,256,4,512]{3,2,1,0:T(4,128)} copy(f32[2,256,4,512]{3,1,0,2:T(8,128)S(1)} %maximum_convert_fusion) | data formatting | bytes 8388608
  164.5 0.0 collective-permute-done.9
  164.6 5.9 %collective-permute-done.10 = bf16[16,8192]{1,0:T(8,128)(2,1)S(1)} collective-permute-done((bf16[16,8192]{1,0:T(8,128)(2,1)}, bf16[16,8192]{1,0:T(8,128)(2,1)S(1)}, u32[]{:S(2)}, u32[]{:S(2)}) %collective-permute-start.10) | collective-permute-done | bytes 262176 | tf_op jit(solution)/shard_map/ppermute | solution.py:37
  170.5 0.6 collective-permute-done.11
  171.1 0.1 select_bitcast_fusion.7
  171.2 1.6 multiply_add_fusion
  (46 shorter events, 0.5 us)
Async XLA Ops:
  0.6 4.6 %copy-start.8 = (s32[32,32,4]{1,2,0:T(4,128)S(1)}, s32[32,32,4]{1,2,0:T(4,128)}, u32[]{:S(2)}) copy-start(s32[32,32,4]{1,2,0:T(4,128)} %param.11) | copy-start | bytes 49156
  0.7 15.7 %copy-start = (bf16[32,64,256]{2,1,0:T(8,128)(2,1)S(1)}, bf16[32,64,256]{2,1,0:T(8,128)(2,1)}, u32[]{:S(2)}) copy-start(bf16[32,64,256]{2,1,0:T(8,128)(2,1)} %radon_ref.7) | copy-start | bytes 3145732
  2.1 8.2 %collective-permute-start = (bf16[16,8192]{1,0:T(8,128)(2,1)S(1)}, bf16[16,8192]{1,0:T(8,128)(2,1)S(1)}, u32[]{:S(2)}, u32[]{:S(2)}) collective-permute-start(bf16[16,8192]{1,0:T(8,128)(2,1)S(1)} %get-tuple-element.89), channel_id=1, source_target_pairs={{0,1},{1,2},{2,3},{3,0},{4,5},{5,6},{6,7},{7,4},{8,9},{9,10},{10,1... | collective-permute-start | bytes 786440 | tf_op jit(solution)/shard_map/ppermute | solution.py:37
  4.7 11.1 %collective-permute-start.1 = (bf16[16,8192]{1,0:T(8,128)(2,1)S(1)}, bf16[16,8192]{1,0:T(8,128)(2,1)S(1)}, u32[]{:S(2)}, u32[]{:S(2)}) collective-permute-start(bf16[16,8192]{1,0:T(8,128)(2,1)S(1)} %get-tuple-element.91), channel_id=1, source_target_pairs={{0,2},{1,3},{2,0},{3,1},{4,6},{5,7},{6,4},{7,5},{8,10},{9,11},{10,... | collective-permute-start | bytes 786440 | tf_op jit(solution)/shard_map/ppermute | solution.py:37
  4.7 11.6 %collective-permute-start.2 = (bf16[16,8192]{1,0:T(8,128)(2,1)S(1)}, bf16[16,8192]{1,0:T(8,128)(2,1)S(1)}, u32[]{:S(2)}, u32[]{:S(2)}) collective-permute-start(bf16[16,8192]{1,0:T(8,128)(2,1)S(1)} %get-tuple-element.88), channel_id=1, source_target_pairs={{0,3},{1,0},{2,1},{3,2},{4,7},{5,4},{6,5},{7,6},{8,11},{9,8},{10,9... | collective-permute-start | bytes 786440 | tf_op jit(solution)/shard_map/ppermute | solution.py:37
  24.0 6.6 %copy-start.10 = (s32[4,1]{0,1:T(1,128)S(1)}, s32[4,1]{0,1:T(1,128)}, u32[]{:S(2)}) copy-start(s32[4,1]{0,1:T(1,128)} %param.15) | copy-start | bytes 52
  24.0 6.7 %copy-start.9 = (s32[4,4]{1,0:T(4,128)S(1)}, s32[4,4]{1,0:T(4,128)}, u32[]{:S(2)}) copy-start(s32[4,4]{1,0:T(4,128)} %param.14) | copy-start | bytes 196
  24.0 37.9 %all-to-all-start = ((bf16[32,16,1280]{2,1,0:T(8,128)(2,1)}), bf16[32,16,1280]{2,1,0:T(8,128)(2,1)S(1)}, u32[]{:S(2)}, u32[]{:S(2)}) async-start(bf16[32,16,1280]{2,1,0:T(8,128)(2,1)} %project_early.1), calls=%async_computation | async-start | bytes 2621440 | tf_op jit(solution)/shard_map/all_to_all | solution.py:547
  30.8 6.5 %collective-permute-start.5 = (s32[1,5]{1,0:T(1,128)S(1)}, s32[1,5]{1,0:T(1,128)S(1)}, u32[]{:S(2)}, u32[]{:S(2)}) collective-permute-start(s32[1,5]{1,0:T(1,128)S(1)} %get-tuple-element.107), channel_id=1, source_target_pairs={{0,1},{1,2},{2,3},{3,0},{4,5},{5,6},{6,7},{7,4},{8,9},{9,10},{10,1... | collective-permute-start | bytes 68 | tf_op jit(solution)/shard_map/ppermute | solution.py:37
  32.5 6.4 %collective-permute-start.4 = (s32[1,5]{1,0:T(1,128)S(1)}, s32[1,5]{1,0:T(1,128)S(1)}, u32[]{:S(2)}, u32[]{:S(2)}) collective-permute-start(s32[1,5]{1,0:T(1,128)S(1)} %get-tuple-element.108), channel_id=1, source_target_pairs={{0,2},{1,3},{2,0},{3,1},{4,6},{5,7},{6,4},{7,5},{8,10},{9,11},{10,... | collective-permute-start | bytes 68 | tf_op jit(solution)/shard_map/ppermute | solution.py:37
  32.5 6.4 %collective-permute-start.3 = (s32[1,5]{1,0:T(1,128)S(1)}, s32[1,5]{1,0:T(1,128)S(1)}, u32[]{:S(2)}, u32[]{:S(2)}) collective-permute-start(s32[1,5]{1,0:T(1,128)S(1)} %get-tuple-element.109), channel_id=1, source_target_pairs={{0,3},{1,0},{2,1},{3,2},{4,7},{5,4},{6,5},{7,6},{8,11},{9,8},{10,9... | collective-permute-start | bytes 68 | tf_op jit(solution)/shard_map/ppermute | solution.py:37
  36.0 30.3 %collective-permute-start.6 = (bf16[4,256,256]{2,1,0:T(8,128)(2,1)}, bf16[4,256,256]{2,1,0:T(8,128)(2,1)}, u32[]{:S(2)}, u32[]{:S(2)}) collective-permute-start(bf16[4,256,256]{2,1,0:T(8,128)(2,1)} %get-tuple-element.80), channel_id=1, source_target_pairs={{0,3},{1,0},{2,1},{3,2},{4,7},{5,4},{6,5},{7,6},{8,11},{9,8},{10,9... | collective-permute-start | bytes 1572872 | tf_op jit(solution)/shard_map/ppermute | solution.py:37
  37.3 29.0 %collective-permute-start.7 = (bf16[4,256,256]{2,1,0:T(8,128)(2,1)}, bf16[4,256,256]{2,1,0:T(8,128)(2,1)}, u32[]{:S(2)}, u32[]{:S(2)}) collective-permute-start(bf16[4,256,256]{2,1,0:T(8,128)(2,1)} %get-tuple-element.79), channel_id=1, source_target_pairs={{0,2},{1,3},{2,0},{3,1},{4,6},{5,7},{6,4},{7,5},{8,10},{9,11},{10,... | collective-permute-start | bytes 1572872 | tf_op jit(solution)/shard_map/ppermute | solution.py:37
  37.3 30.7 %collective-permute-start.8 = (bf16[4,256,256]{2,1,0:T(8,128)(2,1)}, bf16[4,256,256]{2,1,0:T(8,128)(2,1)}, u32[]{:S(2)}, u32[]{:S(2)}) collective-permute-start(bf16[4,256,256]{2,1,0:T(8,128)(2,1)} %get-tuple-element.78), channel_id=1, source_target_pairs={{0,1},{1,2},{2,3},{3,0},{4,5},{5,6},{6,7},{7,4},{8,9},{9,10},{10,1... | collective-permute-start | bytes 1572872 | tf_op jit(solution)/shard_map/ppermute | solution.py:37
  61.9 6.1 %copy-start.4 = (bf16[32,16,1280]{2,1,0:T(8,128)(2,1)}, bf16[32,16,1280]{2,1,0:T(8,128)(2,1)S(1)}, u32[]{:S(2)}) copy-start(bf16[32,16,1280]{2,1,0:T(8,128)(2,1)S(1)} %all-to-all-done.sino_ref.early_ref) | copy-start | bytes 3932164
  61.9 24.5 %all-to-all-start.1 = ((bf16[32,16,768]{2,1,0:T(8,128)(2,1)}), bf16[32,16,768]{2,1,0:T(8,128)(2,1)S(1)}, u32[]{:S(2)}, u32[]{:S(2)}) async-start(bf16[32,16,768]{2,1,0:T(8,128)(2,1)} %project_late.1), calls=%async_computation.1 | async-start | bytes 1572864 | tf_op jit(solution)/shard_map/all_to_all | solution.py:547
  86.4 4.1 %copy-start.6 = (bf16[32,16,768]{2,1,0:T(8,128)(2,1)}, bf16[32,16,768]{2,1,0:T(8,128)(2,1)S(1)}, u32[]{:S(2)}) copy-start(bf16[32,16,768]{2,1,0:T(8,128)(2,1)S(1)} %all-to-all-done.1.late_ref) | copy-start | bytes 2359300
  86.4 24.2 %all-to-all-start.2 = ((bf16[32,16,768]{2,1,0:T(8,128)(2,1)}), bf16[32,16,768]{2,1,0:T(8,128)(2,1)S(1)}, u32[]{:S(2)}, u32[]{:S(2)}) async-start(bf16[32,16,768]{2,1,0:T(8,128)(2,1)} %get-tuple-element.60), calls=%async_computation.2 | async-start | bytes 1572864 | tf_op jit(solution)/shard_map/all_to_all | solution.py:547
  101.1 15.1 %copy-start.3 = (bf16[32,16,768]{2,1,0:T(8,128)(2,1)S(1)}, bf16[32,16,768]{2,1,0:T(8,128)(2,1)}, u32[]{:S(2)}) copy-start(bf16[32,16,768]{2,1,0:T(8,128)(2,1)} %get-tuple-element.60) | copy-start | bytes 2359300
  110.7 4.8 %copy-start.5 = (bf16[32,16,768]{2,1,0:T(8,128)(2,1)}, bf16[32,16,768]{2,1,0:T(8,128)(2,1)S(1)}, u32[]{:S(2)}) copy-start(bf16[32,16,768]{2,1,0:T(8,128)(2,1)S(1)} %all-to-all-done.2.grad_ref) | copy-start | bytes 2359300
  110.7 35.5 %all-to-all-start.3 = ((bf16[32,16,1280]{2,1,0:T(8,128)(2,1)}), bf16[32,16,1280]{2,1,0:T(8,128)(2,1)}, u32[]{:S(2)}, u32[]{:S(2)}) async-start(bf16[32,16,1280]{2,1,0:T(8,128)(2,1)} %exit_rest.1), calls=%async_computation.3 | async-start | bytes 2621440 | tf_op jit(solution)/shard_map/all_to_all | solution.py:547
  114.8 3.2 %copy-start.1 = (bf16[32,16,1280]{2,1,0:T(8,128)(2,1)S(1)}, bf16[32,16,1280]{2,1,0:T(8,128)(2,1)}, u32[]{:S(2)}) copy-start(bf16[32,16,1280]{2,1,0:T(8,128)(2,1)} %exit_rest.1) | copy-start | bytes 3932164
  116.3 42.4 %collective-permute-start.12 = (bf16[32,16,512]{2,1,0:T(8,128)(2,1)S(1)}, bf16[32,16,512]{2,1,0:T(8,128)(2,1)S(1)}, u32[]{:S(2)}, u32[]{:S(2)}) collective-permute-start(bf16[32,16,512]{2,1,0:T(8,128)(2,1)S(1)} %slice.101), channel_id=1, source_target_pairs={{0,1},{1,2},{2,3},{3,0},{4,5},{5,6},{6,7},{7,4},{8,9},{9,10},{10,1... | collective-permute-start | bytes 1572872 | tf_op jit(solution)/shard_map/ppermute | solution.py:37
  118.9 39.8 %collective-permute-start.13 = (bf16[32,16,512]{2,1,0:T(8,128)(2,1)}, bf16[32,16,512]{2,1,0:T(8,128)(2,1)S(1)}, u32[]{:S(2)}, u32[]{:S(2)}) collective-permute-start(bf16[32,16,512]{2,1,0:T(8,128)(2,1)} %get-tuple-element.83), channel_id=1, source_target_pairs={{0,2},{1,3},{2,0},{3,1},{4,6},{5,7},{6,4},{7,5},{8,10},{9,11},{10,... | collective-permute-start | bytes 1572872 | tf_op jit(solution)/shard_map/ppermute | solution.py:37
  119.0 39.7 %collective-permute-start.14 = (bf16[32,16,512]{2,1,0:T(8,128)(2,1)S(1)}, bf16[32,16,512]{2,1,0:T(8,128)(2,1)S(1)}, u32[]{:S(2)}, u32[]{:S(2)}) collective-permute-start(bf16[32,16,512]{2,1,0:T(8,128)(2,1)S(1)} %get-tuple-element.82), channel_id=1, source_target_pairs={{0,3},{1,0},{2,1},{3,2},{4,7},{5,4},{6,5},{7,6},{8,11},{9,8},{10,9... | collective-permute-start | bytes 1572872 | tf_op jit(solution)/shard_map/ppermute | solution.py:37
  156.1 8.4 %collective-permute-start.9 = (bf16[16,8192]{1,0:T(8,128)(2,1)}, bf16[16,8192]{1,0:T(8,128)(2,1)S(1)}, u32[]{:S(2)}, u32[]{:S(2)}) collective-permute-start(bf16[16,8192]{1,0:T(8,128)(2,1)} %get-tuple-element.68), channel_id=1, source_target_pairs={{0,1},{1,2},{2,3},{3,0},{4,5},{5,6},{6,7},{7,4},{8,9},{9,10},{10,1... | collective-permute-start | bytes 786440 | tf_op jit(solution)/shard_map/ppermute | solution.py:37
  158.1 12.4 %collective-permute-start.10 = (bf16[16,8192]{1,0:T(8,128)(2,1)}, bf16[16,8192]{1,0:T(8,128)(2,1)S(1)}, u32[]{:S(2)}, u32[]{:S(2)}) collective-permute-start(bf16[16,8192]{1,0:T(8,128)(2,1)} %get-tuple-element.69), channel_id=1, source_target_pairs={{0,2},{1,3},{2,0},{3,1},{4,6},{5,7},{6,4},{7,5},{8,10},{9,11},{10,... | collective-permute-start | bytes 786440 | tf_op jit(solution)/shard_map/ppermute | solution.py:37
  158.7 12.4 %collective-permute-start.11 = (bf16[16,8192]{1,0:T(8,128)(2,1)}, bf16[16,8192]{1,0:T(8,128)(2,1)S(1)}, u32[]{:S(2)}, u32[]{:S(2)}) collective-permute-start(bf16[16,8192]{1,0:T(8,128)(2,1)} %get-tuple-element.70), channel_id=1, source_target_pairs={{0,3},{1,0},{2,1},{3,2},{4,7},{5,4},{6,5},{7,6},{8,11},{9,8},{10,9... | collective-permute-start | bytes 786440 | tf_op jit(solution)/shard_map/ppermute | solution.py:37
  159.8 11.3 %copy-start.7 = (bf16[16,8192]{1,0:T(8,128)(2,1)S(1)}, bf16[16,8192]{1,0:T(8,128)(2,1)}, u32[]{:S(2)}) copy-start(bf16[16,8192]{1,0:T(8,128)(2,1)} %get-tuple-element.71) | copy-start | bytes 786436
  164.5 6.7 %copy-start.2 = (bf16[2,32,8192]{2,1,0:T(8,128)(2,1)S(1)}, bf16[2,32,8192]{2,1,0:T(8,128)(2,1)}, u32[]{:S(2)}) copy-start(bf16[2,32,8192]{2,1,0:T(8,128)(2,1)} %param.9) | copy-start | bytes 3145732

commit v14 on v13

--- a/solution.py
+++ b/solution.py
@@ -104,17 +104,22 @@
                     )
 
     def multiply(start, lhs_ref):
+        per_half = len(blocks) // 4 * 2 * ROWS
         for n in range(batch):
             a = start + n
-            product = lax.dot_general(
-                lhs_ref[n], radon_ref[a], (((1,), (1,)), ((), ())), preferred_element_type=jnp.float32
-            )
-            for pair in range(len(blocks) // 2):
-                row = 2 * pair * ROWS
-                tile = jnp.concatenate(
-                    [product[row : row + ROWS], product[row + ROWS : row + 2 * ROWS]], axis=1
+            for begin, end in ((0, per_half), (per_half, len(blocks) * ROWS)):
+                product = lax.dot_general(
+                    lhs_ref[n, begin:end, :],
+                    radon_ref[a],
+                    (((1,), (1,)), ((), ())),
+                    preferred_element_type=jnp.float32,
                 )
-                out_ref[a, :, pair * LANES : (pair + 1) * LANES] = tile.astype(jnp.bfloat16)
+                for row in range(0, end - begin, 2 * ROWS):
+                    tile = jnp.concatenate(
+                        [product[row : row + ROWS], product[row + ROWS : row + 2 * ROWS]], axis=1
+                    )
+                    lane = (begin + row) // (2 * ROWS) * LANES
+                    out_ref[a, :, lane : lane + LANES] = tile.astype(jnp.bfloat16)
 
     def leave(step):
         here = pl.ds(step * 2 * batch, 2 * batch)
@@ -218,11 +223,11 @@
                 even = jnp.where(low, real, swap_halves(imag))
                 odd = jnp.where(low, swap_halves(real), imag)
                 lhs.append(jnp.concatenate([even, odd], axis=0).astype(jnp.bfloat16))
-            contrib_ref[n] = jnp.dot(
-                jnp.concatenate(lhs, axis=0),
-                w_ref[half * CHAINS + n],
-                preferred_element_type=jnp.float32,
-            )
+            lhs = jnp.concatenate(lhs, axis=0)
+            for lanes in (slice(0, span), slice(span, 2 * span)):
+                contrib_ref[n, :, lanes] = jnp.dot(
+                    lhs, w_ref[half * CHAINS + n, :, lanes], preferred_element_type=jnp.float32
+                )
 
     per_angle = idx_ref.shape[0] // angles
 

time: 173 us -> 174 us (level)
    pallas_call x1, Pallas kernels: 10.6 us -> 12.6 us  [exit_rest(): pl.pallas_call(functools.partial(exit_rest_kernel, len(amps)), out_shape=...]
    pallas_call x1, Pallas kernels: 9.88 us -> 7.85 us  [exit_first(): pl.pallas_call(functools.partial(exit_first_kernel, len(amps)), out_shape...]
where the time goes in v14:
time: 174 us; the launch traced here: 173 us
  waiting for transfers between devices  72.2 us (41%)
  Pallas kernels  51.5 us (30%)
  starting transfers between devices  32.2 us (19%)
  local copies, waits for them, and re-layouts  12.2 us (7%)
  other arithmetic  3.67 us (2%)
    all_to_all x4, waiting for transfers between devices, everyone(): return lax.all_to_all(chunk, ('ang', 'pos'), 0, 0, tiled=True)  53.8 us
    all_to_all x4, starting transfers between devices, everyone(): return lax.all_to_all(chunk, ('ang', 'pos'), 0, 0, tiled=True)  19.1 us
    ppermute x15, waiting for transfers between devices, rotate_pos(): lax.ppermute(pieces[j], 'pos', [(i, (i + sign * j) % count) for i in rang...  18.4 us
    pallas_call x2, Pallas kernels, back_project(): pl.pallas_call(functools.partial(back_project_kernel, blocks, has_start,...  17.1 us
    pallas_call x2, Pallas kernels, project(): pl.pallas_call(functools.partial(project_kernel, blocks, pieces), out_sha...  13.9 us
    ppermute x15, starting transfers between devices, rotate_pos(): lax.ppermute(pieces[j], 'pos', [(i, (i + sign * j) % count) for i in rang...  13.1 us
    pallas_call x1, Pallas kernels, exit_rest(): pl.pallas_call(functools.partial(exit_rest_kernel, len(amps)), out_shape=...  12.6 us
    pallas_call x1, Pallas kernels, exit_first(): pl.pallas_call(functools.partial(exit_first_kernel, len(amps)), out_shape...  7.85 us
  transfers between devices with their start and end apart: 19, of which 10 were waited for; matrix products, arithmetic and copies ran while one was open for 7% of the time, Pallas kernels for 25%

profile of v14, /device:TPU:1, one launch (start us, length us, event | category | flops | bytes accessed | tf_op | source)
XLA Modules:
  0.0 172.9 jit_solution(6166137585806149164)
XLA Ops:
  0.7 0.0 copy-start
  0.7 1.3 dynamic-slice_bitcast_fusion.4
  2.1 2.7 %collective-permute-start = (bf16[16,8192]{1,0:T(8,128)(2,1)S(1)}, bf16[16,8192]{1,0:T(8,128)(2,1)S(1)}, u32[]{:S(2)}, u32[]{:S(2)}) collective-permute-start(bf16[16,8192]{1,0:T(8,128)(2,1)S(1)} %get-tuple-element.89), channel_id=1, source_target_pairs={{0,1},{1,2},{2,3},{3,0},{4,5},{5,6},{6,7},{7,4},{8,9},{9,10},{10,1... | collective-permute-start | bytes 786440 | tf_op jit(solution)/shard_map/ppermute | solution.py:37
  4.7 0.0 collective-permute-start.1
  4.7 0.5 collective-permute-start.2
  5.2 0.3 fusion.5
  5.5 0.3 copy.27
  5.8 0.2 reshape.194
  6.2 0.1 reshape.195.idx_ref
  6.3 4.0 %collective-permute-done.refs_1_ = bf16[16,8192]{1,0:T(8,128)(2,1)S(1)} collective-permute-done((bf16[16,8192]{1,0:T(8,128)(2,1)S(1)}, bf16[16,8192]{1,0:T(8,128)(2,1)S(1)}, u32[]{:S(2)}, u32[]{:S(2)}) %collective-permute-start) | collective-permute-done | bytes 262176 | tf_op jit(solution)/shard_map/ppermute | solution.py:37
  10.2 5.6 %collective-permute-done.1.refs_2_ = bf16[16,8192]{1,0:T(8,128)(2,1)S(1)} collective-permute-done((bf16[16,8192]{1,0:T(8,128)(2,1)S(1)}, bf16[16,8192]{1,0:T(8,128)(2,1)S(1)}, u32[]{:S(2)}, u32[]{:S(2)}) %collective-permute-start.1) | collective-permute-done | bytes 262176 | tf_op jit(solution)/shard_map/ppermute | solution.py:37
  15.8 0.5 collective-permute-done.2.refs_3_
  16.3 7.7 %project_early.1 = bf16[32,16,1280]{2,1,0:T(8,128)(2,1)} custom-call(s32[4096]{0:T(1024)S(1)} %reshape.195.idx_ref, bf16[32,64,256]{2,1,0:T(8,128)(2,1)S(1)} %copy-done, bf16[16,8192]{1,0:T(8,128)(2,1)S(1)} %get-tuple-element.49.refs_0_, bf16[16,8192]{1,0:T(8,128)(2,1)S(1)} %collective-permute-done.refs_1_, ...), custom_call_target="tpu_custom_call" | custom-call | flops 10350000128 | bytes 900000 | tf_op jit(solution)/shard_map/project_early/pallas_call | solution.py:168
  24.1 0.0 copy-start.10
  24.1 0.0 copy-start.9
  24.1 6.5 %all-to-all-start = ((bf16[32,16,1280]{2,1,0:T(8,128)(2,1)}), bf16[32,16,1280]{2,1,0:T(8,128)(2,1)S(1)}, u32[]{:S(2)}, u32[]{:S(2)}) async-start(bf16[32,16,1280]{2,1,0:T(8,128)(2,1)} %project_early.1), calls=%async_computation | async-start | bytes 2621440 | tf_op jit(solution)/shard_map/all_to_all | solution.py:552
  30.7 0.1 copy.32
  30.8 0.1 pad_add_fusion.2
  30.9 1.7 collective-permute-start.5
  32.6 0.0 collective-permute-start.4
  32.6 0.5 collective-permute-start.3
  33.1 2.9 %dynamic-slice_bitcast_fusion = (bf16[4,256,256]{2,1,0:T(8,128)(2,1)}, bf16[4,256,256]{2,1,0:T(8,128)(2,1)}, bf16[4,256,256]{2,1,0:T(8,128)(2,1)}, bf16[4,256,256]{2,1,0:T(8,128)(2,1)}) fusion(bf16[4,4,256,256]{3,2,1,0:T(8,128)(2,1)} %param.13, s32[]{:T(128)S(6)} %select_n.316, s32[]{:T(128)S(6)} %select_n.314, s32[]{:T(128)S(6)} %select_n.312, s32[]{:T(128)S(6)} %select_n.310), kind=kLoop, calls=%fused_computation.11 | loop fusion | bytes 4194320 | tf_op jit(solution)/shard_map/jit(dynamic_index_in_dim)/squeeze | solution.py:576
  36.0 1.3 collective-permute-start.6
  37.4 0.0 collective-permute-start.7
  37.4 0.0 collective-permute-done.5
  37.4 1.6 collective-permute-start.8
  39.0 0.0 collective-permute-done.4
  39.0 0.6 pad_add_fusion.3.meta_ref
  39.6 6.1 %project_late.1 = bf16[32,16,768]{2,1,0:T(8,128)(2,1)} custom-call(s32[4096]{0:T(1024)S(1)} %reshape.195.idx_ref, bf16[32,64,256]{2,1,0:T(8,128)(2,1)S(1)} %copy-done, bf16[16,8192]{1,0:T(8,128)(2,1)S(1)} %get-tuple-element.49.refs_0_, bf16[16,8192]{1,0:T(8,128)(2,1)S(1)} %collective-permute-done.refs_1_, ...), custom_call_target="tpu_custom_call" | custom-call | flops 8049999872 | bytes 700000 | tf_op jit(solution)/shard_map/project_late/pallas_call | solution.py:168
  45.8 16.2 %all-to-all-done.sino_ref.early_ref = bf16[32,16,1280]{2,1,0:T(8,128)(2,1)S(1)} async-done(((bf16[32,16,1280]{2,1,0:T(8,128)(2,1)}), bf16[32,16,1280]{2,1,0:T(8,128)(2,1)S(1)}, u32[]{:S(2)}, u32[]{:S(2)}) %all-to-all-start) | async-done | bytes 1310752 | tf_op jit(solution)/shard_map/all_to_all | solution.py:552
  62.0 4.4 %all-to-all-start.1 = ((bf16[32,16,768]{2,1,0:T(8,128)(2,1)}), bf16[32,16,768]{2,1,0:T(8,128)(2,1)S(1)}, u32[]{:S(2)}, u32[]{:S(2)}) async-start(bf16[32,16,768]{2,1,0:T(8,128)(2,1)} %project_late.1), calls=%async_computation.1 | async-start | bytes 1572864 | tf_op jit(solution)/shard_map/all_to_all | solution.py:552
  66.4 0.0 collective-permute-done.7.refs_0_
  66.4 1.7 collective-permute-done.8.refs_1_
  68.1 7.9 %exit_first.1 = (f32[2,256,256]{2,1,0:T(8,128)}, bf16[32,16,768]{2,1,0:T(8,128)(2,1)}, f32[2,256,256]{2,1,0:T(8,128)}) custom-call(s32[4,5]{1,0:T(4,128)} %pad_add_fusion.3.meta_ref, bf16[2,256,256]{2,1,0:T(8,128)(2,1)} %probe_ref.3, bf16[512,512]{1,0:T(8,128)(2,1)} %constant.148.forward_ref, bf16[512,512]{1,0:T(8,128)(2,1)} %constant.151.inverse_ref, ...), custom_call_target="tpu_custom_call" | custom-call | flops 11500000256 | bytes 1000000 | tf_op jit(solution)/shard_map/exit_first/pallas_call | solution.py:487
  75.9 10.6 %all-to-all-done.1.late_ref = bf16[32,16,768]{2,1,0:T(8,128)(2,1)S(1)} async-done(((bf16[32,16,768]{2,1,0:T(8,128)(2,1)}), bf16[32,16,768]{2,1,0:T(8,128)(2,1)S(1)}, u32[]{:S(2)}, u32[]{:S(2)}) %all-to-all-start.1) | async-done | bytes 786464 | tf_op jit(solution)/shard_map/all_to_all | solution.py:552
  86.5 4.1 %all-to-all-start.2 = ((bf16[32,16,768]{2,1,0:T(8,128)(2,1)}), bf16[32,16,768]{2,1,0:T(8,128)(2,1)S(1)}, u32[]{:S(2)}, u32[]{:S(2)}) async-start(bf16[32,16,768]{2,1,0:T(8,128)(2,1)} %get-tuple-element.60), calls=%async_computation.2 | async-start | bytes 1572864 | tf_op jit(solution)/shard_map/all_to_all | solution.py:552
  90.6 12.6 %exit_rest.1 = bf16[32,16,1280]{2,1,0:T(8,128)(2,1)} custom-call(s32[4,5]{1,0:T(4,128)} %pad_add_fusion.3.meta_ref, bf16[2,256,256]{2,1,0:T(8,128)(2,1)} %probe_ref.3, bf16[512,512]{1,0:T(8,128)(2,1)} %constant.148.forward_ref, bf16[512,512]{1,0:T(8,128)(2,1)} %constant.151.inverse_ref, bf16[32,16,1280]{2,1,0:T(8,128)(2,1)} %copy-done.4, ...), custom_call_target="tpu_custom_call" | custom-call | flops 11500000256 | bytes 1000000 | tf_op jit(solution)/shard_map/exit_rest/pallas_call | solution.py:503
  103.2 7.5 %all-to-all-done.2.grad_ref = bf16[32,16,768]{2,1,0:T(8,128)(2,1)S(1)} async-done(((bf16[32,16,768]{2,1,0:T(8,128)(2,1)}), bf16[32,16,768]{2,1,0:T(8,128)(2,1)S(1)}, u32[]{:S(2)}, u32[]{:S(2)}) %all-to-all-start.2) | async-done | bytes 786464 | tf_op jit(solution)/shard_map/all_to_all | solution.py:552
  110.7 4.1 %all-to-all-start.3 = ((bf16[32,16,1280]{2,1,0:T(8,128)(2,1)}), bf16[32,16,1280]{2,1,0:T(8,128)(2,1)}, u32[]{:S(2)}, u32[]{:S(2)}) async-start(bf16[32,16,1280]{2,1,0:T(8,128)(2,1)} %exit_rest.1), calls=%async_computation.3 | async-start | bytes 2621440 | tf_op jit(solution)/shard_map/all_to_all | solution.py:552
  114.9 0.0 copy-start.1
  114.9 0.3 copy.22
  115.2 0.2 reshape.192
  115.6 0.7 reshape.193.idx_ref
  116.3 0.1 slice.101
  116.4 1.7 collective-permute-start.12
  118.1 0.9 fusion.9
  119.0 0.0 collective-permute-start.13
  119.1 0.5 collective-permute-start.14
  119.6 7.2 %back_first.1.refs_0_ = f32[512,8,128]{2,1,0:T(8,128)} custom-call(s32[4096]{0:T(1024)} %reshape.193.idx_ref, bf16[32,64,256]{2,1,0:T(8,128)(2,1)} %radon_ref.7, bf16[32,16,768]{2,1,0:T(8,128)(2,1)} %copy-done.5), custom_call_target="tpu_custom_call" | custom-call | flops 8049999872 | bytes 700000 | tf_op jit(solution)/shard_map/back_first/pallas_call | solution.py:291
  126.8 19.5 %all-to-all-done.3.grad_ref = bf16[32,16,1280]{2,1,0:T(8,128)(2,1)} async-done(((bf16[32,16,1280]{2,1,0:T(8,128)(2,1)}), bf16[32,16,1280]{2,1,0:T(8,128)(2,1)}, u32[]{:S(2)}, u32[]{:S(2)}) %all-to-all-start.3) | async-done | bytes 1310752 | tf_op jit(solution)/shard_map/all_to_all | solution.py:552
  146.3 9.9 %back_rest.1 = (bf16[16,8192]{1,0:T(8,128)(2,1)}, bf16[16,8192]{1,0:T(8,128)(2,1)}, bf16[16,8192]{1,0:T(8,128)(2,1)}, bf16[16,8192]{1,0:T(8,128)(2,1)}) custom-call(s32[4096]{0:T(1024)} %reshape.193.idx_ref, bf16[32,64,256]{2,1,0:T(8,128)(2,1)} %radon_ref.7, bf16[32,16,1280]{2,1,0:T(8,128)(2,1)} %all-to-all-done.3.grad_ref, f32[512,8,128]{2,1,0:T(8,128)} %back_first.1.refs_0_), custom_call_target="tpu_custom_call" | custom-call | flops 10350000128 | bytes 900000 | tf_op jit(solution)/shard_map/back_rest/pallas_call | solution.py:291
  156.2 1.9 %collective-permute-start.9 = (bf16[16,8192]{1,0:T(8,128)(2,1)}, bf16[16,8192]{1,0:T(8,128)(2,1)S(1)}, u32[]{:S(2)}, u32[]{:S(2)}) collective-permute-start(bf16[16,8192]{1,0:T(8,128)(2,1)} %get-tuple-element.68), channel_id=1, source_target_pairs={{0,1},{1,2},{2,3},{3,0},{4,5},{5,6},{6,7},{7,4},{8,9},{9,10},{10,1... | collective-permute-start | bytes 786440 | tf_op jit(solution)/shard_map/ppermute | solution.py:37
  158.1 0.7 collective-permute-start.10
  158.8 0.0 collective-permute-done.12
  158.8 0.0 collective-permute-start.11
  158.8 0.0 collective-permute-done.13
  158.8 0.6 select_bitcast_fusion.3
  159.5 0.3 maximum_convert_fusion
  159.9 4.7 %copy.37 = f32[2,256,4,512]{3,2,1,0:T(4,128)} copy(f32[2,256,4,512]{3,1,0,2:T(8,128)S(1)} %maximum_convert_fusion) | data formatting | bytes 8388608
  164.6 0.0 collective-permute-done.9
  164.6 5.9 %collective-permute-done.10 = bf16[16,8192]{1,0:T(8,128)(2,1)S(1)} collective-permute-done((bf16[16,8192]{1,0:T(8,128)(2,1)}, bf16[16,8192]{1,0:T(8,128)(2,1)S(1)}, u32[]{:S(2)}, u32[]{:S(2)}) %collective-permute-start.10) | collective-permute-done | bytes 262176 | tf_op jit(solution)/shard_map/ppermute | solution.py:37
  170.6 0.6 collective-permute-done.11
  171.2 0.1 select_bitcast_fusion.7
  171.3 1.6 multiply_add_fusion
  (46 shorter events, 0.5 us)
Async XLA Ops:
  0.6 4.6 %copy-start.8 = (s32[32,32,4]{1,2,0:T(4,128)S(1)}, s32[32,32,4]{1,2,0:T(4,128)}, u32[]{:S(2)}) copy-start(s32[32,32,4]{1,2,0:T(4,128)} %param.11) | copy-start | bytes 49156
  0.7 15.7 %copy-start = (bf16[32,64,256]{2,1,0:T(8,128)(2,1)S(1)}, bf16[32,64,256]{2,1,0:T(8,128)(2,1)}, u32[]{:S(2)}) copy-start(bf16[32,64,256]{2,1,0:T(8,128)(2,1)} %radon_ref.7) | copy-start | bytes 3145732
  2.1 8.2 %collective-permute-start = (bf16[16,8192]{1,0:T(8,128)(2,1)S(1)}, bf16[16,8192]{1,0:T(8,128)(2,1)S(1)}, u32[]{:S(2)}, u32[]{:S(2)}) collective-permute-start(bf16[16,8192]{1,0:T(8,128)(2,1)S(1)} %get-tuple-element.89), channel_id=1, source_target_pairs={{0,1},{1,2},{2,3},{3,0},{4,5},{5,6},{6,7},{7,4},{8,9},{9,10},{10,1... | collective-permute-start | bytes 786440 | tf_op jit(solution)/shard_map/ppermute | solution.py:37
  4.7 11.1 %collective-permute-start.1 = (bf16[16,8192]{1,0:T(8,128)(2,1)S(1)}, bf16[16,8192]{1,0:T(8,128)(2,1)S(1)}, u32[]{:S(2)}, u32[]{:S(2)}) collective-permute-start(bf16[16,8192]{1,0:T(8,128)(2,1)S(1)} %get-tuple-element.91), channel_id=1, source_target_pairs={{0,2},{1,3},{2,0},{3,1},{4,6},{5,7},{6,4},{7,5},{8,10},{9,11},{10,... | collective-permute-start | bytes 786440 | tf_op jit(solution)/shard_map/ppermute | solution.py:37
  4.7 11.6 %collective-permute-start.2 = (bf16[16,8192]{1,0:T(8,128)(2,1)S(1)}, bf16[16,8192]{1,0:T(8,128)(2,1)S(1)}, u32[]{:S(2)}, u32[]{:S(2)}) collective-permute-start(bf16[16,8192]{1,0:T(8,128)(2,1)S(1)} %get-tuple-element.88), channel_id=1, source_target_pairs={{0,3},{1,0},{2,1},{3,2},{4,7},{5,4},{6,5},{7,6},{8,11},{9,8},{10,9... | collective-permute-start | bytes 786440 | tf_op jit(solution)/shard_map/ppermute | solution.py:37
  24.1 6.6 %copy-start.10 = (s32[4,1]{0,1:T(1,128)S(1)}, s32[4,1]{0,1:T(1,128)}, u32[]{:S(2)}) copy-start(s32[4,1]{0,1:T(1,128)} %param.15) | copy-start | bytes 52
  24.1 6.7 %copy-start.9 = (s32[4,4]{1,0:T(4,128)S(1)}, s32[4,4]{1,0:T(4,128)}, u32[]{:S(2)}) copy-start(s32[4,4]{1,0:T(4,128)} %param.14) | copy-start | bytes 196
  24.1 37.8 %all-to-all-start = ((bf16[32,16,1280]{2,1,0:T(8,128)(2,1)}), bf16[32,16,1280]{2,1,0:T(8,128)(2,1)S(1)}, u32[]{:S(2)}, u32[]{:S(2)}) async-start(bf16[32,16,1280]{2,1,0:T(8,128)(2,1)} %project_early.1), calls=%async_computation | async-start | bytes 2621440 | tf_op jit(solution)/shard_map/all_to_all | solution.py:552
  30.9 6.5 %collective-permute-start.5 = (s32[1,5]{1,0:T(1,128)S(1)}, s32[1,5]{1,0:T(1,128)S(1)}, u32[]{:S(2)}, u32[]{:S(2)}) collective-permute-start(s32[1,5]{1,0:T(1,128)S(1)} %get-tuple-element.107), channel_id=1, source_target_pairs={{0,1},{1,2},{2,3},{3,0},{4,5},{5,6},{6,7},{7,4},{8,9},{9,10},{10,1... | collective-permute-start | bytes 68 | tf_op jit(solution)/shard_map/ppermute | solution.py:37
  32.6 6.4 %collective-permute-start.4 = (s32[1,5]{1,0:T(1,128)S(1)}, s32[1,5]{1,0:T(1,128)S(1)}, u32[]{:S(2)}, u32[]{:S(2)}) collective-permute-start(s32[1,5]{1,0:T(1,128)S(1)} %get-tuple-element.108), channel_id=1, source_target_pairs={{0,2},{1,3},{2,0},{3,1},{4,6},{5,7},{6,4},{7,5},{8,10},{9,11},{10,... | collective-permute-start | bytes 68 | tf_op jit(solution)/shard_map/ppermute | solution.py:37
  32.6 6.4 %collective-permute-start.3 = (s32[1,5]{1,0:T(1,128)S(1)}, s32[1,5]{1,0:T(1,128)S(1)}, u32[]{:S(2)}, u32[]{:S(2)}) collective-permute-start(s32[1,5]{1,0:T(1,128)S(1)} %get-tuple-element.109), channel_id=1, source_target_pairs={{0,3},{1,0},{2,1},{3,2},{4,7},{5,4},{6,5},{7,6},{8,11},{9,8},{10,9... | collective-permute-start | bytes 68 | tf_op jit(solution)/shard_map/ppermute | solution.py:37
  36.0 30.3 %collective-permute-start.6 = (bf16[4,256,256]{2,1,0:T(8,128)(2,1)}, bf16[4,256,256]{2,1,0:T(8,128)(2,1)}, u32[]{:S(2)}, u32[]{:S(2)}) collective-permute-start(bf16[4,256,256]{2,1,0:T(8,128)(2,1)} %get-tuple-element.80), channel_id=1, source_target_pairs={{0,3},{1,0},{2,1},{3,2},{4,7},{5,4},{6,5},{7,6},{8,11},{9,8},{10,9... | collective-permute-start | bytes 1572872 | tf_op jit(solution)/shard_map/ppermute | solution.py:37
  37.4 29.0 %collective-permute-start.7 = (bf16[4,256,256]{2,1,0:T(8,128)(2,1)}, bf16[4,256,256]{2,1,0:T(8,128)(2,1)}, u32[]{:S(2)}, u32[]{:S(2)}) collective-permute-start(bf16[4,256,256]{2,1,0:T(8,128)(2,1)} %get-tuple-element.79), channel_id=1, source_target_pairs={{0,2},{1,3},{2,0},{3,1},{4,6},{5,7},{6,4},{7,5},{8,10},{9,11},{10,... | collective-permute-start | bytes 1572872 | tf_op jit(solution)/shard_map/ppermute | solution.py:37
  37.4 30.7 %collective-permute-start.8 = (bf16[4,256,256]{2,1,0:T(8,128)(2,1)}, bf16[4,256,256]{2,1,0:T(8,128)(2,1)}, u32[]{:S(2)}, u32[]{:S(2)}) collective-permute-start(bf16[4,256,256]{2,1,0:T(8,128)(2,1)} %get-tuple-element.78), channel_id=1, source_target_pairs={{0,1},{1,2},{2,3},{3,0},{4,5},{5,6},{6,7},{7,4},{8,9},{9,10},{10,1... | collective-permute-start | bytes 1572872 | tf_op jit(solution)/shard_map/ppermute | solution.py:37
  62.0 6.1 %copy-start.4 = (bf16[32,16,1280]{2,1,0:T(8,128)(2,1)}, bf16[32,16,1280]{2,1,0:T(8,128)(2,1)S(1)}, u32[]{:S(2)}) copy-start(bf16[32,16,1280]{2,1,0:T(8,128)(2,1)S(1)} %all-to-all-done.sino_ref.early_ref) | copy-start | bytes 3932164
  62.0 24.5 %all-to-all-start.1 = ((bf16[32,16,768]{2,1,0:T(8,128)(2,1)}), bf16[32,16,768]{2,1,0:T(8,128)(2,1)S(1)}, u32[]{:S(2)}, u32[]{:S(2)}) async-start(bf16[32,16,768]{2,1,0:T(8,128)(2,1)} %project_late.1), calls=%async_computation.1 | async-start | bytes 1572864 | tf_op jit(solution)/shard_map/all_to_all | solution.py:552
  86.5 4.1 %copy-start.6 = (bf16[32,16,768]{2,1,0:T(8,128)(2,1)}, bf16[32,16,768]{2,1,0:T(8,128)(2,1)S(1)}, u32[]{:S(2)}) copy-start(bf16[32,16,768]{2,1,0:T(8,128)(2,1)S(1)} %all-to-all-done.1.late_ref) | copy-start | bytes 2359300
  86.5 24.2 %all-to-all-start.2 = ((bf16[32,16,768]{2,1,0:T(8,128)(2,1)}), bf16[32,16,768]{2,1,0:T(8,128)(2,1)S(1)}, u32[]{:S(2)}, u32[]{:S(2)}) async-start(bf16[32,16,768]{2,1,0:T(8,128)(2,1)} %get-tuple-element.60), calls=%async_computation.2 | async-start | bytes 1572864 | tf_op jit(solution)/shard_map/all_to_all | solution.py:552
  103.2 13.1 %copy-start.3 = (bf16[32,16,768]{2,1,0:T(8,128)(2,1)S(1)}, bf16[32,16,768]{2,1,0:T(8,128)(2,1)}, u32[]{:S(2)}) copy-start(bf16[32,16,768]{2,1,0:T(8,128)(2,1)} %get-tuple-element.60) | copy-start | bytes 2359300
  110.7 4.8 %copy-start.5 = (bf16[32,16,768]{2,1,0:T(8,128)(2,1)}, bf16[32,16,768]{2,1,0:T(8,128)(2,1)S(1)}, u32[]{:S(2)}) copy-start(bf16[32,16,768]{2,1,0:T(8,128)(2,1)S(1)} %all-to-all-done.2.grad_ref) | copy-start | bytes 2359300
  110.7 35.5 %all-to-all-start.3 = ((bf16[32,16,1280]{2,1,0:T(8,128)(2,1)}), bf16[32,16,1280]{2,1,0:T(8,128)(2,1)}, u32[]{:S(2)}, u32[]{:S(2)}) async-start(bf16[32,16,1280]{2,1,0:T(8,128)(2,1)} %exit_rest.1), calls=%async_computation.3 | async-start | bytes 2621440 | tf_op jit(solution)/shard_map/all_to_all | solution.py:552
  114.9 3.2 %copy-start.1 = (bf16[32,16,1280]{2,1,0:T(8,128)(2,1)S(1)}, bf16[32,16,1280]{2,1,0:T(8,128)(2,1)}, u32[]{:S(2)}) copy-start(bf16[32,16,1280]{2,1,0:T(8,128)(2,1)} %exit_rest.1) | copy-start | bytes 3932164
  116.4 42.4 %collective-permute-start.12 = (bf16[32,16,512]{2,1,0:T(8,128)(2,1)S(1)}, bf16[32,16,512]{2,1,0:T(8,128)(2,1)S(1)}, u32[]{:S(2)}, u32[]{:S(2)}) collective-permute-start(bf16[32,16,512]{2,1,0:T(8,128)(2,1)S(1)} %slice.101), channel_id=1, source_target_pairs={{0,1},{1,2},{2,3},{3,0},{4,5},{5,6},{6,7},{7,4},{8,9},{9,10},{10,1... | collective-permute-start | bytes 1572872 | tf_op jit(solution)/shard_map/ppermute | solution.py:37
  119.0 39.8 %collective-permute-start.13 = (bf16[32,16,512]{2,1,0:T(8,128)(2,1)}, bf16[32,16,512]{2,1,0:T(8,128)(2,1)S(1)}, u32[]{:S(2)}, u32[]{:S(2)}) collective-permute-start(bf16[32,16,512]{2,1,0:T(8,128)(2,1)} %get-tuple-element.83), channel_id=1, source_target_pairs={{0,2},{1,3},{2,0},{3,1},{4,6},{5,7},{6,4},{7,5},{8,10},{9,11},{10,... | collective-permute-start | bytes 1572872 | tf_op jit(solution)/shard_map/ppermute | solution.py:37
  119.1 39.7 %collective-permute-start.14 = (bf16[32,16,512]{2,1,0:T(8,128)(2,1)S(1)}, bf16[32,16,512]{2,1,0:T(8,128)(2,1)S(1)}, u32[]{:S(2)}, u32[]{:S(2)}) collective-permute-start(bf16[32,16,512]{2,1,0:T(8,128)(2,1)S(1)} %get-tuple-element.82), channel_id=1, source_target_pairs={{0,3},{1,0},{2,1},{3,2},{4,7},{5,4},{6,5},{7,6},{8,11},{9,8},{10,9... | collective-permute-start | bytes 1572872 | tf_op jit(solution)/shard_map/ppermute | solution.py:37
  156.2 8.4 %collective-permute-start.9 = (bf16[16,8192]{1,0:T(8,128)(2,1)}, bf16[16,8192]{1,0:T(8,128)(2,1)S(1)}, u32[]{:S(2)}, u32[]{:S(2)}) collective-permute-start(bf16[16,8192]{1,0:T(8,128)(2,1)} %get-tuple-element.68), channel_id=1, source_target_pairs={{0,1},{1,2},{2,3},{3,0},{4,5},{5,6},{6,7},{7,4},{8,9},{9,10},{10,1... | collective-permute-start | bytes 786440 | tf_op jit(solution)/shard_map/ppermute | solution.py:37
  158.1 12.4 %collective-permute-start.10 = (bf16[16,8192]{1,0:T(8,128)(2,1)}, bf16[16,8192]{1,0:T(8,128)(2,1)S(1)}, u32[]{:S(2)}, u32[]{:S(2)}) collective-permute-start(bf16[16,8192]{1,0:T(8,128)(2,1)} %get-tuple-element.69), channel_id=1, source_target_pairs={{0,2},{1,3},{2,0},{3,1},{4,6},{5,7},{6,4},{7,5},{8,10},{9,11},{10,... | collective-permute-start | bytes 786440 | tf_op jit(solution)/shard_map/ppermute | solution.py:37
  158.8 12.4 %collective-permute-start.11 = (bf16[16,8192]{1,0:T(8,128)(2,1)}, bf16[16,8192]{1,0:T(8,128)(2,1)S(1)}, u32[]{:S(2)}, u32[]{:S(2)}) collective-permute-start(bf16[16,8192]{1,0:T(8,128)(2,1)} %get-tuple-element.70), channel_id=1, source_target_pairs={{0,3},{1,0},{2,1},{3,2},{4,7},{5,4},{6,5},{7,6},{8,11},{9,8},{10,9... | collective-permute-start | bytes 786440 | tf_op jit(solution)/shard_map/ppermute | solution.py:37
  159.9 11.3 %copy-start.7 = (bf16[16,8192]{1,0:T(8,128)(2,1)S(1)}, bf16[16,8192]{1,0:T(8,128)(2,1)}, u32[]{:S(2)}) copy-start(bf16[16,8192]{1,0:T(8,128)(2,1)} %get-tuple-element.71) | copy-start | bytes 786436
  164.6 6.7 %copy-start.2 = (bf16[2,32,8192]{2,1,0:T(8,128)(2,1)S(1)}, bf16[2,32,8192]{2,1,0:T(8,128)(2,1)}, u32[]{:S(2)}) copy-start(bf16[2,32,8192]{2,1,0:T(8,128)(2,1)} %param.9) | copy-start | bytes 3145732

commit v15 on v13

--- a/solution.py
+++ b/solution.py
@@ -18,7 +18,7 @@
 anywhere = pl.BlockSpec(memory_space=pl.ANY)
 scalars = pl.BlockSpec(memory_space=pltpu.SMEM)
 CHAINS = 4
-BATCH = 4
+BATCH = 8
 
 
 def dft_tables(width):
@@ -560,11 +560,12 @@
     rows = 2 * own
     blocks_each = width // block_size
 
-    def slices_for(j):
+    source, cuts = volume, {}
+    for j in list(range(1, n_pos)) + [0]:
         start = (pos + j) % n_pos * own
-        return lax.dynamic_slice_in_dim(volume, start, own, 1).reshape(rows, width)
-
-    vol_pieces = rotate_pos([slices_for(j) for j in range(n_pos)], 1)
+        cuts[j] = lax.dynamic_slice_in_dim(source, start, own, 1).reshape(rows, width)
+        source, cuts[j] = lax.optimization_barrier((source, cuts[j]))
+    vol_pieces = rotate_pos([cuts[j] for j in range(n_pos)], 1)
     vol_pieces, amplitudes = lax.optimization_barrier((vol_pieces, amplitudes))
     amp_pieces = rotate_pos(
         [

time: 173 us -> 175 us (1.012)
  waiting for transfers between devices: 72.2 us -> 61.8 us
  local copies, waits for them, and re-layouts: 12.2 us -> 20.4 us
  other arithmetic: 3.67 us -> 5.66 us
  Pallas kernels: 51.4 us -> 53.3 us
    ppermute x15, waiting for transfers between devices: 18.4 us -> 12.4 us  [rotate_pos(): lax.ppermute(pieces[j], 'pos', [(i, (i + sign * j) % count) for i in rang...]
    all_to_all x4, waiting for transfers between devices: 53.8 us -> 49.4 us  [everyone(): return lax.all_to_all(chunk, ('ang', 'pos'), 0, 0, tiled=True)]
    reshape x1 -> x4, local copies, waits for them, and re-layouts: 1.35 us -> 5.19 us  [on_device(): lax.dynamic_slice_in_dim(source, start, own, 1).reshape(rows, width)]
    pallas_call x1, Pallas kernels: 10.6 us -> 12.6 us  [exit_rest(): pl.pallas_call(functools.partial(exit_rest_kernel, len(amps)), out_shape=...]
    unnamed x25 -> x23, local copies, waits for them, and re-layouts: 4.79 us -> 6.45 us
  transfers between devices with their start and end apart: 19 -> 19, of which waited for: 10 -> 9; matrix products, arithmetic and copies ran while one was open for 7% -> 12% of each run, Pallas kernels for 25% -> 26%
where the time goes in v15:
time: 175 us; the launch traced here: 174 us
  waiting for transfers between devices  61.8 us (35%)
  Pallas kernels  53.3 us (30%)
  starting transfers between devices  32.2 us (18%)
  local copies, waits for them, and re-layouts  20.4 us (12%)
  other arithmetic  5.66 us (3%)
    all_to_all x4, waiting for transfers between devices, everyone(): return lax.all_to_all(chunk, ('ang', 'pos'), 0, 0, tiled=True)  49.4 us
    all_to_all x4, starting transfers between devices, everyone(): return lax.all_to_all(chunk, ('ang', 'pos'), 0, 0, tiled=True)  19.2 us
    pallas_call x2, Pallas kernels, back_project(): pl.pallas_call(functools.partial(back_project_kernel, blocks, has_start,...  17.1 us
    pallas_call x2, Pallas kernels, project(): pl.pallas_call(functools.partial(project_kernel, blocks, pieces), out_sha...  13.7 us
    ppermute x15, starting transfers between devices, rotate_pos(): lax.ppermute(pieces[j], 'pos', [(i, (i + sign * j) % count) for i in rang...  13 us
    pallas_call x1, Pallas kernels, exit_rest(): pl.pallas_call(functools.partial(exit_rest_kernel, len(amps)), out_shape=...  12.6 us
    ppermute x15, waiting for transfers between devices, rotate_pos(): lax.ppermute(pieces[j], 'pos', [(i, (i + sign * j) % count) for i in rang...  12.4 us
    pallas_call x1, Pallas kernels, exit_first(): pl.pallas_call(functools.partial(exit_first_kernel, len(amps)), out_shape...  9.9 us
  transfers between devices with their start and end apart: 19, of which 9 were waited for; matrix products, arithmetic and copies ran while one was open for 12% of the time, Pallas kernels for 26%

profile of v15, /device:TPU:1, one launch (start us, length us, event | category | flops | bytes accessed | tf_op | source)
XLA Modules:
  0.0 174.4 jit_solution(2503078243188940900)
XLA Ops:
  0.6 0.0 copy-start.2
  0.7 0.0 copy-start
  0.7 1.8 %dynamic-slice_bitcast_fusion.7 = bf16[16,8192]{1,0:T(8,128)(2,1)} fusion(bf16[2,32,8192]{2,1,0:T(8,128)(2,1)} %param.9, s32[]{:T(128)S(6)} %select_n.303), kind=kLoop, calls=%fused_computation.26 | loop fusion | bytes 524292 | tf_op jit(solution)/shard_map/reshape | solution.py:566
  2.5 2.6 %collective-permute-start = (bf16[16,8192]{1,0:T(8,128)(2,1)}, bf16[16,8192]{1,0:T(8,128)(2,1)S(1)}, u32[]{:S(2)}, u32[]{:S(2)}) collective-permute-start(bf16[16,8192]{1,0:T(8,128)(2,1)} %dynamic-slice_bitcast_fusion.7), channel_id=1, source_target_pairs={{0,1},{1,2},{2,3},{3,0},{4,5},{5,6},{6,7},{7,4},{8,9},{9,10},{10,1... | collective-permute-start | bytes 786440 | tf_op jit(solution)/shard_map/ppermute | solution.py:37
  5.1 1.7 dynamic-slice_bitcast_fusion.6
  6.8 0.0 collective-permute-start.1
  6.8 1.7 dynamic-slice_bitcast_fusion.5
  8.4 0.4 collective-permute-start.2
  8.8 1.2 fusion.5
  10.0 0.3 copy.27
  10.3 0.2 reshape.194
  10.7 0.1 reshape.195.idx_ref
  10.8 0.0 collective-permute-done.refs_1_
  10.8 4.2 %collective-permute-done.1.refs_2_ = bf16[16,8192]{1,0:T(8,128)(2,1)S(1)} collective-permute-done((bf16[16,8192]{1,0:T(8,128)(2,1)}, bf16[16,8192]{1,0:T(8,128)(2,1)S(1)}, u32[]{:S(2)}, u32[]{:S(2)}) %collective-permute-start.1) | collective-permute-done | bytes 262176 | tf_op jit(solution)/shard_map/ppermute | solution.py:37
  15.0 1.9 %collective-permute-done.2.refs_3_ = bf16[16,8192]{1,0:T(8,128)(2,1)S(1)} collective-permute-done((bf16[16,8192]{1,0:T(8,128)(2,1)}, bf16[16,8192]{1,0:T(8,128)(2,1)S(1)}, u32[]{:S(2)}, u32[]{:S(2)}) %collective-permute-start.2) | collective-permute-done | bytes 262176 | tf_op jit(solution)/shard_map/ppermute | solution.py:37
  16.9 7.7 %project_early.1 = bf16[32,16,1280]{2,1,0:T(8,128)(2,1)} custom-call(s32[4096]{0:T(1024)S(1)} %reshape.195.idx_ref, bf16[32,64,256]{2,1,0:T(8,128)(2,1)S(1)} %copy-done, bf16[16,8192]{1,0:T(8,128)(2,1)S(1)} %dynamic-slice_bitcast_fusion.4.refs_0_, bf16[16,8192]{1,0:T(8,128)(2,1)S(1)} %collective-permute-done.refs_1_, ...), custom_call_target="tpu_custom_call" | custom-call | flops 10350000128 | bytes 900000 | tf_op jit(solution)/shard_map/project_early/pallas_call | solution.py:163
  24.7 0.0 copy-start.9
  24.7 0.0 copy-start.8
  24.7 6.6 %all-to-all-start = ((bf16[32,16,1280]{2,1,0:T(8,128)(2,1)}), bf16[32,16,1280]{2,1,0:T(8,128)(2,1)}, u32[]{:S(2)}, u32[]{:S(2)}) async-start(bf16[32,16,1280]{2,1,0:T(8,128)(2,1)} %project_early.1), calls=%async_computation | async-start | bytes 2621440 | tf_op jit(solution)/shard_map/all_to_all | solution.py:547
  31.3 0.1 copy.32
  31.4 0.1 pad_add_fusion.2
  31.5 1.7 collective-permute-start.5
  33.2 0.0 collective-permute-start.4
  33.3 0.5 collective-permute-start.3
  33.8 2.9 %dynamic-slice_bitcast_fusion = (bf16[4,256,256]{2,1,0:T(8,128)(2,1)}, bf16[4,256,256]{2,1,0:T(8,128)(2,1)}, bf16[4,256,256]{2,1,0:T(8,128)(2,1)}, bf16[4,256,256]{2,1,0:T(8,128)(2,1)}) fusion(bf16[4,4,256,256]{3,2,1,0:T(8,128)(2,1)} %param.13, s32[]{:T(128)S(6)} %select_n.316, s32[]{:T(128)S(6)} %select_n.314, s32[]{:T(128)S(6)} %select_n.312, s32[]{:T(128)S(6)} %select_n.310), kind=kLoop, calls=%fused_computation.11 | loop fusion | bytes 4194320 | tf_op jit(solution)/shard_map/jit(dynamic_index_in_dim)/squeeze | solution.py:572
  36.6 1.3 collective-permute-start.6
  37.9 0.0 collective-permute-start.7
  38.0 1.6 collective-permute-start.8
  39.6 0.6 pad_add_fusion.3.meta_ref
  40.2 5.9 %project_late.1 = bf16[32,16,768]{2,1,0:T(8,128)(2,1)} custom-call(s32[4096]{0:T(1024)S(1)} %reshape.195.idx_ref, bf16[32,64,256]{2,1,0:T(8,128)(2,1)S(1)} %copy-done, bf16[16,8192]{1,0:T(8,128)(2,1)S(1)} %dynamic-slice_bitcast_fusion.4.refs_0_, bf16[16,8192]{1,0:T(8,128)(2,1)S(1)} %collective-permute-done.refs_1_, ...), custom_call_target="tpu_custom_call" | custom-call | flops 8049999872 | bytes 700000 | tf_op jit(solution)/shard_map/project_late/pallas_call | solution.py:163
  46.1 16.5 %all-to-all-done.sino_ref.early_ref = bf16[32,16,1280]{2,1,0:T(8,128)(2,1)} async-done(((bf16[32,16,1280]{2,1,0:T(8,128)(2,1)}), bf16[32,16,1280]{2,1,0:T(8,128)(2,1)}, u32[]{:S(2)}, u32[]{:S(2)}) %all-to-all-start) | async-done | bytes 1310752 | tf_op jit(solution)/shard_map/all_to_all | solution.py:547
  62.6 4.4 %all-to-all-start.1 = ((bf16[32,16,768]{2,1,0:T(8,128)(2,1)}), bf16[32,16,768]{2,1,0:T(8,128)(2,1)S(1)}, u32[]{:S(2)}, u32[]{:S(2)}) async-start(bf16[32,16,768]{2,1,0:T(8,128)(2,1)} %project_late.1), calls=%async_computation.1 | async-start | bytes 1572864 | tf_op jit(solution)/shard_map/all_to_all | solution.py:547
  67.1 1.6 collective-permute-done.8.refs_1_
  68.7 9.9 %exit_first.1 = (f32[2,256,256]{2,1,0:T(8,128)}, bf16[32,16,768]{2,1,0:T(8,128)(2,1)}, f32[2,256,256]{2,1,0:T(8,128)}) custom-call(s32[4,5]{1,0:T(4,128)} %pad_add_fusion.3.meta_ref, bf16[2,256,256]{2,1,0:T(8,128)(2,1)} %probe_ref.3, bf16[512,512]{1,0:T(8,128)(2,1)} %constant.148.forward_ref, bf16[512,512]{1,0:T(8,128)(2,1)} %constant.151.inverse_ref, ...), custom_call_target="tpu_custom_call" | custom-call | flops 11500000256 | bytes 1000000 | tf_op jit(solution)/shard_map/exit_first/pallas_call | solution.py:482
  78.6 8.6 %all-to-all-done.1.late_ref = bf16[32,16,768]{2,1,0:T(8,128)(2,1)S(1)} async-done(((bf16[32,16,768]{2,1,0:T(8,128)(2,1)}), bf16[32,16,768]{2,1,0:T(8,128)(2,1)S(1)}, u32[]{:S(2)}, u32[]{:S(2)}) %all-to-all-start.1) | async-done | bytes 786464 | tf_op jit(solution)/shard_map/all_to_all | solution.py:547
  87.2 4.1 %all-to-all-start.2 = ((bf16[32,16,768]{2,1,0:T(8,128)(2,1)}), bf16[32,16,768]{2,1,0:T(8,128)(2,1)S(1)}, u32[]{:S(2)}, u32[]{:S(2)}) async-start(bf16[32,16,768]{2,1,0:T(8,128)(2,1)} %get-tuple-element.74), calls=%async_computation.2 | async-start | bytes 1572864 | tf_op jit(solution)/shard_map/all_to_all | solution.py:547
  91.3 12.6 %exit_rest.1 = bf16[32,16,1280]{2,1,0:T(8,128)(2,1)} custom-call(s32[4,5]{1,0:T(4,128)} %pad_add_fusion.3.meta_ref, bf16[2,256,256]{2,1,0:T(8,128)(2,1)} %probe_ref.3, bf16[512,512]{1,0:T(8,128)(2,1)} %constant.148.forward_ref, bf16[512,512]{1,0:T(8,128)(2,1)} %constant.151.inverse_ref, bf16[32,16,1280]{2,1,0:T(8,128)(2,1)} %all-to-all-done.sino_ref.early_ref, ...), custom_call_target="tpu_custom_call" | custom-call | flops 11500000256 | bytes 1000000 | tf_op jit(solution)/shard_map/exit_rest/pallas_call | solution.py:498
  103.9 7.5 %all-to-all-done.2.grad_ref = bf16[32,16,768]{2,1,0:T(8,128)(2,1)S(1)} async-done(((bf16[32,16,768]{2,1,0:T(8,128)(2,1)}), bf16[32,16,768]{2,1,0:T(8,128)(2,1)S(1)}, u32[]{:S(2)}, u32[]{:S(2)}) %all-to-all-start.2) | async-done | bytes 786464 | tf_op jit(solution)/shard_map/all_to_all | solution.py:547
  111.4 0.9 copy-done.4
  112.3 4.1 %all-to-all-start.3 = ((bf16[32,16,1280]{2,1,0:T(8,128)(2,1)}), bf16[32,16,1280]{2,1,0:T(8,128)(2,1)}, u32[]{:S(2)}, u32[]{:S(2)}) async-start(bf16[32,16,1280]{2,1,0:T(8,128)(2,1)} %exit_rest.1), calls=%async_computation.3 | async-start | bytes 2621440 | tf_op jit(solution)/shard_map/all_to_all | solution.py:547
  116.5 0.0 copy-start.1
  116.5 1.1 copy.22
  117.6 1.2 reshape.192
  119.0 0.7 reshape.193.idx_ref
  119.7 0.9 slice.101
  120.6 1.7 collective-permute-start.12
  122.3 1.1 fusion.9
  123.4 0.0 collective-permute-start.13
  123.4 0.5 collective-permute-start.14
  123.9 7.2 %back_first.1.refs_0_ = f32[512,8,128]{2,1,0:T(8,128)} custom-call(s32[4096]{0:T(1024)} %reshape.193.idx_ref, bf16[32,64,256]{2,1,0:T(8,128)(2,1)} %radon_ref.7, bf16[32,16,768]{2,1,0:T(8,128)(2,1)} %copy-done.4), custom_call_target="tpu_custom_call" | custom-call | flops 8049999872 | bytes 700000 | tf_op jit(solution)/shard_map/back_first/pallas_call | solution.py:286
  131.1 16.7 %all-to-all-done.3.grad_ref = bf16[32,16,1280]{2,1,0:T(8,128)(2,1)} async-done(((bf16[32,16,1280]{2,1,0:T(8,128)(2,1)}), bf16[32,16,1280]{2,1,0:T(8,128)(2,1)}, u32[]{:S(2)}, u32[]{:S(2)}) %all-to-all-start.3) | async-done | bytes 1310752 | tf_op jit(solution)/shard_map/all_to_all | solution.py:547
  147.8 9.9 %back_rest.1 = (bf16[16,8192]{1,0:T(8,128)(2,1)}, bf16[16,8192]{1,0:T(8,128)(2,1)}, bf16[16,8192]{1,0:T(8,128)(2,1)}, bf16[16,8192]{1,0:T(8,128)(2,1)}) custom-call(s32[4096]{0:T(1024)} %reshape.193.idx_ref, bf16[32,64,256]{2,1,0:T(8,128)(2,1)} %radon_ref.7, bf16[32,16,1280]{2,1,0:T(8,128)(2,1)} %all-to-all-done.3.grad_ref, f32[512,8,128]{2,1,0:T(8,128)} %back_first.1.refs_0_), custom_call_target="tpu_custom_call" | custom-call | flops 10350000128 | bytes 900000 | tf_op jit(solution)/shard_map/back_rest/pallas_call | solution.py:286
  157.7 1.9 %collective-permute-start.9 = (bf16[16,8192]{1,0:T(8,128)(2,1)}, bf16[16,8192]{1,0:T(8,128)(2,1)S(1)}, u32[]{:S(2)}, u32[]{:S(2)}) collective-permute-start(bf16[16,8192]{1,0:T(8,128)(2,1)} %get-tuple-element.82), channel_id=1, source_target_pairs={{0,1},{1,2},{2,3},{3,0},{4,5},{5,6},{6,7},{7,4},{8,9},{9,10},{10,1... | collective-permute-start | bytes 786440 | tf_op jit(solution)/shard_map/ppermute | solution.py:37
  159.7 0.7 collective-permute-start.10
  160.3 0.0 collective-permute-start.11
  160.3 0.0 copy-start.6
  160.3 0.8 copy-done.6
  161.1 1.7 select_bitcast_fusion.3
  163.0 0.3 maximum_convert_fusion
  163.4 4.7 %copy.37 = f32[2,256,4,512]{3,2,1,0:T(4,128)} copy(f32[2,256,4,512]{3,1,0,2:T(8,128)S(1)} %maximum_convert_fusion) | data formatting | bytes 8388608
  168.1 4.0 %collective-permute-done.10 = bf16[16,8192]{1,0:T(8,128)(2,1)S(1)} collective-permute-done((bf16[16,8192]{1,0:T(8,128)(2,1)}, bf16[16,8192]{1,0:T(8,128)(2,1)S(1)}, u32[]{:S(2)}, u32[]{:S(2)}) %collective-permute-start.10) | collective-permute-done | bytes 262176 | tf_op jit(solution)/shard_map/ppermute | solution.py:37
  172.1 0.6 collective-permute-done.11
  172.7 0.1 select_bitcast_fusion.7
  172.8 1.6 multiply_add_fusion
  (47 shorter events, 0.5 us)
Async XLA Ops:
  0.6 9.9 %copy-start.2 = (bf16[2,32,8192]{2,1,0:T(8,128)(2,1)S(1)}, bf16[2,32,8192]{2,1,0:T(8,128)(2,1)}, u32[]{:S(2)}) copy-start(bf16[2,32,8192]{2,1,0:T(8,128)(2,1)} %param.9) | copy-start | bytes 3145732
  0.7 16.3 %copy-start = (bf16[32,64,256]{2,1,0:T(8,128)(2,1)S(1)}, bf16[32,64,256]{2,1,0:T(8,128)(2,1)}, u32[]{:S(2)}) copy-start(bf16[32,64,256]{2,1,0:T(8,128)(2,1)} %radon_ref.7) | copy-start | bytes 3145732
  2.5 8.3 %collective-permute-start = (bf16[16,8192]{1,0:T(8,128)(2,1)}, bf16[16,8192]{1,0:T(8,128)(2,1)S(1)}, u32[]{:S(2)}, u32[]{:S(2)}) collective-permute-start(bf16[16,8192]{1,0:T(8,128)(2,1)} %dynamic-slice_bitcast_fusion.7), channel_id=1, source_target_pairs={{0,1},{1,2},{2,3},{3,0},{4,5},{5,6},{6,7},{7,4},{8,9},{9,10},{10,1... | collective-permute-start | bytes 786440 | tf_op jit(solution)/shard_map/ppermute | solution.py:37
  6.8 8.3 %collective-permute-start.1 = (bf16[16,8192]{1,0:T(8,128)(2,1)}, bf16[16,8192]{1,0:T(8,128)(2,1)S(1)}, u32[]{:S(2)}, u32[]{:S(2)}) collective-permute-start(bf16[16,8192]{1,0:T(8,128)(2,1)} %dynamic-slice_bitcast_fusion.6), channel_id=1, source_target_pairs={{0,2},{1,3},{2,0},{3,1},{4,6},{5,7},{6,4},{7,5},{8,10},{9,11},{10,... | collective-permute-start | bytes 786440 | tf_op jit(solution)/shard_map/ppermute | solution.py:37
  8.4 8.5 %collective-permute-start.2 = (bf16[16,8192]{1,0:T(8,128)(2,1)}, bf16[16,8192]{1,0:T(8,128)(2,1)S(1)}, u32[]{:S(2)}, u32[]{:S(2)}) collective-permute-start(bf16[16,8192]{1,0:T(8,128)(2,1)} %dynamic-slice_bitcast_fusion.5), channel_id=1, source_target_pairs={{0,3},{1,0},{2,1},{3,2},{4,7},{5,4},{6,5},{7,6},{8,11},{9,8},{10,9... | collective-permute-start | bytes 786440 | tf_op jit(solution)/shard_map/ppermute | solution.py:37
  24.7 6.7 %copy-start.9 = (s32[4,1]{0,1:T(1,128)S(1)}, s32[4,1]{0,1:T(1,128)}, u32[]{:S(2)}) copy-start(s32[4,1]{0,1:T(1,128)} %param.15) | copy-start | bytes 52
  24.7 6.8 %copy-start.8 = (s32[4,4]{1,0:T(4,128)S(1)}, s32[4,4]{1,0:T(4,128)}, u32[]{:S(2)}) copy-start(s32[4,4]{1,0:T(4,128)} %param.14) | copy-start | bytes 196
  24.7 38.0 %all-to-all-start = ((bf16[32,16,1280]{2,1,0:T(8,128)(2,1)}), bf16[32,16,1280]{2,1,0:T(8,128)(2,1)}, u32[]{:S(2)}, u32[]{:S(2)}) async-start(bf16[32,16,1280]{2,1,0:T(8,128)(2,1)} %project_early.1), calls=%async_computation | async-start | bytes 2621440 | tf_op jit(solution)/shard_map/all_to_all | solution.py:547
  31.5 6.5 %collective-permute-start.5 = (s32[1,5]{1,0:T(1,128)S(1)}, s32[1,5]{1,0:T(1,128)S(1)}, u32[]{:S(2)}, u32[]{:S(2)}) collective-permute-start(s32[1,5]{1,0:T(1,128)S(1)} %get-tuple-element.117), channel_id=1, source_target_pairs={{0,1},{1,2},{2,3},{3,0},{4,5},{5,6},{6,7},{7,4},{8,9},{9,10},{10,1... | collective-permute-start | bytes 68 | tf_op jit(solution)/shard_map/ppermute | solution.py:37
  33.2 6.4 %collective-permute-start.4 = (s32[1,5]{1,0:T(1,128)S(1)}, s32[1,5]{1,0:T(1,128)S(1)}, u32[]{:S(2)}, u32[]{:S(2)}) collective-permute-start(s32[1,5]{1,0:T(1,128)S(1)} %get-tuple-element.118), channel_id=1, source_target_pairs={{0,2},{1,3},{2,0},{3,1},{4,6},{5,7},{6,4},{7,5},{8,10},{9,11},{10,... | collective-permute-start | bytes 68 | tf_op jit(solution)/shard_map/ppermute | solution.py:37
  33.3 6.3 %collective-permute-start.3 = (s32[1,5]{1,0:T(1,128)S(1)}, s32[1,5]{1,0:T(1,128)S(1)}, u32[]{:S(2)}, u32[]{:S(2)}) collective-permute-start(s32[1,5]{1,0:T(1,128)S(1)} %get-tuple-element.119), channel_id=1, source_target_pairs={{0,3},{1,0},{2,1},{3,2},{4,7},{5,4},{6,5},{7,6},{8,11},{9,8},{10,9... | collective-permute-start | bytes 68 | tf_op jit(solution)/shard_map/ppermute | solution.py:37
  36.6 30.4 %collective-permute-start.6 = (bf16[4,256,256]{2,1,0:T(8,128)(2,1)}, bf16[4,256,256]{2,1,0:T(8,128)(2,1)}, u32[]{:S(2)}, u32[]{:S(2)}) collective-permute-start(bf16[4,256,256]{2,1,0:T(8,128)(2,1)} %get-tuple-element.94), channel_id=1, source_target_pairs={{0,3},{1,0},{2,1},{3,2},{4,7},{5,4},{6,5},{7,6},{8,11},{9,8},{10,9... | collective-permute-start | bytes 1572872 | tf_op jit(solution)/shard_map/ppermute | solution.py:37
  37.9 29.1 %collective-permute-start.7 = (bf16[4,256,256]{2,1,0:T(8,128)(2,1)}, bf16[4,256,256]{2,1,0:T(8,128)(2,1)}, u32[]{:S(2)}, u32[]{:S(2)}) collective-permute-start(bf16[4,256,256]{2,1,0:T(8,128)(2,1)} %get-tuple-element.93), channel_id=1, source_target_pairs={{0,2},{1,3},{2,0},{3,1},{4,6},{5,7},{6,4},{7,5},{8,10},{9,11},{10,... | collective-permute-start | bytes 1572872 | tf_op jit(solution)/shard_map/ppermute | solution.py:37
  38.0 30.7 %collective-permute-start.8 = (bf16[4,256,256]{2,1,0:T(8,128)(2,1)}, bf16[4,256,256]{2,1,0:T(8,128)(2,1)}, u32[]{:S(2)}, u32[]{:S(2)}) collective-permute-start(bf16[4,256,256]{2,1,0:T(8,128)(2,1)} %get-tuple-element.92), channel_id=1, source_target_pairs={{0,1},{1,2},{2,3},{3,0},{4,5},{5,6},{6,7},{7,4},{8,9},{9,10},{10,1... | collective-permute-start | bytes 1572872 | tf_op jit(solution)/shard_map/ppermute | solution.py:37
  62.6 24.5 %all-to-all-start.1 = ((bf16[32,16,768]{2,1,0:T(8,128)(2,1)}), bf16[32,16,768]{2,1,0:T(8,128)(2,1)S(1)}, u32[]{:S(2)}, u32[]{:S(2)}) async-start(bf16[32,16,768]{2,1,0:T(8,128)(2,1)} %project_late.1), calls=%async_computation.1 | async-start | bytes 1572864 | tf_op jit(solution)/shard_map/all_to_all | solution.py:547
  87.2 4.1 %copy-start.5 = (bf16[32,16,768]{2,1,0:T(8,128)(2,1)}, bf16[32,16,768]{2,1,0:T(8,128)(2,1)S(1)}, u32[]{:S(2)}) copy-start(bf16[32,16,768]{2,1,0:T(8,128)(2,1)S(1)} %all-to-all-done.1.late_ref) | copy-start | bytes 2359300
  87.2 24.2 %all-to-all-start.2 = ((bf16[32,16,768]{2,1,0:T(8,128)(2,1)}), bf16[32,16,768]{2,1,0:T(8,128)(2,1)S(1)}, u32[]{:S(2)}, u32[]{:S(2)}) async-start(bf16[32,16,768]{2,1,0:T(8,128)(2,1)} %get-tuple-element.74), calls=%async_computation.2 | async-start | bytes 1572864 | tf_op jit(solution)/shard_map/all_to_all | solution.py:547
  103.9 15.8 %copy-start.3 = (bf16[32,16,768]{2,1,0:T(8,128)(2,1)S(1)}, bf16[32,16,768]{2,1,0:T(8,128)(2,1)}, u32[]{:S(2)}) copy-start(bf16[32,16,768]{2,1,0:T(8,128)(2,1)} %get-tuple-element.74) | copy-start | bytes 2359300
  111.4 0.9 copy-start.4
  112.3 35.5 %all-to-all-start.3 = ((bf16[32,16,1280]{2,1,0:T(8,128)(2,1)}), bf16[32,16,1280]{2,1,0:T(8,128)(2,1)}, u32[]{:S(2)}, u32[]{:S(2)}) async-start(bf16[32,16,1280]{2,1,0:T(8,128)(2,1)} %exit_rest.1), calls=%async_computation.3 | async-start | bytes 2621440 | tf_op jit(solution)/shard_map/all_to_all | solution.py:547
  116.5 5.8 %copy-start.1 = (bf16[32,16,1280]{2,1,0:T(8,128)(2,1)S(1)}, bf16[32,16,1280]{2,1,0:T(8,128)(2,1)}, u32[]{:S(2)}) copy-start(bf16[32,16,1280]{2,1,0:T(8,128)(2,1)} %exit_rest.1) | copy-start | bytes 3932164
  120.6 39.8 %collective-permute-start.12 = (bf16[32,16,512]{2,1,0:T(8,128)(2,1)}, bf16[32,16,512]{2,1,0:T(8,128)(2,1)S(1)}, u32[]{:S(2)}, u32[]{:S(2)}) collective-permute-start(bf16[32,16,512]{2,1,0:T(8,128)(2,1)} %slice.101), channel_id=1, source_target_pairs={{0,1},{1,2},{2,3},{3,0},{4,5},{5,6},{6,7},{7,4},{8,9},{9,10},{10,1... | collective-permute-start | bytes 1572872 | tf_op jit(solution)/shard_map/ppermute | solution.py:37
  123.4 36.9 %collective-permute-start.13 = (bf16[32,16,512]{2,1,0:T(8,128)(2,1)}, bf16[32,16,512]{2,1,0:T(8,128)(2,1)S(1)}, u32[]{:S(2)}, u32[]{:S(2)}) collective-permute-start(bf16[32,16,512]{2,1,0:T(8,128)(2,1)} %get-tuple-element.97), channel_id=1, source_target_pairs={{0,2},{1,3},{2,0},{3,1},{4,6},{5,7},{6,4},{7,5},{8,10},{9,11},{10,... | collective-permute-start | bytes 1572872 | tf_op jit(solution)/shard_map/ppermute | solution.py:37
  123.4 37.7 %collective-permute-start.14 = (bf16[32,16,512]{2,1,0:T(8,128)(2,1)}, bf16[32,16,512]{2,1,0:T(8,128)(2,1)}, u32[]{:S(2)}, u32[]{:S(2)}) collective-permute-start(bf16[32,16,512]{2,1,0:T(8,128)(2,1)} %get-tuple-element.96), channel_id=1, source_target_pairs={{0,3},{1,0},{2,1},{3,2},{4,7},{5,4},{6,5},{7,6},{8,11},{9,8},{10,9... | collective-permute-start | bytes 1572872 | tf_op jit(solution)/shard_map/ppermute | solution.py:37
  157.7 10.3 %collective-permute-start.9 = (bf16[16,8192]{1,0:T(8,128)(2,1)}, bf16[16,8192]{1,0:T(8,128)(2,1)S(1)}, u32[]{:S(2)}, u32[]{:S(2)}) collective-permute-start(bf16[16,8192]{1,0:T(8,128)(2,1)} %get-tuple-element.82), channel_id=1, source_target_pairs={{0,1},{1,2},{2,3},{3,0},{4,5},{5,6},{6,7},{7,4},{8,9},{9,10},{10,1... | collective-permute-start | bytes 786440 | tf_op jit(solution)/shard_map/ppermute | solution.py:37
  159.7 12.4 %collective-permute-start.10 = (bf16[16,8192]{1,0:T(8,128)(2,1)}, bf16[16,8192]{1,0:T(8,128)(2,1)S(1)}, u32[]{:S(2)}, u32[]{:S(2)}) collective-permute-start(bf16[16,8192]{1,0:T(8,128)(2,1)} %get-tuple-element.83), channel_id=1, source_target_pairs={{0,2},{1,3},{2,0},{3,1},{4,6},{5,7},{6,4},{7,5},{8,10},{9,11},{10,... | collective-permute-start | bytes 786440 | tf_op jit(solution)/shard_map/ppermute | solution.py:37
  160.3 12.4 %collective-permute-start.11 = (bf16[16,8192]{1,0:T(8,128)(2,1)}, bf16[16,8192]{1,0:T(8,128)(2,1)S(1)}, u32[]{:S(2)}, u32[]{:S(2)}) collective-permute-start(bf16[16,8192]{1,0:T(8,128)(2,1)} %get-tuple-element.84), channel_id=1, source_target_pairs={{0,3},{1,0},{2,1},{3,2},{4,7},{5,4},{6,5},{7,6},{8,11},{9,8},{10,9... | collective-permute-start | bytes 786440 | tf_op jit(solution)/shard_map/ppermute | solution.py:37
  160.3 0.8 copy-start.6
  163.4 9.3 %copy-start.7 = (bf16[16,8192]{1,0:T(8,128)(2,1)S(1)}, bf16[16,8192]{1,0:T(8,128)(2,1)}, u32[]{:S(2)}) copy-start(bf16[16,8192]{1,0:T(8,128)(2,1)} %get-tuple-element.85) | copy-start | bytes 786436

commit v16 on v13

--- a/solution.py
+++ b/solution.py
@@ -29,6 +29,11 @@
     forward = jnp.block([[cosine, -sine_neg], [sine_neg, cosine]])
     inverse = jnp.block([[cosine, sine_neg], [-sine_neg, cosine]])
     return (forward, inverse)
+
+
+def send_pos(piece, step):
+    count = lax.axis_size("pos")
+    return lax.ppermute(piece, "pos", [(i, (i + step) % count) for i in range(count)])
 
 
 def rotate_pos(pieces, sign):
@@ -179,6 +184,9 @@
 def back_project_kernel(blocks, has_start, outs, idx_ref, radon_ref, grad_ref, *refs):
     start_ref, refs = (refs[0], refs[1:]) if has_start else (None, refs)
     out_refs, refs = refs[:outs], refs[outs:]
+    if has_start:
+        *refs, out_sems = refs
+        *refs, sums_ref = refs
     acc_refs, (w_ref, *contrib_refs) = refs[:CHAINS], refs[CHAINS:]
     if has_start:
         contrib_refs, start_sem = contrib_refs[:-1], contrib_refs[-1]
@@ -261,6 +269,7 @@
 
     else:
         per_piece = out_refs[0].shape[1] // LANES
+        leaving = []
         for k, out_ref in enumerate(out_refs):
 
             @pl.loop(0, per_piece, unroll=16)
@@ -270,7 +279,12 @@
                 odd = total(2 * (k * per_piece + t) + 1)
                 real = jnp.where(low, even, swap_halves(odd))
                 imag = jnp.where(low, swap_halves(even), odd)
-                out_ref[:, lanes] = jnp.concatenate([real, imag], axis=0).astype(out_ref.dtype)
+                sums_ref[k, :, lanes] = jnp.concatenate([real, imag], axis=0).astype(out_ref.dtype)
+
+            leaving.append(pltpu.make_async_copy(sums_ref.at[k], out_ref, out_sems.at[k]))
+            leaving[k].start()
+        for copy in leaving:
+            copy.wait()
 
 
 def back_project(idx, radon_tiles, grads, blocks, start, pieces, piece_width, name):
@@ -287,11 +301,13 @@
         functools.partial(back_project_kernel, blocks, has_start, len(out_shape)),
         out_shape=out_shape,
         in_specs=[scalars] + [everywhere] * 2 + [pl.BlockSpec(memory_space=pl.ANY)] * has_start,
-        out_specs=[everywhere] * len(out_shape),
+        out_specs=[anywhere if has_start else everywhere] * len(out_shape),
         scratch_shapes=[pltpu.VMEM((coef_blocks, GROUP, LANES), jnp.float32)] * CHAINS
         + [pltpu.VMEM((2 * CHAINS, 2 * block, 2 * span), jnp.bfloat16)]
         + [pltpu.VMEM((CHAINS, rows, 2 * span), jnp.float32)] * 2
-        + [pltpu.SemaphoreType.DMA] * has_start,
+        + [pltpu.SemaphoreType.DMA] * has_start
+        + [pltpu.VMEM((pieces, ROWS, piece_width), jnp.bfloat16)] * has_start
+        + [pltpu.SemaphoreType.DMA((pieces,))] * has_start,
         compiler_params=pltpu.CompilerParams(vmem_limit_bytes=60 * MEBI),
         cost_estimate=guess(4 + len(blocks) // 4),
         name=name,
@@ -620,17 +636,20 @@
         meta, probe_field, tables, got_early, got_late, partial, spill, amp_pieces[half:]
     )
     back_first = everyone(from_groups(first_sent, own))
-    back_first, rest_sent = lax.optimization_barrier((back_first, rest_grad))
-    back_rest = everyone(from_groups(rest_sent, own))
-    first_sum = back_project(
-        block_idx, radon_tiles, pad_rows(back_first, own), first_blocks, None, n_pos, width, "back_first"
-    )[0]
     wrapped = rest_grad.shape[2] - probe_width
     tile_pieces = [jnp.concatenate([rest_grad[:, :, wrapped:], first_grad[:, :, : tile_width - probe_width]], axis=2)]
     for j in range(1, n_pos):
         source, begin = (first_grad, j * tile_width - probe_width) if j < half else (rest_grad, (j - half) * tile_width)
         tile_pieces.append(source[:, :, begin : begin + tile_width])
-    tile_pieces = rotate_pos(tile_pieces, 1)
+    tile_pieces = [tile_pieces[0]] + [send_pos(tile_pieces[j], j) for j in range(1, half)] + tile_pieces[half:]
+    back_first, rest_sent, tile_pieces[1:half] = lax.optimization_barrier(
+        (back_first, rest_grad, tile_pieces[1:half])
+    )
+    back_rest = everyone(from_groups(rest_sent, own))
+    first_sum = back_project(
+        block_idx, radon_tiles, pad_rows(back_first, own), first_blocks, None, n_pos, width, "back_first"
+    )[0]
+    tile_pieces = tile_pieces[:half] + [send_pos(tile_pieces[j], j) for j in range(half, n_pos)]
     obj_pieces = back_project(
         block_idx, radon_tiles, pad_rows(back_rest, own), rest_blocks, first_sum, n_pos, width, "back_rest"
     )

time: 173 us -> 175 us (1.012)
  waiting for transfers between devices: 72.2 us -> 67.4 us
  local copies, waits for them, and re-layouts: 12.2 us -> 16.3 us
    all_to_all x4, waiting for transfers between devices: 53.8 us -> 49.8 us  [everyone(): return lax.all_to_all(chunk, ('ang', 'pos'), 0, 0, tiled=True)]
    ppermute x0 -> x3, starting transfers between devices: none -> 3.71 us  [send_pos(): lax.ppermute(piece, 'pos', [(i, (i + step) % count) for i in range(count)])]
    ppermute x15 -> x12, starting transfers between devices: 13.1 us -> 10.9 us  [rotate_pos(): lax.ppermute(pieces[j], 'pos', [(i, (i + sign * j) % count) for i in rang...]
    unnamed x25, local copies, waits for them, and re-layouts: 4.79 us -> 6.74 us
    ppermute x15 -> x12, waiting for transfers between devices: 18.4 us -> 17.3 us  [rotate_pos(): lax.ppermute(pieces[j], 'pos', [(i, (i + sign * j) % count) for i in rang...]
  transfers between devices with their start and end apart: 19 -> 19, of which waited for: 10 -> 11; matrix products, arithmetic and copies ran while one was open for 7% -> 9% of each run, Pallas kernels for 25% -> 25%
where the time goes in v16:
time: 175 us; the launch traced here: 174 us
  waiting for transfers between devices  67.4 us (39%)
  Pallas kernels  51.2 us (29%)
  starting transfers between devices  33.7 us (19%)
  local copies, waits for them, and re-layouts  16.3 us (9%)
  other arithmetic  4.73 us (3%)
    all_to_all x4, waiting for transfers between devices, everyone(): return lax.all_to_all(chunk, ('ang', 'pos'), 0, 0, tiled=True)  49.8 us
    all_to_all x4, starting transfers between devices, everyone(): return lax.all_to_all(chunk, ('ang', 'pos'), 0, 0, tiled=True)  19.1 us
    ppermute x12, waiting for transfers between devices, rotate_pos(): lax.ppermute(pieces[j], 'pos', [(i, (i + sign * j) % count) for i in rang...  17.3 us
    pallas_call x2, Pallas kernels, back_project(): pl.pallas_call(functools.partial(back_project_kernel, blocks, has_start,...  16.9 us
    pallas_call x2, Pallas kernels, project(): pl.pallas_call(functools.partial(project_kernel, blocks, pieces), out_sha...  13.8 us
    ppermute x12, starting transfers between devices, rotate_pos(): lax.ppermute(pieces[j], 'pos', [(i, (i + sign * j) % count) for i in rang...  10.9 us
    pallas_call x1, Pallas kernels, exit_rest(): pl.pallas_call(functools.partial(exit_rest_kernel, len(amps)), out_shape=...  10.6 us
    pallas_call x1, Pallas kernels, exit_first(): pl.pallas_call(functools.partial(exit_first_kernel, len(amps)), out_shape...  9.9 us
  transfers between devices with their start and end apart: 19, of which 11 were waited for; matrix products, arithmetic and copies ran while one was open for 9% of the time, Pallas kernels for 25%

profile of v16, /device:TPU:1, one launch (start us, length us, event | category | flops | bytes accessed | tf_op | source)
XLA Modules:
  0.0 174.4 jit_solution(17833197621641439450)
XLA Ops:
  0.7 0.0 copy-start
  0.7 1.3 dynamic-slice_bitcast_fusion.4
  2.1 2.7 %collective-permute-start = (bf16[16,8192]{1,0:T(8,128)(2,1)S(1)}, bf16[16,8192]{1,0:T(8,128)(2,1)S(1)}, u32[]{:S(2)}, u32[]{:S(2)}) collective-permute-start(bf16[16,8192]{1,0:T(8,128)(2,1)S(1)} %get-tuple-element.91), channel_id=1, source_target_pairs={{0,1},{1,2},{2,3},{3,0},{4,5},{5,6},{6,7},{7,4},{8,9},{9,10},{10,1... | collective-permute-start | bytes 786440 | tf_op jit(solution)/shard_map/ppermute | solution.py:42
  4.7 0.0 collective-permute-start.1
  4.7 0.5 collective-permute-start.2
  5.2 0.3 fusion.5
  5.5 0.3 copy.27
  5.8 0.2 reshape.194
  6.2 0.1 reshape.195.idx_ref
  6.3 4.0 %collective-permute-done.refs_1_ = bf16[16,8192]{1,0:T(8,128)(2,1)S(1)} collective-permute-done((bf16[16,8192]{1,0:T(8,128)(2,1)S(1)}, bf16[16,8192]{1,0:T(8,128)(2,1)S(1)}, u32[]{:S(2)}, u32[]{:S(2)}) %collective-permute-start) | collective-permute-done | bytes 262176 | tf_op jit(solution)/shard_map/ppermute | solution.py:42
  10.2 5.6 %collective-permute-done.1.refs_2_ = bf16[16,8192]{1,0:T(8,128)(2,1)S(1)} collective-permute-done((bf16[16,8192]{1,0:T(8,128)(2,1)S(1)}, bf16[16,8192]{1,0:T(8,128)(2,1)S(1)}, u32[]{:S(2)}, u32[]{:S(2)}) %collective-permute-start.1) | collective-permute-done | bytes 262176 | tf_op jit(solution)/shard_map/ppermute | solution.py:42
  15.8 0.5 collective-permute-done.2.refs_3_
  16.3 7.6 %project_early.1 = bf16[32,16,1280]{2,1,0:T(8,128)(2,1)} custom-call(s32[4096]{0:T(1024)S(1)} %reshape.195.idx_ref, bf16[32,64,256]{2,1,0:T(8,128)(2,1)S(1)} %copy-done, bf16[16,8192]{1,0:T(8,128)(2,1)S(1)} %get-tuple-element.50.refs_0_, bf16[16,8192]{1,0:T(8,128)(2,1)S(1)} %collective-permute-done.refs_1_, ...), custom_call_target="tpu_custom_call" | custom-call | flops 10350000128 | bytes 900000 | tf_op jit(solution)/shard_map/project_early/pallas_call | solution.py:168
  24.0 0.0 copy-start.10
  24.0 0.0 copy-start.9
  24.0 6.5 %all-to-all-start = ((bf16[32,16,1280]{2,1,0:T(8,128)(2,1)}), bf16[32,16,1280]{2,1,0:T(8,128)(2,1)S(1)}, u32[]{:S(2)}, u32[]{:S(2)}) async-start(bf16[32,16,1280]{2,1,0:T(8,128)(2,1)} %project_early.1), calls=%async_computation | async-start | bytes 2621440 | tf_op jit(solution)/shard_map/all_to_all | solution.py:563
  30.6 0.1 copy.32
  30.7 0.1 pad_add_fusion.2
  30.8 1.7 collective-permute-start.5
  32.5 0.0 collective-permute-start.4
  32.5 0.5 collective-permute-start.3
  33.0 2.9 %dynamic-slice_bitcast_fusion = (bf16[4,256,256]{2,1,0:T(8,128)(2,1)}, bf16[4,256,256]{2,1,0:T(8,128)(2,1)}, bf16[4,256,256]{2,1,0:T(8,128)(2,1)}, bf16[4,256,256]{2,1,0:T(8,128)(2,1)}) fusion(bf16[4,4,256,256]{3,2,1,0:T(8,128)(2,1)} %param.13, s32[]{:T(128)S(6)} %select_n.316, s32[]{:T(128)S(6)} %select_n.314, s32[]{:T(128)S(6)} %select_n.312, s32[]{:T(128)S(6)} %select_n.310), kind=kLoop, calls=%fused_computation.11 | loop fusion | bytes 4194320 | tf_op jit(solution)/shard_map/jit(dynamic_index_in_dim)/squeeze | solution.py:587
  36.0 1.3 collective-permute-start.6
  37.3 0.0 collective-permute-start.7
  37.3 0.0 collective-permute-done.5
  37.3 1.6 collective-permute-start.8
  38.9 0.0 collective-permute-done.4
  38.9 0.0 collective-permute-done.3
  38.9 0.6 pad_add_fusion.3.meta_ref
  39.5 6.1 %project_late.1 = bf16[32,16,768]{2,1,0:T(8,128)(2,1)} custom-call(s32[4096]{0:T(1024)S(1)} %reshape.195.idx_ref, bf16[32,64,256]{2,1,0:T(8,128)(2,1)S(1)} %copy-done, bf16[16,8192]{1,0:T(8,128)(2,1)S(1)} %get-tuple-element.50.refs_0_, bf16[16,8192]{1,0:T(8,128)(2,1)S(1)} %collective-permute-done.refs_1_, ...), custom_call_target="tpu_custom_call" | custom-call | flops 8049999872 | bytes 700000 | tf_op jit(solution)/shard_map/project_late/pallas_call | solution.py:168
  45.7 16.2 %all-to-all-done.sino_ref.early_ref = bf16[32,16,1280]{2,1,0:T(8,128)(2,1)S(1)} async-done(((bf16[32,16,1280]{2,1,0:T(8,128)(2,1)}), bf16[32,16,1280]{2,1,0:T(8,128)(2,1)S(1)}, u32[]{:S(2)}, u32[]{:S(2)}) %all-to-all-start) | async-done | bytes 1310752 | tf_op jit(solution)/shard_map/all_to_all | solution.py:563
  61.9 4.4 %all-to-all-start.1 = ((bf16[32,16,768]{2,1,0:T(8,128)(2,1)}), bf16[32,16,768]{2,1,0:T(8,128)(2,1)S(1)}, u32[]{:S(2)}, u32[]{:S(2)}) async-start(bf16[32,16,768]{2,1,0:T(8,128)(2,1)} %project_late.1), calls=%async_computation.1 | async-start | bytes 1572864 | tf_op jit(solution)/shard_map/all_to_all | solution.py:563
  66.3 0.0 collective-permute-done.6.refs_1_
  66.3 1.7 collective-permute-done.8.refs_1_
  68.0 9.9 %exit_first.1 = (f32[2,256,256]{2,1,0:T(8,128)}, bf16[32,16,768]{2,1,0:T(8,128)(2,1)}, f32[2,256,256]{2,1,0:T(8,128)}) custom-call(s32[4,5]{1,0:T(4,128)} %pad_add_fusion.3.meta_ref, bf16[2,256,256]{2,1,0:T(8,128)(2,1)} %probe_ref.3, bf16[512,512]{1,0:T(8,128)(2,1)} %constant.148.forward_ref, bf16[512,512]{1,0:T(8,128)(2,1)} %constant.151.inverse_ref, ...), custom_call_target="tpu_custom_call" | custom-call | flops 11500000256 | bytes 1000000 | tf_op jit(solution)/shard_map/exit_first/pallas_call | solution.py:498
  77.9 8.5 %all-to-all-done.1.late_ref = bf16[32,16,768]{2,1,0:T(8,128)(2,1)S(1)} async-done(((bf16[32,16,768]{2,1,0:T(8,128)(2,1)}), bf16[32,16,768]{2,1,0:T(8,128)(2,1)S(1)}, u32[]{:S(2)}, u32[]{:S(2)}) %all-to-all-start.1) | async-done | bytes 786464 | tf_op jit(solution)/shard_map/all_to_all | solution.py:563
  86.4 4.1 %all-to-all-start.2 = ((bf16[32,16,768]{2,1,0:T(8,128)(2,1)}), bf16[32,16,768]{2,1,0:T(8,128)(2,1)S(1)}, u32[]{:S(2)}, u32[]{:S(2)}) async-start(bf16[32,16,768]{2,1,0:T(8,128)(2,1)} %get-tuple-element.61), calls=%async_computation.2 | async-start | bytes 1572864 | tf_op jit(solution)/shard_map/all_to_all | solution.py:563
  90.5 1.1 slice.101
  91.6 1.7 collective-permute-start.9
  93.3 10.6 %exit_rest.1 = bf16[32,16,1280]{2,1,0:T(8,128)(2,1)} custom-call(s32[4,5]{1,0:T(4,128)} %pad_add_fusion.3.meta_ref, bf16[2,256,256]{2,1,0:T(8,128)(2,1)} %probe_ref.3, bf16[512,512]{1,0:T(8,128)(2,1)} %constant.148.forward_ref, bf16[512,512]{1,0:T(8,128)(2,1)} %constant.151.inverse_ref, bf16[32,16,1280]{2,1,0:T(8,128)(2,1)} %copy-done.3, ...), custom_call_target="tpu_custom_call" | custom-call | flops 11500000256 | bytes 1000000 | tf_op jit(solution)/shard_map/exit_rest/pallas_call | solution.py:514
  103.9 0.3 collective-permute-done.9
  104.2 6.5 %all-to-all-done.2.grad_ref = bf16[32,16,768]{2,1,0:T(8,128)(2,1)S(1)} async-done(((bf16[32,16,768]{2,1,0:T(8,128)(2,1)}), bf16[32,16,768]{2,1,0:T(8,128)(2,1)S(1)}, u32[]{:S(2)}, u32[]{:S(2)}) %all-to-all-start.2) | async-done | bytes 786464 | tf_op jit(solution)/shard_map/all_to_all | solution.py:563
  110.7 0.9 copy-done.5
  111.6 4.1 %all-to-all-start.3 = ((bf16[32,16,1280]{2,1,0:T(8,128)(2,1)}), bf16[32,16,1280]{2,1,0:T(8,128)(2,1)S(1)}, u32[]{:S(2)}, u32[]{:S(2)}) async-start(bf16[32,16,1280]{2,1,0:T(8,128)(2,1)} %exit_rest.1), calls=%async_computation.3 | async-start | bytes 2621440 | tf_op jit(solution)/shard_map/all_to_all | solution.py:563
  115.7 0.3 copy.22
  116.0 0.2 reshape.192
  116.4 0.7 reshape.193.idx_ref
  117.0 1.0 slice.105
  118.1 1.1 fusion.9
  119.2 1.4 collective-permute-start.13
  120.6 0.6 collective-permute-start.14
  121.2 7.2 %back_first.1.refs_0_ = f32[512,8,128]{2,1,0:T(8,128)} custom-call(s32[4096]{0:T(1024)} %reshape.193.idx_ref, bf16[32,64,256]{2,1,0:T(8,128)(2,1)} %radon_ref.7, bf16[32,16,768]{2,1,0:T(8,128)(2,1)} %copy-done.5), custom_call_target="tpu_custom_call" | custom-call | flops 8049999872 | bytes 700000 | tf_op jit(solution)/shard_map/back_first/pallas_call | solution.py:300
  128.4 18.6 %all-to-all-done.3.grad_ref = bf16[32,16,1280]{2,1,0:T(8,128)(2,1)S(1)} async-done(((bf16[32,16,1280]{2,1,0:T(8,128)(2,1)}), bf16[32,16,1280]{2,1,0:T(8,128)(2,1)S(1)}, u32[]{:S(2)}, u32[]{:S(2)}) %all-to-all-start.3) | async-done | bytes 1310752 | tf_op jit(solution)/shard_map/all_to_all | solution.py:563
  147.0 1.1 copy-done.4
  148.0 9.7 %back_rest.1 = (bf16[16,8192]{1,0:T(8,128)(2,1)}, bf16[16,8192]{1,0:T(8,128)(2,1)}, bf16[16,8192]{1,0:T(8,128)(2,1)}, bf16[16,8192]{1,0:T(8,128)(2,1)}) custom-call(s32[4096]{0:T(1024)} %reshape.193.idx_ref, bf16[32,64,256]{2,1,0:T(8,128)(2,1)} %radon_ref.7, bf16[32,16,1280]{2,1,0:T(8,128)(2,1)} %copy-done.4, f32[512,8,128]{2,1,0:T(8,128)} %back_first.1.refs_0_), custom_call_target="tpu_custom_call" | custom-call | flops 10350000128 | bytes 900000 | tf_op jit(solution)/shard_map/back_rest/pallas_call | solution.py:300
  157.8 1.9 %collective-permute-start.10 = (bf16[16,8192]{1,0:T(8,128)(2,1)}, bf16[16,8192]{1,0:T(8,128)(2,1)S(1)}, u32[]{:S(2)}, u32[]{:S(2)}) collective-permute-start(bf16[16,8192]{1,0:T(8,128)(2,1)} %get-tuple-element.69), channel_id=1, source_target_pairs={{0,1},{1,2},{2,3},{3,0},{4,5},{5,6},{6,7},{7,4},{8,9},{9,10},{10,1... | collective-permute-start | bytes 786440 | tf_op jit(solution)/shard_map/ppermute | solution.py:42
  159.7 0.7 collective-permute-start.11
  160.4 1.6 select_bitcast_fusion.3
  162.1 0.3 maximum_convert_fusion
  162.5 4.7 %copy.37 = f32[2,256,4,512]{3,2,1,0:T(4,128)} copy(f32[2,256,4,512]{3,1,0,2:T(8,128)S(1)} %maximum_convert_fusion) | data formatting | bytes 8388608
  167.2 4.9 %collective-permute-done.11 = bf16[16,8192]{1,0:T(8,128)(2,1)S(1)} collective-permute-done((bf16[16,8192]{1,0:T(8,128)(2,1)}, bf16[16,8192]{1,0:T(8,128)(2,1)S(1)}, u32[]{:S(2)}, u32[]{:S(2)}) %collective-permute-start.11) | collective-permute-done | bytes 262176 | tf_op jit(solution)/shard_map/ppermute | solution.py:42
  172.1 0.6 collective-permute-done.12
  172.7 0.1 select_bitcast_fusion.7
  172.8 1.6 multiply_add_fusion
  (46 shorter events, 0.4 us)
Async XLA Ops:
  0.6 4.6 %copy-start.8 = (s32[32,32,4]{1,2,0:T(4,128)S(1)}, s32[32,32,4]{1,2,0:T(4,128)}, u32[]{:S(2)}) copy-start(s32[32,32,4]{1,2,0:T(4,128)} %param.11) | copy-start | bytes 49156
  0.7 15.7 %copy-start = (bf16[32,64,256]{2,1,0:T(8,128)(2,1)S(1)}, bf16[32,64,256]{2,1,0:T(8,128)(2,1)}, u32[]{:S(2)}) copy-start(bf16[32,64,256]{2,1,0:T(8,128)(2,1)} %radon_ref.7) | copy-start | bytes 3145732
  2.1 8.2 %collective-permute-start = (bf16[16,8192]{1,0:T(8,128)(2,1)S(1)}, bf16[16,8192]{1,0:T(8,128)(2,1)S(1)}, u32[]{:S(2)}, u32[]{:S(2)}) collective-permute-start(bf16[16,8192]{1,0:T(8,128)(2,1)S(1)} %get-tuple-element.91), channel_id=1, source_target_pairs={{0,1},{1,2},{2,3},{3,0},{4,5},{5,6},{6,7},{7,4},{8,9},{9,10},{10,1... | collective-permute-start | bytes 786440 | tf_op jit(solution)/shard_map/ppermute | solution.py:42
  4.7 11.1 %collective-permute-start.1 = (bf16[16,8192]{1,0:T(8,128)(2,1)S(1)}, bf16[16,8192]{1,0:T(8,128)(2,1)S(1)}, u32[]{:S(2)}, u32[]{:S(2)}) collective-permute-start(bf16[16,8192]{1,0:T(8,128)(2,1)S(1)} %get-tuple-element.93), channel_id=1, source_target_pairs={{0,2},{1,3},{2,0},{3,1},{4,6},{5,7},{6,4},{7,5},{8,10},{9,11},{10,... | collective-permute-start | bytes 786440 | tf_op jit(solution)/shard_map/ppermute | solution.py:42
  4.7 11.6 %collective-permute-start.2 = (bf16[16,8192]{1,0:T(8,128)(2,1)S(1)}, bf16[16,8192]{1,0:T(8,128)(2,1)S(1)}, u32[]{:S(2)}, u32[]{:S(2)}) collective-permute-start(bf16[16,8192]{1,0:T(8,128)(2,1)S(1)} %get-tuple-element.90), channel_id=1, source_target_pairs={{0,3},{1,0},{2,1},{3,2},{4,7},{5,4},{6,5},{7,6},{8,11},{9,8},{10,9... | collective-permute-start | bytes 786440 | tf_op jit(solution)/shard_map/ppermute | solution.py:42
  24.0 6.6 %copy-start.10 = (s32[4,1]{0,1:T(1,128)S(1)}, s32[4,1]{0,1:T(1,128)}, u32[]{:S(2)}) copy-start(s32[4,1]{0,1:T(1,128)} %param.15) | copy-start | bytes 52
  24.0 6.7 %copy-start.9 = (s32[4,4]{1,0:T(4,128)S(1)}, s32[4,4]{1,0:T(4,128)}, u32[]{:S(2)}) copy-start(s32[4,4]{1,0:T(4,128)} %param.14) | copy-start | bytes 196
  24.0 37.9 %all-to-all-start = ((bf16[32,16,1280]{2,1,0:T(8,128)(2,1)}), bf16[32,16,1280]{2,1,0:T(8,128)(2,1)S(1)}, u32[]{:S(2)}, u32[]{:S(2)}) async-start(bf16[32,16,1280]{2,1,0:T(8,128)(2,1)} %project_early.1), calls=%async_computation | async-start | bytes 2621440 | tf_op jit(solution)/shard_map/all_to_all | solution.py:563
  30.8 6.5 %collective-permute-start.5 = (s32[1,5]{1,0:T(1,128)S(1)}, s32[1,5]{1,0:T(1,128)S(1)}, u32[]{:S(2)}, u32[]{:S(2)}) collective-permute-start(s32[1,5]{1,0:T(1,128)S(1)} %get-tuple-element.109), channel_id=1, source_target_pairs={{0,1},{1,2},{2,3},{3,0},{4,5},{5,6},{6,7},{7,4},{8,9},{9,10},{10,1... | collective-permute-start | bytes 68 | tf_op jit(solution)/shard_map/ppermute | solution.py:42
  32.5 6.4 %collective-permute-start.4 = (s32[1,5]{1,0:T(1,128)S(1)}, s32[1,5]{1,0:T(1,128)S(1)}, u32[]{:S(2)}, u32[]{:S(2)}) collective-permute-start(s32[1,5]{1,0:T(1,128)S(1)} %get-tuple-element.110), channel_id=1, source_target_pairs={{0,2},{1,3},{2,0},{3,1},{4,6},{5,7},{6,4},{7,5},{8,10},{9,11},{10,... | collective-permute-start | bytes 68 | tf_op jit(solution)/shard_map/ppermute | solution.py:42
  32.5 6.4 %collective-permute-start.3 = (s32[1,5]{1,0:T(1,128)S(1)}, s32[1,5]{1,0:T(1,128)S(1)}, u32[]{:S(2)}, u32[]{:S(2)}) collective-permute-start(s32[1,5]{1,0:T(1,128)S(1)} %get-tuple-element.111), channel_id=1, source_target_pairs={{0,3},{1,0},{2,1},{3,2},{4,7},{5,4},{6,5},{7,6},{8,11},{9,8},{10,9... | collective-permute-start | bytes 68 | tf_op jit(solution)/shard_map/ppermute | solution.py:42
  36.0 30.3 %collective-permute-start.6 = (bf16[4,256,256]{2,1,0:T(8,128)(2,1)}, bf16[4,256,256]{2,1,0:T(8,128)(2,1)}, u32[]{:S(2)}, u32[]{:S(2)}) collective-permute-start(bf16[4,256,256]{2,1,0:T(8,128)(2,1)} %get-tuple-element.82), channel_id=1, source_target_pairs={{0,3},{1,0},{2,1},{3,2},{4,7},{5,4},{6,5},{7,6},{8,11},{9,8},{10,9... | collective-permute-start | bytes 1572872 | tf_op jit(solution)/shard_map/ppermute | solution.py:42
  37.3 29.0 %collective-permute-start.7 = (bf16[4,256,256]{2,1,0:T(8,128)(2,1)}, bf16[4,256,256]{2,1,0:T(8,128)(2,1)}, u32[]{:S(2)}, u32[]{:S(2)}) collective-permute-start(bf16[4,256,256]{2,1,0:T(8,128)(2,1)} %get-tuple-element.81), channel_id=1, source_target_pairs={{0,2},{1,3},{2,0},{3,1},{4,6},{5,7},{6,4},{7,5},{8,10},{9,11},{10,... | collective-permute-start | bytes 1572872 | tf_op jit(solution)/shard_map/ppermute | solution.py:42
  37.3 30.7 %collective-permute-start.8 = (bf16[4,256,256]{2,1,0:T(8,128)(2,1)}, bf16[4,256,256]{2,1,0:T(8,128)(2,1)}, u32[]{:S(2)}, u32[]{:S(2)}) collective-permute-start(bf16[4,256,256]{2,1,0:T(8,128)(2,1)} %get-tuple-element.80), channel_id=1, source_target_pairs={{0,1},{1,2},{2,3},{3,0},{4,5},{5,6},{6,7},{7,4},{8,9},{9,10},{10,1... | collective-permute-start | bytes 1572872 | tf_op jit(solution)/shard_map/ppermute | solution.py:42
  61.9 6.1 %copy-start.3 = (bf16[32,16,1280]{2,1,0:T(8,128)(2,1)}, bf16[32,16,1280]{2,1,0:T(8,128)(2,1)S(1)}, u32[]{:S(2)}) copy-start(bf16[32,16,1280]{2,1,0:T(8,128)(2,1)S(1)} %all-to-all-done.sino_ref.early_ref) | copy-start | bytes 3932164
  61.9 24.5 %all-to-all-start.1 = ((bf16[32,16,768]{2,1,0:T(8,128)(2,1)}), bf16[32,16,768]{2,1,0:T(8,128)(2,1)S(1)}, u32[]{:S(2)}, u32[]{:S(2)}) async-start(bf16[32,16,768]{2,1,0:T(8,128)(2,1)} %project_late.1), calls=%async_computation.1 | async-start | bytes 1572864 | tf_op jit(solution)/shard_map/all_to_all | solution.py:563
  86.4 6.9 %copy-start.6 = (bf16[32,16,768]{2,1,0:T(8,128)(2,1)}, bf16[32,16,768]{2,1,0:T(8,128)(2,1)S(1)}, u32[]{:S(2)}) copy-start(bf16[32,16,768]{2,1,0:T(8,128)(2,1)S(1)} %all-to-all-done.1.late_ref) | copy-start | bytes 2359300
  86.4 24.2 %all-to-all-start.2 = ((bf16[32,16,768]{2,1,0:T(8,128)(2,1)}), bf16[32,16,768]{2,1,0:T(8,128)(2,1)S(1)}, u32[]{:S(2)}, u32[]{:S(2)}) async-start(bf16[32,16,768]{2,1,0:T(8,128)(2,1)} %get-tuple-element.61), calls=%async_computation.2 | async-start | bytes 1572864 | tf_op jit(solution)/shard_map/all_to_all | solution.py:563
  91.6 12.5 %collective-permute-start.9 = (bf16[32,16,512]{2,1,0:T(8,128)(2,1)S(1)}, bf16[32,16,512]{2,1,0:T(8,128)(2,1)}, u32[]{:S(2)}, u32[]{:S(2)}) collective-permute-start(bf16[32,16,512]{2,1,0:T(8,128)(2,1)S(1)} %slice.101), channel_id=1, source_target_pairs={{0,1},{1,2},{2,3},{3,0},{4,5},{5,6},{6,7},{7,4},{8,9},{9,10},{10,1... | collective-permute-start | bytes 1572872 | tf_op jit(solution)/shard_map/ppermute | solution.py:36
  103.9 14.1 %copy-start.1 = (bf16[32,16,1280]{2,1,0:T(8,128)(2,1)S(1)}, bf16[32,16,1280]{2,1,0:T(8,128)(2,1)}, u32[]{:S(2)}) copy-start(bf16[32,16,1280]{2,1,0:T(8,128)(2,1)} %exit_rest.1) | copy-start | bytes 3932164
  110.7 0.9 copy-start.5
  111.6 35.4 %all-to-all-start.3 = ((bf16[32,16,1280]{2,1,0:T(8,128)(2,1)}), bf16[32,16,1280]{2,1,0:T(8,128)(2,1)S(1)}, u32[]{:S(2)}, u32[]{:S(2)}) async-start(bf16[32,16,1280]{2,1,0:T(8,128)(2,1)} %exit_rest.1), calls=%async_computation.3 | async-start | bytes 2621440 | tf_op jit(solution)/shard_map/all_to_all | solution.py:563
  119.2 41.2 %collective-permute-start.13 = (bf16[32,16,512]{2,1,0:T(8,128)(2,1)}, bf16[32,16,512]{2,1,0:T(8,128)(2,1)S(1)}, u32[]{:S(2)}, u32[]{:S(2)}) collective-permute-start(bf16[32,16,512]{2,1,0:T(8,128)(2,1)} %get-tuple-element.85), channel_id=1, source_target_pairs={{0,2},{1,3},{2,0},{3,1},{4,6},{5,7},{6,4},{7,5},{8,10},{9,11},{10,... | collective-permute-start | bytes 1572872 | tf_op jit(solution)/shard_map/ppermute | solution.py:36
  120.6 39.8 %collective-permute-start.14 = (bf16[32,16,512]{2,1,0:T(8,128)(2,1)}, bf16[32,16,512]{2,1,0:T(8,128)(2,1)S(1)}, u32[]{:S(2)}, u32[]{:S(2)}) collective-permute-start(bf16[32,16,512]{2,1,0:T(8,128)(2,1)} %get-tuple-element.84), channel_id=1, source_target_pairs={{0,3},{1,0},{2,1},{3,2},{4,7},{5,4},{6,5},{7,6},{8,11},{9,8},{10,9... | collective-permute-start | bytes 1572872 | tf_op jit(solution)/shard_map/ppermute | solution.py:36
  147.0 1.1 copy-start.4
  157.8 9.5 %collective-permute-start.10 = (bf16[16,8192]{1,0:T(8,128)(2,1)}, bf16[16,8192]{1,0:T(8,128)(2,1)S(1)}, u32[]{:S(2)}, u32[]{:S(2)}) collective-permute-start(bf16[16,8192]{1,0:T(8,128)(2,1)} %get-tuple-element.69), channel_id=1, source_target_pairs={{0,1},{1,2},{2,3},{3,0},{4,5},{5,6},{6,7},{7,4},{8,9},{9,10},{10,1... | collective-permute-start | bytes 786440 | tf_op jit(solution)/shard_map/ppermute | solution.py:42
  159.7 12.4 %collective-permute-start.11 = (bf16[16,8192]{1,0:T(8,128)(2,1)}, bf16[16,8192]{1,0:T(8,128)(2,1)S(1)}, u32[]{:S(2)}, u32[]{:S(2)}) collective-permute-start(bf16[16,8192]{1,0:T(8,128)(2,1)} %get-tuple-element.70), channel_id=1, source_target_pairs={{0,2},{1,3},{2,0},{3,1},{4,6},{5,7},{6,4},{7,5},{8,10},{9,11},{10,... | collective-permute-start | bytes 786440 | tf_op jit(solution)/shard_map/ppermute | solution.py:42
  160.3 12.4 %collective-permute-start.12 = (bf16[16,8192]{1,0:T(8,128)(2,1)}, bf16[16,8192]{1,0:T(8,128)(2,1)S(1)}, u32[]{:S(2)}, u32[]{:S(2)}) collective-permute-start(bf16[16,8192]{1,0:T(8,128)(2,1)} %get-tuple-element.71), channel_id=1, source_target_pairs={{0,3},{1,0},{2,1},{3,2},{4,7},{5,4},{6,5},{7,6},{8,11},{9,8},{10,9... | collective-permute-start | bytes 786440 | tf_op jit(solution)/shard_map/ppermute | solution.py:42
  162.5 10.2 %copy-start.7 = (bf16[16,8192]{1,0:T(8,128)(2,1)S(1)}, bf16[16,8192]{1,0:T(8,128)(2,1)}, u32[]{:S(2)}) copy-start(bf16[16,8192]{1,0:T(8,128)(2,1)} %get-tuple-element.72) | copy-start | bytes 786436
  167.2 5.6 %copy-start.2 = (bf16[2,32,8192]{2,1,0:T(8,128)(2,1)S(1)}, bf16[2,32,8192]{2,1,0:T(8,128)(2,1)}, u32[]{:S(2)}) copy-start(bf16[2,32,8192]{2,1,0:T(8,128)(2,1)} %param.9) | copy-start | bytes 3145732
